TPU v7x, 32 devices: a whole 2x2x4 slice. The times are simulated.
32 devices in a mesh: tok: 4 (over y, x), gr: 2 (over core), gc: 4 (over z).
Axes of the slice: x: 2, y: 2, z: 4, core: 2. Of those that a mesh axis runs over, the one named last changes fastest.
Arguments:
- acts: bfloat16 [512, 16384], P('tok', ('gr', 'gc')), may hold values from -24 to 24
- init_basis: float32 [16, 1024, 512], P(('gr', 'gc'), 'tok'), may hold values from -6 to 6
- kept: int32 [16, 16], replicated, may hold values from 0 to 1, as said below
- member: int32 [16], replicated, may hold values from 0 to 1, as said below
Outputs:
- bases: float32 [16, 1024, 512], P(('gr', 'gc'), 'tok')
- latent: bfloat16 [512, 1024], P(('tok', 'gr', 'gc'))
Inputs may be any that keep to these rules, and one draw needn't show every extreme that they name: kept is symmetric with ones on the diagonal. `member`: each of the 2 group numbers names exactly 8 blocks.
All inputs are finite; a program needn't handle non-finite values.
Results may differ from a plain program's by a relative error of at most 0.0095.
Values may be sent and summed in bfloat16 or wider, within the bound.
No kernel may reach another device: no remote copies, remote signals or barrier semaphores. Data moves between devices by JAX's collectives and lax.ppermute only.
A program may use at most 64 MiB of HBM per device.

v0:
```python
import functools
import math

import jax
import jax.numpy as jnp
from jax import lax
from jax.experimental import pallas as pl
from jax.experimental.pallas import tpu as pltpu
from jax.sharding import PartitionSpec as P

GBLK = 8
PANEL = 128
SUB = 8
CHUNKS = 2

ridge = 2.0
HIGHEST = lax.Precision.HIGHEST
HIGH = lax.Precision.HIGH


def split(value):
    high = lax.reduce_precision(value, 8, 7)
    return high.astype(jnp.bfloat16), (value - high).astype(jnp.bfloat16)


def kernel_dot(left, right, exact):
    if exact:
        return jnp.dot(left, right, preferred_element_type=jnp.float32, precision=HIGHEST)
    parts = []
    for value in (left, right):
        high = value.astype(jnp.bfloat16)
        parts.append((high, (value - high.astype(jnp.float32)).astype(jnp.bfloat16)))
    (a, b), (c, d) = parts
    return sum(
        jnp.dot(x, y, preferred_element_type=jnp.float32) for x, y in ((b, c), (a, d), (a, c))
    )


def eliminate(tiles, inv_ref):
    shape = (SUB, PANEL)
    lane = lax.broadcasted_iota(jnp.int32, shape, 1)
    sub = lax.broadcasted_iota(jnp.int32, shape, 0)

    def spread(column):
        return jnp.broadcast_to(column, shape)

    tiles = list(tiles)
    for s in range(PANEL // SUB):
        start = s * SUB
        tile = tiles[s]
        inside = (lane >= start) & (lane < start + SUB)
        columns = [spread(tile[:, start + c : start + c + 1]) for c in range(SUB)]
        pivot = [
            [spread(columns[c][i : i + 1, :]) if c >= i else None for c in range(SUB)]
            for i in range(SUB)
        ]
        base = jnp.where(inside, jnp.where(lane == start + sub, 1.0, 0.0), tile)
        rows = [spread(base[i : i + 1, :]) for i in range(SUB)]
        below = [[None] * SUB for _ in range(SUB)]
        inverse = []
        for b in range(SUB):
            inverse.append(pl.reciprocal(pivot[b][b], approx=True))
            for i in range(b + 1, SUB):
                factor = pivot[b][i] * inverse[b]
                below[i][b] = factor
                for c in range(i, SUB):
                    pivot[i][c] = pivot[i][c] - factor * pivot[b][c]
                rows[i] = rows[i] - factor * rows[b]
        result = jnp.zeros(shape, jnp.float32)
        for b in range(SUB):
            result = jnp.where(sub == b, rows[b] * lax.rsqrt(pivot[b][b]), result)
        inv_ref[start : start + SUB, :] = jnp.where(lane < start + SUB, result, 0.0)
        solved = [None] * SUB
        for b in reversed(range(SUB)):
            value = rows[b] * inverse[b]
            for i in reversed(range(b + 1, SUB)):
                value = value - below[i][b] * solved[i]
            solved[b] = value
        for q in range(s + 1, PANEL // SUB):
            parts = [
                spread(tiles[q][:, start + b : start + b + 1]) * solved[b] for b in range(SUB)
            ]
            while len(parts) > 1:
                parts = [x + y for x, y in zip(parts[::2], parts[1::2])]
            tiles[q] = jnp.where(inside, 0.0, tiles[q]) - parts[0]


def factor_kernel(scale, exact, pos_ref, pieces_ref, out_ref, work_ref, inv_ref):
    tok_count, gc_count, rows, rank = pieces_ref.shape
    panels = rank // PANEL
    tok_pos, gc_pos = pos_ref[0], pos_ref[1]
    for k in range(tok_count):
        for i in range(gc_count):
            place = ((tok_pos ^ k) * gc_count + (gc_pos ^ i)) * rows
            work_ref[pl.ds(pl.multiple_of(place, SUB), rows), :] = pieces_ref[k, i] * scale

    def panel_step(k, carry):
        here = pl.ds(pl.multiple_of(k * PANEL, PANEL), PANEL)
        diag = work_ref[here, here]

        eliminate([diag[SUB * q : SUB * (q + 1), :] for q in range(PANEL // SUB)], inv_ref)
        for here_k in range(panels):

            @pl.when(k == here_k)
            def _():
                panel = slice(here_k * PANEL, (here_k + 1) * PANEL)
                rest = slice((here_k + 1) * PANEL, rank)
                inv = inv_ref[...]
                work_ref[panel, :] = kernel_dot(inv, work_ref[panel, :], exact)
                work_ref[panel, panel] = inv
                if here_k < panels - 1:
                    lower = work_ref[panel, rest].T
                    work_ref[rest, panel] = jnp.zeros((rank - rest.start, PANEL), jnp.float32)
                    work_ref[rest, :] -= kernel_dot(lower, work_ref[panel, :], exact)

        return carry

    lax.fori_loop(0, panels, panel_step, 0)
    for i in range(panels - 1):
        work_ref[i * PANEL : (i + 1) * PANEL, (i + 1) * PANEL :] = jnp.zeros(
            (PANEL, rank - (i + 1) * PANEL), jnp.float32
        )
    out_ref[...] = work_ref[...]


def inverse_factor(pieces, exact, scale):
    tok_count, gc_count, rows, rank = pieces.shape
    tok_pos, gc_pos = lax.axis_index("tok"), lax.axis_index("gc")
    if rows % SUB == 0:
        pos = jnp.stack([tok_pos, gc_pos]).astype(jnp.int32)
    else:
        pos = jnp.zeros((2,), jnp.int32)
        order = (
            (tok_pos ^ jnp.arange(tok_count, dtype=jnp.int32))[:, None] * gc_count
            + (gc_pos ^ jnp.arange(gc_count, dtype=jnp.int32))[None, :]
        ).reshape(-1)
        place = (order[:, None] * rows + jnp.arange(rows, dtype=jnp.int32)[None, :]).reshape(rank)
        full = jnp.zeros((rank, rank), jnp.float32).at[place].set(pieces.reshape(rank, rank))
        pieces = full.reshape(1, 1, rank, rank)
    return pl.pallas_call(
        functools.partial(factor_kernel, scale, exact),
        out_shape=jax.ShapeDtypeStruct((rank, rank), jnp.float32),
        in_specs=[
            pl.BlockSpec(memory_space=pltpu.SMEM),
            pl.BlockSpec(memory_space=pltpu.VMEM),
        ],
        out_specs=pl.BlockSpec(memory_space=pltpu.VMEM),
        scratch_shapes=[
            pltpu.VMEM((rank, rank), jnp.float32),
            pltpu.VMEM((PANEL, PANEL), jnp.float32),
        ],
        compiler_params=pltpu.CompilerParams(vmem_limit_bytes=32 * 1024 * 1024),
        cost_estimate=pl.CostEstimate(
            flops=96 * rank**3, bytes_accessed=8 * rank**2, transcendentals=0
        ),
        name="inverse_factor",
    )(pos, pieces)


def swap(value, axis, k):
    if k == 0:
        return value
    return lax.ppermute(value, axis, [(i, i ^ k) for i in range(lax.axis_size(axis))])


def collect(value, axis):
    return [swap(value, axis, k) for k in range(lax.axis_size(axis))]


def per_device(acts, init_basis, kept, member):
    owned = init_basis.shape[0]
    slice_rows = init_basis.shape[1]
    rank = init_basis.shape[2]
    tok_count = lax.axis_size("tok")
    gr_count = lax.axis_size("gr")
    gc_count = lax.axis_size("gc")
    block_cols = slice_rows * tok_count
    tok_rows = acts.shape[0]
    total_tokens = tok_rows * tok_count
    groups = kept.shape[0] // GBLK
    assert groups == gr_count == 2
    group_cols = GBLK * block_cols
    own_cols = rank // tok_count
    tok_pos = lax.axis_index("tok")
    gr_pos = lax.axis_index("gr")
    gc_pos = lax.axis_index("gc")
    first = (gr_pos * gc_count + gc_pos) * owned
    links = ((member[:, None] == member[None, :]).astype(jnp.int32) * kept).astype(jnp.float32)
    own_links = lax.dynamic_slice_in_dim(links, first, owned, 0)
    partner = ((gr_pos ^ 1) * gc_count + gc_pos) * owned
    partner_links = lax.dynamic_slice_in_dim(links, partner, owned, 0)
    own_groups = lax.dynamic_slice_in_dim(member, first, owned, 0)

    own_x = acts.reshape(tok_rows, owned, block_cols)
    turned_x = jnp.concatenate(
        [
            lax.dynamic_slice_in_dim(own_x, (tok_pos ^ k) * slice_rows, slice_rows, 2)
            for k in range(tok_count)
        ],
        axis=2,
    )
    init_bf = init_basis.astype(jnp.bfloat16)
    width = rank // CHUNKS
    init_pieces = [
        collect(init_bf[:, :, c * width : (c + 1) * width], "tok") for c in range(CHUNKS)
    ]
    init_pieces[-1], acts_late = lax.optimization_barrier((init_pieces[-1], acts))
    x_pieces = collect(acts_late, "tok")

    def combine(rows_of_links, pieces, sources):
        total = 0.0
        for piece, source in zip(pieces, sources):
            weights = lax.dynamic_slice_in_dim(rows_of_links, source, owned, 1)
            for j in range(owned):
                total += weights[:, j][:, None, None] * piece[j][None].astype(jnp.float32)
        return total

    near = []
    for part in init_pieces:
        proj = jnp.einsum(
            "tob,obr->otr",
            turned_x,
            jnp.concatenate(part, axis=1),
            preferred_element_type=jnp.float32,
        ).astype(jnp.bfloat16)
        near.append(collect(proj, "gc"))
    near, x_pieces = lax.optimization_barrier((near, x_pieces))
    full_x = jnp.concatenate(x_pieces, axis=0).reshape(total_tokens, owned, block_cols)
    basis_bf = jnp.concatenate(
        [
            jnp.concatenate(
                [lax.select_n(tok_pos ^ a, *part) for a in range(tok_count)], axis=1
            )
            for part in init_pieces
        ],
        axis=2,
    )
    sources = [(gr_pos * gc_count + (gc_pos ^ b)) * owned for b in range(gc_count)]
    own_part = [combine(own_links, pieces, sources) for pieces in near]
    other_part = [combine(partner_links, pieces, sources) for pieces in near]
    mixed = jnp.concatenate(
        [own + swap(other, "gr", 1) for own, other in zip(own_part, other_part)], axis=2
    ).astype(jnp.bfloat16)

    def image_of(mixed, basis_bf):
        full = jnp.concatenate(collect(mixed, "tok"), axis=1)
        cover = jnp.einsum("tob,otr->obr", full_x, full, preferred_element_type=jnp.float32)
        return cover / total_tokens + ridge * basis_bf.astype(jnp.float32)

    def seen_by(image):
        return sum(
            jnp.einsum("tob,obr->otr", own_x, part, preferred_element_type=jnp.float32)
            for part in split(image)
        )

    def factor(image, last):
        precision = HIGHEST if last else HIGH
        own = lax.dynamic_slice_in_dim(image, tok_pos * own_cols, own_cols, 2)
        grams = jnp.einsum("obr,obs->ors", own, image, precision=precision)

        def group_sum(g):
            mask = (own_groups == g).astype(jnp.float32)
            return jnp.sum(mask[:, None, None] * grams, axis=0)

        total = group_sum(gr_pos) + swap(group_sum(gr_pos ^ 1), "gr", 1)
        rows = own_cols // gc_count

        def rows_of(i):
            return lax.dynamic_slice_in_dim(total, (gc_pos ^ i) * rows, rows, 0)

        piece = sum(swap(rows_of(i), "gc", i) for i in range(gc_count))
        rows_near = jnp.stack(collect(piece, "gc"))
        pieces = jnp.stack(collect(rows_near, "tok"))
        own = inverse_factor(pieces, last, 1.0 / group_cols)
        other = swap(own, "gr", 1)
        of_block = jnp.stack(
            [jnp.where(own_groups[o] == gr_pos, own, other) for o in range(owned)]
        )
        of_group = [jnp.where(gr_pos == g, own, other) for g in range(groups)]
        return of_block, of_group

    image = image_of(mixed, basis_bf)
    seen = lax.all_gather(seen_by(image), ("gr", "gc"), axis=0, tiled=True)
    second = 0.0
    for j in range(seen.shape[0]):
        second += own_links[:, j][:, None, None] * seen[j][None]
    of_block, _ = factor(image, False)
    mixed = jnp.einsum("otr,osr->ots", second, of_block, precision=HIGH).astype(jnp.bfloat16)
    basis_bf = jnp.einsum("obr,osr->obs", image, of_block, precision=HIGH).astype(jnp.bfloat16)
    image = image_of(mixed, basis_bf)
    of_block, of_group = factor(image, True)
    rows = lax.dynamic_slice_in_dim(image, tok_pos * slice_rows, slice_rows, 1)
    basis = jnp.einsum("obr,osr->obs", rows, of_block, precision=HIGH)
    codes = seen_by(image)
    placed = jnp.concatenate(
        [
            jnp.sum((own_groups == g).astype(jnp.float32)[:, None, None] * codes, axis=0)
            for g in range(groups)
        ],
        axis=1,
    )
    placed = lax.psum_scatter(placed, ("gr", "gc"), scatter_dimension=0, tiled=True)
    latent = jnp.concatenate(
        [
            jnp.einsum(
                "tr,sr->ts",
                placed[:, g * rank : (g + 1) * rank],
                of_group[g],
                precision=HIGH,
            )
            for g in range(groups)
        ],
        axis=1,
    )
    latent = latent * (1.0 / math.sqrt(group_cols))
    return (basis, latent.astype(jnp.bfloat16))


def solution(mesh):
    placed = (P("tok", ("gr", "gc")), P(("gr", "gc"), "tok", None), P(), P())
    return jax.shard_map(
        per_device,
        mesh=mesh,
        in_specs=placed,
        out_specs=(P(("gr", "gc"), "tok", None), P(("tok", "gr", "gc"), None)),
        check_vma=False,
    )
```

profile of v0, /device:TPU:0, one launch (start us, length us, event | category | flops | bytes accessed | tf_op | source)
XLA Modules:
  0.0 270.0 jit_solution(6814266693639977795)
XLA Ops:
  9.3 2.9 %collective-permute-start.6 = (bf16[2,256,256]{2,1,0:T(8,128)(2,1)S(1)}, bf16[2,256,256]{2,1,0:T(8,128)(2,1)S(1)}, u32[]{:S(2)}, u32[]{:S(2)}) collective-permute-start(bf16[2,256,256]{2,1,0:T(8,128)(2,1)S(1)} %get-tuple-element.19), channel_id=1, source_target_pairs={{0,8},{8,0},{16,24},{24,16},{1,9},{9,1},{17,25},{25,17},{2,10},{10... | collective-permute-start | bytes 786440 | tf_op jit(solution)/shard_map/ppermute | solution.py:163
  23.9 3.2 %collective-permute-done.7 = bf16[2,256,256]{2,1,0:T(8,128)(2,1)S(1)} collective-permute-done((bf16[2,256,256]{2,1,0:T(8,128)(2,1)S(1)}, bf16[2,256,256]{2,1,0:T(8,128)(2,1)S(1)}, u32[]{:S(2)}, u32[]{:S(2)}) %collective-permute-start.7) | collective-permute-done | bytes 262176 | tf_op jit(solution)/shard_map/ppermute | solution.py:163
  34.2 3.2 %collective-permute-done.1 = bf16[2,256,256]{2,1,0:T(8,128)(2,1)S(1)} collective-permute-done((bf16[2,256,256]{2,1,0:T(8,128)(2,1)}, bf16[2,256,256]{2,1,0:T(8,128)(2,1)S(1)}, u32[]{:S(2)}, u32[]{:S(2)}) %collective-permute-start.1) | collective-permute-done | bytes 262176 | tf_op jit(solution)/shard_map/ppermute | solution.py:163
  45.6 3.3 %collective-permute-done.9 = bf16[2,128,256]{2,1,0:T(8,128)(2,1)S(1)} collective-permute-done((bf16[2,128,256]{2,1,0:T(8,128)(2,1)}, bf16[2,128,256]{2,1,0:T(8,128)(2,1)S(1)}, u32[]{:S(2)}, u32[]{:S(2)}) %collective-permute-start.9) | collective-permute-done | bytes 131104 | tf_op jit(solution)/shard_map/ppermute | solution.py:163
  76.7 6.3 %collective-permute-done.18 = bf16[2,128,512]{2,1,0:T(8,128)(2,1)} collective-permute-done((bf16[2,128,512]{2,1,0:T(8,128)(2,1)}, bf16[2,128,512]{2,1,0:T(8,128)(2,1)}, u32[]{:S(2)}, u32[]{:S(2)}) %collective-permute-start.18) | collective-permute-done | bytes 262176 | tf_op jit(solution)/shard_map/ppermute | solution.py:163
  83.0 3.5 %multiply_add_fusion.1 = f32[2,1024,512]{2,1,0:T(8,128)S(1)} fusion(bf16[2,256,256]{2,1,0:T(8,128)(2,1)S(1)} %copy-done.17, bf16[2,256,256]{2,1,0:T(8,128)(2,1)} %get-tuple-element.102, bf16[2,256,256]{2,1,0:T(8,128)(2,1)} %get-tuple-element.103, bf16[2,256,256]{2,1,0:T(8,128)(2,1)S(1)} %copy-done.16, bf16[2,256,256]{2,1,0:T(8,128)(2,1)} %get-tuple-element.97, ...), kind=kOutput, calls=%fused_computation.7 | convolution fusion | flops 1098907648 | bytes 9437184 | tf_op jit(solution)/shard_map/tob,otr->obr/dot_general | solution.py:247
  90.6 3.9 %multiply_reduce_fusion.4 = (f32[128,512]{1,0:T(8,128)S(1)}, f32[128,512]{1,0:T(8,128)S(1)}) fusion(f32[2]{0:T(128)S(1)} %get-tuple-element.145, f32[2]{0:T(128)S(1)} %get-tuple-element.146, f32[2,1024,512]{2,1,0:T(8,128)} %copy-done, s32[]{:T(128)S(6)} %select_n.337), kind=kOutput, calls=%fused_computation.78 | convolution fusion | flops 805699584 | bytes 5767188 | tf_op jit(solution)/shard_map/obr,obs->ors/dot_general | solution.py:259
  97.7 3.0 %collective-permute-start.22 = (f32[32,512]{1,0:T(8,128)S(1)}, f32[32,512]{1,0:T(8,128)S(1)}, u32[]{:S(2)}, u32[]{:S(2)}) collective-permute-start(f32[32,512]{1,0:T(8,128)S(1)} %get-tuple-element.119), channel_id=1, source_target_pairs={{0,2},{1,3},{2,0},{3,1},{4,6},{5,7},{6,4},{7,5},{8,10},{9,11},{10,... | collective-permute-start | bytes 196616 | tf_op jit(solution)/shard_map/ppermute | solution.py:163
  100.8 7.4 %collective-permute-done.22 = f32[32,512]{1,0:T(8,128)S(1)} collective-permute-done((f32[32,512]{1,0:T(8,128)S(1)}, f32[32,512]{1,0:T(8,128)S(1)}, u32[]{:S(2)}, u32[]{:S(2)}) %collective-permute-start.22) | collective-permute-done | bytes 65568 | tf_op jit(solution)/shard_map/ppermute | solution.py:163
  108.7 6.3 %collective-permute-start.24 = (f32[32,512]{1,0:T(8,128)S(1)}, f32[32,512]{1,0:T(8,128)S(1)}, u32[]{:S(2)}, u32[]{:S(2)}) collective-permute-start(f32[32,512]{1,0:T(8,128)S(1)} %add_add_fusion.1), channel_id=1, source_target_pairs={{0,1},{1,0},{2,3},{3,2},{4,5},{5,4},{6,7},{7,6},{8,9},{9,8},{10,11... | collective-permute-start | bytes 196616 | tf_op jit(solution)/shard_map/ppermute | solution.py:163
  118.4 4.1 %collective-permute-done.24 = f32[32,512]{1,0:T(8,128)S(1)} collective-permute-done((f32[32,512]{1,0:T(8,128)S(1)}, f32[32,512]{1,0:T(8,128)S(1)}, u32[]{:S(2)}, u32[]{:S(2)}) %collective-permute-start.24) | collective-permute-done | bytes 65568 | tf_op jit(solution)/shard_map/ppermute | solution.py:163
  125.2 2.9 %collective-permute-done.26 = f32[32,512]{1,0:T(8,128)S(1)} collective-permute-done((f32[32,512]{1,0:T(8,128)S(1)}, f32[32,512]{1,0:T(8,128)S(1)}, u32[]{:S(2)}, u32[]{:S(2)}) %collective-permute-start.26) | collective-permute-done | bytes 65568 | tf_op jit(solution)/shard_map/ppermute | solution.py:163
  131.8 5.7 %collective-permute-done.27 = f32[4,32,512]{2,1,0:T(8,128)S(1)} collective-permute-done((f32[4,32,512]{2,1,0:T(8,128)S(1)}, f32[4,32,512]{2,1,0:T(8,128)S(1)}, u32[]{:S(2)}, u32[]{:S(2)}) %collective-permute-start.27) | collective-permute-done | bytes 262176 | tf_op jit(solution)/shard_map/ppermute | solution.py:163
  137.4 5.4 %collective-permute-done.28 = f32[4,32,512]{2,1,0:T(8,128)S(1)} collective-permute-done((f32[4,32,512]{2,1,0:T(8,128)S(1)}, f32[4,32,512]{2,1,0:T(8,128)S(1)}, u32[]{:S(2)}, u32[]{:S(2)}) %collective-permute-start.28) | collective-permute-done | bytes 262176 | tf_op jit(solution)/shard_map/ppermute | solution.py:163
  142.9 21.4 %inverse_factor.2 = f32[512,512]{1,0:T(8,128)S(1)} custom-call(s32[2]{0:T(128)S(1)} %pad_add_fusion.pos_ref, f32[4,4,32,512]{3,2,1,0:T(8,128)S(1)} %pad_maximum_fusion.6.pieces_ref), custom_call_target="tpu_custom_call" | custom-call | flops 12884901888 | bytes 2097152 | tf_op jit(solution)/shard_map/inverse_factor/pallas_call | solution.py:140
  177.7 4.0 %fusion.12 = bf16[2,1024,512]{2,1,0:T(8,128)(2,1)S(1)} fusion(f32[2,1024,512]{2,1,0:T(8,128)S(1)} %copy-done.1, f32[1,512,512]{2,1,0:T(8,128)S(1)} %copy-done.3, f32[1,512,512]{2,1,0:T(8,128)S(1)} %get-tuple-element.94), kind=kOutput, calls=%fused_computation.18 | convolution fusion | flops 3221749760 | bytes 8388608 | tf_op jit(solution)/shard_map/obr,osr->obs/dot_general | solution.py:289
  183.4 4.9 %collective-permute-done.32 = bf16[2,128,512]{2,1,0:T(8,128)(2,1)S(1)} collective-permute-done((bf16[2,128,512]{2,1,0:T(8,128)(2,1)S(1)}, bf16[2,128,512]{2,1,0:T(8,128)(2,1)S(1)}, u32[]{:S(2)}, u32[]{:S(2)}) %collective-permute-start.32) | collective-permute-done | bytes 262176 | tf_op jit(solution)/shard_map/ppermute | solution.py:163
  194.1 5.0 %collective-permute-start.35 = (f32[32,512]{1,0:T(8,128)S(1)}, f32[32,512]{1,0:T(8,128)S(1)}, u32[]{:S(2)}, u32[]{:S(2)}) collective-permute-start(f32[32,512]{1,0:T(8,128)S(1)} %get-tuple-element.112), channel_id=1, source_target_pairs={{0,1},{1,0},{2,3},{3,2},{4,5},{5,4},{6,7},{7,6},{8,9},{9,8},{10,11... | collective-permute-start | bytes 196616 | tf_op jit(solution)/shard_map/ppermute | solution.py:163
  204.3 3.8 %collective-permute-done.37 = f32[32,512]{1,0:T(8,128)S(1)} collective-permute-done((f32[32,512]{1,0:T(8,128)S(1)}, f32[32,512]{1,0:T(8,128)S(1)}, u32[]{:S(2)}, u32[]{:S(2)}) %collective-permute-start.37) | collective-permute-done | bytes 65568 | tf_op jit(solution)/shard_map/ppermute | solution.py:163
  213.6 4.2 %collective-permute-done.39 = f32[32,512]{1,0:T(8,128)S(1)} collective-permute-done((f32[32,512]{1,0:T(8,128)S(1)}, f32[32,512]{1,0:T(8,128)S(1)}, u32[]{:S(2)}, u32[]{:S(2)}) %collective-permute-start.39) | collective-permute-done | bytes 65568 | tf_op jit(solution)/shard_map/ppermute | solution.py:163
  223.4 3.8 %collective-permute-done.41 = f32[4,32,512]{2,1,0:T(8,128)S(1)} collective-permute-done((f32[4,32,512]{2,1,0:T(8,128)S(1)}, f32[4,32,512]{2,1,0:T(8,128)S(1)}, u32[]{:S(2)}, u32[]{:S(2)}) %collective-permute-start.41) | collective-permute-done | bytes 262176 | tf_op jit(solution)/shard_map/ppermute | solution.py:163
  227.2 4.6 %collective-permute-done.42 = f32[4,32,512]{2,1,0:T(8,128)S(1)} collective-permute-done((f32[4,32,512]{2,1,0:T(8,128)S(1)}, f32[4,32,512]{2,1,0:T(8,128)S(1)}, u32[]{:S(2)}, u32[]{:S(2)}) %collective-permute-start.42) | collective-permute-done | bytes 262176 | tf_op jit(solution)/shard_map/ppermute | solution.py:163
  231.9 22.4 %inverse_factor.3 = f32[512,512]{1,0:T(8,128)S(1)} custom-call(s32[2]{0:T(128)S(1)} %pad_add_fusion.pos_ref, f32[4,4,32,512]{3,2,1,0:T(8,128)S(1)} %pad_maximum_fusion.7.pieces_ref), custom_call_target="tpu_custom_call" | custom-call | flops 12884901888 | bytes 2097152 | tf_op jit(solution)/shard_map/inverse_factor/pallas_call | solution.py:140
  259.8 3.4 %fusion.8 = f32[2,256,512]{2,1,0:T(8,128)} fusion(f32[1,512,512]{2,1,0:T(8,128)S(1)} %get-tuple-element.93, f32[1,512,512]{2,1,0:T(8,128)S(1)} %get-tuple-element.92, f32[2,1024,512]{2,1,0:T(8,128)} %copy-done.2, s32[]{:T(128)S(6)} %select_n.274), kind=kOutput, calls=%fused_computation.14 | convolution fusion | flops 805830656 | bytes 4194308 | tf_op jit(solution)/shard_map/obr,osr->obs/dot_general | solution.py:293
  (221 shorter events, 115.2 us)
Async XLA Ops:
  7.2 162.4 %all-gather.2.cloned.1.call-start = ((), (), s32[]{:S(2)}) async-start(), calls=%async_computation.1 | async-start | bytes 4718592 | tf_op jit(solution)/shard_map/all_gather | solution.py:283
  9.3 11.2 %collective-permute-start.6 = (bf16[2,256,256]{2,1,0:T(8,128)(2,1)S(1)}, bf16[2,256,256]{2,1,0:T(8,128)(2,1)S(1)}, u32[]{:S(2)}, u32[]{:S(2)}) collective-permute-start(bf16[2,256,256]{2,1,0:T(8,128)(2,1)S(1)} %get-tuple-element.19), channel_id=1, source_target_pairs={{0,8},{8,0},{16,24},{24,16},{1,9},{9,1},{17,25},{25,17},{2,10},{10... | collective-permute-start | bytes 786440 | tf_op jit(solution)/shard_map/ppermute | solution.py:163
  12.3 14.8 %collective-permute-start.7 = (bf16[2,256,256]{2,1,0:T(8,128)(2,1)S(1)}, bf16[2,256,256]{2,1,0:T(8,128)(2,1)S(1)}, u32[]{:S(2)}, u32[]{:S(2)}) collective-permute-start(bf16[2,256,256]{2,1,0:T(8,128)(2,1)S(1)} %get-tuple-element.19), channel_id=1, source_target_pairs={{0,16},{8,24},{16,0},{24,8},{1,17},{9,25},{17,1},{25,9},{2,18},{10... | collective-permute-start | bytes 786440 | tf_op jit(solution)/shard_map/ppermute | solution.py:163
  13.8 13.3 %collective-permute-start.8 = (bf16[2,256,256]{2,1,0:T(8,128)(2,1)S(1)}, bf16[2,256,256]{2,1,0:T(8,128)(2,1)}, u32[]{:S(2)}, u32[]{:S(2)}) collective-permute-start(bf16[2,256,256]{2,1,0:T(8,128)(2,1)S(1)} %get-tuple-element.19), channel_id=1, source_target_pairs={{0,24},{8,16},{16,8},{24,0},{1,25},{9,17},{17,9},{25,1},{2,26},{10... | collective-permute-start | bytes 786440 | tf_op jit(solution)/shard_map/ppermute | solution.py:163
  13.8 19.4 %collective-permute-start = (bf16[2,256,256]{2,1,0:T(8,128)(2,1)}, bf16[2,256,256]{2,1,0:T(8,128)(2,1)S(1)}, u32[]{:S(2)}, u32[]{:S(2)}) collective-permute-start(bf16[2,256,256]{2,1,0:T(8,128)(2,1)} %get-tuple-element.105), channel_id=1, source_target_pairs={{0,8},{8,0},{16,24},{24,16},{1,9},{9,1},{17,25},{25,17},{2,10},{10... | collective-permute-start | bytes 786440 | tf_op jit(solution)/shard_map/ppermute | solution.py:163
  15.7 21.6 %collective-permute-start.1 = (bf16[2,256,256]{2,1,0:T(8,128)(2,1)}, bf16[2,256,256]{2,1,0:T(8,128)(2,1)S(1)}, u32[]{:S(2)}, u32[]{:S(2)}) collective-permute-start(bf16[2,256,256]{2,1,0:T(8,128)(2,1)} %get-tuple-element.105), channel_id=1, source_target_pairs={{0,16},{8,24},{16,0},{24,8},{1,17},{9,25},{17,1},{25,9},{2,18},{10... | collective-permute-start | bytes 786440 | tf_op jit(solution)/shard_map/ppermute | solution.py:163
  20.5 19.2 %collective-permute-start.2 = (bf16[2,256,256]{2,1,0:T(8,128)(2,1)}, bf16[2,256,256]{2,1,0:T(8,128)(2,1)S(1)}, u32[]{:S(2)}, u32[]{:S(2)}) collective-permute-start(bf16[2,256,256]{2,1,0:T(8,128)(2,1)} %get-tuple-element.105), channel_id=1, source_target_pairs={{0,24},{8,16},{16,8},{24,0},{1,25},{9,17},{17,9},{25,1},{2,26},{10... | collective-permute-start | bytes 786440 | tf_op jit(solution)/shard_map/ppermute | solution.py:163
  29.2 12.7 %collective-permute-start.10 = (bf16[2,128,256]{2,1,0:T(8,128)(2,1)}, bf16[2,128,256]{2,1,0:T(8,128)(2,1)S(1)}, u32[]{:S(2)}, u32[]{:S(2)}) collective-permute-start(bf16[2,128,256]{2,1,0:T(8,128)(2,1)} %convolution_convert_fusion), channel_id=1, source_target_pairs={{0,2},{1,3},{2,0},{3,1},{4,6},{5,7},{6,4},{7,5},{8,10},{9,11},{10,... | collective-permute-start | bytes 393224 | tf_op jit(solution)/shard_map/ppermute | solution.py:163
  31.8 12.1 %collective-permute-start.11 = (bf16[2,128,256]{2,1,0:T(8,128)(2,1)}, bf16[2,128,256]{2,1,0:T(8,128)(2,1)}, u32[]{:S(2)}, u32[]{:S(2)}) collective-permute-start(bf16[2,128,256]{2,1,0:T(8,128)(2,1)} %convolution_convert_fusion), channel_id=1, source_target_pairs={{0,3},{1,2},{2,1},{3,0},{4,7},{5,6},{6,5},{7,4},{8,11},{9,10},{10,... | collective-permute-start | bytes 393224 | tf_op jit(solution)/shard_map/ppermute | solution.py:163
  33.2 24.9 %collective-permute-start.12 = (bf16[128,2048]{1,0:T(8,128)(2,1)S(1)}, bf16[128,2048]{1,0:T(8,128)(2,1)S(1)}, u32[]{:S(2)}, u32[]{:S(2)}) collective-permute-start(bf16[128,2048]{1,0:T(8,128)(2,1)S(1)} %copy-done.5), channel_id=1, source_target_pairs={{0,8},{8,0},{16,24},{24,16},{1,9},{9,1},{17,25},{25,17},{2,10},{10... | collective-permute-start | bytes 1572872 | tf_op jit(solution)/shard_map/ppermute | solution.py:163
  37.3 22.0 %collective-permute-start.13 = (bf16[128,2048]{1,0:T(8,128)(2,1)S(1)}, bf16[128,2048]{1,0:T(8,128)(2,1)S(1)}, u32[]{:S(2)}, u32[]{:S(2)}) collective-permute-start(bf16[128,2048]{1,0:T(8,128)(2,1)S(1)} %copy-done.5), channel_id=1, source_target_pairs={{0,16},{8,24},{16,0},{24,8},{1,17},{9,25},{17,1},{25,9},{2,18},{10... | collective-permute-start | bytes 1572872 | tf_op jit(solution)/shard_map/ppermute | solution.py:163
  39.7 19.7 %collective-permute-start.14 = (bf16[128,2048]{1,0:T(8,128)(2,1)S(1)}, bf16[128,2048]{1,0:T(8,128)(2,1)}, u32[]{:S(2)}, u32[]{:S(2)}) collective-permute-start(bf16[128,2048]{1,0:T(8,128)(2,1)S(1)} %copy-done.5), channel_id=1, source_target_pairs={{0,24},{8,16},{16,8},{24,0},{1,25},{9,17},{17,9},{25,1},{2,26},{10... | collective-permute-start | bytes 1572872 | tf_op jit(solution)/shard_map/ppermute | solution.py:163
  68.7 14.2 %collective-permute-start.18 = (bf16[2,128,512]{2,1,0:T(8,128)(2,1)}, bf16[2,128,512]{2,1,0:T(8,128)(2,1)}, u32[]{:S(2)}, u32[]{:S(2)}) collective-permute-start(bf16[2,128,512]{2,1,0:T(8,128)(2,1)} %pad_maximum_fusion.10), channel_id=1, source_target_pairs={{0,16},{8,24},{16,0},{24,8},{1,17},{9,25},{17,1},{25,9},{2,18},{10... | collective-permute-start | bytes 786440 | tf_op jit(solution)/shard_map/ppermute | solution.py:163
  70.7 12.3 %collective-permute-start.19 = (bf16[2,128,512]{2,1,0:T(8,128)(2,1)}, bf16[2,128,512]{2,1,0:T(8,128)(2,1)}, u32[]{:S(2)}, u32[]{:S(2)}) collective-permute-start(bf16[2,128,512]{2,1,0:T(8,128)(2,1)} %pad_maximum_fusion.10), channel_id=1, source_target_pairs={{0,24},{8,16},{16,8},{24,0},{1,25},{9,17},{17,9},{25,1},{2,26},{10... | collective-permute-start | bytes 786440 | tf_op jit(solution)/shard_map/ppermute | solution.py:163
  90.3 165.3 %reduce-scatter.4.cloned.1.call-start = ((), (), s32[]{:S(2)}) async-start(), calls=%async_computation.2 | async-start | bytes 589824
  97.7 10.5 %collective-permute-start.22 = (f32[32,512]{1,0:T(8,128)S(1)}, f32[32,512]{1,0:T(8,128)S(1)}, u32[]{:S(2)}, u32[]{:S(2)}) collective-permute-start(f32[32,512]{1,0:T(8,128)S(1)} %get-tuple-element.119), channel_id=1, source_target_pairs={{0,2},{1,3},{2,0},{3,1},{4,6},{5,7},{6,4},{7,5},{8,10},{9,11},{10,... | collective-permute-start | bytes 196616 | tf_op jit(solution)/shard_map/ppermute | solution.py:163
  108.7 13.8 %collective-permute-start.24 = (f32[32,512]{1,0:T(8,128)S(1)}, f32[32,512]{1,0:T(8,128)S(1)}, u32[]{:S(2)}, u32[]{:S(2)}) collective-permute-start(f32[32,512]{1,0:T(8,128)S(1)} %add_add_fusion.1), channel_id=1, source_target_pairs={{0,1},{1,0},{2,3},{3,2},{4,5},{5,4},{6,7},{7,6},{8,9},{9,8},{10,11... | collective-permute-start | bytes 196616 | tf_op jit(solution)/shard_map/ppermute | solution.py:163
  117.0 11.0 %collective-permute-start.26 = (f32[32,512]{1,0:T(8,128)S(1)}, f32[32,512]{1,0:T(8,128)S(1)}, u32[]{:S(2)}, u32[]{:S(2)}) collective-permute-start(f32[32,512]{1,0:T(8,128)S(1)} %add_add_fusion.1), channel_id=1, source_target_pairs={{0,3},{1,2},{2,1},{3,0},{4,7},{5,6},{6,5},{7,4},{8,11},{9,10},{10,... | collective-permute-start | bytes 196616 | tf_op jit(solution)/shard_map/ppermute | solution.py:163
  130.0 12.8 %collective-permute-start.28 = (f32[4,32,512]{2,1,0:T(8,128)S(1)}, f32[4,32,512]{2,1,0:T(8,128)S(1)}, u32[]{:S(2)}, u32[]{:S(2)}) collective-permute-start(f32[4,32,512]{2,1,0:T(8,128)S(1)} %get-tuple-element.116), channel_id=1, source_target_pairs={{0,16},{8,24},{16,0},{24,8},{1,17},{9,25},{17,1},{25,9},{2,18},{10... | collective-permute-start | bytes 786440 | tf_op jit(solution)/shard_map/ppermute | solution.py:163
  130.1 12.7 %collective-permute-start.29 = (f32[4,32,512]{2,1,0:T(8,128)S(1)}, f32[4,32,512]{2,1,0:T(8,128)S(1)}, u32[]{:S(2)}, u32[]{:S(2)}) collective-permute-start(f32[4,32,512]{2,1,0:T(8,128)S(1)} %get-tuple-element.116), channel_id=1, source_target_pairs={{0,24},{8,16},{16,8},{24,0},{1,25},{9,17},{17,9},{25,1},{2,26},{10... | collective-permute-start | bytes 786440 | tf_op jit(solution)/shard_map/ppermute | solution.py:163
  174.7 13.7 %collective-permute-start.32 = (bf16[2,128,512]{2,1,0:T(8,128)(2,1)S(1)}, bf16[2,128,512]{2,1,0:T(8,128)(2,1)S(1)}, u32[]{:S(2)}, u32[]{:S(2)}) collective-permute-start(bf16[2,128,512]{2,1,0:T(8,128)(2,1)S(1)} %fusion.17), channel_id=1, source_target_pairs={{0,16},{8,24},{16,0},{24,8},{1,17},{9,25},{17,1},{25,9},{2,18},{10... | collective-permute-start | bytes 786440 | tf_op jit(solution)/shard_map/ppermute | solution.py:163
  176.4 12.0 %collective-permute-start.33 = (bf16[2,128,512]{2,1,0:T(8,128)(2,1)S(1)}, bf16[2,128,512]{2,1,0:T(8,128)(2,1)S(1)}, u32[]{:S(2)}, u32[]{:S(2)}) collective-permute-start(bf16[2,128,512]{2,1,0:T(8,128)(2,1)S(1)} %fusion.17), channel_id=1, source_target_pairs={{0,24},{8,16},{16,8},{24,0},{1,25},{9,17},{17,9},{25,1},{2,26},{10... | collective-permute-start | bytes 786440 | tf_op jit(solution)/shard_map/ppermute | solution.py:163
  219.6 12.2 %collective-permute-start.42 = (f32[4,32,512]{2,1,0:T(8,128)S(1)}, f32[4,32,512]{2,1,0:T(8,128)S(1)}, u32[]{:S(2)}, u32[]{:S(2)}) collective-permute-start(f32[4,32,512]{2,1,0:T(8,128)S(1)} %get-tuple-element.111), channel_id=1, source_target_pairs={{0,16},{8,24},{16,0},{24,8},{1,17},{9,25},{17,1},{25,9},{2,18},{10... | collective-permute-start | bytes 786440 | tf_op jit(solution)/shard_map/ppermute | solution.py:163
  219.9 11.9 %collective-permute-start.43 = (f32[4,32,512]{2,1,0:T(8,128)S(1)}, f32[4,32,512]{2,1,0:T(8,128)S(1)}, u32[]{:S(2)}, u32[]{:S(2)}) collective-permute-start(f32[4,32,512]{2,1,0:T(8,128)S(1)} %get-tuple-element.111), channel_id=1, source_target_pairs={{0,24},{8,16},{16,8},{24,0},{1,25},{9,17},{17,9},{25,1},{2,26},{10... | collective-permute-start | bytes 786440 | tf_op jit(solution)/shard_map/ppermute | solution.py:163
  (64 other events, 441.3 us)
Sparse Core Ops, SparseCore 0:
  90.4 57.6 all-gather.1
  223.6 31.9 reduce-scatter.3
where the time goes:
time: 271 us; the launch traced here: 270 us
  waiting for transfers between devices  80.6 us (30%)
  starting transfers between devices  67 us (25%)
  Pallas kernels  43.8 us (16%)
  matrix products  30.3 us (11%)
  local copies, waits for them, and re-layouts  17.2 us (6%)
  between operations  16.2 us (6%)
  other arithmetic  14.9 us (5%)
    ppermute x45, waiting for transfers between devices, swap(): lax.ppermute(value, axis, [(i, i ^ k) for i in range(lax.axis_size(axis))])  79.4 us
    ppermute x45, starting transfers between devices, swap(): lax.ppermute(value, axis, [(i, i ^ k) for i in range(lax.axis_size(axis))])  66.7 us
    pallas_call x2, Pallas kernels, inverse_factor(): pl.pallas_call(functools.partial(factor_kernel, scale, exact), out_shape=...  43.8 us
    dot_general x2, matrix products, factor(): grams = jnp.einsum('obr,obs->ors', own, image, precision=precision)  6.69 us
  transfers between devices with their start and end apart: 47, of which 27 were waited for; matrix products, arithmetic and copies ran while one was open for 13% of the time, Pallas kernels for 16%

commit v1 on v0

--- a/solution.py
+++ b/solution.py
@@ -58,14 +58,25 @@
         rows = [spread(base[i : i + 1, :]) for i in range(SUB)]
         below = [[None] * SUB for _ in range(SUB)]
         inverse = []
-        for b in range(SUB):
-            inverse.append(pl.reciprocal(pivot[b][b], approx=True))
-            for i in range(b + 1, SUB):
-                factor = pivot[b][i] * inverse[b]
-                below[i][b] = factor
+        for b in range(0, SUB, 2):
+            head, side, tail = pivot[b][b], pivot[b][b + 1], pivot[b + 1][b + 1]
+            det = head * tail - side * side
+            inverse.append(pl.reciprocal(head, approx=True))
+            inverse.append(head * pl.reciprocal(det, approx=True))
+            link = side * inverse[b]
+            below[b + 1][b] = link
+            rows[b + 1] = rows[b + 1] - link * rows[b]
+            pivot[b + 1][b + 1] = det * inverse[b]
+            for i in range(b + 2, SUB):
+                pivot[b + 1][i] = pivot[b + 1][i] - link * pivot[b][i]
+                below[i][b] = pivot[b][i] * inverse[b]
+                below[i][b + 1] = pivot[b + 1][i] * inverse[b + 1]
+            for i in range(b + 2, SUB):
                 for c in range(i, SUB):
-                    pivot[i][c] = pivot[i][c] - factor * pivot[b][c]
-                rows[i] = rows[i] - factor * rows[b]
+                    pivot[i][c] = (pivot[i][c] - below[i][b] * pivot[b][c]) - (
+                        below[i][b + 1] * pivot[b + 1][c]
+                    )
+                rows[i] = (rows[i] - below[i][b] * rows[b]) - below[i][b + 1] * rows[b + 1]
         result = jnp.zeros(shape, jnp.float32)
         for b in range(SUB):
             result = jnp.where(sub == b, rows[b] * lax.rsqrt(pivot[b][b]), result)
@@ -94,6 +105,18 @@
             place = ((tok_pos ^ k) * gc_count + (gc_pos ^ i)) * rows
             work_ref[pl.ds(pl.multiple_of(place, SUB), rows), :] = pieces_ref[k, i] * scale
 
+    on_diag = lax.broadcasted_iota(jnp.int32, (PANEL, PANEL), 0) == lax.broadcasted_iota(
+        jnp.int32, (PANEL, PANEL), 1
+    )
+    by_column = []
+    for k in range(panels):
+        panel = slice(k * PANEL, (k + 1) * PANEL)
+        diag = jnp.where(on_diag, work_ref[panel, panel], 0.0)
+        by_column.append(lax.rsqrt(jnp.sum(diag, axis=0, keepdims=True)))
+        work_ref[panel, :] *= lax.rsqrt(jnp.sum(diag, axis=1, keepdims=True))
+    for k in range(panels):
+        work_ref[:, k * PANEL : (k + 1) * PANEL] *= by_column[k]
+
     def panel_step(k, carry):
         here = pl.ds(pl.multiple_of(k * PANEL, PANEL), PANEL)
         diag = work_ref[here, here]
@@ -120,7 +143,9 @@
         work_ref[i * PANEL : (i + 1) * PANEL, (i + 1) * PANEL :] = jnp.zeros(
             (PANEL, rank - (i + 1) * PANEL), jnp.float32
         )
-    out_ref[...] = work_ref[...]
+    for k in range(panels):
+        panel = slice(k * PANEL, (k + 1) * PANEL)
+        out_ref[:, panel] = work_ref[:, panel] * by_column[k]
 
 
 def inverse_factor(pieces, exact, scale):
@@ -224,7 +249,7 @@
             preferred_element_type=jnp.float32,
         ).astype(jnp.bfloat16)
         near.append(collect(proj, "gc"))
-    near, x_pieces = lax.optimization_barrier((near, x_pieces))
+    near[-1], x_pieces = lax.optimization_barrier((near[-1], x_pieces))
     full_x = jnp.concatenate(x_pieces, axis=0).reshape(total_tokens, owned, block_cols)
     basis_bf = jnp.concatenate(
         [
@@ -236,14 +261,16 @@
         axis=2,
     )
     sources = [(gr_pos * gc_count + (gc_pos ^ b)) * owned for b in range(gc_count)]
-    own_part = [combine(own_links, pieces, sources) for pieces in near]
-    other_part = [combine(partner_links, pieces, sources) for pieces in near]
-    mixed = jnp.concatenate(
-        [own + swap(other, "gr", 1) for own, other in zip(own_part, other_part)], axis=2
-    ).astype(jnp.bfloat16)
-
-    def image_of(mixed, basis_bf):
-        full = jnp.concatenate(collect(mixed, "tok"), axis=1)
+    mixed = []
+    for pieces in near:
+        own = combine(own_links, pieces, sources)
+        other = combine(partner_links, pieces, sources)
+        mixed.append((own + swap(other, "gr", 1)).astype(jnp.bfloat16))
+
+    def image_of(parts, basis_bf):
+        full = jnp.concatenate(
+            [jnp.concatenate(collect(part, "tok"), axis=1) for part in parts], axis=2
+        )
         cover = jnp.einsum("tob,otr->obr", full_x, full, preferred_element_type=jnp.float32)
         return cover / total_tokens + ridge * basis_bf.astype(jnp.float32)
 
@@ -253,7 +280,7 @@
             for part in split(image)
         )
 
-    def factor(image, last):
+    def factor(image, last, beside=None):
         precision = HIGHEST if last else HIGH
         own = lax.dynamic_slice_in_dim(image, tok_pos * own_cols, own_cols, 2)
         grams = jnp.einsum("obr,obs->ors", own, image, precision=precision)
@@ -273,22 +300,24 @@
         pieces = jnp.stack(collect(rows_near, "tok"))
         own = inverse_factor(pieces, last, 1.0 / group_cols)
         other = swap(own, "gr", 1)
+        if beside is not None:
+            other, beside = lax.optimization_barrier((other, beside))
         of_block = jnp.stack(
             [jnp.where(own_groups[o] == gr_pos, own, other) for o in range(owned)]
         )
         of_group = [jnp.where(gr_pos == g, own, other) for g in range(groups)]
-        return of_block, of_group
+        return of_block, of_group, beside
 
     image = image_of(mixed, basis_bf)
     seen = lax.all_gather(seen_by(image), ("gr", "gc"), axis=0, tiled=True)
     second = 0.0
     for j in range(seen.shape[0]):
         second += own_links[:, j][:, None, None] * seen[j][None]
-    of_block, _ = factor(image, False)
+    of_block, _, second = factor(image, False, second)
     mixed = jnp.einsum("otr,osr->ots", second, of_block, precision=HIGH).astype(jnp.bfloat16)
     basis_bf = jnp.einsum("obr,osr->obs", image, of_block, precision=HIGH).astype(jnp.bfloat16)
-    image = image_of(mixed, basis_bf)
-    of_block, of_group = factor(image, True)
+    image = image_of([mixed], basis_bf)
+    of_block, of_group, _ = factor(image, True)
     rows = lax.dynamic_slice_in_dim(image, tok_pos * slice_rows, slice_rows, 1)
     basis = jnp.einsum("obr,osr->obs", rows, of_block, precision=HIGH)
     codes = seen_by(image)

time: 271 us -> 260 us (0.959)
  other arithmetic: 14.9 us -> 8.6 us
  starting transfers between devices: 67 us -> 73.3 us
  Pallas kernels: 43.8 us -> 38.9 us
    ppermute x45 -> x48, starting transfers between devices: 66.7 us -> 73 us  [swap(): lax.ppermute(value, axis, [(i, i ^ k) for i in range(lax.axis_size(axis))])]
    ppermute x45 -> x48, waiting for transfers between devices: 79.4 us -> 74.5 us  [swap(): lax.ppermute(value, axis, [(i, i ^ k) for i in range(lax.axis_size(axis))])]
    pallas_call x2, Pallas kernels: 43.8 us -> 38.9 us  [inverse_factor(): pl.pallas_call(functools.partial(factor_kernel, scale, exact), out_shape=...]
  transfers between devices with their start and end apart: 47 -> 50, of which waited for: 27 -> 24; matrix products, arithmetic and copies ran while one was open for 13% -> 12% of each run, Pallas kernels for 16% -> 15%
where the time goes in v1:
time: 260 us
  waiting for transfers between devices  77.9 us (30%)
  starting transfers between devices  73.3 us (28%)
  Pallas kernels  38.9 us (15%)
  matrix products  28.5 us (11%)
  local copies, waits for them, and re-layouts  16.4 us (6%)
  between operations  16.2 us (6%)
  other arithmetic  8.6 us (3%)
    ppermute x48, waiting for transfers between devices, swap(): lax.ppermute(value, axis, [(i, i ^ k) for i in range(lax.axis_size(axis))])  74.5 us
    ppermute x48, starting transfers between devices, swap(): lax.ppermute(value, axis, [(i, i ^ k) for i in range(lax.axis_size(axis))])  73 us
    pallas_call x2, Pallas kernels, inverse_factor(): pl.pallas_call(functools.partial(factor_kernel, scale, exact), out_shape=...  38.9 us
    dot_general x2, matrix products, factor(): grams = jnp.einsum('obr,obs->ors', own, image, precision=precision)  6.69 us
  transfers between devices with their start and end apart: 50, of which 24 were waited for; matrix products, arithmetic and copies ran while one was open for 12% of the time, Pallas kernels for 15%

profile of v1, /device:TPU:0, one launch (start us, length us, event | category | flops | bytes accessed | tf_op | source)
XLA Modules:
  0.0 259.9 jit_solution(14839580248546507385)
XLA Ops:
  25.2 3.0 %collective-permute-start.2 = (bf16[2,256,256]{2,1,0:T(8,128)(2,1)S(1)}, bf16[2,256,256]{2,1,0:T(8,128)(2,1)S(1)}, u32[]{:S(2)}, u32[]{:S(2)}) collective-permute-start(bf16[2,256,256]{2,1,0:T(8,128)(2,1)S(1)} %get-tuple-element.17), channel_id=1, source_target_pairs={{0,24},{8,16},{16,8},{24,0},{1,25},{9,17},{17,9},{25,1},{2,26},{10... | collective-permute-start | bytes 786440 | tf_op jit(solution)/shard_map/ppermute | solution.py:188
  50.5 3.8 %collective-permute-start.5 = (bf16[2,128,256]{2,1,0:T(8,128)(2,1)S(1)}, bf16[2,128,256]{2,1,0:T(8,128)(2,1)S(1)}, u32[]{:S(2)}, u32[]{:S(2)}) collective-permute-start(bf16[2,128,256]{2,1,0:T(8,128)(2,1)S(1)} %convolution_convert_fusion.1), channel_id=1, source_target_pairs={{0,3},{1,2},{2,1},{3,0},{4,7},{5,6},{6,5},{7,4},{8,11},{9,10},{10,... | collective-permute-start | bytes 393224 | tf_op jit(solution)/shard_map/ppermute | solution.py:188
  54.6 3.1 %collective-permute-done.4 = bf16[2,128,256]{2,1,0:T(8,128)(2,1)S(1)} collective-permute-done((bf16[2,128,256]{2,1,0:T(8,128)(2,1)S(1)}, bf16[2,128,256]{2,1,0:T(8,128)(2,1)S(1)}, u32[]{:S(2)}, u32[]{:S(2)}) %collective-permute-start.4) | collective-permute-done | bytes 131104 | tf_op jit(solution)/shard_map/ppermute | solution.py:188
  57.7 5.3 %collective-permute-done.7 = bf16[128,2048]{1,0:T(8,128)(2,1)S(1)} collective-permute-done((bf16[128,2048]{1,0:T(8,128)(2,1)S(1)}, bf16[128,2048]{1,0:T(8,128)(2,1)S(1)}, u32[]{:S(2)}, u32[]{:S(2)}) %collective-permute-start.7) | collective-permute-done | bytes 524320 | tf_op jit(solution)/shard_map/ppermute | solution.py:188
  79.5 3.4 %multiply_add_fusion.1 = f32[2,1024,512]{2,1,0:T(8,128)S(1)} fusion(bf16[2,256,256]{2,1,0:T(8,128)(2,1)S(1)} %copy-done.10, bf16[2,256,256]{2,1,0:T(8,128)(2,1)S(1)} %copy-done.11, bf16[2,256,256]{2,1,0:T(8,128)(2,1)} %get-tuple-element.99, bf16[2,256,256]{2,1,0:T(8,128)(2,1)S(1)} %copy-done.9, bf16[2,256,256]{2,1,0:T(8,128)(2,1)} %get-tuple-element.93, ...), kind=kOutput, calls=%fused_computation.7 | convolution fusion | flops 1102053376 | bytes 9437184 | tf_op jit(solution)/shard_map/tob,otr->obr/dot_general | solution.py:274
  87.1 3.9 %multiply_reduce_fusion.4 = (f32[128,512]{1,0:T(8,128)S(1)}, f32[128,512]{1,0:T(8,128)S(1)}) fusion(f32[2]{0:T(128)S(1)} %get-tuple-element.141, f32[2]{0:T(128)S(1)} %get-tuple-element.142, f32[2,1024,512]{2,1,0:T(8,128)} %copy-done, s32[]{:T(128)S(6)} %select_n.336), kind=kOutput, calls=%fused_computation.85 | convolution fusion | flops 805699584 | bytes 5767188 | tf_op jit(solution)/shard_map/obr,obs->ors/dot_general | solution.py:286
  97.7 9.1 %collective-permute-done.25 = f32[32,512]{1,0:T(8,128)S(1)} collective-permute-done((f32[32,512]{1,0:T(8,128)S(1)}, f32[32,512]{1,0:T(8,128)S(1)}, u32[]{:S(2)}, u32[]{:S(2)}) %collective-permute-start.25) | collective-permute-done | bytes 65568 | tf_op jit(solution)/shard_map/ppermute | solution.py:188
  106.8 5.6 %collective-permute-start.27 = (f32[32,512]{1,0:T(8,128)S(1)}, f32[32,512]{1,0:T(8,128)S(1)}, u32[]{:S(2)}, u32[]{:S(2)}) collective-permute-start(f32[32,512]{1,0:T(8,128)S(1)} %add_add_fusion.1), channel_id=1, source_target_pairs={{0,1},{1,0},{2,3},{3,2},{4,5},{5,4},{6,7},{7,6},{8,9},{9,8},{10,11... | collective-permute-start | bytes 196616 | tf_op jit(solution)/shard_map/ppermute | solution.py:188
  114.8 3.6 %collective-permute-done.27 = f32[32,512]{1,0:T(8,128)S(1)} collective-permute-done((f32[32,512]{1,0:T(8,128)S(1)}, f32[32,512]{1,0:T(8,128)S(1)}, u32[]{:S(2)}, u32[]{:S(2)}) %collective-permute-start.27) | collective-permute-done | bytes 65568 | tf_op jit(solution)/shard_map/ppermute | solution.py:188
  118.5 6.6 %collective-permute-done.28 = f32[32,512]{1,0:T(8,128)S(1)} collective-permute-done((f32[32,512]{1,0:T(8,128)S(1)}, f32[32,512]{1,0:T(8,128)S(1)}, u32[]{:S(2)}, u32[]{:S(2)}) %collective-permute-start.28) | collective-permute-done | bytes 65568 | tf_op jit(solution)/shard_map/ppermute | solution.py:188
  128.7 5.7 %collective-permute-done.30 = f32[4,32,512]{2,1,0:T(8,128)S(1)} collective-permute-done((f32[4,32,512]{2,1,0:T(8,128)S(1)}, f32[4,32,512]{2,1,0:T(8,128)S(1)}, u32[]{:S(2)}, u32[]{:S(2)}) %collective-permute-start.30) | collective-permute-done | bytes 262176 | tf_op jit(solution)/shard_map/ppermute | solution.py:188
  134.4 4.3 %collective-permute-done.31 = f32[4,32,512]{2,1,0:T(8,128)S(1)} collective-permute-done((f32[4,32,512]{2,1,0:T(8,128)S(1)}, f32[4,32,512]{2,1,0:T(8,128)S(1)}, u32[]{:S(2)}, u32[]{:S(2)}) %collective-permute-start.31) | collective-permute-done | bytes 262176 | tf_op jit(solution)/shard_map/ppermute | solution.py:188
  138.8 18.9 %inverse_factor.2 = f32[512,512]{1,0:T(8,128)S(1)} custom-call(s32[2]{0:T(128)S(1)} %pad_add_fusion.pos_ref, f32[4,4,32,512]{3,2,1,0:T(8,128)S(1)} %pad_maximum_fusion.6.pieces_ref), custom_call_target="tpu_custom_call" | custom-call | flops 12884901888 | bytes 2097152 | tf_op jit(solution)/shard_map/inverse_factor/pallas_call | solution.py:165
  168.8 4.0 %fusion.12 = bf16[2,1024,512]{2,1,0:T(8,128)(2,1)S(1)} fusion(f32[2,1024,512]{2,1,0:T(8,128)S(1)} %copy-done.1, f32[1,512,512]{2,1,0:T(8,128)S(1)} %get-tuple-element.91, f32[1,512,512]{2,1,0:T(8,128)S(1)} %get-tuple-element.90), kind=kOutput, calls=%fused_computation.18 | convolution fusion | flops 3221749760 | bytes 8388608 | tf_op jit(solution)/shard_map/obr,osr->obs/dot_general | solution.py:318
  174.4 5.3 %collective-permute-done.35 = bf16[2,128,512]{2,1,0:T(8,128)(2,1)S(1)} collective-permute-done((bf16[2,128,512]{2,1,0:T(8,128)(2,1)S(1)}, bf16[2,128,512]{2,1,0:T(8,128)(2,1)S(1)}, u32[]{:S(2)}, u32[]{:S(2)}) %collective-permute-start.35) | collective-permute-done | bytes 262176 | tf_op jit(solution)/shard_map/ppermute | solution.py:188
  185.5 4.1 %collective-permute-start.38 = (f32[32,512]{1,0:T(8,128)S(1)}, f32[32,512]{1,0:T(8,128)S(1)}, u32[]{:S(2)}, u32[]{:S(2)}) collective-permute-start(f32[32,512]{1,0:T(8,128)S(1)} %get-tuple-element.108), channel_id=1, source_target_pairs={{0,1},{1,0},{2,3},{3,2},{4,5},{5,4},{6,7},{7,6},{8,9},{9,8},{10,11... | collective-permute-start | bytes 196616 | tf_op jit(solution)/shard_map/ppermute | solution.py:188
  189.5 3.7 %collective-permute-start.39 = (f32[32,512]{1,0:T(8,128)S(1)}, f32[32,512]{1,0:T(8,128)S(1)}, u32[]{:S(2)}, u32[]{:S(2)}) collective-permute-start(f32[32,512]{1,0:T(8,128)S(1)} %get-tuple-element.110), channel_id=1, source_target_pairs={{0,2},{1,3},{2,0},{3,1},{4,6},{5,7},{6,4},{7,5},{8,10},{9,11},{10,... | collective-permute-start | bytes 196616 | tf_op jit(solution)/shard_map/ppermute | solution.py:188
  195.6 4.0 %collective-permute-done.40 = f32[32,512]{1,0:T(8,128)S(1)} collective-permute-done((f32[32,512]{1,0:T(8,128)S(1)}, f32[32,512]{1,0:T(8,128)S(1)}, u32[]{:S(2)}, u32[]{:S(2)}) %collective-permute-start.40) | collective-permute-done | bytes 65568 | tf_op jit(solution)/shard_map/ppermute | solution.py:188
  205.1 4.2 %collective-permute-done.42 = f32[32,512]{1,0:T(8,128)S(1)} collective-permute-done((f32[32,512]{1,0:T(8,128)S(1)}, f32[32,512]{1,0:T(8,128)S(1)}, u32[]{:S(2)}, u32[]{:S(2)}) %collective-permute-start.42) | collective-permute-done | bytes 65568 | tf_op jit(solution)/shard_map/ppermute | solution.py:188
  214.9 3.8 %collective-permute-done.44 = f32[4,32,512]{2,1,0:T(8,128)S(1)} collective-permute-done((f32[4,32,512]{2,1,0:T(8,128)S(1)}, f32[4,32,512]{2,1,0:T(8,128)S(1)}, u32[]{:S(2)}, u32[]{:S(2)}) %collective-permute-start.44) | collective-permute-done | bytes 262176 | tf_op jit(solution)/shard_map/ppermute | solution.py:188
  218.7 4.7 %collective-permute-done.45 = f32[4,32,512]{2,1,0:T(8,128)S(1)} collective-permute-done((f32[4,32,512]{2,1,0:T(8,128)S(1)}, f32[4,32,512]{2,1,0:T(8,128)S(1)}, u32[]{:S(2)}, u32[]{:S(2)}) %collective-permute-start.45) | collective-permute-done | bytes 262176 | tf_op jit(solution)/shard_map/ppermute | solution.py:188
  223.5 20.0 %inverse_factor.3 = f32[512,512]{1,0:T(8,128)S(1)} custom-call(s32[2]{0:T(128)S(1)} %pad_add_fusion.pos_ref, f32[4,4,32,512]{3,2,1,0:T(8,128)S(1)} %pad_maximum_fusion.7.pieces_ref), custom_call_target="tpu_custom_call" | custom-call | flops 12884901888 | bytes 2097152 | tf_op jit(solution)/shard_map/inverse_factor/pallas_call | solution.py:165
  243.6 3.3 %reduce-scatter.4.cloned.1.call-done = f32[16,1024]{1,0:T(8,128)} async-done(((f32[128,1024]{1,0:T(8,128)}), f32[16,1024]{1,0:T(8,128)}) %reduce-scatter.4.cloned.1.call-update) | async-done | bytes 65552
  249.7 3.4 %fusion.8 = f32[2,256,512]{2,1,0:T(8,128)} fusion(f32[1,512,512]{2,1,0:T(8,128)S(1)} %get-tuple-element.89, f32[1,512,512]{2,1,0:T(8,128)S(1)} %get-tuple-element.88, f32[2,1024,512]{2,1,0:T(8,128)} %copy-done.2, s32[]{:T(128)S(6)} %select_n.274), kind=kOutput, calls=%fused_computation.14 | convolution fusion | flops 805830656 | bytes 4194308 | tf_op jit(solution)/shard_map/obr,osr->obs/dot_general | solution.py:322
  (205 shorter events, 106.9 us)
Async XLA Ops:
  7.2 153.1 %all-gather.2.cloned.1.call-start = ((), (), s32[]{:S(2)}) async-start(), calls=%async_computation.1 | async-start | bytes 4718592 | tf_op jit(solution)/shard_map/all_gather | solution.py:312
  9.3 15.9 %collective-permute-start.10 = (bf16[2,256,256]{2,1,0:T(8,128)(2,1)}, bf16[2,256,256]{2,1,0:T(8,128)(2,1)S(1)}, u32[]{:S(2)}, u32[]{:S(2)}) collective-permute-start(bf16[2,256,256]{2,1,0:T(8,128)(2,1)} %get-tuple-element.100), channel_id=1, source_target_pairs={{0,16},{8,24},{16,0},{24,8},{1,17},{9,25},{17,1},{25,9},{2,18},{10... | collective-permute-start | bytes 786440 | tf_op jit(solution)/shard_map/ppermute | solution.py:188
  12.3 15.9 %collective-permute-start.11 = (bf16[2,256,256]{2,1,0:T(8,128)(2,1)}, bf16[2,256,256]{2,1,0:T(8,128)(2,1)S(1)}, u32[]{:S(2)}, u32[]{:S(2)}) collective-permute-start(bf16[2,256,256]{2,1,0:T(8,128)(2,1)} %get-tuple-element.100), channel_id=1, source_target_pairs={{0,24},{8,16},{16,8},{24,0},{1,25},{9,17},{17,9},{25,1},{2,26},{10... | collective-permute-start | bytes 786440 | tf_op jit(solution)/shard_map/ppermute | solution.py:188
  13.7 14.5 %collective-permute-start.9 = (bf16[2,256,256]{2,1,0:T(8,128)(2,1)}, bf16[2,256,256]{2,1,0:T(8,128)(2,1)S(1)}, u32[]{:S(2)}, u32[]{:S(2)}) collective-permute-start(bf16[2,256,256]{2,1,0:T(8,128)(2,1)} %get-tuple-element.100), channel_id=1, source_target_pairs={{0,8},{8,0},{16,24},{24,16},{1,9},{9,1},{17,25},{25,17},{2,10},{10... | collective-permute-start | bytes 786440 | tf_op jit(solution)/shard_map/ppermute | solution.py:188
  13.8 20.4 %collective-permute-start = (bf16[2,256,256]{2,1,0:T(8,128)(2,1)S(1)}, bf16[2,256,256]{2,1,0:T(8,128)(2,1)S(1)}, u32[]{:S(2)}, u32[]{:S(2)}) collective-permute-start(bf16[2,256,256]{2,1,0:T(8,128)(2,1)S(1)} %get-tuple-element.17), channel_id=1, source_target_pairs={{0,8},{8,0},{16,24},{24,16},{1,9},{9,1},{17,25},{25,17},{2,10},{10... | collective-permute-start | bytes 786440 | tf_op jit(solution)/shard_map/ppermute | solution.py:188
  15.7 20.8 %collective-permute-start.1 = (bf16[2,256,256]{2,1,0:T(8,128)(2,1)S(1)}, bf16[2,256,256]{2,1,0:T(8,128)(2,1)}, u32[]{:S(2)}, u32[]{:S(2)}) collective-permute-start(bf16[2,256,256]{2,1,0:T(8,128)(2,1)S(1)} %get-tuple-element.17), channel_id=1, source_target_pairs={{0,16},{8,24},{16,0},{24,8},{1,17},{9,25},{17,1},{25,9},{2,18},{10... | collective-permute-start | bytes 786440 | tf_op jit(solution)/shard_map/ppermute | solution.py:188
  25.2 12.8 %collective-permute-start.2 = (bf16[2,256,256]{2,1,0:T(8,128)(2,1)S(1)}, bf16[2,256,256]{2,1,0:T(8,128)(2,1)S(1)}, u32[]{:S(2)}, u32[]{:S(2)}) collective-permute-start(bf16[2,256,256]{2,1,0:T(8,128)(2,1)S(1)} %get-tuple-element.17), channel_id=1, source_target_pairs={{0,24},{8,16},{16,8},{24,0},{1,25},{9,17},{17,9},{25,1},{2,26},{10... | collective-permute-start | bytes 786440 | tf_op jit(solution)/shard_map/ppermute | solution.py:188
  29.9 13.6 %collective-permute-start.12 = (bf16[2,128,256]{2,1,0:T(8,128)(2,1)S(1)}, bf16[2,128,256]{2,1,0:T(8,128)(2,1)S(1)}, u32[]{:S(2)}, u32[]{:S(2)}) collective-permute-start(bf16[2,128,256]{2,1,0:T(8,128)(2,1)S(1)} %convolution_convert_fusion), channel_id=1, source_target_pairs={{0,1},{1,0},{2,3},{3,2},{4,5},{5,4},{6,7},{7,6},{8,9},{9,8},{10,11... | collective-permute-start | bytes 393224 | tf_op jit(solution)/shard_map/ppermute | solution.py:188
  31.5 13.5 %collective-permute-start.13 = (bf16[2,128,256]{2,1,0:T(8,128)(2,1)S(1)}, bf16[2,128,256]{2,1,0:T(8,128)(2,1)S(1)}, u32[]{:S(2)}, u32[]{:S(2)}) collective-permute-start(bf16[2,128,256]{2,1,0:T(8,128)(2,1)S(1)} %convolution_convert_fusion), channel_id=1, source_target_pairs={{0,2},{1,3},{2,0},{3,1},{4,6},{5,7},{6,4},{7,5},{8,10},{9,11},{10,... | collective-permute-start | bytes 393224 | tf_op jit(solution)/shard_map/ppermute | solution.py:188
  34.1 12.6 %collective-permute-start.14 = (bf16[2,128,256]{2,1,0:T(8,128)(2,1)S(1)}, bf16[2,128,256]{2,1,0:T(8,128)(2,1)S(1)}, u32[]{:S(2)}, u32[]{:S(2)}) collective-permute-start(bf16[2,128,256]{2,1,0:T(8,128)(2,1)S(1)} %convolution_convert_fusion), channel_id=1, source_target_pairs={{0,3},{1,2},{2,1},{3,0},{4,7},{5,6},{6,5},{7,4},{8,11},{9,10},{10,... | collective-permute-start | bytes 393224 | tf_op jit(solution)/shard_map/ppermute | solution.py:188
  38.1 19.6 %collective-permute-start.6 = (bf16[128,2048]{1,0:T(8,128)(2,1)S(1)}, bf16[128,2048]{1,0:T(8,128)(2,1)S(1)}, u32[]{:S(2)}, u32[]{:S(2)}) collective-permute-start(bf16[128,2048]{1,0:T(8,128)(2,1)S(1)} %copy-done.4), channel_id=1, source_target_pairs={{0,8},{8,0},{16,24},{24,16},{1,9},{9,1},{17,25},{25,17},{2,10},{10... | collective-permute-start | bytes 1572872 | tf_op jit(solution)/shard_map/ppermute | solution.py:188
  39.6 23.5 %collective-permute-start.7 = (bf16[128,2048]{1,0:T(8,128)(2,1)S(1)}, bf16[128,2048]{1,0:T(8,128)(2,1)S(1)}, u32[]{:S(2)}, u32[]{:S(2)}) collective-permute-start(bf16[128,2048]{1,0:T(8,128)(2,1)S(1)} %copy-done.4), channel_id=1, source_target_pairs={{0,16},{8,24},{16,0},{24,8},{1,17},{9,25},{17,1},{25,9},{2,18},{10... | collective-permute-start | bytes 1572872 | tf_op jit(solution)/shard_map/ppermute | solution.py:188
  43.4 19.6 %collective-permute-start.8 = (bf16[128,2048]{1,0:T(8,128)(2,1)S(1)}, bf16[128,2048]{1,0:T(8,128)(2,1)S(1)}, u32[]{:S(2)}, u32[]{:S(2)}) collective-permute-start(bf16[128,2048]{1,0:T(8,128)(2,1)S(1)} %copy-done.4), channel_id=1, source_target_pairs={{0,24},{8,16},{16,8},{24,0},{1,25},{9,17},{17,9},{25,1},{2,26},{10... | collective-permute-start | bytes 1572872 | tf_op jit(solution)/shard_map/ppermute | solution.py:188
  86.8 160.1 %reduce-scatter.4.cloned.1.call-start = ((), (), s32[]{:S(2)}) async-start(), calls=%async_computation.2 | async-start | bytes 589824
  94.4 12.4 %collective-permute-start.25 = (f32[32,512]{1,0:T(8,128)S(1)}, f32[32,512]{1,0:T(8,128)S(1)}, u32[]{:S(2)}, u32[]{:S(2)}) collective-permute-start(f32[32,512]{1,0:T(8,128)S(1)} %get-tuple-element.115), channel_id=1, source_target_pairs={{0,2},{1,3},{2,0},{3,1},{4,6},{5,7},{6,4},{7,5},{8,10},{9,11},{10,... | collective-permute-start | bytes 196616 | tf_op jit(solution)/shard_map/ppermute | solution.py:188
  106.8 11.7 %collective-permute-start.27 = (f32[32,512]{1,0:T(8,128)S(1)}, f32[32,512]{1,0:T(8,128)S(1)}, u32[]{:S(2)}, u32[]{:S(2)}) collective-permute-start(f32[32,512]{1,0:T(8,128)S(1)} %add_add_fusion.1), channel_id=1, source_target_pairs={{0,1},{1,0},{2,3},{3,2},{4,5},{5,4},{6,7},{7,6},{8,9},{9,8},{10,11... | collective-permute-start | bytes 196616 | tf_op jit(solution)/shard_map/ppermute | solution.py:188
  112.4 12.7 %collective-permute-start.28 = (f32[32,512]{1,0:T(8,128)S(1)}, f32[32,512]{1,0:T(8,128)S(1)}, u32[]{:S(2)}, u32[]{:S(2)}) collective-permute-start(f32[32,512]{1,0:T(8,128)S(1)} %add_add_fusion.1), channel_id=1, source_target_pairs={{0,2},{1,3},{2,0},{3,1},{4,6},{5,7},{6,4},{7,5},{8,10},{9,11},{10,... | collective-permute-start | bytes 196616 | tf_op jit(solution)/shard_map/ppermute | solution.py:188
  113.2 11.8 %collective-permute-start.29 = (f32[32,512]{1,0:T(8,128)S(1)}, f32[32,512]{1,0:T(8,128)S(1)}, u32[]{:S(2)}, u32[]{:S(2)}) collective-permute-start(f32[32,512]{1,0:T(8,128)S(1)} %add_add_fusion.1), channel_id=1, source_target_pairs={{0,3},{1,2},{2,1},{3,0},{4,7},{5,6},{6,5},{7,4},{8,11},{9,10},{10,... | collective-permute-start | bytes 196616 | tf_op jit(solution)/shard_map/ppermute | solution.py:188
  126.5 12.2 %collective-permute-start.31 = (f32[4,32,512]{2,1,0:T(8,128)S(1)}, f32[4,32,512]{2,1,0:T(8,128)S(1)}, u32[]{:S(2)}, u32[]{:S(2)}) collective-permute-start(f32[4,32,512]{2,1,0:T(8,128)S(1)} %get-tuple-element.112), channel_id=1, source_target_pairs={{0,16},{8,24},{16,0},{24,8},{1,17},{9,25},{17,1},{25,9},{2,18},{10... | collective-permute-start | bytes 786440 | tf_op jit(solution)/shard_map/ppermute | solution.py:188
  126.5 12.2 %collective-permute-start.32 = (f32[4,32,512]{2,1,0:T(8,128)S(1)}, f32[4,32,512]{2,1,0:T(8,128)S(1)}, u32[]{:S(2)}, u32[]{:S(2)}) collective-permute-start(f32[4,32,512]{2,1,0:T(8,128)S(1)} %get-tuple-element.112), channel_id=1, source_target_pairs={{0,24},{8,16},{16,8},{24,0},{1,25},{9,17},{17,9},{25,1},{2,26},{10... | collective-permute-start | bytes 786440 | tf_op jit(solution)/shard_map/ppermute | solution.py:188
  165.7 14.0 %collective-permute-start.35 = (bf16[2,128,512]{2,1,0:T(8,128)(2,1)S(1)}, bf16[2,128,512]{2,1,0:T(8,128)(2,1)S(1)}, u32[]{:S(2)}, u32[]{:S(2)}) collective-permute-start(bf16[2,128,512]{2,1,0:T(8,128)(2,1)S(1)} %fusion.17), channel_id=1, source_target_pairs={{0,16},{8,24},{16,0},{24,8},{1,17},{9,25},{17,1},{25,9},{2,18},{10... | collective-permute-start | bytes 786440 | tf_op jit(solution)/shard_map/ppermute | solution.py:188
  167.1 12.7 %collective-permute-start.36 = (bf16[2,128,512]{2,1,0:T(8,128)(2,1)S(1)}, bf16[2,128,512]{2,1,0:T(8,128)(2,1)S(1)}, u32[]{:S(2)}, u32[]{:S(2)}) collective-permute-start(bf16[2,128,512]{2,1,0:T(8,128)(2,1)S(1)} %fusion.17), channel_id=1, source_target_pairs={{0,24},{8,16},{16,8},{24,0},{1,25},{9,17},{17,9},{25,1},{2,26},{10... | collective-permute-start | bytes 786440 | tf_op jit(solution)/shard_map/ppermute | solution.py:188
  211.2 12.2 %collective-permute-start.45 = (f32[4,32,512]{2,1,0:T(8,128)S(1)}, f32[4,32,512]{2,1,0:T(8,128)S(1)}, u32[]{:S(2)}, u32[]{:S(2)}) collective-permute-start(f32[4,32,512]{2,1,0:T(8,128)S(1)} %get-tuple-element.107), channel_id=1, source_target_pairs={{0,16},{8,24},{16,0},{24,8},{1,17},{9,25},{17,1},{25,9},{2,18},{10... | collective-permute-start | bytes 786440 | tf_op jit(solution)/shard_map/ppermute | solution.py:188
  211.3 12.1 %collective-permute-start.46 = (f32[4,32,512]{2,1,0:T(8,128)S(1)}, f32[4,32,512]{2,1,0:T(8,128)S(1)}, u32[]{:S(2)}, u32[]{:S(2)}) collective-permute-start(f32[4,32,512]{2,1,0:T(8,128)S(1)} %get-tuple-element.107), channel_id=1, source_target_pairs={{0,24},{8,16},{16,8},{24,0},{1,25},{9,17},{17,9},{25,1},{2,26},{10... | collective-permute-start | bytes 786440 | tf_op jit(solution)/shard_map/ppermute | solution.py:188
  (55 other events, 452.7 us)
Sparse Core Ops, SparseCore 0:
  86.9 57.4 all-gather.1
  215.1 31.7 reduce-scatter.3

commit v2 on v1

--- a/solution.py
+++ b/solution.py
@@ -96,14 +96,31 @@
             tiles[q] = jnp.where(inside, 0.0, tiles[q]) - parts[0]
 
 
-def factor_kernel(scale, exact, pos_ref, pieces_ref, out_ref, work_ref, inv_ref):
-    tok_count, gc_count, rows, rank = pieces_ref.shape
+def factor_kernel(scale, exact, pos_ref, *refs):
+    *piece_refs, out_ref, work_ref, inv_ref = refs
+    rank = work_ref.shape[0]
     panels = rank // PANEL
-    tok_pos, gc_pos = pos_ref[0], pos_ref[1]
-    for k in range(tok_count):
-        for i in range(gc_count):
-            place = ((tok_pos ^ k) * gc_count + (gc_pos ^ i)) * rows
-            work_ref[pl.ds(pl.multiple_of(place, SUB), rows), :] = pieces_ref[k, i] * scale
+    count = len(piece_refs)
+    if count == 1:
+        work_ref[...] = piece_refs[0][...] * scale
+    else:
+        work_ref[...] = jnp.zeros((rank, rank), jnp.float32)
+    own_cols = rank // count
+    for k in range(count if count > 1 else 0):
+        for s in range(count):
+
+            @pl.when(pos_ref[0] ^ k == s)
+            def _():
+                for d in range(piece_refs[k].shape[1] // own_cols):
+                    other = (s + d) % count
+                    block = piece_refs[k][:, d * own_cols : (d + 1) * own_cols] * scale
+                    low, high = min(s, other), max(s, other)
+                    if s > other and 2 * d == count:
+                        continue
+                    work_ref[
+                        low * own_cols : (low + 1) * own_cols,
+                        high * own_cols : (high + 1) * own_cols,
+                    ] = block.T if s > other else block
 
     on_diag = lax.broadcasted_iota(jnp.int32, (PANEL, PANEL), 0) == lax.broadcasted_iota(
         jnp.int32, (PANEL, PANEL), 1
@@ -149,25 +166,14 @@
 
 
 def inverse_factor(pieces, exact, scale):
-    tok_count, gc_count, rows, rank = pieces.shape
-    tok_pos, gc_pos = lax.axis_index("tok"), lax.axis_index("gc")
-    if rows % SUB == 0:
-        pos = jnp.stack([tok_pos, gc_pos]).astype(jnp.int32)
-    else:
-        pos = jnp.zeros((2,), jnp.int32)
-        order = (
-            (tok_pos ^ jnp.arange(tok_count, dtype=jnp.int32))[:, None] * gc_count
-            + (gc_pos ^ jnp.arange(gc_count, dtype=jnp.int32))[None, :]
-        ).reshape(-1)
-        place = (order[:, None] * rows + jnp.arange(rows, dtype=jnp.int32)[None, :]).reshape(rank)
-        full = jnp.zeros((rank, rank), jnp.float32).at[place].set(pieces.reshape(rank, rank))
-        pieces = full.reshape(1, 1, rank, rank)
+    rank = pieces[0].shape[0] * len(pieces)
+    pos = lax.axis_index("tok").astype(jnp.int32).reshape(1)
     return pl.pallas_call(
         functools.partial(factor_kernel, scale, exact),
         out_shape=jax.ShapeDtypeStruct((rank, rank), jnp.float32),
         in_specs=[
             pl.BlockSpec(memory_space=pltpu.SMEM),
-            pl.BlockSpec(memory_space=pltpu.VMEM),
+            *[pl.BlockSpec(memory_space=pltpu.VMEM) for _ in pieces],
         ],
         out_specs=pl.BlockSpec(memory_space=pltpu.VMEM),
         scratch_shapes=[
@@ -179,7 +185,7 @@
             flops=96 * rank**3, bytes_accessed=8 * rank**2, transcendentals=0
         ),
         name="inverse_factor",
-    )(pos, pieces)
+    )(pos, *pieces)
 
 
 def swap(value, axis, k):
@@ -190,6 +196,15 @@
 
 def collect(value, axis):
     return [swap(value, axis, k) for k in range(lax.axis_size(axis))]
+
+
+def collect_relayed(value, axis):
+    if lax.axis_size(axis) != 4:
+        return collect(value, axis)
+    half = value.shape[0] // 2
+    near, side = swap(value, axis, 1), swap(value, axis, 2)
+    far = [swap(side[:half], axis, 1), swap(near[half:], axis, 2)]
+    return [value, near, side, jnp.concatenate(far, axis=0)]
 
 
 def per_device(acts, init_basis, kept, member):
@@ -230,7 +245,7 @@
         collect(init_bf[:, :, c * width : (c + 1) * width], "tok") for c in range(CHUNKS)
     ]
     init_pieces[-1], acts_late = lax.optimization_barrier((init_pieces[-1], acts))
-    x_pieces = collect(acts_late, "tok")
+    x_pieces = collect_relayed(acts_late, "tok")
 
     def combine(rows_of_links, pieces, sources):
         total = 0.0
@@ -280,7 +295,7 @@
             for part in split(image)
         )
 
-    def factor(image, last, beside=None):
+    def factor(image, last, beside=None, aside=None):
         precision = HIGHEST if last else HIGH
         own = lax.dynamic_slice_in_dim(image, tok_pos * own_cols, own_cols, 2)
         grams = jnp.einsum("obr,obs->ors", own, image, precision=precision)
@@ -290,14 +305,27 @@
             return jnp.sum(mask[:, None, None] * grams, axis=0)
 
         total = group_sum(gr_pos) + swap(group_sum(gr_pos ^ 1), "gr", 1)
-        rows = own_cols // gc_count
-
-        def rows_of(i):
-            return lax.dynamic_slice_in_dim(total, (gc_pos ^ i) * rows, rows, 0)
-
-        piece = sum(swap(rows_of(i), "gc", i) for i in range(gc_count))
-        rows_near = jnp.stack(collect(piece, "gc"))
-        pieces = jnp.stack(collect(rows_near, "tok"))
+        packed = tok_count == 4 and own_cols % PANEL == 0
+        if packed:
+            total = jnp.concatenate(
+                [
+                    lax.dynamic_slice_in_dim(
+                        total, (tok_pos + d) % tok_count * own_cols, own_cols, 1
+                    )
+                    for d in range(tok_count // 2 + 1)
+                ],
+                axis=1,
+            )
+        step = 1
+        while step < gc_count:
+            if aside is not None and 2 * step == gc_count:
+                total, aside = lax.optimization_barrier((total, aside))
+            total += swap(total, "gc", step)
+            step *= 2
+        if packed:
+            pieces = collect(total, "tok")
+        else:
+            pieces = [lax.all_gather(total, "tok", axis=0, tiled=True)]
         own = inverse_factor(pieces, last, 1.0 / group_cols)
         other = swap(own, "gr", 1)
         if beside is not None:
@@ -306,20 +334,17 @@
             [jnp.where(own_groups[o] == gr_pos, own, other) for o in range(owned)]
         )
         of_group = [jnp.where(gr_pos == g, own, other) for g in range(groups)]
-        return of_block, of_group, beside
+        return of_block, of_group, beside, aside
 
     image = image_of(mixed, basis_bf)
     seen = lax.all_gather(seen_by(image), ("gr", "gc"), axis=0, tiled=True)
     second = 0.0
     for j in range(seen.shape[0]):
         second += own_links[:, j][:, None, None] * seen[j][None]
-    of_block, _, second = factor(image, False, second)
+    of_block, _, second, _ = factor(image, False, second)
     mixed = jnp.einsum("otr,osr->ots", second, of_block, precision=HIGH).astype(jnp.bfloat16)
     basis_bf = jnp.einsum("obr,osr->obs", image, of_block, precision=HIGH).astype(jnp.bfloat16)
     image = image_of([mixed], basis_bf)
-    of_block, of_group, _ = factor(image, True)
-    rows = lax.dynamic_slice_in_dim(image, tok_pos * slice_rows, slice_rows, 1)
-    basis = jnp.einsum("obr,osr->obs", rows, of_block, precision=HIGH)
     codes = seen_by(image)
     placed = jnp.concatenate(
         [
@@ -328,6 +353,9 @@
         ],
         axis=1,
     )
+    of_block, of_group, _, placed = factor(image, True, aside=placed)
+    rows = lax.dynamic_slice_in_dim(image, tok_pos * slice_rows, slice_rows, 1)
+    basis = jnp.einsum("obr,osr->obs", rows, of_block, precision=HIGH)
     placed = lax.psum_scatter(placed, ("gr", "gc"), scatter_dimension=0, tiled=True)
     latent = jnp.concatenate(
         [

time: 260 us -> 260 us (level)
  starting transfers between devices: 73.3 us -> 43.7 us
  waiting for transfers between devices: 77.9 us -> 107 us
    ppermute x48 -> x41, waiting for transfers between devices: 74.5 us -> 105 us  [swap(): lax.ppermute(value, axis, [(i, i ^ k) for i in range(lax.axis_size(axis))])]
    ppermute x48 -> x41, starting transfers between devices: 73 us -> 43.6 us  [swap(): lax.ppermute(value, axis, [(i, i ^ k) for i in range(lax.axis_size(axis))])]
  transfers between devices with their start and end apart: 50 -> 43, of which waited for: 24 -> 22; matrix products, arithmetic and copies ran while one was open for 12% -> 12% of each run, Pallas kernels for 15% -> 15%
where the time goes in v2:
time: 260 us; the launch traced here: 259 us
  waiting for transfers between devices  107 us (41%)
  starting transfers between devices  43.7 us (17%)
  Pallas kernels  38.8 us (15%)
  matrix products  28.4 us (11%)
  local copies, waits for them, and re-layouts  16.4 us (6%)
  between operations  16.2 us (6%)
  other arithmetic  8.37 us (3%)
    ppermute x41, waiting for transfers between devices, swap(): lax.ppermute(value, axis, [(i, i ^ k) for i in range(lax.axis_size(axis))])  105 us
    ppermute x41, starting transfers between devices, swap(): lax.ppermute(value, axis, [(i, i ^ k) for i in range(lax.axis_size(axis))])  43.6 us
    pallas_call x2, Pallas kernels, inverse_factor(): pl.pallas_call(functools.partial(factor_kernel, scale, exact), out_shape=...  38.8 us
    dot_general x2, matrix products, factor(): grams = jnp.einsum('obr,obs->ors', own, image, precision=precision)  6.69 us
  transfers between devices with their start and end apart: 43, of which 22 were waited for; matrix products, arithmetic and copies ran while one was open for 12% of the time, Pallas kernels for 15%

profile of v2, /device:TPU:0, one launch (start us, length us, event | category | flops | bytes accessed | tf_op | source)
XLA Modules:
  0.0 259.2 jit_solution(7819108271963255225)
XLA Ops:
  9.3 2.9 %collective-permute-start.10 = (bf16[2,256,256]{2,1,0:T(8,128)(2,1)}, bf16[2,256,256]{2,1,0:T(8,128)(2,1)S(1)}, u32[]{:S(2)}, u32[]{:S(2)}) collective-permute-start(bf16[2,256,256]{2,1,0:T(8,128)(2,1)} %get-tuple-element.104), channel_id=1, source_target_pairs={{0,8},{8,0},{16,24},{24,16},{1,9},{9,1},{17,25},{25,17},{2,10},{10... | collective-permute-start | bytes 786440 | tf_op jit(solution)/shard_map/ppermute | solution.py:194
  23.0 4.3 %collective-permute-done.11 = bf16[2,256,256]{2,1,0:T(8,128)(2,1)S(1)} collective-permute-done((bf16[2,256,256]{2,1,0:T(8,128)(2,1)}, bf16[2,256,256]{2,1,0:T(8,128)(2,1)S(1)}, u32[]{:S(2)}, u32[]{:S(2)}) %collective-permute-start.11) | collective-permute-done | bytes 262176 | tf_op jit(solution)/shard_map/ppermute | solution.py:194
  44.3 2.7 %collective-permute-start.4 = (bf16[2,128,256]{2,1,0:T(8,128)(2,1)S(1)}, bf16[2,128,256]{2,1,0:T(8,128)(2,1)S(1)}, u32[]{:S(2)}, u32[]{:S(2)}) collective-permute-start(bf16[2,128,256]{2,1,0:T(8,128)(2,1)S(1)} %convolution_convert_fusion.1), channel_id=1, source_target_pairs={{0,2},{1,3},{2,0},{3,1},{4,6},{5,7},{6,4},{7,5},{8,10},{9,11},{10,... | collective-permute-start | bytes 393224 | tf_op jit(solution)/shard_map/ppermute | solution.py:194
  47.0 2.7 %collective-permute-done.7 = bf16[128,2048]{1,0:T(8,128)(2,1)S(1)} collective-permute-done((bf16[128,2048]{1,0:T(8,128)(2,1)S(1)}, bf16[128,2048]{1,0:T(8,128)(2,1)S(1)}, u32[]{:S(2)}, u32[]{:S(2)}) %collective-permute-start.7) | collective-permute-done | bytes 524320 | tf_op jit(solution)/shard_map/ppermute | solution.py:194
  49.7 3.6 %collective-permute-start.5 = (bf16[2,128,256]{2,1,0:T(8,128)(2,1)S(1)}, bf16[2,128,256]{2,1,0:T(8,128)(2,1)S(1)}, u32[]{:S(2)}, u32[]{:S(2)}) collective-permute-start(bf16[2,128,256]{2,1,0:T(8,128)(2,1)S(1)} %convolution_convert_fusion.1), channel_id=1, source_target_pairs={{0,3},{1,2},{2,1},{3,0},{4,7},{5,6},{6,5},{7,4},{8,11},{9,10},{10,... | collective-permute-start | bytes 393224 | tf_op jit(solution)/shard_map/ppermute | solution.py:194
  55.8 3.9 %collective-permute-done.8 = bf16[64,2048]{1,0:T(8,128)(2,1)S(1)} collective-permute-done((bf16[64,2048]{1,0:T(8,128)(2,1)S(1)}, bf16[64,2048]{1,0:T(8,128)(2,1)S(1)}, u32[]{:S(2)}, u32[]{:S(2)}) %collective-permute-start.8) | collective-permute-done | bytes 262176 | tf_op jit(solution)/shard_map/ppermute | solution.py:194
  75.3 2.6 %collective-permute-done.22 = bf16[2,128,256]{2,1,0:T(8,128)(2,1)} collective-permute-done((bf16[2,128,256]{2,1,0:T(8,128)(2,1)}, bf16[2,128,256]{2,1,0:T(8,128)(2,1)}, u32[]{:S(2)}, u32[]{:S(2)}) %collective-permute-start.22) | collective-permute-done | bytes 131104 | tf_op jit(solution)/shard_map/ppermute | solution.py:194
  77.9 3.4 %multiply_add_fusion.1 = f32[2,1024,512]{2,1,0:T(8,128)S(1)} fusion(bf16[2,256,256]{2,1,0:T(8,128)(2,1)S(1)} %copy-done.10, bf16[2,256,256]{2,1,0:T(8,128)(2,1)S(1)} %copy-done.11, bf16[2,256,256]{2,1,0:T(8,128)(2,1)} %get-tuple-element.103, bf16[2,256,256]{2,1,0:T(8,128)(2,1)S(1)} %copy-done.9, bf16[2,256,256]{2,1,0:T(8,128)(2,1)} %get-tuple-element.97, ...), kind=kOutput, calls=%fused_computation.7 | convolution fusion | flops 1102053376 | bytes 9437184 | tf_op jit(solution)/shard_map/tob,otr->obr/dot_general | solution.py:289
  85.4 3.9 %multiply_reduce_fusion.4 = (f32[128,512]{1,0:T(8,128)S(1)}, f32[128,512]{1,0:T(8,128)S(1)}) fusion(f32[2]{0:T(128)S(1)} %get-tuple-element.141, f32[2]{0:T(128)S(1)} %get-tuple-element.142, f32[2,1024,512]{2,1,0:T(8,128)} %copy-done, s32[]{:T(128)S(6)} %select_n.353), kind=kOutput, calls=%fused_computation.84 | convolution fusion | flops 805699584 | bytes 5767188 | tf_op jit(solution)/shard_map/obr,obs->ors/dot_general | solution.py:301
  91.1 20.9 %collective-permute-done.25 = f32[128,384]{1,0:T(8,128)S(1)} collective-permute-done((f32[128,384]{1,0:T(8,128)S(1)}, f32[128,384]{1,0:T(8,128)S(1)}, u32[]{:S(2)}, u32[]{:S(2)}) %collective-permute-start.25) | collective-permute-done | bytes 196640 | tf_op jit(solution)/shard_map/ppermute | solution.py:194
  112.1 23.1 %collective-permute-done.26 = f32[128,384]{1,0:T(8,128)S(1)} collective-permute-done((f32[128,384]{1,0:T(8,128)S(1)}, f32[128,384]{1,0:T(8,128)S(1)}, u32[]{:S(2)}, u32[]{:S(2)}) %collective-permute-start.26) | collective-permute-done | bytes 196640 | tf_op jit(solution)/shard_map/ppermute | solution.py:194
  138.8 4.3 %collective-permute-done.27.refs_1_ = f32[128,384]{1,0:T(8,128)S(1)} collective-permute-done((f32[128,384]{1,0:T(8,128)S(1)}, f32[128,384]{1,0:T(8,128)S(1)}, u32[]{:S(2)}, u32[]{:S(2)}) %collective-permute-start.27) | collective-permute-done | bytes 196640 | tf_op jit(solution)/shard_map/ppermute | solution.py:194
  143.1 3.3 %collective-permute-done.28.refs_2_ = f32[128,384]{1,0:T(8,128)S(1)} collective-permute-done((f32[128,384]{1,0:T(8,128)S(1)}, f32[128,384]{1,0:T(8,128)S(1)}, u32[]{:S(2)}, u32[]{:S(2)}) %collective-permute-start.28) | collective-permute-done | bytes 196640 | tf_op jit(solution)/shard_map/ppermute | solution.py:194
  146.4 18.8 %inverse_factor.2 = f32[512,512]{1,0:T(8,128)S(1)} custom-call(s32[1]{0:T(128)} %bitcast.2.pos_ref, f32[128,384]{1,0:T(8,128)S(1)} %add.338.refs_0_, f32[128,384]{1,0:T(8,128)S(1)} %collective-permute-done.27.refs_1_, f32[128,384]{1,0:T(8,128)S(1)} %collective-permute-done.28.refs_2_, f32[128,384]{1,0:T(8,128)S(1)} %collective-permute-done.29.refs_3_), custom_call_target="tpu_custom_call" | custom-call | flops 12884901888 | bytes 2097152 | tf_op jit(solution)/shard_map/inverse_factor/pallas_call | solution.py:171
  167.5 2.8 %slice_bitcast_fusion.15 = (f32[128,512]{1,0:T(8,128)S(1)}, f32[128,512]{1,0:T(8,128)S(1)}, f32[128,512]{1,0:T(8,128)S(1)}, f32[128,512]{1,0:T(8,128)S(1)}, f32[...) fusion(f32[16,128,512]{2,1,0:T(8,128)} %all-gather.2.cloned.1.c, ...), kind=kLoop, calls=%fused_computation.103 | loop fusion | bytes 8388608 | tf_op jit(solution)/shard_map/mul | solution.py:343
  176.0 4.0 %fusion.12 = bf16[2,1024,512]{2,1,0:T(8,128)(2,1)S(1)} fusion(f32[2,1024,512]{2,1,0:T(8,128)S(1)} %copy-done.1, f32[1,512,512]{2,1,0:T(8,128)S(1)} %get-tuple-element.95, f32[1,512,512]{2,1,0:T(8,128)S(1)} %get-tuple-element.94), kind=kOutput, calls=%fused_computation.18 | convolution fusion | flops 3221749760 | bytes 8388608 | tf_op jit(solution)/shard_map/obr,osr->obs/dot_general | solution.py:346
  181.7 5.9 %collective-permute-done.32 = bf16[2,128,512]{2,1,0:T(8,128)(2,1)S(1)} collective-permute-done((bf16[2,128,512]{2,1,0:T(8,128)(2,1)S(1)}, bf16[2,128,512]{2,1,0:T(8,128)(2,1)S(1)}, u32[]{:S(2)}, u32[]{:S(2)}) %collective-permute-start.32) | collective-permute-done | bytes 262176 | tf_op jit(solution)/shard_map/ppermute | solution.py:194
  188.8 2.8 %multiply_reduce_fusion.2 = (f32[128,512]{1,0:T(8,128)S(1)}, f32[128,512]{1,0:T(8,128)S(1)}) fusion(f32[2]{0:T(128)S(1)} %get-tuple-element.141, f32[2]{0:T(128)S(1)} %get-tuple-element.142, f32[2,1024,512]{2,1,0:T(8,128)S(1)} %multiply_add_fusion, s32[]{:T(128)S(6)} %select_n.353), kind=kOutput, calls=%fused_computation.81 | convolution fusion | flops 1611005952 | bytes 5768196 | tf_op jit(solution)/shard_map/obr,obs->ors/dot_general | solution.py:301
  194.4 5.9 %collective-permute-done.35 = f32[128,384]{1,0:T(8,128)S(1)} collective-permute-done((f32[128,384]{1,0:T(8,128)S(1)}, f32[128,384]{1,0:T(8,128)S(1)}, u32[]{:S(2)}, u32[]{:S(2)}) %collective-permute-start.35) | collective-permute-done | bytes 196640 | tf_op jit(solution)/shard_map/ppermute | solution.py:194
  200.4 11.2 %collective-permute-done.36 = f32[128,384]{1,0:T(8,128)S(1)} collective-permute-done((f32[128,384]{1,0:T(8,128)S(1)}, f32[128,384]{1,0:T(8,128)S(1)}, u32[]{:S(2)}, u32[]{:S(2)}) %collective-permute-start.36) | collective-permute-done | bytes 196640 | tf_op jit(solution)/shard_map/ppermute | solution.py:194
  216.3 3.3 %collective-permute-done.37.refs_1_ = f32[128,384]{1,0:T(8,128)S(1)} collective-permute-done((f32[128,384]{1,0:T(8,128)S(1)}, f32[128,384]{1,0:T(8,128)S(1)}, u32[]{:S(2)}, u32[]{:S(2)}) %collective-permute-start.37) | collective-permute-done | bytes 196640 | tf_op jit(solution)/shard_map/ppermute | solution.py:194
  219.5 4.1 %collective-permute-done.38.refs_2_ = f32[128,384]{1,0:T(8,128)S(1)} collective-permute-done((f32[128,384]{1,0:T(8,128)S(1)}, f32[128,384]{1,0:T(8,128)S(1)}, u32[]{:S(2)}, u32[]{:S(2)}) %collective-permute-start.38) | collective-permute-done | bytes 196640 | tf_op jit(solution)/shard_map/ppermute | solution.py:194
  223.6 20.0 %inverse_factor.3 = f32[512,512]{1,0:T(8,128)S(1)} custom-call(s32[1]{0:T(128)} %bitcast.2.pos_ref, f32[128,384]{1,0:T(8,128)S(1)} %add.360.refs_0_, f32[128,384]{1,0:T(8,128)S(1)} %collective-permute-done.37.refs_1_, f32[128,384]{1,0:T(8,128)S(1)} %collective-permute-done.38.refs_2_, f32[128,384]{1,0:T(8,128)S(1)} %collective-permute-done.39.refs_3_), custom_call_target="tpu_custom_call" | custom-call | flops 12884901888 | bytes 2097152 | tf_op jit(solution)/shard_map/inverse_factor/pallas_call | solution.py:171
  249.0 3.4 %fusion.8 = f32[2,256,512]{2,1,0:T(8,128)} fusion(f32[1,512,512]{2,1,0:T(8,128)S(1)} %get-tuple-element.93, f32[1,512,512]{2,1,0:T(8,128)S(1)} %get-tuple-element.92, f32[2,1024,512]{2,1,0:T(8,128)} %copy-done.2, s32[]{:T(128)S(6)} %select_n.291), kind=kOutput, calls=%fused_computation.14 | convolution fusion | flops 805830656 | bytes 4194308 | tf_op jit(solution)/shard_map/obr,osr->obs/dot_general | solution.py:358
  (193 shorter events, 79.1 us)
Async XLA Ops:
  7.2 160.3 %all-gather.2.cloned.1.call-start = ((), (), s32[]{:S(2)}) async-start(), calls=%async_computation.1 | async-start | bytes 4718592 | tf_op jit(solution)/shard_map/all_gather | solution.py:340
  9.3 13.6 %collective-permute-start.10 = (bf16[2,256,256]{2,1,0:T(8,128)(2,1)}, bf16[2,256,256]{2,1,0:T(8,128)(2,1)S(1)}, u32[]{:S(2)}, u32[]{:S(2)}) collective-permute-start(bf16[2,256,256]{2,1,0:T(8,128)(2,1)} %get-tuple-element.104), channel_id=1, source_target_pairs={{0,8},{8,0},{16,24},{24,16},{1,9},{9,1},{17,25},{25,17},{2,10},{10... | collective-permute-start | bytes 786440 | tf_op jit(solution)/shard_map/ppermute | solution.py:194
  12.3 15.1 %collective-permute-start.11 = (bf16[2,256,256]{2,1,0:T(8,128)(2,1)}, bf16[2,256,256]{2,1,0:T(8,128)(2,1)S(1)}, u32[]{:S(2)}, u32[]{:S(2)}) collective-permute-start(bf16[2,256,256]{2,1,0:T(8,128)(2,1)} %get-tuple-element.104), channel_id=1, source_target_pairs={{0,16},{8,24},{16,0},{24,8},{1,17},{9,25},{17,1},{25,9},{2,18},{10... | collective-permute-start | bytes 786440 | tf_op jit(solution)/shard_map/ppermute | solution.py:194
  13.8 13.5 %collective-permute-start.12 = (bf16[2,256,256]{2,1,0:T(8,128)(2,1)}, bf16[2,256,256]{2,1,0:T(8,128)(2,1)S(1)}, u32[]{:S(2)}, u32[]{:S(2)}) collective-permute-start(bf16[2,256,256]{2,1,0:T(8,128)(2,1)} %get-tuple-element.104), channel_id=1, source_target_pairs={{0,24},{8,16},{16,8},{24,0},{1,25},{9,17},{17,9},{25,1},{2,26},{10... | collective-permute-start | bytes 786440 | tf_op jit(solution)/shard_map/ppermute | solution.py:194
  13.8 19.4 %collective-permute-start = (bf16[2,256,256]{2,1,0:T(8,128)(2,1)S(1)}, bf16[2,256,256]{2,1,0:T(8,128)(2,1)S(1)}, u32[]{:S(2)}, u32[]{:S(2)}) collective-permute-start(bf16[2,256,256]{2,1,0:T(8,128)(2,1)S(1)} %get-tuple-element.19), channel_id=1, source_target_pairs={{0,8},{8,0},{16,24},{24,16},{1,9},{9,1},{17,25},{25,17},{2,10},{10... | collective-permute-start | bytes 786440 | tf_op jit(solution)/shard_map/ppermute | solution.py:194
  15.7 21.4 %collective-permute-start.1 = (bf16[2,256,256]{2,1,0:T(8,128)(2,1)S(1)}, bf16[2,256,256]{2,1,0:T(8,128)(2,1)}, u32[]{:S(2)}, u32[]{:S(2)}) collective-permute-start(bf16[2,256,256]{2,1,0:T(8,128)(2,1)S(1)} %get-tuple-element.19), channel_id=1, source_target_pairs={{0,16},{8,24},{16,0},{24,8},{1,17},{9,25},{17,1},{25,9},{2,18},{10... | collective-permute-start | bytes 786440 | tf_op jit(solution)/shard_map/ppermute | solution.py:194
  23.0 14.2 %collective-permute-start.2 = (bf16[2,256,256]{2,1,0:T(8,128)(2,1)S(1)}, bf16[2,256,256]{2,1,0:T(8,128)(2,1)S(1)}, u32[]{:S(2)}, u32[]{:S(2)}) collective-permute-start(bf16[2,256,256]{2,1,0:T(8,128)(2,1)S(1)} %get-tuple-element.19), channel_id=1, source_target_pairs={{0,24},{8,16},{16,8},{24,0},{1,25},{9,17},{17,9},{25,1},{2,26},{10... | collective-permute-start | bytes 786440 | tf_op jit(solution)/shard_map/ppermute | solution.py:194
  29.0 13.7 %collective-permute-start.13 = (bf16[2,128,256]{2,1,0:T(8,128)(2,1)S(1)}, bf16[2,128,256]{2,1,0:T(8,128)(2,1)S(1)}, u32[]{:S(2)}, u32[]{:S(2)}) collective-permute-start(bf16[2,128,256]{2,1,0:T(8,128)(2,1)S(1)} %convolution_convert_fusion), channel_id=1, source_target_pairs={{0,1},{1,0},{2,3},{3,2},{4,5},{5,4},{6,7},{7,6},{8,9},{9,8},{10,11... | collective-permute-start | bytes 393224 | tf_op jit(solution)/shard_map/ppermute | solution.py:194
  30.6 13.7 %collective-permute-start.14 = (bf16[2,128,256]{2,1,0:T(8,128)(2,1)S(1)}, bf16[2,128,256]{2,1,0:T(8,128)(2,1)S(1)}, u32[]{:S(2)}, u32[]{:S(2)}) collective-permute-start(bf16[2,128,256]{2,1,0:T(8,128)(2,1)S(1)} %convolution_convert_fusion), channel_id=1, source_target_pairs={{0,2},{1,3},{2,0},{3,1},{4,6},{5,7},{6,4},{7,5},{8,10},{9,11},{10,... | collective-permute-start | bytes 393224 | tf_op jit(solution)/shard_map/ppermute | solution.py:194
  33.2 21.7 %collective-permute-start.15 = (bf16[2,128,256]{2,1,0:T(8,128)(2,1)S(1)}, bf16[2,128,256]{2,1,0:T(8,128)(2,1)S(1)}, u32[]{:S(2)}, u32[]{:S(2)}) collective-permute-start(bf16[2,128,256]{2,1,0:T(8,128)(2,1)S(1)} %convolution_convert_fusion), channel_id=1, source_target_pairs={{0,3},{1,2},{2,1},{3,0},{4,7},{5,6},{6,5},{7,4},{8,11},{9,10},{10,... | collective-permute-start | bytes 393224 | tf_op jit(solution)/shard_map/ppermute | solution.py:194
  37.2 12.5 %collective-permute-start.7 = (bf16[128,2048]{1,0:T(8,128)(2,1)S(1)}, bf16[128,2048]{1,0:T(8,128)(2,1)S(1)}, u32[]{:S(2)}, u32[]{:S(2)}) collective-permute-start(bf16[128,2048]{1,0:T(8,128)(2,1)S(1)} %copy-done.4), channel_id=1, source_target_pairs={{0,16},{8,24},{16,0},{24,8},{1,17},{9,25},{17,1},{25,9},{2,18},{10... | collective-permute-start | bytes 1572872 | tf_op jit(solution)/shard_map/ppermute | solution.py:194
  38.7 14.6 %collective-permute-start.6 = (bf16[128,2048]{1,0:T(8,128)(2,1)S(1)}, bf16[128,2048]{1,0:T(8,128)(2,1)S(1)}, u32[]{:S(2)}, u32[]{:S(2)}) collective-permute-start(bf16[128,2048]{1,0:T(8,128)(2,1)S(1)} %copy-done.4), channel_id=1, source_target_pairs={{0,8},{8,0},{16,24},{24,16},{1,9},{9,1},{17,25},{25,17},{2,10},{10... | collective-permute-start | bytes 1572872 | tf_op jit(solution)/shard_map/ppermute | solution.py:194
  42.6 18.7 %collective-permute-start.3 = (bf16[2,128,256]{2,1,0:T(8,128)(2,1)S(1)}, bf16[2,128,256]{2,1,0:T(8,128)(2,1)S(1)}, u32[]{:S(2)}, u32[]{:S(2)}) collective-permute-start(bf16[2,128,256]{2,1,0:T(8,128)(2,1)S(1)} %convolution_convert_fusion.1), channel_id=1, source_target_pairs={{0,1},{1,0},{2,3},{3,2},{4,5},{5,4},{6,7},{7,6},{8,9},{9,8},{10,11... | collective-permute-start | bytes 393224 | tf_op jit(solution)/shard_map/ppermute | solution.py:194
  44.3 17.1 %collective-permute-start.4 = (bf16[2,128,256]{2,1,0:T(8,128)(2,1)S(1)}, bf16[2,128,256]{2,1,0:T(8,128)(2,1)S(1)}, u32[]{:S(2)}, u32[]{:S(2)}) collective-permute-start(bf16[2,128,256]{2,1,0:T(8,128)(2,1)S(1)} %convolution_convert_fusion.1), channel_id=1, source_target_pairs={{0,2},{1,3},{2,0},{3,1},{4,6},{5,7},{6,4},{7,5},{8,10},{9,11},{10,... | collective-permute-start | bytes 393224 | tf_op jit(solution)/shard_map/ppermute | solution.py:194
  49.7 11.7 %collective-permute-start.5 = (bf16[2,128,256]{2,1,0:T(8,128)(2,1)S(1)}, bf16[2,128,256]{2,1,0:T(8,128)(2,1)S(1)}, u32[]{:S(2)}, u32[]{:S(2)}) collective-permute-start(bf16[2,128,256]{2,1,0:T(8,128)(2,1)S(1)} %convolution_convert_fusion.1), channel_id=1, source_target_pairs={{0,3},{1,2},{2,1},{3,0},{4,7},{5,6},{6,5},{7,4},{8,11},{9,10},{10,... | collective-permute-start | bytes 393224 | tf_op jit(solution)/shard_map/ppermute | solution.py:194
  63.8 10.6 %collective-permute-start.18 = (bf16[2,128,256]{2,1,0:T(8,128)(2,1)S(1)}, bf16[2,128,256]{2,1,0:T(8,128)(2,1)}, u32[]{:S(2)}, u32[]{:S(2)}) collective-permute-start(bf16[2,128,256]{2,1,0:T(8,128)(2,1)S(1)} %add_convert_fusion.1), channel_id=1, source_target_pairs={{0,16},{8,24},{16,0},{24,8},{1,17},{9,25},{17,1},{25,9},{2,18},{10... | collective-permute-start | bytes 393224 | tf_op jit(solution)/shard_map/ppermute | solution.py:194
  85.2 160.6 %reduce-scatter.4.cloned.1.call-start = ((), (), s32[]{:S(2)}) async-start(), calls=%async_computation.2 | async-start | bytes 589824
  91.0 21.0 %collective-permute-start.25 = (f32[128,384]{1,0:T(8,128)S(1)}, f32[128,384]{1,0:T(8,128)S(1)}, u32[]{:S(2)}, u32[]{:S(2)}) collective-permute-start(f32[128,384]{1,0:T(8,128)S(1)} %pad_maximum_fusion.9), channel_id=1, source_target_pairs={{0,1},{1,0},{2,3},{3,2},{4,5},{5,4},{6,7},{7,6},{8,9},{9,8},{10,11... | collective-permute-start | bytes 589832 | tf_op jit(solution)/shard_map/ppermute | solution.py:194
  112.0 23.1 %collective-permute-start.26 = (f32[128,384]{1,0:T(8,128)S(1)}, f32[128,384]{1,0:T(8,128)S(1)}, u32[]{:S(2)}, u32[]{:S(2)}) collective-permute-start(f32[128,384]{1,0:T(8,128)S(1)} %fusion.90), channel_id=1, source_target_pairs={{0,2},{1,3},{2,0},{3,1},{4,6},{5,7},{6,4},{7,5},{8,10},{9,11},{10,... | collective-permute-start | bytes 589832 | tf_op jit(solution)/shard_map/ppermute | solution.py:194
  173.5 14.0 %collective-permute-start.32 = (bf16[2,128,512]{2,1,0:T(8,128)(2,1)S(1)}, bf16[2,128,512]{2,1,0:T(8,128)(2,1)S(1)}, u32[]{:S(2)}, u32[]{:S(2)}) collective-permute-start(bf16[2,128,512]{2,1,0:T(8,128)(2,1)S(1)} %fusion.17), channel_id=1, source_target_pairs={{0,16},{8,24},{16,0},{24,8},{1,17},{9,25},{17,1},{25,9},{2,18},{10... | collective-permute-start | bytes 786440 | tf_op jit(solution)/shard_map/ppermute | solution.py:194
  174.3 13.3 %collective-permute-start.33 = (bf16[2,128,512]{2,1,0:T(8,128)(2,1)S(1)}, bf16[2,128,512]{2,1,0:T(8,128)(2,1)S(1)}, u32[]{:S(2)}, u32[]{:S(2)}) collective-permute-start(bf16[2,128,512]{2,1,0:T(8,128)(2,1)S(1)} %fusion.17), channel_id=1, source_target_pairs={{0,24},{8,16},{16,8},{24,0},{1,25},{9,17},{17,9},{25,1},{2,26},{10... | collective-permute-start | bytes 786440 | tf_op jit(solution)/shard_map/ppermute | solution.py:194
  200.4 11.3 %collective-permute-start.36 = (f32[128,384]{1,0:T(8,128)S(1)}, f32[128,384]{1,0:T(8,128)S(1)}, u32[]{:S(2)}, u32[]{:S(2)}) collective-permute-start(f32[128,384]{1,0:T(8,128)S(1)} %fusion.89), channel_id=1, source_target_pairs={{0,2},{1,3},{2,0},{3,1},{4,6},{5,7},{6,4},{7,5},{8,10},{9,11},{10,... | collective-permute-start | bytes 589832 | tf_op jit(solution)/shard_map/ppermute | solution.py:194
  212.9 10.7 %collective-permute-start.38 = (f32[128,384]{1,0:T(8,128)S(1)}, f32[128,384]{1,0:T(8,128)S(1)}, u32[]{:S(2)}, u32[]{:S(2)}) collective-permute-start(f32[128,384]{1,0:T(8,128)S(1)} %add.360.refs_0_), channel_id=1, source_target_pairs={{0,16},{8,24},{16,0},{24,8},{1,17},{9,25},{17,1},{25,9},{2,18},{10... | collective-permute-start | bytes 589832 | tf_op jit(solution)/shard_map/ppermute | solution.py:194
  213.4 10.2 %collective-permute-start.39 = (f32[128,384]{1,0:T(8,128)S(1)}, f32[128,384]{1,0:T(8,128)S(1)}, u32[]{:S(2)}, u32[]{:S(2)}) collective-permute-start(f32[128,384]{1,0:T(8,128)S(1)} %add.360.refs_0_), channel_id=1, source_target_pairs={{0,24},{8,16},{16,8},{24,0},{1,25},{9,17},{17,9},{25,1},{2,26},{10... | collective-permute-start | bytes 589832 | tf_op jit(solution)/shard_map/ppermute | solution.py:194
  (48 other events, 368.2 us)
Sparse Core Ops, SparseCore 0:
  85.4 53.3 all-gather.1
  216.4 29.4 reduce-scatter.3

commit v3 on v2

--- a/solution.py
+++ b/solution.py
@@ -198,13 +198,15 @@
     return [swap(value, axis, k) for k in range(lax.axis_size(axis))]
 
 
-def collect_relayed(value, axis):
+def collect_relayed(value, axis, dim):
     if lax.axis_size(axis) != 4:
         return collect(value, axis)
-    half = value.shape[0] // 2
     near, side = swap(value, axis, 1), swap(value, axis, 2)
-    far = [swap(side[:half], axis, 1), swap(near[half:], axis, 2)]
-    return [value, near, side, jnp.concatenate(far, axis=0)]
+    far = [
+        swap(jnp.split(side, 2, axis=dim)[0], axis, 1),
+        swap(jnp.split(near, 2, axis=dim)[1], axis, 2),
+    ]
+    return [value, near, side, jnp.concatenate(far, axis=dim)]
 
 
 def per_device(acts, init_basis, kept, member):
@@ -242,10 +244,11 @@
     init_bf = init_basis.astype(jnp.bfloat16)
     width = rank // CHUNKS
     init_pieces = [
-        collect(init_bf[:, :, c * width : (c + 1) * width], "tok") for c in range(CHUNKS)
+        collect_relayed(init_bf[:, :, c * width : (c + 1) * width], "tok", 1)
+        for c in range(CHUNKS)
     ]
     init_pieces[-1], acts_late = lax.optimization_barrier((init_pieces[-1], acts))
-    x_pieces = collect_relayed(acts_late, "tok")
+    x_pieces = collect_relayed(acts_late, "tok", 0)
 
     def combine(rows_of_links, pieces, sources):
         total = 0.0
@@ -264,7 +267,16 @@
             preferred_element_type=jnp.float32,
         ).astype(jnp.bfloat16)
         near.append(collect(proj, "gc"))
-    near[-1], x_pieces = lax.optimization_barrier((near[-1], x_pieces))
+    sources = [(gr_pos * gc_count + (gc_pos ^ b)) * owned for b in range(gc_count)]
+
+    def mix(pieces):
+        own = combine(own_links, pieces, sources)
+        other = combine(partner_links, pieces, sources)
+        return collect((own + swap(other, "gr", 1)).astype(jnp.bfloat16), "tok")
+
+    mixed = [mix(pieces) for pieces in near[:-1]]
+    near[-1], x_pieces, mixed = lax.optimization_barrier((near[-1], x_pieces, mixed))
+    mixed.append(mix(near[-1]))
     full_x = jnp.concatenate(x_pieces, axis=0).reshape(total_tokens, owned, block_cols)
     basis_bf = jnp.concatenate(
         [
@@ -275,17 +287,9 @@
         ],
         axis=2,
     )
-    sources = [(gr_pos * gc_count + (gc_pos ^ b)) * owned for b in range(gc_count)]
-    mixed = []
-    for pieces in near:
-        own = combine(own_links, pieces, sources)
-        other = combine(partner_links, pieces, sources)
-        mixed.append((own + swap(other, "gr", 1)).astype(jnp.bfloat16))
 
     def image_of(parts, basis_bf):
-        full = jnp.concatenate(
-            [jnp.concatenate(collect(part, "tok"), axis=1) for part in parts], axis=2
-        )
+        full = jnp.concatenate([jnp.concatenate(part, axis=1) for part in parts], axis=2)
         cover = jnp.einsum("tob,otr->obr", full_x, full, preferred_element_type=jnp.float32)
         return cover / total_tokens + ridge * basis_bf.astype(jnp.float32)
 
@@ -295,7 +299,7 @@
             for part in split(image)
         )
 
-    def factor(image, last, beside=None, aside=None):
+    def factor(image, last, beside):
         precision = HIGHEST if last else HIGH
         own = lax.dynamic_slice_in_dim(image, tok_pos * own_cols, own_cols, 2)
         grams = jnp.einsum("obr,obs->ors", own, image, precision=precision)
@@ -318,33 +322,39 @@
             )
         step = 1
         while step < gc_count:
-            if aside is not None and 2 * step == gc_count:
-                total, aside = lax.optimization_barrier((total, aside))
+            if last and 2 * step == gc_count:
+                total, beside = lax.optimization_barrier((total, beside))
             total += swap(total, "gc", step)
             step *= 2
+        if not last:
+            total, beside = lax.optimization_barrier((total, beside))
+            beside = mix_seen(beside)
         if packed:
             pieces = collect(total, "tok")
         else:
             pieces = [lax.all_gather(total, "tok", axis=0, tiled=True)]
         own = inverse_factor(pieces, last, 1.0 / group_cols)
         other = swap(own, "gr", 1)
-        if beside is not None:
+        if not last:
             other, beside = lax.optimization_barrier((other, beside))
         of_block = jnp.stack(
             [jnp.where(own_groups[o] == gr_pos, own, other) for o in range(owned)]
         )
         of_group = [jnp.where(gr_pos == g, own, other) for g in range(groups)]
-        return of_block, of_group, beside, aside
+        return of_block, of_group, beside
 
     image = image_of(mixed, basis_bf)
-    seen = lax.all_gather(seen_by(image), ("gr", "gc"), axis=0, tiled=True)
-    second = 0.0
-    for j in range(seen.shape[0]):
-        second += own_links[:, j][:, None, None] * seen[j][None]
-    of_block, _, second, _ = factor(image, False, second)
+    def mix_seen(seen):
+        seen = lax.all_gather(seen, ("gr", "gc"), axis=0, tiled=True)
+        total = 0.0
+        for j in range(seen.shape[0]):
+            total += own_links[:, j][:, None, None] * seen[j][None]
+        return total
+
+    of_block, _, second = factor(image, False, seen_by(image))
     mixed = jnp.einsum("otr,osr->ots", second, of_block, precision=HIGH).astype(jnp.bfloat16)
     basis_bf = jnp.einsum("obr,osr->obs", image, of_block, precision=HIGH).astype(jnp.bfloat16)
-    image = image_of([mixed], basis_bf)
+    image = image_of([collect(mixed, "tok")], basis_bf)
     codes = seen_by(image)
     placed = jnp.concatenate(
         [
@@ -353,7 +363,7 @@
         ],
         axis=1,
     )
-    of_block, of_group, _, placed = factor(image, True, aside=placed)
+    of_block, of_group, placed = factor(image, True, placed)
     rows = lax.dynamic_slice_in_dim(image, tok_pos * slice_rows, slice_rows, 1)
     basis = jnp.einsum("obr,osr->obs", rows, of_block, precision=HIGH)
     placed = lax.psum_scatter(placed, ("gr", "gc"), scatter_dimension=0, tiled=True)

time: 260 us -> 250 us (0.962)
  waiting for transfers between devices: 107 us -> 93.7 us
    ppermute x41 -> x43, waiting for transfers between devices: 105 us -> 77.6 us  [swap(): lax.ppermute(value, axis, [(i, i ^ k) for i in range(lax.axis_size(axis))])]
    all_gather x1, waiting for transfers between devices: 0.02 us -> 12.9 us  [mix_seen(): seen = lax.all_gather(seen, ('gr', 'gc'), axis=0, tiled=True)]
    ppermute x41 -> x43, starting transfers between devices: 43.6 us -> 45.9 us  [swap(): lax.ppermute(value, axis, [(i, i ^ k) for i in range(lax.axis_size(axis))])]
    unnamed x64 -> x93, local copies, waits for them, and re-layouts: 4.69 us -> 5.68 us
  transfers between devices with their start and end apart: 43 -> 45, of which waited for: 22 -> 27; matrix products, arithmetic and copies ran while one was open for 12% -> 13% of each run, Pallas kernels for 15% -> 16%
where the time goes in v3:
time: 250 us; the launch traced here: 249 us
  waiting for transfers between devices  93.7 us (37%)
  starting transfers between devices  45.9 us (18%)
  Pallas kernels  38.8 us (16%)
  matrix products  28.3 us (11%)
  local copies, waits for them, and re-layouts  17.9 us (7%)
  between operations  16.2 us (6%)
  other arithmetic  8.58 us (3%)
    ppermute x43, waiting for transfers between devices, swap(): lax.ppermute(value, axis, [(i, i ^ k) for i in range(lax.axis_size(axis))])  77.6 us
    ppermute x43, starting transfers between devices, swap(): lax.ppermute(value, axis, [(i, i ^ k) for i in range(lax.axis_size(axis))])  45.9 us
    pallas_call x2, Pallas kernels, inverse_factor(): pl.pallas_call(functools.partial(factor_kernel, scale, exact), out_shape=...  38.8 us
    all_gather x1, waiting for transfers between devices, mix_seen(): seen = lax.all_gather(seen, ('gr', 'gc'), axis=0, tiled=True)  12.9 us
    dot_general x4, matrix products, seen_by(): jnp.einsum('tob,obr->otr', own_x, part, preferred_element_type=jnp.float32)  6.09 us
    unnamed x93, local copies, waits for them, and re-layouts  5.68 us
  transfers between devices with their start and end apart: 45, of which 27 were waited for; matrix products, arithmetic and copies ran while one was open for 13% of the time, Pallas kernels for 16%

profile of v3, /device:TPU:0, one launch (start us, length us, event | category | flops | bytes accessed | tf_op | source)
XLA Modules:
  0.0 249.4 jit_solution(5253540595994590492)
XLA Ops:
  9.4 2.9 %collective-permute-start.11 = (bf16[2,256,256]{2,1,0:T(8,128)(2,1)}, bf16[2,256,256]{2,1,0:T(8,128)(2,1)S(1)}, u32[]{:S(2)}, u32[]{:S(2)}) collective-permute-start(bf16[2,256,256]{2,1,0:T(8,128)(2,1)} %get-tuple-element.116), channel_id=1, source_target_pairs={{0,8},{8,0},{16,24},{24,16},{1,9},{9,1},{17,25},{25,17},{2,10},{10... | collective-permute-start | bytes 786440 | tf_op jit(solution)/shard_map/ppermute | solution.py:194
  40.5 3.5 %collective-permute-start.5 = (bf16[2,128,256]{2,1,0:T(8,128)(2,1)S(1)}, bf16[2,128,256]{2,1,0:T(8,128)(2,1)S(1)}, u32[]{:S(2)}, u32[]{:S(2)}) collective-permute-start(bf16[2,128,256]{2,1,0:T(8,128)(2,1)S(1)} %convolution_convert_fusion.1), channel_id=1, source_target_pairs={{0,2},{1,3},{2,0},{3,1},{4,6},{5,7},{6,4},{7,5},{8,10},{9,11},{10,... | collective-permute-start | bytes 393224 | tf_op jit(solution)/shard_map/ppermute | solution.py:194
  48.4 5.1 %collective-permute-done.7 = bf16[128,2048]{1,0:T(8,128)(2,1)S(1)} collective-permute-done((bf16[128,2048]{1,0:T(8,128)(2,1)S(1)}, bf16[128,2048]{1,0:T(8,128)(2,1)S(1)}, u32[]{:S(2)}, u32[]{:S(2)}) %collective-permute-start.7) | collective-permute-done | bytes 524320 | tf_op jit(solution)/shard_map/ppermute | solution.py:194
  54.1 5.3 %collective-permute-done.8 = bf16[128,2048]{1,0:T(8,128)(2,1)S(1)} collective-permute-done((bf16[128,2048]{1,0:T(8,128)(2,1)S(1)}, bf16[128,2048]{1,0:T(8,128)(2,1)S(1)}, u32[]{:S(2)}, u32[]{:S(2)}) %collective-permute-start.8) | collective-permute-done | bytes 524320 | tf_op jit(solution)/shard_map/ppermute | solution.py:194
  80.7 3.7 %collective-permute-done.24 = bf16[2,128,256]{2,1,0:T(8,128)(2,1)} collective-permute-done((bf16[2,128,256]{2,1,0:T(8,128)(2,1)}, bf16[2,128,256]{2,1,0:T(8,128)(2,1)}, u32[]{:S(2)}, u32[]{:S(2)}) %collective-permute-start.24) | collective-permute-done | bytes 131104 | tf_op jit(solution)/shard_map/ppermute | solution.py:194
  84.4 3.4 %multiply_add_fusion.1 = f32[2,1024,512]{2,1,0:T(8,128)S(1)} fusion(bf16[2,256,256]{2,1,0:T(8,128)(2,1)S(1)} %copy-done.11, bf16[2,256,256]{2,1,0:T(8,128)(2,1)S(1)} %copy-done.12, bf16[2,256,256]{2,1,0:T(8,128)(2,1)} %get-tuple-element.115, bf16[2,256,256]{2,1,0:T(8,128)(2,1)S(1)} %copy-done.10, bf16[2,256,256]{2,1,0:T(8,128)(2,1)} %get-tuple-element.109, ...), kind=kOutput, calls=%fused_computation.7 | convolution fusion | flops 1102053376 | bytes 9437184 | tf_op jit(solution)/shard_map/tob,otr->obr/dot_general | solution.py:293
  91.5 3.3 %fusion.4 = f32[2,512,128]{2,1,0:T(8,128)S(1)} fusion(bf16[128,2,1024]{0,2,1:T(8,128)(2,1)S(1)} %bitcast.126, f32[2,1024,512]{2,1,0:T(8,128)} %copy-done), kind=kOutput, calls=%fused_computation.9 | convolution fusion | flops 271581184 | bytes 5242880 | tf_op jit(solution)/shard_map/tob,obr->otr/dot_general | solution.py:298
  94.8 3.7 %collective-permute-done.27 = f32[128,384]{1,0:T(8,128)S(1)} collective-permute-done((f32[128,384]{1,0:T(8,128)S(1)}, f32[128,384]{1,0:T(8,128)S(1)}, u32[]{:S(2)}, u32[]{:S(2)}) %collective-permute-start.27) | collective-permute-done | bytes 196640 | tf_op jit(solution)/shard_map/ppermute | solution.py:194
  100.6 9.1 %collective-permute-done.28 = f32[128,384]{1,0:T(8,128)S(1)} collective-permute-done((f32[128,384]{1,0:T(8,128)S(1)}, f32[128,384]{1,0:T(8,128)S(1)}, u32[]{:S(2)}, u32[]{:S(2)}) %collective-permute-start.28) | collective-permute-done | bytes 196640 | tf_op jit(solution)/shard_map/ppermute | solution.py:194
  114.4 4.3 %collective-permute-done.29.refs_1_ = f32[128,384]{1,0:T(8,128)S(1)} collective-permute-done((f32[128,384]{1,0:T(8,128)S(1)}, f32[128,384]{1,0:T(8,128)S(1)}, u32[]{:S(2)}, u32[]{:S(2)}) %collective-permute-start.29) | collective-permute-done | bytes 196640 | tf_op jit(solution)/shard_map/ppermute | solution.py:194
  119.6 3.2 %collective-permute-done.31.refs_3_ = f32[128,384]{1,0:T(8,128)S(1)} collective-permute-done((f32[128,384]{1,0:T(8,128)S(1)}, f32[128,384]{1,0:T(8,128)S(1)}, u32[]{:S(2)}, u32[]{:S(2)}) %collective-permute-start.31) | collective-permute-done | bytes 196640 | tf_op jit(solution)/shard_map/ppermute | solution.py:194
  122.8 18.8 %inverse_factor.2 = f32[512,512]{1,0:T(8,128)S(1)} custom-call(s32[1]{0:T(128)} %bitcast.10.pos_ref, f32[128,384]{1,0:T(8,128)S(1)} %add.338.refs_0_, f32[128,384]{1,0:T(8,128)S(1)} %collective-permute-done.29.refs_1_, f32[128,384]{1,0:T(8,128)S(1)} %collective-permute-done.30.refs_2_, f32[128,384]{1,0:T(8,128)S(1)} %collective-permute-done.31.refs_3_), custom_call_target="tpu_custom_call" | custom-call | flops 12884901888 | bytes 2097152 | tf_op jit(solution)/shard_map/inverse_factor/pallas_call | solution.py:171
  143.9 12.9 %all-gather.2.cloned.1.call-done = f32[16,128,512]{2,1,0:T(8,128)} async-done(((f32[2,128,512]{2,1,0:T(8,128)}), f32[16,128,512]{2,1,0:T(8,128)}) %all-gather.2.cloned.1.call-update) | async-done | bytes 4194320 | tf_op jit(solution)/shard_map/all_gather | solution.py:348
  156.9 2.8 %slice_bitcast_fusion.15 = (f32[128,512]{1,0:T(8,128)S(1)}, f32[128,512]{1,0:T(8,128)S(1)}, f32[128,512]{1,0:T(8,128)S(1)}, f32[128,512]{1,0:T(8,128)S(1)}, f32[...) fusion(f32[16,128,512]{2,1,0:T(8,128)} %all-gather.2.cloned.1.c, ...), kind=kLoop, calls=%fused_computation.96 | loop fusion | bytes 8388608 | tf_op jit(solution)/shard_map/mul | solution.py:351
  165.4 4.0 %fusion.12 = bf16[2,1024,512]{2,1,0:T(8,128)(2,1)S(1)} fusion(f32[2,1024,512]{2,1,0:T(8,128)S(1)} %copy-done.2, f32[1,512,512]{2,1,0:T(8,128)S(1)} %get-tuple-element.107, f32[1,512,512]{2,1,0:T(8,128)S(1)} %get-tuple-element.106), kind=kOutput, calls=%fused_computation.18 | convolution fusion | flops 3221749760 | bytes 8388608 | tf_op jit(solution)/shard_map/obr,osr->obs/dot_general | solution.py:356
  171.0 6.1 %collective-permute-done.34 = bf16[2,128,512]{2,1,0:T(8,128)(2,1)S(1)} collective-permute-done((bf16[2,128,512]{2,1,0:T(8,128)(2,1)S(1)}, bf16[2,128,512]{2,1,0:T(8,128)(2,1)S(1)}, u32[]{:S(2)}, u32[]{:S(2)}) %collective-permute-start.34) | collective-permute-done | bytes 262176 | tf_op jit(solution)/shard_map/ppermute | solution.py:194
  178.4 2.8 %multiply_reduce_fusion.2 = (f32[128,512]{1,0:T(8,128)S(1)}, f32[128,512]{1,0:T(8,128)S(1)}) fusion(f32[2]{0:T(128)S(1)} %copy-done.34, f32[2]{0:T(128)S(1)} %copy-done.36, f32[2,1024,512]{2,1,0:T(8,128)S(1)} %multiply_add_fusion, s32[]{:T(128)S(6)} %select_n.353), kind=kOutput, calls=%fused_computation.74 | convolution fusion | flops 1611005952 | bytes 5768196 | tf_op jit(solution)/shard_map/obr,obs->ors/dot_general | solution.py:305
  184.0 5.9 %collective-permute-done.37 = f32[128,384]{1,0:T(8,128)S(1)} collective-permute-done((f32[128,384]{1,0:T(8,128)S(1)}, f32[128,384]{1,0:T(8,128)S(1)}, u32[]{:S(2)}, u32[]{:S(2)}) %collective-permute-start.37) | collective-permute-done | bytes 196640 | tf_op jit(solution)/shard_map/ppermute | solution.py:194
  191.1 10.2 %collective-permute-done.38 = f32[128,384]{1,0:T(8,128)S(1)} collective-permute-done((f32[128,384]{1,0:T(8,128)S(1)}, f32[128,384]{1,0:T(8,128)S(1)}, u32[]{:S(2)}, u32[]{:S(2)}) %collective-permute-start.38) | collective-permute-done | bytes 196640 | tf_op jit(solution)/shard_map/ppermute | solution.py:194
  205.9 3.3 %collective-permute-done.39.refs_1_ = f32[128,384]{1,0:T(8,128)S(1)} collective-permute-done((f32[128,384]{1,0:T(8,128)S(1)}, f32[128,384]{1,0:T(8,128)S(1)}, u32[]{:S(2)}, u32[]{:S(2)}) %collective-permute-start.39) | collective-permute-done | bytes 196640 | tf_op jit(solution)/shard_map/ppermute | solution.py:194
  210.1 3.2 %collective-permute-done.41.refs_3_ = f32[128,384]{1,0:T(8,128)S(1)} collective-permute-done((f32[128,384]{1,0:T(8,128)S(1)}, f32[128,384]{1,0:T(8,128)S(1)}, u32[]{:S(2)}, u32[]{:S(2)}) %collective-permute-start.41) | collective-permute-done | bytes 196640 | tf_op jit(solution)/shard_map/ppermute | solution.py:194
  213.3 20.0 %inverse_factor.3 = f32[512,512]{1,0:T(8,128)S(1)} custom-call(s32[1]{0:T(128)} %bitcast.10.pos_ref, f32[128,384]{1,0:T(8,128)S(1)} %add.360.refs_0_, f32[128,384]{1,0:T(8,128)S(1)} %collective-permute-done.39.refs_1_, f32[128,384]{1,0:T(8,128)S(1)} %collective-permute-done.40.refs_2_, f32[128,384]{1,0:T(8,128)S(1)} %collective-permute-done.41.refs_3_), custom_call_target="tpu_custom_call" | custom-call | flops 12884901888 | bytes 2097152 | tf_op jit(solution)/shard_map/inverse_factor/pallas_call | solution.py:171
  233.4 3.1 %reduce-scatter.4.cloned.1.call-done = f32[16,1024]{1,0:T(8,128)} async-done(((f32[128,1024]{1,0:T(8,128)}), f32[16,1024]{1,0:T(8,128)}) %reduce-scatter.4.cloned.1.call-update) | async-done | bytes 65552
  239.2 3.4 %fusion.8 = f32[2,256,512]{2,1,0:T(8,128)} fusion(f32[1,512,512]{2,1,0:T(8,128)S(1)} %get-tuple-element.105, f32[1,512,512]{2,1,0:T(8,128)S(1)} %get-tuple-element.104, f32[2,1024,512]{2,1,0:T(8,128)} %copy-done.3, s32[]{:T(128)S(6)} %select_n.291), kind=kOutput, calls=%fused_computation.14 | convolution fusion | flops 805830656 | bytes 4194308 | tf_op jit(solution)/shard_map/obr,osr->obs/dot_general | solution.py:368
  (234 shorter events, 89.2 us)
Async XLA Ops:
  7.2 149.7 %all-gather.2.cloned.1.call-start = ((), (), s32[]{:S(2)}) async-start(), calls=%async_computation.1 | async-start | bytes 4718592 | tf_op jit(solution)/shard_map/all_gather | solution.py:348
  9.4 13.7 %collective-permute-start.11 = (bf16[2,256,256]{2,1,0:T(8,128)(2,1)}, bf16[2,256,256]{2,1,0:T(8,128)(2,1)S(1)}, u32[]{:S(2)}, u32[]{:S(2)}) collective-permute-start(bf16[2,256,256]{2,1,0:T(8,128)(2,1)} %get-tuple-element.116), channel_id=1, source_target_pairs={{0,8},{8,0},{16,24},{24,16},{1,9},{9,1},{17,25},{25,17},{2,10},{10... | collective-permute-start | bytes 786440 | tf_op jit(solution)/shard_map/ppermute | solution.py:194
  12.4 9.4 %collective-permute-start.12 = (bf16[2,256,256]{2,1,0:T(8,128)(2,1)}, bf16[2,256,256]{2,1,0:T(8,128)(2,1)S(1)}, u32[]{:S(2)}, u32[]{:S(2)}) collective-permute-start(bf16[2,256,256]{2,1,0:T(8,128)(2,1)} %get-tuple-element.116), channel_id=1, source_target_pairs={{0,16},{8,24},{16,0},{24,8},{1,17},{9,25},{17,1},{25,9},{2,18},{10... | collective-permute-start | bytes 786440 | tf_op jit(solution)/shard_map/ppermute | solution.py:194
  13.9 13.5 %collective-permute-start.1 = (bf16[2,256,256]{2,1,0:T(8,128)(2,1)S(1)}, bf16[2,256,256]{2,1,0:T(8,128)(2,1)S(1)}, u32[]{:S(2)}, u32[]{:S(2)}) collective-permute-start(bf16[2,256,256]{2,1,0:T(8,128)(2,1)S(1)} %get-tuple-element.25), channel_id=1, source_target_pairs={{0,16},{8,24},{16,0},{24,8},{1,17},{9,25},{17,1},{25,9},{2,18},{10... | collective-permute-start | bytes 786440 | tf_op jit(solution)/shard_map/ppermute | solution.py:194
  14.4 13.1 %collective-permute-start = (bf16[2,256,256]{2,1,0:T(8,128)(2,1)S(1)}, bf16[2,256,256]{2,1,0:T(8,128)(2,1)S(1)}, u32[]{:S(2)}, u32[]{:S(2)}) collective-permute-start(bf16[2,256,256]{2,1,0:T(8,128)(2,1)S(1)} %get-tuple-element.25), channel_id=1, source_target_pairs={{0,8},{8,0},{16,24},{24,16},{1,9},{9,1},{17,25},{25,17},{2,10},{10... | collective-permute-start | bytes 786440 | tf_op jit(solution)/shard_map/ppermute | solution.py:194
  27.4 11.0 %collective-permute-start.2 = (bf16[2,128,256]{2,1,0:T(8,128)(2,1)S(1)}, bf16[2,128,256]{2,1,0:T(8,128)(2,1)S(1)}, u32[]{:S(2)}, u32[]{:S(2)}) collective-permute-start(bf16[2,128,256]{2,1,0:T(8,128)(2,1)S(1)} %split.24), channel_id=1, source_target_pairs={{0,8},{8,0},{16,24},{24,16},{1,9},{9,1},{17,25},{25,17},{2,10},{10... | collective-permute-start | bytes 393224 | tf_op jit(solution)/shard_map/ppermute | solution.py:194
  27.5 10.8 %collective-permute-start.3 = (bf16[2,128,256]{2,1,0:T(8,128)(2,1)S(1)}, bf16[2,128,256]{2,1,0:T(8,128)(2,1)S(1)}, u32[]{:S(2)}, u32[]{:S(2)}) collective-permute-start(bf16[2,128,256]{2,1,0:T(8,128)(2,1)S(1)} %split.25), channel_id=1, source_target_pairs={{0,16},{8,24},{16,0},{24,8},{1,17},{9,25},{17,1},{25,9},{2,18},{10... | collective-permute-start | bytes 393224 | tf_op jit(solution)/shard_map/ppermute | solution.py:194
  33.9 10.1 %collective-permute-start.15 = (bf16[2,128,256]{2,1,0:T(8,128)(2,1)S(1)}, bf16[2,128,256]{2,1,0:T(8,128)(2,1)S(1)}, u32[]{:S(2)}, u32[]{:S(2)}) collective-permute-start(bf16[2,128,256]{2,1,0:T(8,128)(2,1)S(1)} %convolution_convert_fusion), channel_id=1, source_target_pairs={{0,1},{1,0},{2,3},{3,2},{4,5},{5,4},{6,7},{7,6},{8,9},{9,8},{10,11... | collective-permute-start | bytes 393224 | tf_op jit(solution)/shard_map/ppermute | solution.py:194
  35.6 11.8 %collective-permute-start.16 = (bf16[2,128,256]{2,1,0:T(8,128)(2,1)S(1)}, bf16[2,128,256]{2,1,0:T(8,128)(2,1)S(1)}, u32[]{:S(2)}, u32[]{:S(2)}) collective-permute-start(bf16[2,128,256]{2,1,0:T(8,128)(2,1)S(1)} %convolution_convert_fusion), channel_id=1, source_target_pairs={{0,2},{1,3},{2,0},{3,1},{4,6},{5,7},{6,4},{7,5},{8,10},{9,11},{10,... | collective-permute-start | bytes 393224 | tf_op jit(solution)/shard_map/ppermute | solution.py:194
  38.2 9.8 %collective-permute-start.17 = (bf16[2,128,256]{2,1,0:T(8,128)(2,1)S(1)}, bf16[2,128,256]{2,1,0:T(8,128)(2,1)S(1)}, u32[]{:S(2)}, u32[]{:S(2)}) collective-permute-start(bf16[2,128,256]{2,1,0:T(8,128)(2,1)S(1)} %convolution_convert_fusion), channel_id=1, source_target_pairs={{0,3},{1,2},{2,1},{3,0},{4,7},{5,6},{6,5},{7,4},{8,11},{9,10},{10,... | collective-permute-start | bytes 393224 | tf_op jit(solution)/shard_map/ppermute | solution.py:194
  39.7 24.9 %collective-permute-start.4 = (bf16[2,128,256]{2,1,0:T(8,128)(2,1)S(1)}, bf16[2,128,256]{2,1,0:T(8,128)(2,1)S(1)}, u32[]{:S(2)}, u32[]{:S(2)}) collective-permute-start(bf16[2,128,256]{2,1,0:T(8,128)(2,1)S(1)} %convolution_convert_fusion.1), channel_id=1, source_target_pairs={{0,1},{1,0},{2,3},{3,2},{4,5},{5,4},{6,7},{7,6},{8,9},{9,8},{10,11... | collective-permute-start | bytes 393224 | tf_op jit(solution)/shard_map/ppermute | solution.py:194
  40.5 27.8 %collective-permute-start.5 = (bf16[2,128,256]{2,1,0:T(8,128)(2,1)S(1)}, bf16[2,128,256]{2,1,0:T(8,128)(2,1)S(1)}, u32[]{:S(2)}, u32[]{:S(2)}) collective-permute-start(bf16[2,128,256]{2,1,0:T(8,128)(2,1)S(1)} %convolution_convert_fusion.1), channel_id=1, source_target_pairs={{0,2},{1,3},{2,0},{3,1},{4,6},{5,7},{6,4},{7,5},{8,10},{9,11},{10,... | collective-permute-start | bytes 393224 | tf_op jit(solution)/shard_map/ppermute | solution.py:194
  44.0 9.5 %collective-permute-start.7 = (bf16[128,2048]{1,0:T(8,128)(2,1)S(1)}, bf16[128,2048]{1,0:T(8,128)(2,1)S(1)}, u32[]{:S(2)}, u32[]{:S(2)}) collective-permute-start(bf16[128,2048]{1,0:T(8,128)(2,1)S(1)} %copy-done.5), channel_id=1, source_target_pairs={{0,8},{8,0},{16,24},{24,16},{1,9},{9,1},{17,25},{25,17},{2,10},{10... | collective-permute-start | bytes 1572872 | tf_op jit(solution)/shard_map/ppermute | solution.py:194
  47.4 12.0 %collective-permute-start.8 = (bf16[128,2048]{1,0:T(8,128)(2,1)S(1)}, bf16[128,2048]{1,0:T(8,128)(2,1)S(1)}, u32[]{:S(2)}, u32[]{:S(2)}) collective-permute-start(bf16[128,2048]{1,0:T(8,128)(2,1)S(1)} %copy-done.5), channel_id=1, source_target_pairs={{0,16},{8,24},{16,0},{24,8},{1,17},{9,25},{17,1},{25,9},{2,18},{10... | collective-permute-start | bytes 1572872 | tf_op jit(solution)/shard_map/ppermute | solution.py:194
  48.4 13.7 %collective-permute-start.18 = (f32[2,128,256]{2,1,0:T(8,128)S(1)}, f32[2,128,256]{2,1,0:T(8,128)S(1)}, u32[]{:S(2)}, u32[]{:S(2)}) collective-permute-start(f32[2,128,256]{2,1,0:T(8,128)S(1)} %multiply_add_fusion.4), channel_id=1, source_target_pairs={{0,4},{4,0},{1,5},{5,1},{2,6},{6,2},{3,7},{7,3},{8,12},{12,8},{9,1... | collective-permute-start | bytes 786440 | tf_op jit(solution)/shard_map/ppermute | solution.py:194
  53.6 11.7 %collective-permute-start.10 = (bf16[64,2048]{1,0:T(8,128)(2,1)S(1)}, bf16[64,2048]{1,0:T(8,128)(2,1)S(1)}, u32[]{:S(2)}, u32[]{:S(2)}) collective-permute-start(bf16[64,2048]{1,0:T(8,128)(2,1)S(1)} %split.27), channel_id=1, source_target_pairs={{0,16},{8,24},{16,0},{24,8},{1,17},{9,25},{17,1},{25,9},{2,18},{10... | collective-permute-start | bytes 786440 | tf_op jit(solution)/shard_map/ppermute | solution.py:194
  98.5 11.3 %collective-permute-start.28 = (f32[128,384]{1,0:T(8,128)S(1)}, f32[128,384]{1,0:T(8,128)S(1)}, u32[]{:S(2)}, u32[]{:S(2)}) collective-permute-start(f32[128,384]{1,0:T(8,128)S(1)} %fusion.83), channel_id=1, source_target_pairs={{0,2},{1,3},{2,0},{3,1},{4,6},{5,7},{6,4},{7,5},{8,10},{9,11},{10,... | collective-permute-start | bytes 589832 | tf_op jit(solution)/shard_map/ppermute | solution.py:194
  110.8 125.6 %reduce-scatter.4.cloned.1.call-start = ((), (), s32[]{:S(2)}) async-start(), calls=%async_computation.2 | async-start | bytes 589824
  112.9 9.9 %collective-permute-start.31 = (f32[128,384]{1,0:T(8,128)S(1)}, f32[128,384]{1,0:T(8,128)S(1)}, u32[]{:S(2)}, u32[]{:S(2)}) collective-permute-start(f32[128,384]{1,0:T(8,128)S(1)} %add.338.refs_0_), channel_id=1, source_target_pairs={{0,24},{8,16},{16,8},{24,0},{1,25},{9,17},{17,9},{25,1},{2,26},{10... | collective-permute-start | bytes 589832 | tf_op jit(solution)/shard_map/ppermute | solution.py:194
  141.6 18.7 %collective-permute-start.32 = (f32[512,512]{1,0:T(8,128)S(1)}, f32[512,512]{1,0:T(8,128)S(1)}, u32[]{:S(2)}, u32[]{:S(2)}) collective-permute-start(f32[512,512]{1,0:T(8,128)S(1)} %inverse_factor.2), channel_id=1, source_target_pairs={{0,4},{4,0},{1,5},{5,1},{2,6},{6,2},{3,7},{7,3},{8,12},{12,8},{9,1... | collective-permute-start | bytes 3145736 | tf_op jit(solution)/shard_map/ppermute | solution.py:194
  163.4 13.8 %collective-permute-start.34 = (bf16[2,128,512]{2,1,0:T(8,128)(2,1)S(1)}, bf16[2,128,512]{2,1,0:T(8,128)(2,1)S(1)}, u32[]{:S(2)}, u32[]{:S(2)}) collective-permute-start(bf16[2,128,512]{2,1,0:T(8,128)(2,1)S(1)} %fusion.17), channel_id=1, source_target_pairs={{0,16},{8,24},{16,0},{24,8},{1,17},{9,25},{17,1},{25,9},{2,18},{10... | collective-permute-start | bytes 786440 | tf_op jit(solution)/shard_map/ppermute | solution.py:194
  164.8 12.3 %collective-permute-start.35 = (bf16[2,128,512]{2,1,0:T(8,128)(2,1)S(1)}, bf16[2,128,512]{2,1,0:T(8,128)(2,1)S(1)}, u32[]{:S(2)}, u32[]{:S(2)}) collective-permute-start(bf16[2,128,512]{2,1,0:T(8,128)(2,1)S(1)} %fusion.17), channel_id=1, source_target_pairs={{0,24},{8,16},{16,8},{24,0},{1,25},{9,17},{17,9},{25,1},{2,26},{10... | collective-permute-start | bytes 786440 | tf_op jit(solution)/shard_map/ppermute | solution.py:194
  190.0 11.3 %collective-permute-start.38 = (f32[128,384]{1,0:T(8,128)S(1)}, f32[128,384]{1,0:T(8,128)S(1)}, u32[]{:S(2)}, u32[]{:S(2)}) collective-permute-start(f32[128,384]{1,0:T(8,128)S(1)} %fusion.82), channel_id=1, source_target_pairs={{0,2},{1,3},{2,0},{3,1},{4,6},{5,7},{6,4},{7,5},{8,10},{9,11},{10,... | collective-permute-start | bytes 589832 | tf_op jit(solution)/shard_map/ppermute | solution.py:194
  203.3 10.0 %collective-permute-start.41 = (f32[128,384]{1,0:T(8,128)S(1)}, f32[128,384]{1,0:T(8,128)S(1)}, u32[]{:S(2)}, u32[]{:S(2)}) collective-permute-start(f32[128,384]{1,0:T(8,128)S(1)} %add.360.refs_0_), channel_id=1, source_target_pairs={{0,24},{8,16},{16,8},{24,0},{1,25},{9,17},{17,9},{25,1},{2,26},{10... | collective-permute-start | bytes 589832 | tf_op jit(solution)/shard_map/ppermute | solution.py:194
  (63 other events, 536.2 us)
Sparse Core Ops, SparseCore 0:
  110.9 45.8 all-gather.1
  206.0 30.3 reduce-scatter.3

commit v4 on v3

--- a/solution.py
+++ b/solution.py
@@ -198,17 +198,6 @@
     return [swap(value, axis, k) for k in range(lax.axis_size(axis))]
 
 
-def collect_relayed(value, axis, dim):
-    if lax.axis_size(axis) != 4:
-        return collect(value, axis)
-    near, side = swap(value, axis, 1), swap(value, axis, 2)
-    far = [
-        swap(jnp.split(side, 2, axis=dim)[0], axis, 1),
-        swap(jnp.split(near, 2, axis=dim)[1], axis, 2),
-    ]
-    return [value, near, side, jnp.concatenate(far, axis=dim)]
-
-
 def per_device(acts, init_basis, kept, member):
     owned = init_basis.shape[0]
     slice_rows = init_basis.shape[1]
@@ -244,11 +233,16 @@
     init_bf = init_basis.astype(jnp.bfloat16)
     width = rank // CHUNKS
     init_pieces = [
-        collect_relayed(init_bf[:, :, c * width : (c + 1) * width], "tok", 1)
-        for c in range(CHUNKS)
+        collect(init_bf[:, :, c * width : (c + 1) * width], "tok") for c in range(CHUNKS)
     ]
-    init_pieces[-1], acts_late = lax.optimization_barrier((init_pieces[-1], acts))
-    x_pieces = collect_relayed(acts_late, "tok", 0)
+    gathered_x = lax.all_gather(acts, "tok", axis=0, tiled=True)
+    full_x = jnp.concatenate(
+        [
+            lax.dynamic_slice_in_dim(gathered_x, (tok_pos ^ k) * tok_rows, tok_rows, 0)
+            for k in range(tok_count)
+        ],
+        axis=0,
+    ).reshape(total_tokens, owned, block_cols)
 
     def combine(rows_of_links, pieces, sources):
         total = 0.0
@@ -272,12 +266,9 @@
     def mix(pieces):
         own = combine(own_links, pieces, sources)
         other = combine(partner_links, pieces, sources)
-        return collect((own + swap(other, "gr", 1)).astype(jnp.bfloat16), "tok")
-
-    mixed = [mix(pieces) for pieces in near[:-1]]
-    near[-1], x_pieces, mixed = lax.optimization_barrier((near[-1], x_pieces, mixed))
-    mixed.append(mix(near[-1]))
-    full_x = jnp.concatenate(x_pieces, axis=0).reshape(total_tokens, owned, block_cols)
+        return (own + swap(other, "gr", 1)).astype(jnp.bfloat16)
+
+    mixed = jnp.concatenate([mix(pieces) for pieces in near], axis=2)
     basis_bf = jnp.concatenate(
         [
             jnp.concatenate(
@@ -288,8 +279,8 @@
         axis=2,
     )
 
-    def image_of(parts, basis_bf):
-        full = jnp.concatenate([jnp.concatenate(part, axis=1) for part in parts], axis=2)
+    def image_of(mixed, basis_bf):
+        full = jnp.concatenate(collect(mixed, "tok"), axis=1)
         cover = jnp.einsum("tob,otr->obr", full_x, full, preferred_element_type=jnp.float32)
         return cover / total_tokens + ridge * basis_bf.astype(jnp.float32)
 
@@ -354,7 +345,7 @@
     of_block, _, second = factor(image, False, seen_by(image))
     mixed = jnp.einsum("otr,osr->ots", second, of_block, precision=HIGH).astype(jnp.bfloat16)
     basis_bf = jnp.einsum("obr,osr->obs", image, of_block, precision=HIGH).astype(jnp.bfloat16)
-    image = image_of([collect(mixed, "tok")], basis_bf)
+    image = image_of(mixed, basis_bf)
     codes = seen_by(image)
     placed = jnp.concatenate(
         [

time: 250 us -> 241 us (0.964)
  starting transfers between devices: 45.9 us -> 41.2 us
    ppermute x43 -> x34, starting transfers between devices: 45.9 us -> 41.1 us  [swap(): lax.ppermute(value, axis, [(i, i ^ k) for i in range(lax.axis_size(axis))])]
    ppermute x43 -> x34, waiting for transfers between devices: 77.6 us -> 74.3 us  [swap(): lax.ppermute(value, axis, [(i, i ^ k) for i in range(lax.axis_size(axis))])]
    unnamed x93 -> x58, local copies, waits for them, and re-layouts: 5.68 us -> 3.5 us
  transfers between devices with their start and end apart: 45 -> 37, of which waited for: 27 -> 24; matrix products, arithmetic and copies ran while one was open for 13% -> 14% of each run, Pallas kernels for 16% -> 16%
where the time goes in v4:
time: 241 us; the launch traced here: 240 us
  waiting for transfers between devices  92 us (38%)
  starting transfers between devices  41.2 us (17%)
  Pallas kernels  38.8 us (16%)
  matrix products  27.9 us (12%)
  local copies, waits for them, and re-layouts  16.3 us (7%)
  between operations  15.8 us (7%)
  other arithmetic  8.35 us (3%)
    ppermute x34, waiting for transfers between devices, swap(): lax.ppermute(value, axis, [(i, i ^ k) for i in range(lax.axis_size(axis))])  74.3 us
    ppermute x34, starting transfers between devices, swap(): lax.ppermute(value, axis, [(i, i ^ k) for i in range(lax.axis_size(axis))])  41.1 us
    pallas_call x2, Pallas kernels, inverse_factor(): pl.pallas_call(functools.partial(factor_kernel, scale, exact), out_shape=...  38.8 us
    all_gather x1, waiting for transfers between devices, mix_seen(): seen = lax.all_gather(seen, ('gr', 'gc'), axis=0, tiled=True)  14.5 us
    dot_general x4, matrix products, seen_by(): jnp.einsum('tob,obr->otr', own_x, part, preferred_element_type=jnp.float32)  5.94 us
  transfers between devices with their start and end apart: 37, of which 24 were waited for; matrix products, arithmetic and copies ran while one was open for 14% of the time, Pallas kernels for 16%

profile of v4, /device:TPU:0, one launch (start us, length us, event | category | flops | bytes accessed | tf_op | source)
XLA Modules:
  0.0 240.3 jit_solution(3370400972928789025)
XLA Ops:
  8.6 3.0 %collective-permute-start = (bf16[2,256,256]{2,1,0:T(8,128)(2,1)S(1)}, bf16[2,256,256]{2,1,0:T(8,128)(2,1)S(1)}, u32[]{:S(2)}, u32[]{:S(2)}) collective-permute-start(bf16[2,256,256]{2,1,0:T(8,128)(2,1)S(1)} %get-tuple-element.90), channel_id=1, source_target_pairs={{0,8},{8,0},{16,24},{24,16},{1,9},{9,1},{17,25},{25,17},{2,10},{10... | collective-permute-start | bytes 786440 | tf_op jit(solution)/shard_map/ppermute | solution.py:194
  23.7 2.8 %collective-permute-done.1 = bf16[2,256,256]{2,1,0:T(8,128)(2,1)S(1)} collective-permute-done((bf16[2,256,256]{2,1,0:T(8,128)(2,1)S(1)}, bf16[2,256,256]{2,1,0:T(8,128)(2,1)S(1)}, u32[]{:S(2)}, u32[]{:S(2)}) %collective-permute-start.1) | collective-permute-done | bytes 262176 | tf_op jit(solution)/shard_map/ppermute | solution.py:194
  32.0 2.9 %collective-permute-done.7 = bf16[2,256,256]{2,1,0:T(8,128)(2,1)S(1)} collective-permute-done((bf16[2,256,256]{2,1,0:T(8,128)(2,1)S(1)}, bf16[2,256,256]{2,1,0:T(8,128)(2,1)S(1)}, u32[]{:S(2)}, u32[]{:S(2)}) %collective-permute-start.7) | collective-permute-done | bytes 262176 | tf_op jit(solution)/shard_map/ppermute | solution.py:194
  34.9 3.7 %collective-permute-start.5 = (bf16[2,128,256]{2,1,0:T(8,128)(2,1)S(1)}, bf16[2,128,256]{2,1,0:T(8,128)(2,1)S(1)}, u32[]{:S(2)}, u32[]{:S(2)}) collective-permute-start(bf16[2,128,256]{2,1,0:T(8,128)(2,1)S(1)} %convolution_convert_fusion.1), channel_id=1, source_target_pairs={{0,3},{1,2},{2,1},{3,0},{4,7},{5,6},{6,5},{7,4},{8,11},{9,10},{10,... | collective-permute-start | bytes 393224 | tf_op jit(solution)/shard_map/ppermute | solution.py:194
  49.5 7.1 %collective-permute-done.11 = bf16[2,128,256]{2,1,0:T(8,128)(2,1)S(1)} collective-permute-done((bf16[2,128,256]{2,1,0:T(8,128)(2,1)S(1)}, bf16[2,128,256]{2,1,0:T(8,128)(2,1)S(1)}, u32[]{:S(2)}, u32[]{:S(2)}) %collective-permute-start.11) | collective-permute-done | bytes 131104 | tf_op jit(solution)/shard_map/ppermute | solution.py:194
  68.9 6.2 %collective-permute-done.15 = bf16[2,128,512]{2,1,0:T(8,128)(2,1)} collective-permute-done((bf16[2,128,512]{2,1,0:T(8,128)(2,1)}, bf16[2,128,512]{2,1,0:T(8,128)(2,1)}, u32[]{:S(2)}, u32[]{:S(2)}) %collective-permute-start.15) | collective-permute-done | bytes 262176 | tf_op jit(solution)/shard_map/ppermute | solution.py:194
  75.1 3.5 %multiply_add_fusion.1 = f32[2,1024,512]{2,1,0:T(8,128)S(1)} fusion(bf16[2,256,256]{2,1,0:T(8,128)(2,1)} %get-tuple-element.83, bf16[2,256,256]{2,1,0:T(8,128)(2,1)} %get-tuple-element.84, bf16[2,256,256]{2,1,0:T(8,128)(2,1)} %get-tuple-element.85, bf16[2,256,256]{2,1,0:T(8,128)(2,1)} %get-tuple-element.82, bf16[2,256,256]{2,1,0:T(8,128)(2,1)S(1)} %get-tuple-element.79, ...), kind=kOutput, calls=%fused_computation.7 | convolution fusion | flops 1098907648 | bytes 9437184 | tf_op jit(solution)/shard_map/tob,otr->obr/dot_general | solution.py:284
  84.2 3.1 %fusion.4 = f32[2,512,128]{2,1,0:T(8,128)S(1)} fusion(bf16[128,2,1024]{0,2,1:T(8,128)(2,1)S(1)} %bitcast.141, f32[2,1024,512]{2,1,0:T(8,128)} %copy-done), kind=kOutput, calls=%fused_computation.9 | convolution fusion | flops 271581184 | bytes 5242880 | tf_op jit(solution)/shard_map/tob,obr->otr/dot_general | solution.py:289
  89.4 2.8 %collective-permute-start.19 = (f32[128,384]{1,0:T(8,128)S(1)}, f32[128,384]{1,0:T(8,128)S(1)}, u32[]{:S(2)}, u32[]{:S(2)}) collective-permute-start(f32[128,384]{1,0:T(8,128)S(1)} %fusion.92), channel_id=1, source_target_pairs={{0,2},{1,3},{2,0},{3,1},{4,6},{5,7},{6,4},{7,5},{8,10},{9,11},{10,... | collective-permute-start | bytes 589832 | tf_op jit(solution)/shard_map/ppermute | solution.py:194
  93.1 7.8 %collective-permute-done.19 = f32[128,384]{1,0:T(8,128)S(1)} collective-permute-done((f32[128,384]{1,0:T(8,128)S(1)}, f32[128,384]{1,0:T(8,128)S(1)}, u32[]{:S(2)}, u32[]{:S(2)}) %collective-permute-start.19) | collective-permute-done | bytes 196640 | tf_op jit(solution)/shard_map/ppermute | solution.py:194
  105.5 4.3 %collective-permute-done.20.refs_1_ = f32[128,384]{1,0:T(8,128)S(1)} collective-permute-done((f32[128,384]{1,0:T(8,128)S(1)}, f32[128,384]{1,0:T(8,128)S(1)}, u32[]{:S(2)}, u32[]{:S(2)}) %collective-permute-start.20) | collective-permute-done | bytes 196640 | tf_op jit(solution)/shard_map/ppermute | solution.py:194
  112.3 18.8 %inverse_factor.2 = f32[512,512]{1,0:T(8,128)S(1)} custom-call(s32[1]{0:T(128)} %bitcast.1.pos_ref, f32[128,384]{1,0:T(8,128)S(1)} %add.351.refs_0_, f32[128,384]{1,0:T(8,128)S(1)} %collective-permute-done.20.refs_1_, f32[128,384]{1,0:T(8,128)S(1)} %collective-permute-done.21.refs_2_, f32[128,384]{1,0:T(8,128)S(1)} %collective-permute-done.22.refs_3_), custom_call_target="tpu_custom_call" | custom-call | flops 12884901888 | bytes 2097152 | tf_op jit(solution)/shard_map/inverse_factor/pallas_call | solution.py:171
  133.5 14.5 %all-gather.5.cloned.1.call-done = f32[16,128,512]{2,1,0:T(8,128)} async-done(((f32[2,128,512]{2,1,0:T(8,128)}), f32[16,128,512]{2,1,0:T(8,128)}) %all-gather.5.cloned.1.call-update) | async-done | bytes 4194320 | tf_op jit(solution)/shard_map/all_gather | solution.py:339
  148.1 2.8 %slice_bitcast_fusion.15 = (f32[128,512]{1,0:T(8,128)S(1)}, f32[128,512]{1,0:T(8,128)S(1)}, f32[128,512]{1,0:T(8,128)S(1)}, f32[128,512]{1,0:T(8,128)S(1)}, f32[...) fusion(f32[16,128,512]{2,1,0:T(8,128)} %all-gather.5.cloned.1.c, ...), kind=kLoop, calls=%fused_computation.96 | loop fusion | bytes 8388608 | tf_op jit(solution)/shard_map/mul | solution.py:342
  156.6 4.0 %fusion.12 = bf16[2,1024,512]{2,1,0:T(8,128)(2,1)S(1)} fusion(f32[2,1024,512]{2,1,0:T(8,128)S(1)} %copy-done.2, f32[1,512,512]{2,1,0:T(8,128)S(1)} %get-tuple-element.73, f32[1,512,512]{2,1,0:T(8,128)S(1)} %get-tuple-element.72), kind=kOutput, calls=%fused_computation.18 | convolution fusion | flops 3221749760 | bytes 8388608 | tf_op jit(solution)/shard_map/obr,osr->obs/dot_general | solution.py:347
  162.3 6.1 %collective-permute-done.25 = bf16[2,128,512]{2,1,0:T(8,128)(2,1)S(1)} collective-permute-done((bf16[2,128,512]{2,1,0:T(8,128)(2,1)S(1)}, bf16[2,128,512]{2,1,0:T(8,128)(2,1)S(1)}, u32[]{:S(2)}, u32[]{:S(2)}) %collective-permute-start.25) | collective-permute-done | bytes 262176 | tf_op jit(solution)/shard_map/ppermute | solution.py:194
  169.6 2.8 %multiply_reduce_fusion.2 = (f32[128,512]{1,0:T(8,128)S(1)}, f32[128,512]{1,0:T(8,128)S(1)}) fusion(f32[2]{0:T(128)S(1)} %copy-done.22, f32[2]{0:T(128)S(1)} %copy-done.23, f32[2,1024,512]{2,1,0:T(8,128)S(1)} %multiply_add_fusion, s32[]{:T(128)S(6)} %select_n.301), kind=kOutput, calls=%fused_computation.74 | convolution fusion | flops 1611005952 | bytes 5768196 | tf_op jit(solution)/shard_map/obr,obs->ors/dot_general | solution.py:296
  175.2 5.9 %collective-permute-done.28 = f32[128,384]{1,0:T(8,128)S(1)} collective-permute-done((f32[128,384]{1,0:T(8,128)S(1)}, f32[128,384]{1,0:T(8,128)S(1)}, u32[]{:S(2)}, u32[]{:S(2)}) %collective-permute-start.28) | collective-permute-done | bytes 196640 | tf_op jit(solution)/shard_map/ppermute | solution.py:194
  182.3 10.2 %collective-permute-done.29 = f32[128,384]{1,0:T(8,128)S(1)} collective-permute-done((f32[128,384]{1,0:T(8,128)S(1)}, f32[128,384]{1,0:T(8,128)S(1)}, u32[]{:S(2)}, u32[]{:S(2)}) %collective-permute-start.29) | collective-permute-done | bytes 196640 | tf_op jit(solution)/shard_map/ppermute | solution.py:194
  197.1 3.3 %collective-permute-done.30.refs_1_ = f32[128,384]{1,0:T(8,128)S(1)} collective-permute-done((f32[128,384]{1,0:T(8,128)S(1)}, f32[128,384]{1,0:T(8,128)S(1)}, u32[]{:S(2)}, u32[]{:S(2)}) %collective-permute-start.30) | collective-permute-done | bytes 196640 | tf_op jit(solution)/shard_map/ppermute | solution.py:194
  201.3 3.2 %collective-permute-done.32.refs_3_ = f32[128,384]{1,0:T(8,128)S(1)} collective-permute-done((f32[128,384]{1,0:T(8,128)S(1)}, f32[128,384]{1,0:T(8,128)S(1)}, u32[]{:S(2)}, u32[]{:S(2)}) %collective-permute-start.32) | collective-permute-done | bytes 196640 | tf_op jit(solution)/shard_map/ppermute | solution.py:194
  204.5 20.0 %inverse_factor.3 = f32[512,512]{1,0:T(8,128)S(1)} custom-call(s32[1]{0:T(128)} %bitcast.1.pos_ref, f32[128,384]{1,0:T(8,128)S(1)} %add.373.refs_0_, f32[128,384]{1,0:T(8,128)S(1)} %collective-permute-done.30.refs_1_, f32[128,384]{1,0:T(8,128)S(1)} %collective-permute-done.31.refs_2_, f32[128,384]{1,0:T(8,128)S(1)} %collective-permute-done.32.refs_3_), custom_call_target="tpu_custom_call" | custom-call | flops 12884901888 | bytes 2097152 | tf_op jit(solution)/shard_map/inverse_factor/pallas_call | solution.py:171
  224.6 3.1 %reduce-scatter.4.cloned.1.call-done = f32[16,1024]{1,0:T(8,128)} async-done(((f32[128,1024]{1,0:T(8,128)}), f32[16,1024]{1,0:T(8,128)}) %reduce-scatter.4.cloned.1.call-update) | async-done | bytes 65552
  230.4 3.4 %fusion.8 = f32[2,256,512]{2,1,0:T(8,128)} fusion(f32[1,512,512]{2,1,0:T(8,128)S(1)} %get-tuple-element.71, f32[1,512,512]{2,1,0:T(8,128)S(1)} %get-tuple-element.70, f32[2,1024,512]{2,1,0:T(8,128)} %copy-done.3, s32[]{:T(128)S(6)} %select_n.307), kind=kOutput, calls=%fused_computation.14 | convolution fusion | flops 805830656 | bytes 4194308 | tf_op jit(solution)/shard_map/obr,osr->obs/dot_general | solution.py:359
  (177 shorter events, 79.2 us)
Async XLA Ops:
  7.2 55.7 %all-gather.3.cloned.1.call-start = ((), (), s32[]{:S(2)}) async-start(), calls=%async_computation.1 | async-start | bytes 2621440 | tf_op jit(solution)/shard_map/all_gather | solution.py:238
  8.6 14.7 %collective-permute-start = (bf16[2,256,256]{2,1,0:T(8,128)(2,1)S(1)}, bf16[2,256,256]{2,1,0:T(8,128)(2,1)S(1)}, u32[]{:S(2)}, u32[]{:S(2)}) collective-permute-start(bf16[2,256,256]{2,1,0:T(8,128)(2,1)S(1)} %get-tuple-element.90), channel_id=1, source_target_pairs={{0,8},{8,0},{16,24},{24,16},{1,9},{9,1},{17,25},{25,17},{2,10},{10... | collective-permute-start | bytes 786440 | tf_op jit(solution)/shard_map/ppermute | solution.py:194
  11.6 14.8 %collective-permute-start.1 = (bf16[2,256,256]{2,1,0:T(8,128)(2,1)S(1)}, bf16[2,256,256]{2,1,0:T(8,128)(2,1)S(1)}, u32[]{:S(2)}, u32[]{:S(2)}) collective-permute-start(bf16[2,256,256]{2,1,0:T(8,128)(2,1)S(1)} %get-tuple-element.90), channel_id=1, source_target_pairs={{0,16},{8,24},{16,0},{24,8},{1,17},{9,25},{17,1},{25,9},{2,18},{10... | collective-permute-start | bytes 786440 | tf_op jit(solution)/shard_map/ppermute | solution.py:194
  13.1 13.3 %collective-permute-start.2 = (bf16[2,256,256]{2,1,0:T(8,128)(2,1)S(1)}, bf16[2,256,256]{2,1,0:T(8,128)(2,1)S(1)}, u32[]{:S(2)}, u32[]{:S(2)}) collective-permute-start(bf16[2,256,256]{2,1,0:T(8,128)(2,1)S(1)} %get-tuple-element.90), channel_id=1, source_target_pairs={{0,24},{8,16},{16,8},{24,0},{1,25},{9,17},{17,9},{25,1},{2,26},{10... | collective-permute-start | bytes 786440 | tf_op jit(solution)/shard_map/ppermute | solution.py:194
  13.2 21.7 %collective-permute-start.7 = (bf16[2,256,256]{2,1,0:T(8,128)(2,1)S(1)}, bf16[2,256,256]{2,1,0:T(8,128)(2,1)S(1)}, u32[]{:S(2)}, u32[]{:S(2)}) collective-permute-start(bf16[2,256,256]{2,1,0:T(8,128)(2,1)S(1)} %get-tuple-element.91), channel_id=1, source_target_pairs={{0,8},{8,0},{16,24},{24,16},{1,9},{9,1},{17,25},{25,17},{2,10},{10... | collective-permute-start | bytes 786440 | tf_op jit(solution)/shard_map/ppermute | solution.py:194
  15.1 25.8 %collective-permute-start.8 = (bf16[2,256,256]{2,1,0:T(8,128)(2,1)S(1)}, bf16[2,256,256]{2,1,0:T(8,128)(2,1)S(1)}, u32[]{:S(2)}, u32[]{:S(2)}) collective-permute-start(bf16[2,256,256]{2,1,0:T(8,128)(2,1)S(1)} %get-tuple-element.91), channel_id=1, source_target_pairs={{0,16},{8,24},{16,0},{24,8},{1,17},{9,25},{17,1},{25,9},{2,18},{10... | collective-permute-start | bytes 786440 | tf_op jit(solution)/shard_map/ppermute | solution.py:194
  16.7 131.4 %all-gather.5.cloned.1.call-start = ((), (), s32[]{:S(2)}) async-start(), calls=%async_computation.2 | async-start | bytes 4718592 | tf_op jit(solution)/shard_map/all_gather | solution.py:339
  23.4 18.3 %collective-permute-start.9 = (bf16[2,256,256]{2,1,0:T(8,128)(2,1)S(1)}, bf16[2,256,256]{2,1,0:T(8,128)(2,1)S(1)}, u32[]{:S(2)}, u32[]{:S(2)}) collective-permute-start(bf16[2,256,256]{2,1,0:T(8,128)(2,1)S(1)} %get-tuple-element.91), channel_id=1, source_target_pairs={{0,24},{8,16},{16,8},{24,0},{1,25},{9,17},{17,9},{25,1},{2,26},{10... | collective-permute-start | bytes 786440 | tf_op jit(solution)/shard_map/ppermute | solution.py:194
  27.8 20.6 %collective-permute-start.3 = (bf16[2,128,256]{2,1,0:T(8,128)(2,1)S(1)}, bf16[2,128,256]{2,1,0:T(8,128)(2,1)S(1)}, u32[]{:S(2)}, u32[]{:S(2)}) collective-permute-start(bf16[2,128,256]{2,1,0:T(8,128)(2,1)S(1)} %convolution_convert_fusion.1), channel_id=1, source_target_pairs={{0,1},{1,0},{2,3},{3,2},{4,5},{5,4},{6,7},{7,6},{8,9},{9,8},{10,11... | collective-permute-start | bytes 393224 | tf_op jit(solution)/shard_map/ppermute | solution.py:194
  29.4 19.1 %collective-permute-start.4 = (bf16[2,128,256]{2,1,0:T(8,128)(2,1)S(1)}, bf16[2,128,256]{2,1,0:T(8,128)(2,1)S(1)}, u32[]{:S(2)}, u32[]{:S(2)}) collective-permute-start(bf16[2,128,256]{2,1,0:T(8,128)(2,1)S(1)} %convolution_convert_fusion.1), channel_id=1, source_target_pairs={{0,2},{1,3},{2,0},{3,1},{4,6},{5,7},{6,4},{7,5},{8,10},{9,11},{10,... | collective-permute-start | bytes 393224 | tf_op jit(solution)/shard_map/ppermute | solution.py:194
  34.9 13.7 %collective-permute-start.5 = (bf16[2,128,256]{2,1,0:T(8,128)(2,1)S(1)}, bf16[2,128,256]{2,1,0:T(8,128)(2,1)S(1)}, u32[]{:S(2)}, u32[]{:S(2)}) collective-permute-start(bf16[2,128,256]{2,1,0:T(8,128)(2,1)S(1)} %convolution_convert_fusion.1), channel_id=1, source_target_pairs={{0,3},{1,2},{2,1},{3,0},{4,7},{5,6},{6,5},{7,4},{8,11},{9,10},{10,... | collective-permute-start | bytes 393224 | tf_op jit(solution)/shard_map/ppermute | solution.py:194
  44.7 12.0 %collective-permute-start.11 = (bf16[2,128,256]{2,1,0:T(8,128)(2,1)S(1)}, bf16[2,128,256]{2,1,0:T(8,128)(2,1)S(1)}, u32[]{:S(2)}, u32[]{:S(2)}) collective-permute-start(bf16[2,128,256]{2,1,0:T(8,128)(2,1)S(1)} %convolution_convert_fusion), channel_id=1, source_target_pairs={{0,2},{1,3},{2,0},{3,1},{4,6},{5,7},{6,4},{7,5},{8,10},{9,11},{10,... | collective-permute-start | bytes 393224 | tf_op jit(solution)/shard_map/ppermute | solution.py:194
  59.4 9.4 %collective-permute-start.14 = (bf16[2,128,512]{2,1,0:T(8,128)(2,1)}, bf16[2,128,512]{2,1,0:T(8,128)(2,1)}, u32[]{:S(2)}, u32[]{:S(2)}) collective-permute-start(bf16[2,128,512]{2,1,0:T(8,128)(2,1)} %pad_maximum_fusion.8), channel_id=1, source_target_pairs={{0,8},{8,0},{16,24},{24,16},{1,9},{9,1},{17,25},{25,17},{2,10},{10... | collective-permute-start | bytes 786440 | tf_op jit(solution)/shard_map/ppermute | solution.py:194
  60.9 14.2 %collective-permute-start.15 = (bf16[2,128,512]{2,1,0:T(8,128)(2,1)}, bf16[2,128,512]{2,1,0:T(8,128)(2,1)}, u32[]{:S(2)}, u32[]{:S(2)}) collective-permute-start(bf16[2,128,512]{2,1,0:T(8,128)(2,1)} %pad_maximum_fusion.8), channel_id=1, source_target_pairs={{0,16},{8,24},{16,0},{24,8},{1,17},{9,25},{17,1},{25,9},{2,18},{10... | collective-permute-start | bytes 786440 | tf_op jit(solution)/shard_map/ppermute | solution.py:194
  61.5 13.6 %collective-permute-start.16 = (bf16[2,128,512]{2,1,0:T(8,128)(2,1)}, bf16[2,128,512]{2,1,0:T(8,128)(2,1)}, u32[]{:S(2)}, u32[]{:S(2)}) collective-permute-start(bf16[2,128,512]{2,1,0:T(8,128)(2,1)} %pad_maximum_fusion.8), channel_id=1, source_target_pairs={{0,24},{8,16},{16,8},{24,0},{1,25},{9,17},{17,9},{25,1},{2,26},{10... | collective-permute-start | bytes 786440 | tf_op jit(solution)/shard_map/ppermute | solution.py:194
  89.4 11.5 %collective-permute-start.19 = (f32[128,384]{1,0:T(8,128)S(1)}, f32[128,384]{1,0:T(8,128)S(1)}, u32[]{:S(2)}, u32[]{:S(2)}) collective-permute-start(f32[128,384]{1,0:T(8,128)S(1)} %fusion.92), channel_id=1, source_target_pairs={{0,2},{1,3},{2,0},{3,1},{4,6},{5,7},{6,4},{7,5},{8,10},{9,11},{10,... | collective-permute-start | bytes 589832 | tf_op jit(solution)/shard_map/ppermute | solution.py:194
  101.9 125.7 %reduce-scatter.4.cloned.1.call-start = ((), (), s32[]{:S(2)}) async-start(), calls=%async_computation.3 | async-start | bytes 589824
  102.6 9.7 %collective-permute-start.21 = (f32[128,384]{1,0:T(8,128)S(1)}, f32[128,384]{1,0:T(8,128)S(1)}, u32[]{:S(2)}, u32[]{:S(2)}) collective-permute-start(f32[128,384]{1,0:T(8,128)S(1)} %add.351.refs_0_), channel_id=1, source_target_pairs={{0,16},{8,24},{16,0},{24,8},{1,17},{9,25},{17,1},{25,9},{2,18},{10... | collective-permute-start | bytes 589832 | tf_op jit(solution)/shard_map/ppermute | solution.py:194
  131.1 20.4 %collective-permute-start.23 = (f32[512,512]{1,0:T(8,128)S(1)}, f32[512,512]{1,0:T(8,128)S(1)}, u32[]{:S(2)}, u32[]{:S(2)}) collective-permute-start(f32[512,512]{1,0:T(8,128)S(1)} %inverse_factor.2), channel_id=1, source_target_pairs={{0,4},{4,0},{1,5},{5,1},{2,6},{6,2},{3,7},{7,3},{8,12},{12,8},{9,1... | collective-permute-start | bytes 3145736 | tf_op jit(solution)/shard_map/ppermute | solution.py:194
  153.1 9.2 %collective-permute-start.24 = (bf16[2,128,512]{2,1,0:T(8,128)(2,1)S(1)}, bf16[2,128,512]{2,1,0:T(8,128)(2,1)S(1)}, u32[]{:S(2)}, u32[]{:S(2)}) collective-permute-start(bf16[2,128,512]{2,1,0:T(8,128)(2,1)S(1)} %fusion.17), channel_id=1, source_target_pairs={{0,8},{8,0},{16,24},{24,16},{1,9},{9,1},{17,25},{25,17},{2,10},{10... | collective-permute-start | bytes 786440 | tf_op jit(solution)/shard_map/ppermute | solution.py:194
  154.6 13.8 %collective-permute-start.25 = (bf16[2,128,512]{2,1,0:T(8,128)(2,1)S(1)}, bf16[2,128,512]{2,1,0:T(8,128)(2,1)S(1)}, u32[]{:S(2)}, u32[]{:S(2)}) collective-permute-start(bf16[2,128,512]{2,1,0:T(8,128)(2,1)S(1)} %fusion.17), channel_id=1, source_target_pairs={{0,16},{8,24},{16,0},{24,8},{1,17},{9,25},{17,1},{25,9},{2,18},{10... | collective-permute-start | bytes 786440 | tf_op jit(solution)/shard_map/ppermute | solution.py:194
  156.0 12.3 %collective-permute-start.26 = (bf16[2,128,512]{2,1,0:T(8,128)(2,1)S(1)}, bf16[2,128,512]{2,1,0:T(8,128)(2,1)S(1)}, u32[]{:S(2)}, u32[]{:S(2)}) collective-permute-start(bf16[2,128,512]{2,1,0:T(8,128)(2,1)S(1)} %fusion.17), channel_id=1, source_target_pairs={{0,24},{8,16},{16,8},{24,0},{1,25},{9,17},{17,9},{25,1},{2,26},{10... | collective-permute-start | bytes 786440 | tf_op jit(solution)/shard_map/ppermute | solution.py:194
  181.2 11.3 %collective-permute-start.29 = (f32[128,384]{1,0:T(8,128)S(1)}, f32[128,384]{1,0:T(8,128)S(1)}, u32[]{:S(2)}, u32[]{:S(2)}) collective-permute-start(f32[128,384]{1,0:T(8,128)S(1)} %fusion.91), channel_id=1, source_target_pairs={{0,2},{1,3},{2,0},{3,1},{4,6},{5,7},{6,4},{7,5},{8,10},{9,11},{10,... | collective-permute-start | bytes 589832 | tf_op jit(solution)/shard_map/ppermute | solution.py:194
  194.5 10.0 %collective-permute-start.32 = (f32[128,384]{1,0:T(8,128)S(1)}, f32[128,384]{1,0:T(8,128)S(1)}, u32[]{:S(2)}, u32[]{:S(2)}) collective-permute-start(f32[128,384]{1,0:T(8,128)S(1)} %add.373.refs_0_), channel_id=1, source_target_pairs={{0,24},{8,16},{16,8},{24,0},{1,25},{9,17},{17,9},{25,1},{2,26},{10... | collective-permute-start | bytes 589832 | tf_op jit(solution)/shard_map/ppermute | solution.py:194
  (39 other events, 264.7 us)
Sparse Core Ops, SparseCore 0:
  16.8 44.5 all-gather.2
  102.1 45.9 all-gather.4
  197.2 30.3 reduce-scatter.3

commit v5 on v4

--- a/solution.py
+++ b/solution.py
@@ -279,8 +279,11 @@
         axis=2,
     )
 
-    def image_of(mixed, basis_bf):
-        full = jnp.concatenate(collect(mixed, "tok"), axis=1)
+    def image_of(*operands):
+        *parts, basis_bf = operands
+        full = jnp.concatenate(
+            [jnp.concatenate(collect(part, "tok"), axis=1) for part in parts], axis=2
+        )
         cover = jnp.einsum("tob,otr->obr", full_x, full, preferred_element_type=jnp.float32)
         return cover / total_tokens + ridge * basis_bf.astype(jnp.float32)
 
@@ -335,17 +338,25 @@
         return of_block, of_group, beside
 
     image = image_of(mixed, basis_bf)
+    wide = rank // 2
+
     def mix_seen(seen):
-        seen = lax.all_gather(seen, ("gr", "gc"), axis=0, tiled=True)
+        pieces = lax.all_gather(seen[:, :, :wide], ("gr", "gc"), axis=0, tiled=True)
         total = 0.0
-        for j in range(seen.shape[0]):
-            total += own_links[:, j][:, None, None] * seen[j][None]
+        for j in range(pieces.shape[0]):
+            total += own_links[:, j][:, None, None] * pieces[j][None]
         return total
 
-    of_block, _, second = factor(image, False, seen_by(image))
-    mixed = jnp.einsum("otr,osr->ots", second, of_block, precision=HIGH).astype(jnp.bfloat16)
+    seen = seen_by(image)
+    of_block, _, second = factor(image, False, seen)
+    proj = jnp.einsum("otr,osr->ots", seen, of_block[:, wide:], precision=HIGH)
+    proj = proj.astype(jnp.bfloat16)
+    first_part = jnp.einsum(
+        "otr,osr->ots", second, of_block[:, :wide, :wide], precision=HIGH
+    ).astype(jnp.bfloat16)
+    last_part = mix(collect(proj, "gc"))
     basis_bf = jnp.einsum("obr,osr->obs", image, of_block, precision=HIGH).astype(jnp.bfloat16)
-    image = image_of(mixed, basis_bf)
+    image = image_of(first_part, last_part, basis_bf)
     codes = seen_by(image)
     placed = jnp.concatenate(
         [

time: 241 us -> 242 us (level)
  starting transfers between devices: 41.2 us -> 53.9 us
  waiting for transfers between devices: 92 us -> 80.8 us
    all_gather x1, waiting for transfers between devices: 14.5 us -> 0.02 us  [mix_seen(): pieces = lax.all_gather(seen[:, :, :wide], ('gr', 'gc'), axis=0, tiled=True)]
    ppermute x34 -> x41, starting transfers between devices: 41.1 us -> 53.8 us  [swap(): lax.ppermute(value, axis, [(i, i ^ k) for i in range(lax.axis_size(axis))])]
    unnamed x4, waiting for transfers between devices: 3.1 us -> 5.67 us
    ppermute x34 -> x41, waiting for transfers between devices: 74.3 us -> 75.1 us  [swap(): lax.ppermute(value, axis, [(i, i ^ k) for i in range(lax.axis_size(axis))])]
  transfers between devices with their start and end apart: 37 -> 44, of which waited for: 24 -> 25; matrix products, arithmetic and copies ran while one was open for 14% -> 13% of each run, Pallas kernels for 16% -> 16%
where the time goes in v5:
time: 242 us; the launch traced here: 241 us
  waiting for transfers between devices  80.8 us (33%)
  starting transfers between devices  53.9 us (22%)
  Pallas kernels  38.8 us (16%)
  matrix products  27.7 us (11%)
  between operations  16.2 us (7%)
  local copies, waits for them, and re-layouts  15 us (6%)
  other arithmetic  8.67 us (4%)
    ppermute x41, waiting for transfers between devices, swap(): lax.ppermute(value, axis, [(i, i ^ k) for i in range(lax.axis_size(axis))])  75.1 us
    ppermute x41, starting transfers between devices, swap(): lax.ppermute(value, axis, [(i, i ^ k) for i in range(lax.axis_size(axis))])  53.8 us
    pallas_call x2, Pallas kernels, inverse_factor(): pl.pallas_call(functools.partial(factor_kernel, scale, exact), out_shape=...  38.8 us
    dot_general x4, matrix products, seen_by(): jnp.einsum('tob,obr->otr', own_x, part, preferred_element_type=jnp.float32)  5.81 us
    unnamed x4, waiting for transfers between devices  5.67 us
    dot_general x2, matrix products, image_of(): jnp.einsum('tob,otr->obr', full_x, full, preferred_element_type=jnp.float32)  5.13 us
  transfers between devices with their start and end apart: 44, of which 25 were waited for; matrix products, arithmetic and copies ran while one was open for 13% of the time, Pallas kernels for 16%

profile of v5, /device:TPU:0, one launch (start us, length us, event | category | flops | bytes accessed | tf_op | source)
XLA Modules:
  0.0 241.1 jit_solution(9629568799618167798)
XLA Ops:
  8.6 3.0 %collective-permute-start = (bf16[2,256,256]{2,1,0:T(8,128)(2,1)S(1)}, bf16[2,256,256]{2,1,0:T(8,128)(2,1)S(1)}, u32[]{:S(2)}, u32[]{:S(2)}) collective-permute-start(bf16[2,256,256]{2,1,0:T(8,128)(2,1)S(1)} %get-tuple-element.90), channel_id=1, source_target_pairs={{0,8},{8,0},{16,24},{24,16},{1,9},{9,1},{17,25},{25,17},{2,10},{10... | collective-permute-start | bytes 786440 | tf_op jit(solution)/shard_map/ppermute | solution.py:194
  32.0 2.8 %collective-permute-done.7 = bf16[2,256,256]{2,1,0:T(8,128)(2,1)S(1)} collective-permute-done((bf16[2,256,256]{2,1,0:T(8,128)(2,1)S(1)}, bf16[2,256,256]{2,1,0:T(8,128)(2,1)S(1)}, u32[]{:S(2)}, u32[]{:S(2)}) %collective-permute-start.7) | collective-permute-done | bytes 262176 | tf_op jit(solution)/shard_map/ppermute | solution.py:194
  34.8 3.7 %collective-permute-start.5 = (bf16[2,128,256]{2,1,0:T(8,128)(2,1)S(1)}, bf16[2,128,256]{2,1,0:T(8,128)(2,1)S(1)}, u32[]{:S(2)}, u32[]{:S(2)}) collective-permute-start(bf16[2,128,256]{2,1,0:T(8,128)(2,1)S(1)} %convolution_convert_fusion.3), channel_id=1, source_target_pairs={{0,3},{1,2},{2,1},{3,0},{4,7},{5,6},{6,5},{7,4},{8,11},{9,10},{10,... | collective-permute-start | bytes 393224 | tf_op jit(solution)/shard_map/ppermute | solution.py:194
  49.5 7.1 %collective-permute-done.11 = bf16[2,128,256]{2,1,0:T(8,128)(2,1)S(1)} collective-permute-done((bf16[2,128,256]{2,1,0:T(8,128)(2,1)S(1)}, bf16[2,128,256]{2,1,0:T(8,128)(2,1)S(1)}, u32[]{:S(2)}, u32[]{:S(2)}) %collective-permute-start.11) | collective-permute-done | bytes 131104 | tf_op jit(solution)/shard_map/ppermute | solution.py:194
  69.0 6.2 %collective-permute-done.15 = bf16[2,128,512]{2,1,0:T(8,128)(2,1)} collective-permute-done((bf16[2,128,512]{2,1,0:T(8,128)(2,1)}, bf16[2,128,512]{2,1,0:T(8,128)(2,1)}, u32[]{:S(2)}, u32[]{:S(2)}) %collective-permute-start.15) | collective-permute-done | bytes 262176 | tf_op jit(solution)/shard_map/ppermute | solution.py:194
  75.2 3.5 %multiply_add_fusion.1 = f32[2,1024,512]{2,1,0:T(8,128)S(1)} fusion(bf16[2,256,256]{2,1,0:T(8,128)(2,1)} %get-tuple-element.83, bf16[2,256,256]{2,1,0:T(8,128)(2,1)} %get-tuple-element.84, bf16[2,256,256]{2,1,0:T(8,128)(2,1)} %get-tuple-element.85, bf16[2,256,256]{2,1,0:T(8,128)(2,1)} %get-tuple-element.82, bf16[2,256,256]{2,1,0:T(8,128)(2,1)S(1)} %get-tuple-element.79, ...), kind=kOutput, calls=%fused_computation.7 | convolution fusion | flops 1098907648 | bytes 9437184 | tf_op jit(solution)/shard_map/tob,otr->obr/dot_general | solution.py:287
  84.2 3.1 %fusion.4 = f32[2,512,128]{2,1,0:T(8,128)S(1)} fusion(bf16[128,2,1024]{0,2,1:T(8,128)(2,1)S(1)} %bitcast.181, f32[2,1024,512]{2,1,0:T(8,128)} %copy-done), kind=kOutput, calls=%fused_computation.9 | convolution fusion | flops 271581184 | bytes 5242880 | tf_op jit(solution)/shard_map/tob,obr->otr/dot_general | solution.py:292
  89.5 2.8 %collective-permute-start.19 = (f32[128,384]{1,0:T(8,128)S(1)}, f32[128,384]{1,0:T(8,128)S(1)}, u32[]{:S(2)}, u32[]{:S(2)}) collective-permute-start(f32[128,384]{1,0:T(8,128)S(1)} %fusion.115), channel_id=1, source_target_pairs={{0,2},{1,3},{2,0},{3,1},{4,6},{5,7},{6,4},{7,5},{8,10},{9,11},{10,... | collective-permute-start | bytes 589832 | tf_op jit(solution)/shard_map/ppermute | solution.py:194
  93.2 7.8 %collective-permute-done.19 = f32[128,384]{1,0:T(8,128)S(1)} collective-permute-done((f32[128,384]{1,0:T(8,128)S(1)}, f32[128,384]{1,0:T(8,128)S(1)}, u32[]{:S(2)}, u32[]{:S(2)}) %collective-permute-start.19) | collective-permute-done | bytes 196640 | tf_op jit(solution)/shard_map/ppermute | solution.py:194
  105.5 4.3 %collective-permute-done.20.refs_1_ = f32[128,384]{1,0:T(8,128)S(1)} collective-permute-done((f32[128,384]{1,0:T(8,128)S(1)}, f32[128,384]{1,0:T(8,128)S(1)}, u32[]{:S(2)}, u32[]{:S(2)}) %collective-permute-start.20) | collective-permute-done | bytes 196640 | tf_op jit(solution)/shard_map/ppermute | solution.py:194
  112.3 18.8 %inverse_factor.2 = f32[512,512]{1,0:T(8,128)S(1)} custom-call(s32[1]{0:T(128)} %bitcast.1.pos_ref, f32[128,384]{1,0:T(8,128)S(1)} %add.404.refs_0_, f32[128,384]{1,0:T(8,128)S(1)} %collective-permute-done.20.refs_1_, f32[128,384]{1,0:T(8,128)S(1)} %collective-permute-done.21.refs_2_, f32[128,384]{1,0:T(8,128)S(1)} %collective-permute-done.22.refs_3_), custom_call_target="tpu_custom_call" | custom-call | flops 12884901888 | bytes 2097152 | tf_op jit(solution)/shard_map/inverse_factor/pallas_call | solution.py:171
  136.8 3.0 %collective-permute-start.28 = (bf16[2,128,256]{2,1,0:T(8,128)(2,1)S(1)}, bf16[2,128,256]{2,1,0:T(8,128)(2,1)S(1)}, u32[]{:S(2)}, u32[]{:S(2)}) collective-permute-start(bf16[2,128,256]{2,1,0:T(8,128)(2,1)S(1)} %convolution_convert_fusion.1), channel_id=1, source_target_pairs={{0,2},{1,3},{2,0},{3,1},{4,6},{5,7},{6,4},{7,5},{8,10},{9,11},{10,... | collective-permute-start | bytes 393224 | tf_op jit(solution)/shard_map/ppermute | solution.py:194
  141.2 4.0 %collective-permute-done.27 = bf16[2,128,256]{2,1,0:T(8,128)(2,1)S(1)} collective-permute-done((bf16[2,128,256]{2,1,0:T(8,128)(2,1)S(1)}, bf16[2,128,256]{2,1,0:T(8,128)(2,1)S(1)}, u32[]{:S(2)}, u32[]{:S(2)}) %collective-permute-start.27) | collective-permute-done | bytes 131104 | tf_op jit(solution)/shard_map/ppermute | solution.py:194
  145.2 4.6 %collective-permute-done.28 = bf16[2,128,256]{2,1,0:T(8,128)(2,1)S(1)} collective-permute-done((bf16[2,128,256]{2,1,0:T(8,128)(2,1)S(1)}, bf16[2,128,256]{2,1,0:T(8,128)(2,1)S(1)}, u32[]{:S(2)}, u32[]{:S(2)}) %collective-permute-start.28) | collective-permute-done | bytes 131104 | tf_op jit(solution)/shard_map/ppermute | solution.py:194
  158.5 3.8 %fusion.8 = bf16[2,1024,512]{2,1,0:T(8,128)(2,1)S(1)} fusion(f32[2,1024,512]{2,1,0:T(8,128)S(1)} %copy-done.2, f32[1,512,512]{2,1,0:T(8,128)S(1)} %get-tuple-element.57, f32[1,512,512]{2,1,0:T(8,128)S(1)} %get-tuple-element.56), kind=kOutput, calls=%fused_computation.13 | convolution fusion | flops 3221749760 | bytes 8388608 | tf_op jit(solution)/shard_map/obr,osr->obs/dot_general | solution.py:358
  163.0 3.3 %collective-permute-done.32 = bf16[2,128,256]{2,1,0:T(8,128)(2,1)S(1)} collective-permute-done((bf16[2,128,256]{2,1,0:T(8,128)(2,1)S(1)}, bf16[2,128,256]{2,1,0:T(8,128)(2,1)S(1)}, u32[]{:S(2)}, u32[]{:S(2)}) %collective-permute-start.32) | collective-permute-done | bytes 131104 | tf_op jit(solution)/shard_map/ppermute | solution.py:194
  172.3 2.9 %collective-permute-start.35 = (f32[128,384]{1,0:T(8,128)S(1)}, f32[128,384]{1,0:T(8,128)S(1)}, u32[]{:S(2)}, u32[]{:S(2)}) collective-permute-start(f32[128,384]{1,0:T(8,128)S(1)} %pad_maximum_fusion.5), channel_id=1, source_target_pairs={{0,1},{1,0},{2,3},{3,2},{4,5},{5,4},{6,7},{7,6},{8,9},{9,8},{10,11... | collective-permute-start | bytes 589832 | tf_op jit(solution)/shard_map/ppermute | solution.py:194
  176.2 4.3 %collective-permute-done.35 = f32[128,384]{1,0:T(8,128)S(1)} collective-permute-done((f32[128,384]{1,0:T(8,128)S(1)}, f32[128,384]{1,0:T(8,128)S(1)}, u32[]{:S(2)}, u32[]{:S(2)}) %collective-permute-start.35) | collective-permute-done | bytes 196640 | tf_op jit(solution)/shard_map/ppermute | solution.py:194
  180.5 2.8 %collective-permute-start.36 = (f32[128,384]{1,0:T(8,128)S(1)}, f32[128,384]{1,0:T(8,128)S(1)}, u32[]{:S(2)}, u32[]{:S(2)}) collective-permute-start(f32[128,384]{1,0:T(8,128)S(1)} %fusion.114), channel_id=1, source_target_pairs={{0,2},{1,3},{2,0},{3,1},{4,6},{5,7},{6,4},{7,5},{8,10},{9,11},{10,... | collective-permute-start | bytes 589832 | tf_op jit(solution)/shard_map/ppermute | solution.py:194
  183.2 8.8 %collective-permute-done.36 = f32[128,384]{1,0:T(8,128)S(1)} collective-permute-done((f32[128,384]{1,0:T(8,128)S(1)}, f32[128,384]{1,0:T(8,128)S(1)}, u32[]{:S(2)}, u32[]{:S(2)}) %collective-permute-start.36) | collective-permute-done | bytes 196640 | tf_op jit(solution)/shard_map/ppermute | solution.py:194
  196.7 3.3 %collective-permute-done.37.refs_1_ = f32[128,384]{1,0:T(8,128)S(1)} collective-permute-done((f32[128,384]{1,0:T(8,128)S(1)}, f32[128,384]{1,0:T(8,128)S(1)}, u32[]{:S(2)}, u32[]{:S(2)}) %collective-permute-start.37) | collective-permute-done | bytes 196640 | tf_op jit(solution)/shard_map/ppermute | solution.py:194
  202.8 20.0 %inverse_factor.3 = f32[512,512]{1,0:T(8,128)S(1)} custom-call(s32[1]{0:T(128)} %bitcast.1.pos_ref, f32[128,384]{1,0:T(8,128)S(1)} %add.441.refs_0_, f32[128,384]{1,0:T(8,128)S(1)} %collective-permute-done.37.refs_1_, f32[128,384]{1,0:T(8,128)S(1)} %collective-permute-done.38.refs_2_, f32[128,384]{1,0:T(8,128)S(1)} %collective-permute-done.39.refs_3_), custom_call_target="tpu_custom_call" | custom-call | flops 12884901888 | bytes 2097152 | tf_op jit(solution)/shard_map/inverse_factor/pallas_call | solution.py:171
  222.8 5.6 %reduce-scatter.4.cloned.1.call-done = f32[16,1024]{1,0:T(8,128)} async-done(((f32[128,1024]{1,0:T(8,128)}), f32[16,1024]{1,0:T(8,128)}) %reduce-scatter.4.cloned.1.call-update) | async-done | bytes 65552
  231.2 3.4 %fusion.12 = f32[2,256,512]{2,1,0:T(8,128)} fusion(f32[1,512,512]{2,1,0:T(8,128)S(1)} %get-tuple-element.55, f32[1,512,512]{2,1,0:T(8,128)S(1)} %get-tuple-element.54, f32[2,1024,512]{2,1,0:T(8,128)} %copy-done.3, s32[]{:T(128)S(6)} %select_n.315), kind=kOutput, calls=%fused_computation.17 | convolution fusion | flops 805830656 | bytes 4194308 | tf_op jit(solution)/shard_map/obr,osr->obs/dot_general | solution.py:370
  (231 shorter events, 92.0 us)
Async XLA Ops:
  7.2 55.8 %all-gather.3.cloned.1.call-start = ((), (), s32[]{:S(2)}) async-start(), calls=%async_computation.1 | async-start | bytes 2621440 | tf_op jit(solution)/shard_map/all_gather | solution.py:238
  8.6 14.8 %collective-permute-start = (bf16[2,256,256]{2,1,0:T(8,128)(2,1)S(1)}, bf16[2,256,256]{2,1,0:T(8,128)(2,1)S(1)}, u32[]{:S(2)}, u32[]{:S(2)}) collective-permute-start(bf16[2,256,256]{2,1,0:T(8,128)(2,1)S(1)} %get-tuple-element.90), channel_id=1, source_target_pairs={{0,8},{8,0},{16,24},{24,16},{1,9},{9,1},{17,25},{25,17},{2,10},{10... | collective-permute-start | bytes 786440 | tf_op jit(solution)/shard_map/ppermute | solution.py:194
  11.6 14.8 %collective-permute-start.1 = (bf16[2,256,256]{2,1,0:T(8,128)(2,1)S(1)}, bf16[2,256,256]{2,1,0:T(8,128)(2,1)S(1)}, u32[]{:S(2)}, u32[]{:S(2)}) collective-permute-start(bf16[2,256,256]{2,1,0:T(8,128)(2,1)S(1)} %get-tuple-element.90), channel_id=1, source_target_pairs={{0,16},{8,24},{16,0},{24,8},{1,17},{9,25},{17,1},{25,9},{2,18},{10... | collective-permute-start | bytes 786440 | tf_op jit(solution)/shard_map/ppermute | solution.py:194
  13.1 13.3 %collective-permute-start.2 = (bf16[2,256,256]{2,1,0:T(8,128)(2,1)S(1)}, bf16[2,256,256]{2,1,0:T(8,128)(2,1)S(1)}, u32[]{:S(2)}, u32[]{:S(2)}) collective-permute-start(bf16[2,256,256]{2,1,0:T(8,128)(2,1)S(1)} %get-tuple-element.90), channel_id=1, source_target_pairs={{0,24},{8,16},{16,8},{24,0},{1,25},{9,17},{17,9},{25,1},{2,26},{10... | collective-permute-start | bytes 786440 | tf_op jit(solution)/shard_map/ppermute | solution.py:194
  13.2 21.7 %collective-permute-start.7 = (bf16[2,256,256]{2,1,0:T(8,128)(2,1)S(1)}, bf16[2,256,256]{2,1,0:T(8,128)(2,1)S(1)}, u32[]{:S(2)}, u32[]{:S(2)}) collective-permute-start(bf16[2,256,256]{2,1,0:T(8,128)(2,1)S(1)} %get-tuple-element.91), channel_id=1, source_target_pairs={{0,8},{8,0},{16,24},{24,16},{1,9},{9,1},{17,25},{25,17},{2,10},{10... | collective-permute-start | bytes 786440 | tf_op jit(solution)/shard_map/ppermute | solution.py:194
  15.1 25.8 %collective-permute-start.8 = (bf16[2,256,256]{2,1,0:T(8,128)(2,1)S(1)}, bf16[2,256,256]{2,1,0:T(8,128)(2,1)S(1)}, u32[]{:S(2)}, u32[]{:S(2)}) collective-permute-start(bf16[2,256,256]{2,1,0:T(8,128)(2,1)S(1)} %get-tuple-element.91), channel_id=1, source_target_pairs={{0,16},{8,24},{16,0},{24,8},{1,17},{9,25},{17,1},{25,9},{2,18},{10... | collective-permute-start | bytes 786440 | tf_op jit(solution)/shard_map/ppermute | solution.py:194
  16.7 117.0 %all-gather.5.cloned.1.call-start = ((), (), s32[]{:S(2)}) async-start(), calls=%async_computation.2 | async-start | bytes 2359296 | tf_op jit(solution)/shard_map/all_gather | solution.py:344
  23.4 18.3 %collective-permute-start.9 = (bf16[2,256,256]{2,1,0:T(8,128)(2,1)S(1)}, bf16[2,256,256]{2,1,0:T(8,128)(2,1)S(1)}, u32[]{:S(2)}, u32[]{:S(2)}) collective-permute-start(bf16[2,256,256]{2,1,0:T(8,128)(2,1)S(1)} %get-tuple-element.91), channel_id=1, source_target_pairs={{0,24},{8,16},{16,8},{24,0},{1,25},{9,17},{17,9},{25,1},{2,26},{10... | collective-permute-start | bytes 786440 | tf_op jit(solution)/shard_map/ppermute | solution.py:194
  27.8 20.6 %collective-permute-start.3 = (bf16[2,128,256]{2,1,0:T(8,128)(2,1)S(1)}, bf16[2,128,256]{2,1,0:T(8,128)(2,1)S(1)}, u32[]{:S(2)}, u32[]{:S(2)}) collective-permute-start(bf16[2,128,256]{2,1,0:T(8,128)(2,1)S(1)} %convolution_convert_fusion.3), channel_id=1, source_target_pairs={{0,1},{1,0},{2,3},{3,2},{4,5},{5,4},{6,7},{7,6},{8,9},{9,8},{10,11... | collective-permute-start | bytes 393224 | tf_op jit(solution)/shard_map/ppermute | solution.py:194
  29.4 19.1 %collective-permute-start.4 = (bf16[2,128,256]{2,1,0:T(8,128)(2,1)S(1)}, bf16[2,128,256]{2,1,0:T(8,128)(2,1)S(1)}, u32[]{:S(2)}, u32[]{:S(2)}) collective-permute-start(bf16[2,128,256]{2,1,0:T(8,128)(2,1)S(1)} %convolution_convert_fusion.3), channel_id=1, source_target_pairs={{0,2},{1,3},{2,0},{3,1},{4,6},{5,7},{6,4},{7,5},{8,10},{9,11},{10,... | collective-permute-start | bytes 393224 | tf_op jit(solution)/shard_map/ppermute | solution.py:194
  34.8 13.7 %collective-permute-start.5 = (bf16[2,128,256]{2,1,0:T(8,128)(2,1)S(1)}, bf16[2,128,256]{2,1,0:T(8,128)(2,1)S(1)}, u32[]{:S(2)}, u32[]{:S(2)}) collective-permute-start(bf16[2,128,256]{2,1,0:T(8,128)(2,1)S(1)} %convolution_convert_fusion.3), channel_id=1, source_target_pairs={{0,3},{1,2},{2,1},{3,0},{4,7},{5,6},{6,5},{7,4},{8,11},{9,10},{10,... | collective-permute-start | bytes 393224 | tf_op jit(solution)/shard_map/ppermute | solution.py:194
  44.7 12.0 %collective-permute-start.11 = (bf16[2,128,256]{2,1,0:T(8,128)(2,1)S(1)}, bf16[2,128,256]{2,1,0:T(8,128)(2,1)S(1)}, u32[]{:S(2)}, u32[]{:S(2)}) collective-permute-start(bf16[2,128,256]{2,1,0:T(8,128)(2,1)S(1)} %convolution_convert_fusion.2), channel_id=1, source_target_pairs={{0,2},{1,3},{2,0},{3,1},{4,6},{5,7},{6,4},{7,5},{8,10},{9,11},{10,... | collective-permute-start | bytes 393224 | tf_op jit(solution)/shard_map/ppermute | solution.py:194
  61.0 14.2 %collective-permute-start.15 = (bf16[2,128,512]{2,1,0:T(8,128)(2,1)}, bf16[2,128,512]{2,1,0:T(8,128)(2,1)}, u32[]{:S(2)}, u32[]{:S(2)}) collective-permute-start(bf16[2,128,512]{2,1,0:T(8,128)(2,1)} %pad_maximum_fusion.3), channel_id=1, source_target_pairs={{0,16},{8,24},{16,0},{24,8},{1,17},{9,25},{17,1},{25,9},{2,18},{10... | collective-permute-start | bytes 786440 | tf_op jit(solution)/shard_map/ppermute | solution.py:194
  61.5 13.6 %collective-permute-start.16 = (bf16[2,128,512]{2,1,0:T(8,128)(2,1)}, bf16[2,128,512]{2,1,0:T(8,128)(2,1)}, u32[]{:S(2)}, u32[]{:S(2)}) collective-permute-start(bf16[2,128,512]{2,1,0:T(8,128)(2,1)} %pad_maximum_fusion.3), channel_id=1, source_target_pairs={{0,24},{8,16},{16,8},{24,0},{1,25},{9,17},{17,9},{25,1},{2,26},{10... | collective-permute-start | bytes 786440 | tf_op jit(solution)/shard_map/ppermute | solution.py:194
  89.5 11.5 %collective-permute-start.19 = (f32[128,384]{1,0:T(8,128)S(1)}, f32[128,384]{1,0:T(8,128)S(1)}, u32[]{:S(2)}, u32[]{:S(2)}) collective-permute-start(f32[128,384]{1,0:T(8,128)S(1)} %fusion.115), channel_id=1, source_target_pairs={{0,2},{1,3},{2,0},{3,1},{4,6},{5,7},{6,4},{7,5},{8,10},{9,11},{10,... | collective-permute-start | bytes 589832 | tf_op jit(solution)/shard_map/ppermute | solution.py:194
  101.9 126.5 %reduce-scatter.4.cloned.1.call-start = ((), (), s32[]{:S(2)}) async-start(), calls=%async_computation.3 | async-start | bytes 589824
  102.5 9.7 %collective-permute-start.21 = (f32[128,384]{1,0:T(8,128)S(1)}, f32[128,384]{1,0:T(8,128)S(1)}, u32[]{:S(2)}, u32[]{:S(2)}) collective-permute-start(f32[128,384]{1,0:T(8,128)S(1)} %add.404.refs_0_), channel_id=1, source_target_pairs={{0,16},{8,24},{16,0},{24,8},{1,17},{9,25},{17,1},{25,9},{2,18},{10... | collective-permute-start | bytes 589832 | tf_op jit(solution)/shard_map/ppermute | solution.py:194
  136.8 13.0 %collective-permute-start.28 = (bf16[2,128,256]{2,1,0:T(8,128)(2,1)S(1)}, bf16[2,128,256]{2,1,0:T(8,128)(2,1)S(1)}, u32[]{:S(2)}, u32[]{:S(2)}) collective-permute-start(bf16[2,128,256]{2,1,0:T(8,128)(2,1)S(1)} %convolution_convert_fusion.1), channel_id=1, source_target_pairs={{0,2},{1,3},{2,0},{3,1},{4,6},{5,7},{6,4},{7,5},{8,10},{9,11},{10,... | collective-permute-start | bytes 393224 | tf_op jit(solution)/shard_map/ppermute | solution.py:194
  139.9 10.0 %collective-permute-start.29 = (bf16[2,128,256]{2,1,0:T(8,128)(2,1)S(1)}, bf16[2,128,256]{2,1,0:T(8,128)(2,1)S(1)}, u32[]{:S(2)}, u32[]{:S(2)}) collective-permute-start(bf16[2,128,256]{2,1,0:T(8,128)(2,1)S(1)} %convolution_convert_fusion.1), channel_id=1, source_target_pairs={{0,3},{1,2},{2,1},{3,0},{4,7},{5,6},{6,5},{7,4},{8,11},{9,10},{10,... | collective-permute-start | bytes 393224 | tf_op jit(solution)/shard_map/ppermute | solution.py:194
  152.2 10.1 %collective-permute-start.25 = (bf16[2,128,256]{2,1,0:T(8,128)(2,1)S(1)}, bf16[2,128,256]{2,1,0:T(8,128)(2,1)S(1)}, u32[]{:S(2)}, u32[]{:S(2)}) collective-permute-start(bf16[2,128,256]{2,1,0:T(8,128)(2,1)S(1)} %convolution_convert_fusion), channel_id=1, source_target_pairs={{0,16},{8,24},{16,0},{24,8},{1,17},{9,25},{17,1},{25,9},{2,18},{10... | collective-permute-start | bytes 393224 | tf_op jit(solution)/shard_map/ppermute | solution.py:194
  152.8 9.5 %collective-permute-start.26 = (bf16[2,128,256]{2,1,0:T(8,128)(2,1)S(1)}, bf16[2,128,256]{2,1,0:T(8,128)(2,1)S(1)}, u32[]{:S(2)}, u32[]{:S(2)}) collective-permute-start(bf16[2,128,256]{2,1,0:T(8,128)(2,1)S(1)} %convolution_convert_fusion), channel_id=1, source_target_pairs={{0,24},{8,16},{16,8},{24,0},{1,25},{9,17},{17,9},{25,1},{2,26},{10... | collective-permute-start | bytes 393224 | tf_op jit(solution)/shard_map/ppermute | solution.py:194
  156.1 10.2 %collective-permute-start.32 = (bf16[2,128,256]{2,1,0:T(8,128)(2,1)S(1)}, bf16[2,128,256]{2,1,0:T(8,128)(2,1)S(1)}, u32[]{:S(2)}, u32[]{:S(2)}) collective-permute-start(bf16[2,128,256]{2,1,0:T(8,128)(2,1)S(1)} %add_convert_fusion), channel_id=1, source_target_pairs={{0,16},{8,24},{16,0},{24,8},{1,17},{9,25},{17,1},{25,9},{2,18},{10... | collective-permute-start | bytes 393224 | tf_op jit(solution)/shard_map/ppermute | solution.py:194
  180.5 11.6 %collective-permute-start.36 = (f32[128,384]{1,0:T(8,128)S(1)}, f32[128,384]{1,0:T(8,128)S(1)}, u32[]{:S(2)}, u32[]{:S(2)}) collective-permute-start(f32[128,384]{1,0:T(8,128)S(1)} %fusion.114), channel_id=1, source_target_pairs={{0,2},{1,3},{2,0},{3,1},{4,6},{5,7},{6,4},{7,5},{8,10},{9,11},{10,... | collective-permute-start | bytes 589832 | tf_op jit(solution)/shard_map/ppermute | solution.py:194
  192.9 9.9 %collective-permute-start.38 = (f32[128,384]{1,0:T(8,128)S(1)}, f32[128,384]{1,0:T(8,128)S(1)}, u32[]{:S(2)}, u32[]{:S(2)}) collective-permute-start(f32[128,384]{1,0:T(8,128)S(1)} %add.441.refs_0_), channel_id=1, source_target_pairs={{0,16},{8,24},{16,0},{24,8},{1,17},{9,25},{17,1},{25,9},{2,18},{10... | collective-permute-start | bytes 589832 | tf_op jit(solution)/shard_map/ppermute | solution.py:194
  (62 other events, 643.5 us)
Sparse Core Ops, SparseCore 0:
  16.8 44.5 all-gather.2
  102.0 27.9 all-gather.4
  196.8 31.5 reduce-scatter.3

commit v6 on v5

--- a/solution.py
+++ b/solution.py
@@ -282,7 +282,7 @@
     def image_of(*operands):
         *parts, basis_bf = operands
         full = jnp.concatenate(
-            [jnp.concatenate(collect(part, "tok"), axis=1) for part in parts], axis=2
+            [jnp.concatenate(part, axis=1) for part in parts], axis=2
         )
         cover = jnp.einsum("tob,otr->obr", full_x, full, preferred_element_type=jnp.float32)
         return cover / total_tokens + ridge * basis_bf.astype(jnp.float32)
@@ -292,6 +292,12 @@
             jnp.einsum("tob,obr->otr", own_x, part, preferred_element_type=jnp.float32)
             for part in split(image)
         )
+
+    def half_over_gr(value):
+        half = value.shape[0] // 2
+        own = lax.dynamic_slice_in_dim(value, gr_pos * half, half, 0)
+        other = lax.dynamic_slice_in_dim(value, (gr_pos ^ 1) * half, half, 0)
+        return own + swap(other, "gr", 1)
 
     def factor(image, last, beside):
         precision = HIGHEST if last else HIGH
@@ -318,10 +324,11 @@
         while step < gc_count:
             if last and 2 * step == gc_count:
                 total, beside = lax.optimization_barrier((total, beside))
+                beside = half_over_gr(beside)
             total += swap(total, "gc", step)
             step *= 2
+        total, beside = lax.optimization_barrier((total, beside))
         if not last:
-            total, beside = lax.optimization_barrier((total, beside))
             beside = mix_seen(beside)
         if packed:
             pieces = collect(total, "tok")
@@ -337,7 +344,7 @@
         of_group = [jnp.where(gr_pos == g, own, other) for g in range(groups)]
         return of_block, of_group, beside
 
-    image = image_of(mixed, basis_bf)
+    image = image_of(collect(mixed, "tok"), basis_bf)
     wide = rank // 2
 
     def mix_seen(seen):
@@ -354,9 +361,10 @@
     first_part = jnp.einsum(
         "otr,osr->ots", second, of_block[:, :wide, :wide], precision=HIGH
     ).astype(jnp.bfloat16)
-    last_part = mix(collect(proj, "gc"))
+    near, first_pieces = lax.optimization_barrier((collect(proj, "gc"), collect(first_part, "tok")))
+    last_pieces = collect(mix(near), "tok")
     basis_bf = jnp.einsum("obr,osr->obs", image, of_block, precision=HIGH).astype(jnp.bfloat16)
-    image = image_of(first_part, last_part, basis_bf)
+    image = image_of(first_pieces, last_pieces, basis_bf)
     codes = seen_by(image)
     placed = jnp.concatenate(
         [
@@ -368,7 +376,7 @@
     of_block, of_group, placed = factor(image, True, placed)
     rows = lax.dynamic_slice_in_dim(image, tok_pos * slice_rows, slice_rows, 1)
     basis = jnp.einsum("obr,osr->obs", rows, of_block, precision=HIGH)
-    placed = lax.psum_scatter(placed, ("gr", "gc"), scatter_dimension=0, tiled=True)
+    placed = lax.psum_scatter(placed, "gc", scatter_dimension=0, tiled=True)
     latent = jnp.concatenate(
         [
             jnp.einsum(

time: 242 us -> 261 us (1.079)
  waiting for transfers between devices: 80.8 us -> 95 us
  other arithmetic: 8.67 us -> 11.8 us
    unnamed x4, waiting for transfers between devices: 5.67 us -> 18.7 us
    ppermute x41 -> x42, waiting for transfers between devices: 75.1 us -> 76.3 us  [swap(): lax.ppermute(value, axis, [(i, i ^ k) for i in range(lax.axis_size(axis))])]
    ppermute x41 -> x42, starting transfers between devices: 53.8 us -> 52.8 us  [swap(): lax.ppermute(value, axis, [(i, i ^ k) for i in range(lax.axis_size(axis))])]
  transfers between devices with their start and end apart: 44 -> 45, of which waited for: 25 -> 25; matrix products, arithmetic and copies ran while one was open for 13% -> 13% of each run, Pallas kernels for 16% -> 7%
where the time goes in v6:
time: 261 us; the launch traced here: 260 us
  waiting for transfers between devices  95 us (36%)
  starting transfers between devices  52.9 us (20%)
  Pallas kernels  38.8 us (15%)
  matrix products  30 us (11%)
  between operations  16.2 us (6%)
  local copies, waits for them, and re-layouts  15.8 us (6%)
  other arithmetic  11.8 us (5%)
    ppermute x42, waiting for transfers between devices, swap(): lax.ppermute(value, axis, [(i, i ^ k) for i in range(lax.axis_size(axis))])  76.3 us
    ppermute x42, starting transfers between devices, swap(): lax.ppermute(value, axis, [(i, i ^ k) for i in range(lax.axis_size(axis))])  52.8 us
    pallas_call x2, Pallas kernels, inverse_factor(): pl.pallas_call(functools.partial(factor_kernel, scale, exact), out_shape=...  38.8 us
    unnamed x4, waiting for transfers between devices  18.7 us
    dot_general x1, matrix products, per_device(): jnp.einsum('obr,osr->obs', image, of_block, precision=HIGH)  5.98 us
    dot_general x4, matrix products, seen_by(): jnp.einsum('tob,obr->otr', own_x, part, preferred_element_type=jnp.float32)  5.81 us
  transfers between devices with their start and end apart: 45, of which 25 were waited for; matrix products, arithmetic and copies ran while one was open for 13% of the time, Pallas kernels for 7%

profile of v6, /device:TPU:0, one launch (start us, length us, event | category | flops | bytes accessed | tf_op | source)
XLA Modules:
  0.0 260.5 jit_solution(5704309136227816020)
XLA Ops:
  8.6 3.0 %collective-permute-start = (bf16[2,256,256]{2,1,0:T(8,128)(2,1)S(1)}, bf16[2,256,256]{2,1,0:T(8,128)(2,1)S(1)}, u32[]{:S(2)}, u32[]{:S(2)}) collective-permute-start(bf16[2,256,256]{2,1,0:T(8,128)(2,1)S(1)} %get-tuple-element.110), channel_id=1, source_target_pairs={{0,8},{8,0},{16,24},{24,16},{1,9},{9,1},{17,25},{25,17},{2,10},{10... | collective-permute-start | bytes 786440 | tf_op jit(solution)/shard_map/ppermute | solution.py:194
  23.8 2.7 %collective-permute-done.1 = bf16[2,256,256]{2,1,0:T(8,128)(2,1)S(1)} collective-permute-done((bf16[2,256,256]{2,1,0:T(8,128)(2,1)S(1)}, bf16[2,256,256]{2,1,0:T(8,128)(2,1)S(1)}, u32[]{:S(2)}, u32[]{:S(2)}) %collective-permute-start.1) | collective-permute-done | bytes 262176 | tf_op jit(solution)/shard_map/ppermute | solution.py:194
  32.0 2.9 %collective-permute-done.7 = bf16[2,256,256]{2,1,0:T(8,128)(2,1)S(1)} collective-permute-done((bf16[2,256,256]{2,1,0:T(8,128)(2,1)S(1)}, bf16[2,256,256]{2,1,0:T(8,128)(2,1)S(1)}, u32[]{:S(2)}, u32[]{:S(2)}) %collective-permute-start.7) | collective-permute-done | bytes 262176 | tf_op jit(solution)/shard_map/ppermute | solution.py:194
  34.9 3.7 %collective-permute-start.5 = (bf16[2,128,256]{2,1,0:T(8,128)(2,1)S(1)}, bf16[2,128,256]{2,1,0:T(8,128)(2,1)S(1)}, u32[]{:S(2)}, u32[]{:S(2)}) collective-permute-start(bf16[2,128,256]{2,1,0:T(8,128)(2,1)S(1)} %convolution_convert_fusion.3), channel_id=1, source_target_pairs={{0,3},{1,2},{2,1},{3,0},{4,7},{5,6},{6,5},{7,4},{8,11},{9,10},{10,... | collective-permute-start | bytes 393224 | tf_op jit(solution)/shard_map/ppermute | solution.py:194
  44.7 2.7 %collective-permute-start.11 = (bf16[2,128,256]{2,1,0:T(8,128)(2,1)S(1)}, bf16[2,128,256]{2,1,0:T(8,128)(2,1)S(1)}, u32[]{:S(2)}, u32[]{:S(2)}) collective-permute-start(bf16[2,128,256]{2,1,0:T(8,128)(2,1)S(1)} %convolution_convert_fusion.2), channel_id=1, source_target_pairs={{0,2},{1,3},{2,0},{3,1},{4,6},{5,7},{6,4},{7,5},{8,10},{9,11},{10,... | collective-permute-start | bytes 393224 | tf_op jit(solution)/shard_map/ppermute | solution.py:194
  49.5 7.1 %collective-permute-done.11 = bf16[2,128,256]{2,1,0:T(8,128)(2,1)S(1)} collective-permute-done((bf16[2,128,256]{2,1,0:T(8,128)(2,1)S(1)}, bf16[2,128,256]{2,1,0:T(8,128)(2,1)S(1)}, u32[]{:S(2)}, u32[]{:S(2)}) %collective-permute-start.11) | collective-permute-done | bytes 131104 | tf_op jit(solution)/shard_map/ppermute | solution.py:194
  69.0 6.2 %collective-permute-done.15 = bf16[2,128,512]{2,1,0:T(8,128)(2,1)} collective-permute-done((bf16[2,128,512]{2,1,0:T(8,128)(2,1)}, bf16[2,128,512]{2,1,0:T(8,128)(2,1)}, u32[]{:S(2)}, u32[]{:S(2)}) %collective-permute-start.15) | collective-permute-done | bytes 262176 | tf_op jit(solution)/shard_map/ppermute | solution.py:194
  75.2 3.5 %multiply_add_fusion.1 = f32[2,1024,512]{2,1,0:T(8,128)S(1)} fusion(bf16[2,256,256]{2,1,0:T(8,128)(2,1)} %get-tuple-element.103, bf16[2,256,256]{2,1,0:T(8,128)(2,1)} %get-tuple-element.104, bf16[2,256,256]{2,1,0:T(8,128)(2,1)} %get-tuple-element.105, bf16[2,256,256]{2,1,0:T(8,128)(2,1)} %get-tuple-element.102, ...), kind=kOutput, calls=%fused_computation.7 | convolution fusion | flops 1098907648 | bytes 9437184 | tf_op jit(solution)/shard_map/tob,otr->obr/dot_general | solution.py:287
  84.3 3.1 %fusion.5 = f32[2,512,128]{2,1,0:T(8,128)S(1)} fusion(bf16[128,2,1024]{0,2,1:T(8,128)(2,1)S(1)} %bitcast.165, f32[2,1024,512]{2,1,0:T(8,128)} %copy-done), kind=kOutput, calls=%fused_computation.15 | convolution fusion | flops 271581184 | bytes 5242880 | tf_op jit(solution)/shard_map/tob,obr->otr/dot_general | solution.py:292
  89.5 2.8 %collective-permute-start.19 = (f32[128,384]{1,0:T(8,128)S(1)}, f32[128,384]{1,0:T(8,128)S(1)}, u32[]{:S(2)}, u32[]{:S(2)}) collective-permute-start(f32[128,384]{1,0:T(8,128)S(1)} %fusion.102), channel_id=1, source_target_pairs={{0,2},{1,3},{2,0},{3,1},{4,6},{5,7},{6,4},{7,5},{8,10},{9,11},{10,... | collective-permute-start | bytes 589832 | tf_op jit(solution)/shard_map/ppermute | solution.py:194
  93.2 7.8 %collective-permute-done.19 = f32[128,384]{1,0:T(8,128)S(1)} collective-permute-done((f32[128,384]{1,0:T(8,128)S(1)}, f32[128,384]{1,0:T(8,128)S(1)}, u32[]{:S(2)}, u32[]{:S(2)}) %collective-permute-start.19) | collective-permute-done | bytes 196640 | tf_op jit(solution)/shard_map/ppermute | solution.py:194
  105.5 4.3 %collective-permute-done.20.refs_1_ = f32[128,384]{1,0:T(8,128)S(1)} collective-permute-done((f32[128,384]{1,0:T(8,128)S(1)}, f32[128,384]{1,0:T(8,128)S(1)}, u32[]{:S(2)}, u32[]{:S(2)}) %collective-permute-start.20) | collective-permute-done | bytes 196640 | tf_op jit(solution)/shard_map/ppermute | solution.py:194
  112.3 18.8 %inverse_factor.2 = f32[512,512]{1,0:T(8,128)S(1)} custom-call(s32[1]{0:T(128)} %bitcast.19.pos_ref, f32[128,384]{1,0:T(8,128)S(1)} %add.414.refs_0_, f32[128,384]{1,0:T(8,128)S(1)} %collective-permute-done.20.refs_1_, f32[128,384]{1,0:T(8,128)S(1)} %collective-permute-done.21.refs_2_, f32[128,384]{1,0:T(8,128)S(1)} %collective-permute-done.22.refs_3_), custom_call_target="tpu_custom_call" | custom-call | flops 12884901888 | bytes 2097152 | tf_op jit(solution)/shard_map/inverse_factor/pallas_call | solution.py:171
  141.9 3.0 %collective-permute-start.25 = (bf16[2,128,256]{2,1,0:T(8,128)(2,1)S(1)}, bf16[2,128,256]{2,1,0:T(8,128)(2,1)S(1)}, u32[]{:S(2)}, u32[]{:S(2)}) collective-permute-start(bf16[2,128,256]{2,1,0:T(8,128)(2,1)S(1)} %convolution_convert_fusion.1), channel_id=1, source_target_pairs={{0,2},{1,3},{2,0},{3,1},{4,6},{5,7},{6,4},{7,5},{8,10},{9,11},{10,... | collective-permute-start | bytes 393224 | tf_op jit(solution)/shard_map/ppermute | solution.py:194
  148.9 6.0 %collective-permute-done.25 = bf16[2,128,256]{2,1,0:T(8,128)(2,1)S(1)} collective-permute-done((bf16[2,128,256]{2,1,0:T(8,128)(2,1)S(1)}, bf16[2,128,256]{2,1,0:T(8,128)(2,1)S(1)}, u32[]{:S(2)}, u32[]{:S(2)}) %collective-permute-start.25) | collective-permute-done | bytes 131104 | tf_op jit(solution)/shard_map/ppermute | solution.py:194
  163.4 6.0 %fusion.2 = bf16[2,1024,512]{2,1,0:T(8,128)(2,1)S(1)} fusion(f32[2,1024,512]{2,1,0:T(8,128)} %copy-done, f32[1,512,512]{2,1,0:T(8,128)S(1)} %copy-done.4, f32[1,512,512]{2,1,0:T(8,128)S(1)} %get-tuple-element.76), kind=kOutput, calls=%fused_computation.13 | convolution fusion | flops 3221749760 | bytes 8388608 | tf_op jit(solution)/shard_map/obr,osr->obs/dot_general | solution.py:366
  178.6 4.3 %collective-permute-done.35 = f32[128,384]{1,0:T(8,128)S(1)} collective-permute-done((f32[128,384]{1,0:T(8,128)S(1)}, f32[128,384]{1,0:T(8,128)S(1)}, u32[]{:S(2)}, u32[]{:S(2)}) %collective-permute-start.35) | collective-permute-done | bytes 196640 | tf_op jit(solution)/shard_map/ppermute | solution.py:194
  183.2 2.8 %collective-permute-start.36 = (f32[128,384]{1,0:T(8,128)S(1)}, f32[128,384]{1,0:T(8,128)S(1)}, u32[]{:S(2)}, u32[]{:S(2)}) collective-permute-start(f32[128,384]{1,0:T(8,128)S(1)} %fusion.101), channel_id=1, source_target_pairs={{0,2},{1,3},{2,0},{3,1},{4,6},{5,7},{6,4},{7,5},{8,10},{9,11},{10,... | collective-permute-start | bytes 589832 | tf_op jit(solution)/shard_map/ppermute | solution.py:194
  186.0 9.7 %collective-permute-done.36 = f32[128,384]{1,0:T(8,128)S(1)} collective-permute-done((f32[128,384]{1,0:T(8,128)S(1)}, f32[128,384]{1,0:T(8,128)S(1)}, u32[]{:S(2)}, u32[]{:S(2)}) %collective-permute-start.36) | collective-permute-done | bytes 196640 | tf_op jit(solution)/shard_map/ppermute | solution.py:194
  199.5 4.3 %collective-permute-done.38.refs_1_ = f32[128,384]{1,0:T(8,128)S(1)} collective-permute-done((f32[128,384]{1,0:T(8,128)S(1)}, f32[128,384]{1,0:T(8,128)S(1)}, u32[]{:S(2)}, u32[]{:S(2)}) %collective-permute-start.38) | collective-permute-done | bytes 196640 | tf_op jit(solution)/shard_map/ppermute | solution.py:194
  203.8 4.3 %collective-permute-done.39.refs_2_ = f32[128,384]{1,0:T(8,128)S(1)} collective-permute-done((f32[128,384]{1,0:T(8,128)S(1)}, f32[128,384]{1,0:T(8,128)S(1)}, u32[]{:S(2)}, u32[]{:S(2)}) %collective-permute-start.39) | collective-permute-done | bytes 196640 | tf_op jit(solution)/shard_map/ppermute | solution.py:194
  208.2 20.0 %inverse_factor.3 = f32[512,512]{1,0:T(8,128)S(1)} custom-call(s32[1]{0:T(128)} %bitcast.19.pos_ref, f32[128,384]{1,0:T(8,128)S(1)} %add.450.refs_0_, f32[128,384]{1,0:T(8,128)S(1)} %collective-permute-done.38.refs_1_, f32[128,384]{1,0:T(8,128)S(1)} %collective-permute-done.39.refs_2_, f32[128,384]{1,0:T(8,128)S(1)} %collective-permute-done.40.refs_3_), custom_call_target="tpu_custom_call" | custom-call | flops 12884901888 | bytes 2097152 | tf_op jit(solution)/shard_map/inverse_factor/pallas_call | solution.py:171
  229.1 18.7 %reduce-scatter.4.cloned.1.call-done = f32[16,1024]{1,0:T(8,128)} async-done(((f32[64,1024]{1,0:T(8,128)}), f32[16,1024]{1,0:T(8,128)}) %reduce-scatter.4.cloned.1.call-update) | async-done | bytes 65552
  250.6 3.4 %fusion.9 = f32[2,256,512]{2,1,0:T(8,128)} fusion(f32[1,512,512]{2,1,0:T(8,128)S(1)} %get-tuple-element.75, f32[1,512,512]{2,1,0:T(8,128)S(1)} %get-tuple-element.74, f32[2,1024,512]{2,1,0:T(8,128)} %copy-done.2, s32[]{:T(128)S(6)} %select_n.321), kind=kOutput, calls=%fused_computation.19 | convolution fusion | flops 805830656 | bytes 4194308 | tf_op jit(solution)/shard_map/obr,osr->obs/dot_general | solution.py:378
  (255 shorter events, 93.3 us)
Async XLA Ops:
  7.2 55.8 %all-gather.3.cloned.1.call-start = ((), (), s32[]{:S(2)}) async-start(), calls=%async_computation.1 | async-start | bytes 2621440 | tf_op jit(solution)/shard_map/all_gather | solution.py:238
  8.6 14.8 %collective-permute-start = (bf16[2,256,256]{2,1,0:T(8,128)(2,1)S(1)}, bf16[2,256,256]{2,1,0:T(8,128)(2,1)S(1)}, u32[]{:S(2)}, u32[]{:S(2)}) collective-permute-start(bf16[2,256,256]{2,1,0:T(8,128)(2,1)S(1)} %get-tuple-element.110), channel_id=1, source_target_pairs={{0,8},{8,0},{16,24},{24,16},{1,9},{9,1},{17,25},{25,17},{2,10},{10... | collective-permute-start | bytes 786440 | tf_op jit(solution)/shard_map/ppermute | solution.py:194
  11.6 14.8 %collective-permute-start.1 = (bf16[2,256,256]{2,1,0:T(8,128)(2,1)S(1)}, bf16[2,256,256]{2,1,0:T(8,128)(2,1)S(1)}, u32[]{:S(2)}, u32[]{:S(2)}) collective-permute-start(bf16[2,256,256]{2,1,0:T(8,128)(2,1)S(1)} %get-tuple-element.110), channel_id=1, source_target_pairs={{0,16},{8,24},{16,0},{24,8},{1,17},{9,25},{17,1},{25,9},{2,18},{10... | collective-permute-start | bytes 786440 | tf_op jit(solution)/shard_map/ppermute | solution.py:194
  13.1 13.3 %collective-permute-start.2 = (bf16[2,256,256]{2,1,0:T(8,128)(2,1)S(1)}, bf16[2,256,256]{2,1,0:T(8,128)(2,1)S(1)}, u32[]{:S(2)}, u32[]{:S(2)}) collective-permute-start(bf16[2,256,256]{2,1,0:T(8,128)(2,1)S(1)} %get-tuple-element.110), channel_id=1, source_target_pairs={{0,24},{8,16},{16,8},{24,0},{1,25},{9,17},{17,9},{25,1},{2,26},{10... | collective-permute-start | bytes 786440 | tf_op jit(solution)/shard_map/ppermute | solution.py:194
  13.2 21.7 %collective-permute-start.7 = (bf16[2,256,256]{2,1,0:T(8,128)(2,1)S(1)}, bf16[2,256,256]{2,1,0:T(8,128)(2,1)S(1)}, u32[]{:S(2)}, u32[]{:S(2)}) collective-permute-start(bf16[2,256,256]{2,1,0:T(8,128)(2,1)S(1)} %get-tuple-element.111), channel_id=1, source_target_pairs={{0,8},{8,0},{16,24},{24,16},{1,9},{9,1},{17,25},{25,17},{2,10},{10... | collective-permute-start | bytes 786440 | tf_op jit(solution)/shard_map/ppermute | solution.py:194
  15.1 25.8 %collective-permute-start.8 = (bf16[2,256,256]{2,1,0:T(8,128)(2,1)S(1)}, bf16[2,256,256]{2,1,0:T(8,128)(2,1)S(1)}, u32[]{:S(2)}, u32[]{:S(2)}) collective-permute-start(bf16[2,256,256]{2,1,0:T(8,128)(2,1)S(1)} %get-tuple-element.111), channel_id=1, source_target_pairs={{0,16},{8,24},{16,0},{24,8},{1,17},{9,25},{17,1},{25,9},{2,18},{10... | collective-permute-start | bytes 786440 | tf_op jit(solution)/shard_map/ppermute | solution.py:194
  16.7 116.7 %all-gather.5.cloned.1.call-start = ((), (), s32[]{:S(2)}) async-start(), calls=%async_computation.2 | async-start | bytes 2359296 | tf_op jit(solution)/shard_map/all_gather | solution.py:351
  23.4 18.3 %collective-permute-start.9 = (bf16[2,256,256]{2,1,0:T(8,128)(2,1)S(1)}, bf16[2,256,256]{2,1,0:T(8,128)(2,1)S(1)}, u32[]{:S(2)}, u32[]{:S(2)}) collective-permute-start(bf16[2,256,256]{2,1,0:T(8,128)(2,1)S(1)} %get-tuple-element.111), channel_id=1, source_target_pairs={{0,24},{8,16},{16,8},{24,0},{1,25},{9,17},{17,9},{25,1},{2,26},{10... | collective-permute-start | bytes 786440 | tf_op jit(solution)/shard_map/ppermute | solution.py:194
  27.8 20.6 %collective-permute-start.3 = (bf16[2,128,256]{2,1,0:T(8,128)(2,1)S(1)}, bf16[2,128,256]{2,1,0:T(8,128)(2,1)S(1)}, u32[]{:S(2)}, u32[]{:S(2)}) collective-permute-start(bf16[2,128,256]{2,1,0:T(8,128)(2,1)S(1)} %convolution_convert_fusion.3), channel_id=1, source_target_pairs={{0,1},{1,0},{2,3},{3,2},{4,5},{5,4},{6,7},{7,6},{8,9},{9,8},{10,11... | collective-permute-start | bytes 393224 | tf_op jit(solution)/shard_map/ppermute | solution.py:194
  29.4 19.1 %collective-permute-start.4 = (bf16[2,128,256]{2,1,0:T(8,128)(2,1)S(1)}, bf16[2,128,256]{2,1,0:T(8,128)(2,1)S(1)}, u32[]{:S(2)}, u32[]{:S(2)}) collective-permute-start(bf16[2,128,256]{2,1,0:T(8,128)(2,1)S(1)} %convolution_convert_fusion.3), channel_id=1, source_target_pairs={{0,2},{1,3},{2,0},{3,1},{4,6},{5,7},{6,4},{7,5},{8,10},{9,11},{10,... | collective-permute-start | bytes 393224 | tf_op jit(solution)/shard_map/ppermute | solution.py:194
  34.9 13.7 %collective-permute-start.5 = (bf16[2,128,256]{2,1,0:T(8,128)(2,1)S(1)}, bf16[2,128,256]{2,1,0:T(8,128)(2,1)S(1)}, u32[]{:S(2)}, u32[]{:S(2)}) collective-permute-start(bf16[2,128,256]{2,1,0:T(8,128)(2,1)S(1)} %convolution_convert_fusion.3), channel_id=1, source_target_pairs={{0,3},{1,2},{2,1},{3,0},{4,7},{5,6},{6,5},{7,4},{8,11},{9,10},{10,... | collective-permute-start | bytes 393224 | tf_op jit(solution)/shard_map/ppermute | solution.py:194
  44.7 12.0 %collective-permute-start.11 = (bf16[2,128,256]{2,1,0:T(8,128)(2,1)S(1)}, bf16[2,128,256]{2,1,0:T(8,128)(2,1)S(1)}, u32[]{:S(2)}, u32[]{:S(2)}) collective-permute-start(bf16[2,128,256]{2,1,0:T(8,128)(2,1)S(1)} %convolution_convert_fusion.2), channel_id=1, source_target_pairs={{0,2},{1,3},{2,0},{3,1},{4,6},{5,7},{6,4},{7,5},{8,10},{9,11},{10,... | collective-permute-start | bytes 393224 | tf_op jit(solution)/shard_map/ppermute | solution.py:194
  61.0 14.2 %collective-permute-start.15 = (bf16[2,128,512]{2,1,0:T(8,128)(2,1)}, bf16[2,128,512]{2,1,0:T(8,128)(2,1)}, u32[]{:S(2)}, u32[]{:S(2)}) collective-permute-start(bf16[2,128,512]{2,1,0:T(8,128)(2,1)} %pad_maximum_fusion.5), channel_id=1, source_target_pairs={{0,16},{8,24},{16,0},{24,8},{1,17},{9,25},{17,1},{25,9},{2,18},{10... | collective-permute-start | bytes 786440 | tf_op jit(solution)/shard_map/ppermute | solution.py:194
  61.5 13.6 %collective-permute-start.16 = (bf16[2,128,512]{2,1,0:T(8,128)(2,1)}, bf16[2,128,512]{2,1,0:T(8,128)(2,1)}, u32[]{:S(2)}, u32[]{:S(2)}) collective-permute-start(bf16[2,128,512]{2,1,0:T(8,128)(2,1)} %pad_maximum_fusion.5), channel_id=1, source_target_pairs={{0,24},{8,16},{16,8},{24,0},{1,25},{9,17},{17,9},{25,1},{2,26},{10... | collective-permute-start | bytes 786440 | tf_op jit(solution)/shard_map/ppermute | solution.py:194
  89.5 11.5 %collective-permute-start.19 = (f32[128,384]{1,0:T(8,128)S(1)}, f32[128,384]{1,0:T(8,128)S(1)}, u32[]{:S(2)}, u32[]{:S(2)}) collective-permute-start(f32[128,384]{1,0:T(8,128)S(1)} %fusion.102), channel_id=1, source_target_pairs={{0,2},{1,3},{2,0},{3,1},{4,6},{5,7},{6,4},{7,5},{8,10},{9,11},{10,... | collective-permute-start | bytes 589832 | tf_op jit(solution)/shard_map/ppermute | solution.py:194
  101.9 145.9 %reduce-scatter.4.cloned.1.call-start = ((), (), s32[]{:S(2)}) async-start(), calls=%async_computation.3 | async-start | bytes 327680
  102.6 9.7 %collective-permute-start.21 = (f32[128,384]{1,0:T(8,128)S(1)}, f32[128,384]{1,0:T(8,128)S(1)}, u32[]{:S(2)}, u32[]{:S(2)}) collective-permute-start(f32[128,384]{1,0:T(8,128)S(1)} %add.414.refs_0_), channel_id=1, source_target_pairs={{0,16},{8,24},{16,0},{24,8},{1,17},{9,25},{17,1},{25,9},{2,18},{10... | collective-permute-start | bytes 589832 | tf_op jit(solution)/shard_map/ppermute | solution.py:194
  141.9 13.0 %collective-permute-start.25 = (bf16[2,128,256]{2,1,0:T(8,128)(2,1)S(1)}, bf16[2,128,256]{2,1,0:T(8,128)(2,1)S(1)}, u32[]{:S(2)}, u32[]{:S(2)}) collective-permute-start(bf16[2,128,256]{2,1,0:T(8,128)(2,1)S(1)} %convolution_convert_fusion.1), channel_id=1, source_target_pairs={{0,2},{1,3},{2,0},{3,1},{4,6},{5,7},{6,4},{7,5},{8,10},{9,11},{10,... | collective-permute-start | bytes 393224 | tf_op jit(solution)/shard_map/ppermute | solution.py:194
  144.9 10.0 %collective-permute-start.26 = (bf16[2,128,256]{2,1,0:T(8,128)(2,1)S(1)}, bf16[2,128,256]{2,1,0:T(8,128)(2,1)S(1)}, u32[]{:S(2)}, u32[]{:S(2)}) collective-permute-start(bf16[2,128,256]{2,1,0:T(8,128)(2,1)S(1)} %convolution_convert_fusion.1), channel_id=1, source_target_pairs={{0,3},{1,2},{2,1},{3,0},{4,7},{5,6},{6,5},{7,4},{8,11},{9,10},{10,... | collective-permute-start | bytes 393224 | tf_op jit(solution)/shard_map/ppermute | solution.py:194
  183.1 12.6 %collective-permute-start.37 = (f32[64,1024]{0,1:T(8,128)S(1)}, f32[64,1024]{0,1:T(8,128)S(1)}, u32[]{:S(2)}, u32[]{:S(2)}) collective-permute-start(f32[64,1024]{0,1:T(8,128)S(1)} %constant_dynamic-slice_fusion), channel_id=1, source_target_pairs={{0,4},{4,0},{1,5},{5,1},{2,6},{6,2},{3,7},{7,3},{8,12},{12,8},{9,1... | collective-permute-start | bytes 786440 | tf_op jit(solution)/shard_map/ppermute | solution.py:194
  183.2 12.5 %collective-permute-start.36 = (f32[128,384]{1,0:T(8,128)S(1)}, f32[128,384]{1,0:T(8,128)S(1)}, u32[]{:S(2)}, u32[]{:S(2)}) collective-permute-start(f32[128,384]{1,0:T(8,128)S(1)} %fusion.101), channel_id=1, source_target_pairs={{0,2},{1,3},{2,0},{3,1},{4,6},{5,7},{6,4},{7,5},{8,10},{9,11},{10,... | collective-permute-start | bytes 589832 | tf_op jit(solution)/shard_map/ppermute | solution.py:194
  197.7 10.5 %collective-permute-start.39 = (f32[128,384]{1,0:T(8,128)S(1)}, f32[128,384]{1,0:T(8,128)S(1)}, u32[]{:S(2)}, u32[]{:S(2)}) collective-permute-start(f32[128,384]{1,0:T(8,128)S(1)} %add.450.refs_0_), channel_id=1, source_target_pairs={{0,16},{8,24},{16,0},{24,8},{1,17},{9,25},{17,1},{25,9},{2,18},{10... | collective-permute-start | bytes 589832 | tf_op jit(solution)/shard_map/ppermute | solution.py:194
  198.3 9.9 %collective-permute-start.40 = (f32[128,384]{1,0:T(8,128)S(1)}, f32[128,384]{1,0:T(8,128)S(1)}, u32[]{:S(2)}, u32[]{:S(2)}) collective-permute-start(f32[128,384]{1,0:T(8,128)S(1)} %add.450.refs_0_), channel_id=1, source_target_pairs={{0,24},{8,16},{16,8},{24,0},{1,25},{9,17},{17,9},{25,1},{2,26},{10... | collective-permute-start | bytes 589832 | tf_op jit(solution)/shard_map/ppermute | solution.py:194
  228.1 19.7 %collective-permute-start.41 = (f32[512,512]{1,0:T(8,128)S(1)}, f32[512,512]{1,0:T(8,128)S(1)}, u32[]{:S(2)}, u32[]{:S(2)}) collective-permute-start(f32[512,512]{1,0:T(8,128)S(1)} %inverse_factor.3), channel_id=1, source_target_pairs={{0,4},{4,0},{1,5},{5,1},{2,6},{6,2},{3,7},{7,3},{8,12},{12,8},{9,1... | collective-permute-start | bytes 3145736 | tf_op jit(solution)/shard_map/ppermute | solution.py:194
  (73 other events, 822.0 us)
Sparse Core Ops, SparseCore 0:
  16.8 44.5 all-gather.2
  102.0 27.9 all-gather.4
  229.2 18.5 reduce-scatter.3

commit v7 on v4

--- a/solution.py
+++ b/solution.py
@@ -313,13 +313,12 @@
             )
         step = 1
         while step < gc_count:
-            if last and 2 * step == gc_count:
+            if 2 * step == gc_count:
                 total, beside = lax.optimization_barrier((total, beside))
+                if not last:
+                    beside = mix_seen(beside)
             total += swap(total, "gc", step)
             step *= 2
-        if not last:
-            total, beside = lax.optimization_barrier((total, beside))
-            beside = mix_seen(beside)
         if packed:
             pieces = collect(total, "tok")
         else:

time: 241 us -> 233 us (0.967)
  waiting for transfers between devices: 92 us -> 83.8 us
  starting transfers between devices: 41.2 us -> 47.4 us
  matrix products: 27.9 us -> 23.9 us
    all_gather x1, waiting for transfers between devices: 14.5 us -> 2.09 us  [mix_seen(): seen = lax.all_gather(seen, ('gr', 'gc'), axis=0, tiled=True)]
    ppermute x34, starting transfers between devices: 41.1 us -> 47.3 us  [swap(): lax.ppermute(value, axis, [(i, i ^ k) for i in range(lax.axis_size(axis))])]
    unnamed x4, waiting for transfers between devices: 3.1 us -> 6.49 us
  transfers between devices with their start and end apart: 37 -> 37, of which waited for: 24 -> 24; matrix products, arithmetic and copies ran while one was open for 14% -> 12% of each run, Pallas kernels for 16% -> 17%
where the time goes in v7:
time: 233 us
  waiting for transfers between devices  83.8 us (36%)
  starting transfers between devices  47.4 us (20%)
  Pallas kernels  38.8 us (17%)
  matrix products  23.9 us (10%)
  between operations  15.9 us (7%)
  local copies, waits for them, and re-layouts  14.6 us (6%)
  other arithmetic  8.53 us (4%)
    ppermute x34, waiting for transfers between devices, swap(): lax.ppermute(value, axis, [(i, i ^ k) for i in range(lax.axis_size(axis))])  75.3 us
    ppermute x34, starting transfers between devices, swap(): lax.ppermute(value, axis, [(i, i ^ k) for i in range(lax.axis_size(axis))])  47.3 us
    pallas_call x2, Pallas kernels, inverse_factor(): pl.pallas_call(functools.partial(factor_kernel, scale, exact), out_shape=...  38.8 us
    unnamed x4, waiting for transfers between devices  6.49 us
    dot_general x2, matrix products, image_of(): jnp.einsum('tob,otr->obr', full_x, full, preferred_element_type=jnp.float32)  4.71 us
  transfers between devices with their start and end apart: 37, of which 24 were waited for; matrix products, arithmetic and copies ran while one was open for 12% of the time, Pallas kernels for 17%

profile of v7, /device:TPU:0, one launch (start us, length us, event | category | flops | bytes accessed | tf_op | source)
XLA Modules:
  0.0 232.9 jit_solution(6432925308745647191)
XLA Ops:
  8.6 3.0 %collective-permute-start = (bf16[2,256,256]{2,1,0:T(8,128)(2,1)S(1)}, bf16[2,256,256]{2,1,0:T(8,128)(2,1)S(1)}, u32[]{:S(2)}, u32[]{:S(2)}) collective-permute-start(bf16[2,256,256]{2,1,0:T(8,128)(2,1)S(1)} %get-tuple-element.90), channel_id=1, source_target_pairs={{0,8},{8,0},{16,24},{24,16},{1,9},{9,1},{17,25},{25,17},{2,10},{10... | collective-permute-start | bytes 786440 | tf_op jit(solution)/shard_map/ppermute | solution.py:194
  22.3 4.1 %collective-permute-done.1 = bf16[2,256,256]{2,1,0:T(8,128)(2,1)S(1)} collective-permute-done((bf16[2,256,256]{2,1,0:T(8,128)(2,1)S(1)}, bf16[2,256,256]{2,1,0:T(8,128)(2,1)S(1)}, u32[]{:S(2)}, u32[]{:S(2)}) %collective-permute-start.1) | collective-permute-done | bytes 262176 | tf_op jit(solution)/shard_map/ppermute | solution.py:194
  31.0 3.9 %collective-permute-done.7 = bf16[2,256,256]{2,1,0:T(8,128)(2,1)S(1)} collective-permute-done((bf16[2,256,256]{2,1,0:T(8,128)(2,1)S(1)}, bf16[2,256,256]{2,1,0:T(8,128)(2,1)S(1)}, u32[]{:S(2)}, u32[]{:S(2)}) %collective-permute-start.7) | collective-permute-done | bytes 262176 | tf_op jit(solution)/shard_map/ppermute | solution.py:194
  34.9 3.7 %collective-permute-start.5 = (bf16[2,128,256]{2,1,0:T(8,128)(2,1)S(1)}, bf16[2,128,256]{2,1,0:T(8,128)(2,1)S(1)}, u32[]{:S(2)}, u32[]{:S(2)}) collective-permute-start(bf16[2,128,256]{2,1,0:T(8,128)(2,1)S(1)} %convolution_convert_fusion.1), channel_id=1, source_target_pairs={{0,3},{1,2},{2,1},{3,0},{4,7},{5,6},{6,5},{7,4},{8,11},{9,10},{10,... | collective-permute-start | bytes 393224 | tf_op jit(solution)/shard_map/ppermute | solution.py:194
  48.7 7.0 %collective-permute-done.11 = bf16[2,128,256]{2,1,0:T(8,128)(2,1)S(1)} collective-permute-done((bf16[2,128,256]{2,1,0:T(8,128)(2,1)S(1)}, bf16[2,128,256]{2,1,0:T(8,128)(2,1)S(1)}, u32[]{:S(2)}, u32[]{:S(2)}) %collective-permute-start.11) | collective-permute-done | bytes 131104 | tf_op jit(solution)/shard_map/ppermute | solution.py:194
  67.9 6.2 %collective-permute-done.15 = bf16[2,128,512]{2,1,0:T(8,128)(2,1)} collective-permute-done((bf16[2,128,512]{2,1,0:T(8,128)(2,1)}, bf16[2,128,512]{2,1,0:T(8,128)(2,1)}, u32[]{:S(2)}, u32[]{:S(2)}) %collective-permute-start.15) | collective-permute-done | bytes 262176 | tf_op jit(solution)/shard_map/ppermute | solution.py:194
  74.1 3.5 %multiply_add_fusion.1 = f32[2,1024,512]{2,1,0:T(8,128)S(1)} fusion(bf16[2,256,256]{2,1,0:T(8,128)(2,1)} %get-tuple-element.83, bf16[2,256,256]{2,1,0:T(8,128)(2,1)} %get-tuple-element.84, bf16[2,256,256]{2,1,0:T(8,128)(2,1)} %get-tuple-element.85, bf16[2,256,256]{2,1,0:T(8,128)(2,1)} %get-tuple-element.82, bf16[2,256,256]{2,1,0:T(8,128)(2,1)S(1)} %copy-done.6, ...), kind=kOutput, calls=%fused_computation.7 | convolution fusion | flops 1098907648 | bytes 9437184 | tf_op jit(solution)/shard_map/tob,otr->obr/dot_general | solution.py:284
  83.9 4.3 %collective-permute-done.18 = f32[128,384]{1,0:T(8,128)S(1)} collective-permute-done((f32[128,384]{1,0:T(8,128)S(1)}, f32[128,384]{1,0:T(8,128)S(1)}, u32[]{:S(2)}, u32[]{:S(2)}) %collective-permute-start.18) | collective-permute-done | bytes 196640 | tf_op jit(solution)/shard_map/ppermute | solution.py:194
  89.3 2.8 %collective-permute-start.19 = (f32[128,384]{1,0:T(8,128)S(1)}, f32[128,384]{1,0:T(8,128)S(1)}, u32[]{:S(2)}, u32[]{:S(2)}) collective-permute-start(f32[128,384]{1,0:T(8,128)S(1)} %fusion.92), channel_id=1, source_target_pairs={{0,2},{1,3},{2,0},{3,1},{4,6},{5,7},{6,4},{7,5},{8,10},{9,11},{10,... | collective-permute-start | bytes 589832 | tf_op jit(solution)/shard_map/ppermute | solution.py:194
  92.1 13.1 %collective-permute-done.19 = f32[128,384]{1,0:T(8,128)S(1)} collective-permute-done((f32[128,384]{1,0:T(8,128)S(1)}, f32[128,384]{1,0:T(8,128)S(1)}, u32[]{:S(2)}, u32[]{:S(2)}) %collective-permute-start.19) | collective-permute-done | bytes 196640 | tf_op jit(solution)/shard_map/ppermute | solution.py:194
  105.4 3.4 %collective-permute-start.22 = (f32[128,384]{1,0:T(8,128)S(1)}, f32[128,384]{1,0:T(8,128)S(1)}, u32[]{:S(2)}, u32[]{:S(2)}) collective-permute-start(f32[128,384]{1,0:T(8,128)S(1)} %add.353.refs_0_), channel_id=1, source_target_pairs={{0,24},{8,16},{16,8},{24,0},{1,25},{9,17},{17,9},{25,1},{2,26},{10... | collective-permute-start | bytes 589832 | tf_op jit(solution)/shard_map/ppermute | solution.py:194
  113.1 18.8 %inverse_factor.2 = f32[512,512]{1,0:T(8,128)S(1)} custom-call(s32[1]{0:T(128)} %bitcast.1.pos_ref, f32[128,384]{1,0:T(8,128)S(1)} %add.353.refs_0_, f32[128,384]{1,0:T(8,128)S(1)} %collective-permute-done.20.refs_1_, f32[128,384]{1,0:T(8,128)S(1)} %collective-permute-done.21.refs_2_, f32[128,384]{1,0:T(8,128)S(1)} %collective-permute-done.22.refs_3_), custom_call_target="tpu_custom_call" | custom-call | flops 12884901888 | bytes 2097152 | tf_op jit(solution)/shard_map/inverse_factor/pallas_call | solution.py:171
  136.5 2.8 %slice_bitcast_fusion.15 = (f32[128,512]{1,0:T(8,128)S(1)}, f32[128,512]{1,0:T(8,128)S(1)}, f32[128,512]{1,0:T(8,128)S(1)}, f32[128,512]{1,0:T(8,128)S(1)}, f32[...) fusion(f32[16,128,512]{2,1,0:T(8,128)} %all-gather.5.cloned.1.c, ...), kind=kLoop, calls=%fused_computation.96 | loop fusion | bytes 8388608 | tf_op jit(solution)/shard_map/mul | solution.py:341
  145.0 4.0 %fusion.12 = bf16[2,1024,512]{2,1,0:T(8,128)(2,1)S(1)} fusion(f32[2,1024,512]{2,1,0:T(8,128)S(1)} %copy-done.1, f32[1,512,512]{2,1,0:T(8,128)S(1)} %get-tuple-element.73, f32[1,512,512]{2,1,0:T(8,128)S(1)} %get-tuple-element.72), kind=kOutput, calls=%fused_computation.18 | convolution fusion | flops 3221749760 | bytes 8388608 | tf_op jit(solution)/shard_map/obr,osr->obs/dot_general | solution.py:346
  150.6 5.3 %collective-permute-done.25 = bf16[2,128,512]{2,1,0:T(8,128)(2,1)S(1)} collective-permute-done((bf16[2,128,512]{2,1,0:T(8,128)(2,1)S(1)}, bf16[2,128,512]{2,1,0:T(8,128)(2,1)S(1)}, u32[]{:S(2)}, u32[]{:S(2)}) %collective-permute-start.25) | collective-permute-done | bytes 262176 | tf_op jit(solution)/shard_map/ppermute | solution.py:194
  157.2 2.8 %multiply_reduce_fusion.2 = (f32[128,512]{1,0:T(8,128)S(1)}, f32[128,512]{1,0:T(8,128)S(1)}) fusion(f32[2]{0:T(128)S(1)} %copy-done.20, f32[2]{0:T(128)S(1)} %copy-done.21, f32[2,1024,512]{2,1,0:T(8,128)S(1)} %multiply_add_fusion, s32[]{:T(128)S(6)} %select_n.301), kind=kOutput, calls=%fused_computation.74 | convolution fusion | flops 1611005952 | bytes 5768196 | tf_op jit(solution)/shard_map/obr,obs->ors/dot_general | solution.py:296
  161.7 3.8 %collective-permute-start.28 = (f32[128,384]{1,0:T(8,128)S(1)}, f32[128,384]{1,0:T(8,128)S(1)}, u32[]{:S(2)}, u32[]{:S(2)}) collective-permute-start(f32[128,384]{1,0:T(8,128)S(1)} %pad_maximum_fusion.10), channel_id=1, source_target_pairs={{0,1},{1,0},{2,3},{3,2},{4,5},{5,4},{6,7},{7,6},{8,9},{9,8},{10,11... | collective-permute-start | bytes 589832 | tf_op jit(solution)/shard_map/ppermute | solution.py:194
  166.5 4.2 %collective-permute-done.28 = f32[128,384]{1,0:T(8,128)S(1)} collective-permute-done((f32[128,384]{1,0:T(8,128)S(1)}, f32[128,384]{1,0:T(8,128)S(1)}, u32[]{:S(2)}, u32[]{:S(2)}) %collective-permute-start.28) | collective-permute-done | bytes 196640 | tf_op jit(solution)/shard_map/ppermute | solution.py:194
  170.8 3.5 %collective-permute-start.29 = (f32[128,384]{1,0:T(8,128)S(1)}, f32[128,384]{1,0:T(8,128)S(1)}, u32[]{:S(2)}, u32[]{:S(2)}) collective-permute-start(f32[128,384]{1,0:T(8,128)S(1)} %fusion.91), channel_id=1, source_target_pairs={{0,2},{1,3},{2,0},{3,1},{4,6},{5,7},{6,4},{7,5},{8,10},{9,11},{10,... | collective-permute-start | bytes 589832 | tf_op jit(solution)/shard_map/ppermute | solution.py:194
  174.3 8.9 %collective-permute-done.29 = f32[128,384]{1,0:T(8,128)S(1)} collective-permute-done((f32[128,384]{1,0:T(8,128)S(1)}, f32[128,384]{1,0:T(8,128)S(1)}, u32[]{:S(2)}, u32[]{:S(2)}) %collective-permute-start.29) | collective-permute-done | bytes 196640 | tf_op jit(solution)/shard_map/ppermute | solution.py:194
  187.8 3.3 %collective-permute-done.30.refs_1_ = f32[128,384]{1,0:T(8,128)S(1)} collective-permute-done((f32[128,384]{1,0:T(8,128)S(1)}, f32[128,384]{1,0:T(8,128)S(1)}, u32[]{:S(2)}, u32[]{:S(2)}) %collective-permute-start.30) | collective-permute-done | bytes 196640 | tf_op jit(solution)/shard_map/ppermute | solution.py:194
  193.7 20.0 %inverse_factor.3 = f32[512,512]{1,0:T(8,128)S(1)} custom-call(s32[1]{0:T(128)} %bitcast.1.pos_ref, f32[128,384]{1,0:T(8,128)S(1)} %add.373.refs_0_, f32[128,384]{1,0:T(8,128)S(1)} %collective-permute-done.30.refs_1_, f32[128,384]{1,0:T(8,128)S(1)} %collective-permute-done.31.refs_2_, f32[128,384]{1,0:T(8,128)S(1)} %collective-permute-done.32.refs_3_), custom_call_target="tpu_custom_call" | custom-call | flops 12884901888 | bytes 2097152 | tf_op jit(solution)/shard_map/inverse_factor/pallas_call | solution.py:171
  213.8 6.4 %reduce-scatter.4.cloned.1.call-done = f32[16,1024]{1,0:T(8,128)} async-done(((f32[128,1024]{1,0:T(8,128)}), f32[16,1024]{1,0:T(8,128)}) %reduce-scatter.4.cloned.1.call-update) | async-done | bytes 65552
  223.0 3.4 %fusion.8 = f32[2,256,512]{2,1,0:T(8,128)} fusion(f32[1,512,512]{2,1,0:T(8,128)S(1)} %get-tuple-element.71, f32[1,512,512]{2,1,0:T(8,128)S(1)} %get-tuple-element.70, f32[2,1024,512]{2,1,0:T(8,128)} %copy-done.2, s32[]{:T(128)S(6)} %select_n.307), kind=kOutput, calls=%fused_computation.14 | convolution fusion | flops 805830656 | bytes 4194308 | tf_op jit(solution)/shard_map/obr,osr->obs/dot_general | solution.py:358
  (173 shorter events, 74.9 us)
Async XLA Ops:
  7.2 54.8 %all-gather.3.cloned.1.call-start = ((), (), s32[]{:S(2)}) async-start(), calls=%async_computation.1 | async-start | bytes 2621440 | tf_op jit(solution)/shard_map/all_gather | solution.py:238
  8.6 13.4 %collective-permute-start = (bf16[2,256,256]{2,1,0:T(8,128)(2,1)S(1)}, bf16[2,256,256]{2,1,0:T(8,128)(2,1)S(1)}, u32[]{:S(2)}, u32[]{:S(2)}) collective-permute-start(bf16[2,256,256]{2,1,0:T(8,128)(2,1)S(1)} %get-tuple-element.90), channel_id=1, source_target_pairs={{0,8},{8,0},{16,24},{24,16},{1,9},{9,1},{17,25},{25,17},{2,10},{10... | collective-permute-start | bytes 786440 | tf_op jit(solution)/shard_map/ppermute | solution.py:194
  11.6 14.8 %collective-permute-start.1 = (bf16[2,256,256]{2,1,0:T(8,128)(2,1)S(1)}, bf16[2,256,256]{2,1,0:T(8,128)(2,1)S(1)}, u32[]{:S(2)}, u32[]{:S(2)}) collective-permute-start(bf16[2,256,256]{2,1,0:T(8,128)(2,1)S(1)} %get-tuple-element.90), channel_id=1, source_target_pairs={{0,16},{8,24},{16,0},{24,8},{1,17},{9,25},{17,1},{25,9},{2,18},{10... | collective-permute-start | bytes 786440 | tf_op jit(solution)/shard_map/ppermute | solution.py:194
  13.1 13.3 %collective-permute-start.2 = (bf16[2,256,256]{2,1,0:T(8,128)(2,1)S(1)}, bf16[2,256,256]{2,1,0:T(8,128)(2,1)S(1)}, u32[]{:S(2)}, u32[]{:S(2)}) collective-permute-start(bf16[2,256,256]{2,1,0:T(8,128)(2,1)S(1)} %get-tuple-element.90), channel_id=1, source_target_pairs={{0,24},{8,16},{16,8},{24,0},{1,25},{9,17},{17,9},{25,1},{2,26},{10... | collective-permute-start | bytes 786440 | tf_op jit(solution)/shard_map/ppermute | solution.py:194
  13.2 21.7 %collective-permute-start.7 = (bf16[2,256,256]{2,1,0:T(8,128)(2,1)S(1)}, bf16[2,256,256]{2,1,0:T(8,128)(2,1)S(1)}, u32[]{:S(2)}, u32[]{:S(2)}) collective-permute-start(bf16[2,256,256]{2,1,0:T(8,128)(2,1)S(1)} %get-tuple-element.91), channel_id=1, source_target_pairs={{0,8},{8,0},{16,24},{24,16},{1,9},{9,1},{17,25},{25,17},{2,10},{10... | collective-permute-start | bytes 786440 | tf_op jit(solution)/shard_map/ppermute | solution.py:194
  15.1 25.8 %collective-permute-start.8 = (bf16[2,256,256]{2,1,0:T(8,128)(2,1)S(1)}, bf16[2,256,256]{2,1,0:T(8,128)(2,1)S(1)}, u32[]{:S(2)}, u32[]{:S(2)}) collective-permute-start(bf16[2,256,256]{2,1,0:T(8,128)(2,1)S(1)} %get-tuple-element.91), channel_id=1, source_target_pairs={{0,16},{8,24},{16,0},{24,8},{1,17},{9,25},{17,1},{25,9},{2,18},{10... | collective-permute-start | bytes 786440 | tf_op jit(solution)/shard_map/ppermute | solution.py:194
  16.7 119.8 %all-gather.5.cloned.1.call-start = ((), (), s32[]{:S(2)}) async-start(), calls=%async_computation.2 | async-start | bytes 4718592 | tf_op jit(solution)/shard_map/all_gather | solution.py:338
  22.0 19.7 %collective-permute-start.9 = (bf16[2,256,256]{2,1,0:T(8,128)(2,1)S(1)}, bf16[2,256,256]{2,1,0:T(8,128)(2,1)S(1)}, u32[]{:S(2)}, u32[]{:S(2)}) collective-permute-start(bf16[2,256,256]{2,1,0:T(8,128)(2,1)S(1)} %get-tuple-element.91), channel_id=1, source_target_pairs={{0,24},{8,16},{16,8},{24,0},{1,25},{9,17},{17,9},{25,1},{2,26},{10... | collective-permute-start | bytes 786440 | tf_op jit(solution)/shard_map/ppermute | solution.py:194
  26.8 20.8 %collective-permute-start.3 = (bf16[2,128,256]{2,1,0:T(8,128)(2,1)S(1)}, bf16[2,128,256]{2,1,0:T(8,128)(2,1)S(1)}, u32[]{:S(2)}, u32[]{:S(2)}) collective-permute-start(bf16[2,128,256]{2,1,0:T(8,128)(2,1)S(1)} %convolution_convert_fusion.1), channel_id=1, source_target_pairs={{0,1},{1,0},{2,3},{3,2},{4,5},{5,4},{6,7},{7,6},{8,9},{9,8},{10,11... | collective-permute-start | bytes 393224 | tf_op jit(solution)/shard_map/ppermute | solution.py:194
  28.4 19.4 %collective-permute-start.4 = (bf16[2,128,256]{2,1,0:T(8,128)(2,1)S(1)}, bf16[2,128,256]{2,1,0:T(8,128)(2,1)S(1)}, u32[]{:S(2)}, u32[]{:S(2)}) collective-permute-start(bf16[2,128,256]{2,1,0:T(8,128)(2,1)S(1)} %convolution_convert_fusion.1), channel_id=1, source_target_pairs={{0,2},{1,3},{2,0},{3,1},{4,6},{5,7},{6,4},{7,5},{8,10},{9,11},{10,... | collective-permute-start | bytes 393224 | tf_op jit(solution)/shard_map/ppermute | solution.py:194
  34.9 13.0 %collective-permute-start.5 = (bf16[2,128,256]{2,1,0:T(8,128)(2,1)S(1)}, bf16[2,128,256]{2,1,0:T(8,128)(2,1)S(1)}, u32[]{:S(2)}, u32[]{:S(2)}) collective-permute-start(bf16[2,128,256]{2,1,0:T(8,128)(2,1)S(1)} %convolution_convert_fusion.1), channel_id=1, source_target_pairs={{0,3},{1,2},{2,1},{3,0},{4,7},{5,6},{6,5},{7,4},{8,11},{9,10},{10,... | collective-permute-start | bytes 393224 | tf_op jit(solution)/shard_map/ppermute | solution.py:194
  43.7 11.9 %collective-permute-start.11 = (bf16[2,128,256]{2,1,0:T(8,128)(2,1)S(1)}, bf16[2,128,256]{2,1,0:T(8,128)(2,1)S(1)}, u32[]{:S(2)}, u32[]{:S(2)}) collective-permute-start(bf16[2,128,256]{2,1,0:T(8,128)(2,1)S(1)} %convolution_convert_fusion), channel_id=1, source_target_pairs={{0,2},{1,3},{2,0},{3,1},{4,6},{5,7},{6,4},{7,5},{8,10},{9,11},{10,... | collective-permute-start | bytes 393224 | tf_op jit(solution)/shard_map/ppermute | solution.py:194
  48.2 9.0 %collective-permute-start.6 = (f32[2,128,256]{2,1,0:T(8,128)S(1)}, f32[2,128,256]{2,1,0:T(8,128)S(1)}, u32[]{:S(2)}, u32[]{:S(2)}) collective-permute-start(f32[2,128,256]{2,1,0:T(8,128)S(1)} %multiply_add_fusion.4), channel_id=1, source_target_pairs={{0,4},{4,0},{1,5},{5,1},{2,6},{6,2},{3,7},{7,3},{8,12},{12,8},{9,1... | collective-permute-start | bytes 786440 | tf_op jit(solution)/shard_map/ppermute | solution.py:194
  58.5 9.4 %collective-permute-start.14 = (bf16[2,128,512]{2,1,0:T(8,128)(2,1)}, bf16[2,128,512]{2,1,0:T(8,128)(2,1)}, u32[]{:S(2)}, u32[]{:S(2)}) collective-permute-start(bf16[2,128,512]{2,1,0:T(8,128)(2,1)} %pad_maximum_fusion.8), channel_id=1, source_target_pairs={{0,8},{8,0},{16,24},{24,16},{1,9},{9,1},{17,25},{25,17},{2,10},{10... | collective-permute-start | bytes 786440 | tf_op jit(solution)/shard_map/ppermute | solution.py:194
  60.0 14.2 %collective-permute-start.15 = (bf16[2,128,512]{2,1,0:T(8,128)(2,1)}, bf16[2,128,512]{2,1,0:T(8,128)(2,1)}, u32[]{:S(2)}, u32[]{:S(2)}) collective-permute-start(bf16[2,128,512]{2,1,0:T(8,128)(2,1)} %pad_maximum_fusion.8), channel_id=1, source_target_pairs={{0,16},{8,24},{16,0},{24,8},{1,17},{9,25},{17,1},{25,9},{2,18},{10... | collective-permute-start | bytes 786440 | tf_op jit(solution)/shard_map/ppermute | solution.py:194
  60.6 13.6 %collective-permute-start.16 = (bf16[2,128,512]{2,1,0:T(8,128)(2,1)}, bf16[2,128,512]{2,1,0:T(8,128)(2,1)}, u32[]{:S(2)}, u32[]{:S(2)}) collective-permute-start(bf16[2,128,512]{2,1,0:T(8,128)(2,1)} %pad_maximum_fusion.8), channel_id=1, source_target_pairs={{0,24},{8,16},{16,8},{24,0},{1,25},{9,17},{17,9},{25,1},{2,26},{10... | collective-permute-start | bytes 786440 | tf_op jit(solution)/shard_map/ppermute | solution.py:194
  89.2 131.0 %reduce-scatter.4.cloned.1.call-start = ((), (), s32[]{:S(2)}) async-start(), calls=%async_computation.3 | async-start | bytes 589824
  89.3 15.9 %collective-permute-start.19 = (f32[128,384]{1,0:T(8,128)S(1)}, f32[128,384]{1,0:T(8,128)S(1)}, u32[]{:S(2)}, u32[]{:S(2)}) collective-permute-start(f32[128,384]{1,0:T(8,128)S(1)} %fusion.92), channel_id=1, source_target_pairs={{0,2},{1,3},{2,0},{3,1},{4,6},{5,7},{6,4},{7,5},{8,10},{9,11},{10,... | collective-permute-start | bytes 589832 | tf_op jit(solution)/shard_map/ppermute | solution.py:194
  141.4 9.2 %collective-permute-start.24 = (bf16[2,128,512]{2,1,0:T(8,128)(2,1)S(1)}, bf16[2,128,512]{2,1,0:T(8,128)(2,1)S(1)}, u32[]{:S(2)}, u32[]{:S(2)}) collective-permute-start(bf16[2,128,512]{2,1,0:T(8,128)(2,1)S(1)} %fusion.17), channel_id=1, source_target_pairs={{0,8},{8,0},{16,24},{24,16},{1,9},{9,1},{17,25},{25,17},{2,10},{10... | collective-permute-start | bytes 786440 | tf_op jit(solution)/shard_map/ppermute | solution.py:194
  142.1 13.8 %collective-permute-start.25 = (bf16[2,128,512]{2,1,0:T(8,128)(2,1)S(1)}, bf16[2,128,512]{2,1,0:T(8,128)(2,1)S(1)}, u32[]{:S(2)}, u32[]{:S(2)}) collective-permute-start(bf16[2,128,512]{2,1,0:T(8,128)(2,1)S(1)} %fusion.17), channel_id=1, source_target_pairs={{0,16},{8,24},{16,0},{24,8},{1,17},{9,25},{17,1},{25,9},{2,18},{10... | collective-permute-start | bytes 786440 | tf_op jit(solution)/shard_map/ppermute | solution.py:194
  143.6 12.3 %collective-permute-start.26 = (bf16[2,128,512]{2,1,0:T(8,128)(2,1)S(1)}, bf16[2,128,512]{2,1,0:T(8,128)(2,1)S(1)}, u32[]{:S(2)}, u32[]{:S(2)}) collective-permute-start(bf16[2,128,512]{2,1,0:T(8,128)(2,1)S(1)} %fusion.17), channel_id=1, source_target_pairs={{0,24},{8,16},{16,8},{24,0},{1,25},{9,17},{17,9},{25,1},{2,26},{10... | collective-permute-start | bytes 786440 | tf_op jit(solution)/shard_map/ppermute | solution.py:194
  161.7 9.0 %collective-permute-start.28 = (f32[128,384]{1,0:T(8,128)S(1)}, f32[128,384]{1,0:T(8,128)S(1)}, u32[]{:S(2)}, u32[]{:S(2)}) collective-permute-start(f32[128,384]{1,0:T(8,128)S(1)} %pad_maximum_fusion.10), channel_id=1, source_target_pairs={{0,1},{1,0},{2,3},{3,2},{4,5},{5,4},{6,7},{7,6},{8,9},{9,8},{10,11... | collective-permute-start | bytes 589832 | tf_op jit(solution)/shard_map/ppermute | solution.py:194
  170.8 12.4 %collective-permute-start.29 = (f32[128,384]{1,0:T(8,128)S(1)}, f32[128,384]{1,0:T(8,128)S(1)}, u32[]{:S(2)}, u32[]{:S(2)}) collective-permute-start(f32[128,384]{1,0:T(8,128)S(1)} %fusion.91), channel_id=1, source_target_pairs={{0,2},{1,3},{2,0},{3,1},{4,6},{5,7},{6,4},{7,5},{8,10},{9,11},{10,... | collective-permute-start | bytes 589832 | tf_op jit(solution)/shard_map/ppermute | solution.py:194
  184.9 8.9 %collective-permute-start.32 = (f32[128,384]{1,0:T(8,128)S(1)}, f32[128,384]{1,0:T(8,128)S(1)}, u32[]{:S(2)}, u32[]{:S(2)}) collective-permute-start(f32[128,384]{1,0:T(8,128)S(1)} %add.373.refs_0_), channel_id=1, source_target_pairs={{0,24},{8,16},{16,8},{24,0},{1,25},{9,17},{17,9},{25,1},{2,26},{10... | collective-permute-start | bytes 589832 | tf_op jit(solution)/shard_map/ppermute | solution.py:194
  (37 other events, 247.5 us)
Sparse Core Ops, SparseCore 0:
  16.8 44.5 all-gather.2
  89.4 47.0 all-gather.4
  187.9 32.2 reduce-scatter.3

commit v8 on v7

--- a/solution.py
+++ b/solution.py
@@ -290,6 +290,13 @@
             for part in split(image)
         )
 
+    def halve(value, axis, bit):
+        half = value.shape[0] // 2
+        mine = lax.axis_index(axis) // bit % 2
+        own = lax.dynamic_slice_in_dim(value, mine * half, half, 0)
+        other = lax.dynamic_slice_in_dim(value, (1 - mine) * half, half, 0)
+        return own + swap(other, axis, bit)
+
     def factor(image, last, beside):
         precision = HIGHEST if last else HIGH
         own = lax.dynamic_slice_in_dim(image, tok_pos * own_cols, own_cols, 2)
@@ -315,10 +322,17 @@
         while step < gc_count:
             if 2 * step == gc_count:
                 total, beside = lax.optimization_barrier((total, beside))
-                if not last:
-                    beside = mix_seen(beside)
+                beside = halve(beside, "gr", 1) if last else mix_seen(beside)
+                if last and gc_count > 1:
+                    beside = halve(beside, "gc", gc_count // 2)
             total += swap(total, "gc", step)
             step *= 2
+        if last:
+            total, beside = lax.optimization_barrier((total, beside))
+            step = gc_count // 4
+            while step:
+                beside = halve(beside, "gc", step)
+                step //= 2
         if packed:
             pieces = collect(total, "tok")
         else:
@@ -356,7 +370,7 @@
     of_block, of_group, placed = factor(image, True, placed)
     rows = lax.dynamic_slice_in_dim(image, tok_pos * slice_rows, slice_rows, 1)
     basis = jnp.einsum("obr,osr->obs", rows, of_block, precision=HIGH)
-    placed = lax.psum_scatter(placed, ("gr", "gc"), scatter_dimension=0, tiled=True)
+    placed, basis = lax.optimization_barrier((placed, basis))
     latent = jnp.concatenate(
         [
             jnp.einsum(

time: 233 us -> 267 us (1.15)
  waiting for transfers between devices: 83.8 us -> 111 us
  starting transfers between devices: 47.4 us -> 50.1 us
    ppermute x34 -> x37, waiting for transfers between devices: 75.3 us -> 109 us  [swap(): lax.ppermute(value, axis, [(i, i ^ k) for i in range(lax.axis_size(axis))])]
    unnamed x4 -> x2, waiting for transfers between devices: 6.49 us -> 0.03 us
    ppermute x34 -> x37, starting transfers between devices: 47.3 us -> 50 us  [swap(): lax.ppermute(value, axis, [(i, i ^ k) for i in range(lax.axis_size(axis))])]
  transfers between devices with their start and end apart: 37 -> 39, of which waited for: 24 -> 25; matrix products, arithmetic and copies ran while one was open for 12% -> 12% of each run, Pallas kernels for 17% -> 7%
where the time goes in v8:
time: 267 us
  waiting for transfers between devices  111 us (42%)
  starting transfers between devices  50.1 us (19%)
  Pallas kernels  38.8 us (15%)
  matrix products  25.1 us (9%)
  local copies, waits for them, and re-layouts  16.3 us (6%)
  between operations  16.2 us (6%)
  other arithmetic  8.96 us (3%)
    ppermute x37, waiting for transfers between devices, swap(): lax.ppermute(value, axis, [(i, i ^ k) for i in range(lax.axis_size(axis))])  109 us
    ppermute x37, starting transfers between devices, swap(): lax.ppermute(value, axis, [(i, i ^ k) for i in range(lax.axis_size(axis))])  50 us
    pallas_call x2, Pallas kernels, inverse_factor(): pl.pallas_call(functools.partial(factor_kernel, scale, exact), out_shape=...  38.8 us
  transfers between devices with their start and end apart: 39, of which 25 were waited for; matrix products, arithmetic and copies ran while one was open for 12% of the time, Pallas kernels for 7%

profile of v8, /device:TPU:0, one launch (start us, length us, event | category | flops | bytes accessed | tf_op | source)
XLA Modules:
  0.0 266.9 jit_solution(9640213746220187914)
XLA Ops:
  8.6 3.0 %collective-permute-start = (bf16[2,256,256]{2,1,0:T(8,128)(2,1)S(1)}, bf16[2,256,256]{2,1,0:T(8,128)(2,1)S(1)}, u32[]{:S(2)}, u32[]{:S(2)}) collective-permute-start(bf16[2,256,256]{2,1,0:T(8,128)(2,1)S(1)} %get-tuple-element.98), channel_id=1, source_target_pairs={{0,8},{8,0},{16,24},{24,16},{1,9},{9,1},{17,25},{25,17},{2,10},{10... | collective-permute-start | bytes 786440 | tf_op jit(solution)/shard_map/ppermute | solution.py:194
  32.0 2.9 %collective-permute-done.7 = bf16[2,256,256]{2,1,0:T(8,128)(2,1)S(1)} collective-permute-done((bf16[2,256,256]{2,1,0:T(8,128)(2,1)S(1)}, bf16[2,256,256]{2,1,0:T(8,128)(2,1)S(1)}, u32[]{:S(2)}, u32[]{:S(2)}) %collective-permute-start.7) | collective-permute-done | bytes 262176 | tf_op jit(solution)/shard_map/ppermute | solution.py:194
  34.9 3.7 %collective-permute-start.5 = (bf16[2,128,256]{2,1,0:T(8,128)(2,1)S(1)}, bf16[2,128,256]{2,1,0:T(8,128)(2,1)S(1)}, u32[]{:S(2)}, u32[]{:S(2)}) collective-permute-start(bf16[2,128,256]{2,1,0:T(8,128)(2,1)S(1)} %convolution_convert_fusion.1), channel_id=1, source_target_pairs={{0,3},{1,2},{2,1},{3,0},{4,7},{5,6},{6,5},{7,4},{8,11},{9,10},{10,... | collective-permute-start | bytes 393224 | tf_op jit(solution)/shard_map/ppermute | solution.py:194
  49.5 7.1 %collective-permute-done.11 = bf16[2,128,256]{2,1,0:T(8,128)(2,1)S(1)} collective-permute-done((bf16[2,128,256]{2,1,0:T(8,128)(2,1)S(1)}, bf16[2,128,256]{2,1,0:T(8,128)(2,1)S(1)}, u32[]{:S(2)}, u32[]{:S(2)}) %collective-permute-start.11) | collective-permute-done | bytes 131104 | tf_op jit(solution)/shard_map/ppermute | solution.py:194
  68.9 6.2 %collective-permute-done.15 = bf16[2,128,512]{2,1,0:T(8,128)(2,1)} collective-permute-done((bf16[2,128,512]{2,1,0:T(8,128)(2,1)}, bf16[2,128,512]{2,1,0:T(8,128)(2,1)}, u32[]{:S(2)}, u32[]{:S(2)}) %collective-permute-start.15) | collective-permute-done | bytes 262176 | tf_op jit(solution)/shard_map/ppermute | solution.py:194
  75.1 3.5 %multiply_add_fusion.1 = f32[2,1024,512]{2,1,0:T(8,128)S(1)} fusion(bf16[2,256,256]{2,1,0:T(8,128)(2,1)} %get-tuple-element.91, bf16[2,256,256]{2,1,0:T(8,128)(2,1)} %get-tuple-element.92, bf16[2,256,256]{2,1,0:T(8,128)(2,1)} %get-tuple-element.93, bf16[2,256,256]{2,1,0:T(8,128)(2,1)} %get-tuple-element.90, bf16[2,256,256]{2,1,0:T(8,128)(2,1)S(1)} %get-tuple-element.87, ...), kind=kOutput, calls=%fused_computation.7 | convolution fusion | flops 1098907648 | bytes 9437184 | tf_op jit(solution)/shard_map/tob,otr->obr/dot_general | solution.py:284
  84.8 4.3 %collective-permute-done.18 = f32[128,384]{1,0:T(8,128)S(1)} collective-permute-done((f32[128,384]{1,0:T(8,128)S(1)}, f32[128,384]{1,0:T(8,128)S(1)}, u32[]{:S(2)}, u32[]{:S(2)}) %collective-permute-start.18) | collective-permute-done | bytes 196640 | tf_op jit(solution)/shard_map/ppermute | solution.py:194
  92.9 11.4 %collective-permute-done.19 = f32[128,384]{1,0:T(8,128)S(1)} collective-permute-done((f32[128,384]{1,0:T(8,128)S(1)}, f32[128,384]{1,0:T(8,128)S(1)}, u32[]{:S(2)}, u32[]{:S(2)}) %collective-permute-start.19) | collective-permute-done | bytes 196640 | tf_op jit(solution)/shard_map/ppermute | solution.py:194
  104.5 3.4 %collective-permute-start.22 = (f32[128,384]{1,0:T(8,128)S(1)}, f32[128,384]{1,0:T(8,128)S(1)}, u32[]{:S(2)}, u32[]{:S(2)}) collective-permute-start(f32[128,384]{1,0:T(8,128)S(1)} %add.390.refs_0_), channel_id=1, source_target_pairs={{0,24},{8,16},{16,8},{24,0},{1,25},{9,17},{17,9},{25,1},{2,26},{10... | collective-permute-start | bytes 589832 | tf_op jit(solution)/shard_map/ppermute | solution.py:194
  110.0 3.0 %collective-permute-done.21.refs_2_ = f32[128,384]{1,0:T(8,128)S(1)} collective-permute-done((f32[128,384]{1,0:T(8,128)S(1)}, f32[128,384]{1,0:T(8,128)S(1)}, u32[]{:S(2)}, u32[]{:S(2)}) %collective-permute-start.21) | collective-permute-done | bytes 196640 | tf_op jit(solution)/shard_map/ppermute | solution.py:194
  113.0 18.8 %inverse_factor.2 = f32[512,512]{1,0:T(8,128)S(1)} custom-call(s32[1]{0:T(128)} %bitcast.1.pos_ref, f32[128,384]{1,0:T(8,128)S(1)} %add.390.refs_0_, f32[128,384]{1,0:T(8,128)S(1)} %collective-permute-done.20.refs_1_, f32[128,384]{1,0:T(8,128)S(1)} %collective-permute-done.21.refs_2_, f32[128,384]{1,0:T(8,128)S(1)} %collective-permute-done.22.refs_3_), custom_call_target="tpu_custom_call" | custom-call | flops 12884901888 | bytes 2097152 | tf_op jit(solution)/shard_map/inverse_factor/pallas_call | solution.py:171
  134.2 2.9 %all-gather.5.cloned.1.call-done = f32[16,128,512]{2,1,0:T(8,128)} async-done(((f32[2,128,512]{2,1,0:T(8,128)}), f32[16,128,512]{2,1,0:T(8,128)}) %all-gather.5.cloned.1.call-update) | async-done | bytes 4194320 | tf_op jit(solution)/shard_map/all_gather | solution.py:352
  145.7 4.0 %fusion.12 = bf16[2,1024,512]{2,1,0:T(8,128)(2,1)S(1)} fusion(f32[2,1024,512]{2,1,0:T(8,128)S(1)} %copy-done.1, f32[1,512,512]{2,1,0:T(8,128)S(1)} %get-tuple-element.81, f32[1,512,512]{2,1,0:T(8,128)S(1)} %get-tuple-element.80), kind=kOutput, calls=%fused_computation.18 | convolution fusion | flops 3221749760 | bytes 8388608 | tf_op jit(solution)/shard_map/obr,osr->obs/dot_general | solution.py:360
  151.4 5.4 %collective-permute-done.25 = bf16[2,128,512]{2,1,0:T(8,128)(2,1)S(1)} collective-permute-done((bf16[2,128,512]{2,1,0:T(8,128)(2,1)S(1)}, bf16[2,128,512]{2,1,0:T(8,128)(2,1)S(1)}, u32[]{:S(2)}, u32[]{:S(2)}) %collective-permute-start.25) | collective-permute-done | bytes 262176 | tf_op jit(solution)/shard_map/ppermute | solution.py:194
  162.6 3.7 %collective-permute-start.28 = (f32[128,384]{1,0:T(8,128)S(1)}, f32[128,384]{1,0:T(8,128)S(1)}, u32[]{:S(2)}, u32[]{:S(2)}) collective-permute-start(f32[128,384]{1,0:T(8,128)S(1)} %pad_maximum_fusion.10), channel_id=1, source_target_pairs={{0,1},{1,0},{2,3},{3,2},{4,5},{5,4},{6,7},{7,6},{8,9},{9,8},{10,11... | collective-permute-start | bytes 589832 | tf_op jit(solution)/shard_map/ppermute | solution.py:194
  167.2 4.2 %collective-permute-done.28 = f32[128,384]{1,0:T(8,128)S(1)} collective-permute-done((f32[128,384]{1,0:T(8,128)S(1)}, f32[128,384]{1,0:T(8,128)S(1)}, u32[]{:S(2)}, u32[]{:S(2)}) %collective-permute-start.28) | collective-permute-done | bytes 196640 | tf_op jit(solution)/shard_map/ppermute | solution.py:194
  171.8 3.6 %collective-permute-start.29 = (f32[128,384]{1,0:T(8,128)S(1)}, f32[128,384]{1,0:T(8,128)S(1)}, u32[]{:S(2)}, u32[]{:S(2)}) collective-permute-start(f32[128,384]{1,0:T(8,128)S(1)} %fusion.91), channel_id=1, source_target_pairs={{0,2},{1,3},{2,0},{3,1},{4,6},{5,7},{6,4},{7,5},{8,10},{9,11},{10,... | collective-permute-start | bytes 589832 | tf_op jit(solution)/shard_map/ppermute | solution.py:194
  177.6 18.9 %collective-permute-done.29 = f32[128,384]{1,0:T(8,128)S(1)} collective-permute-done((f32[128,384]{1,0:T(8,128)S(1)}, f32[128,384]{1,0:T(8,128)S(1)}, u32[]{:S(2)}, u32[]{:S(2)}) %collective-permute-start.29) | collective-permute-done | bytes 196640 | tf_op jit(solution)/shard_map/ppermute | solution.py:194
  196.5 10.9 %collective-permute-done.31 = f32[32,1024]{0,1:T(8,128)S(1)} collective-permute-done((f32[32,1024]{0,1:T(8,128)S(1)}, f32[32,1024]{0,1:T(8,128)S(1)}, u32[]{:S(2)}, u32[]{:S(2)}) %collective-permute-start.31) | collective-permute-done | bytes 131104 | tf_op jit(solution)/shard_map/ppermute | solution.py:194
  211.2 4.3 %collective-permute-done.33.refs_1_ = f32[128,384]{1,0:T(8,128)S(1)} collective-permute-done((f32[128,384]{1,0:T(8,128)S(1)}, f32[128,384]{1,0:T(8,128)S(1)}, u32[]{:S(2)}, u32[]{:S(2)}) %collective-permute-start.33) | collective-permute-done | bytes 196640 | tf_op jit(solution)/shard_map/ppermute | solution.py:194
  215.8 3.1 %collective-permute-done.35.refs_3_ = f32[128,384]{1,0:T(8,128)S(1)} collective-permute-done((f32[128,384]{1,0:T(8,128)S(1)}, f32[128,384]{1,0:T(8,128)S(1)}, u32[]{:S(2)}, u32[]{:S(2)}) %collective-permute-start.35) | collective-permute-done | bytes 196640 | tf_op jit(solution)/shard_map/ppermute | solution.py:194
  218.9 20.0 %inverse_factor.3 = f32[512,512]{1,0:T(8,128)S(1)} custom-call(s32[1]{0:T(128)} %bitcast.1.pos_ref, f32[128,384]{1,0:T(8,128)S(1)} %add.410.refs_0_, f32[128,384]{1,0:T(8,128)S(1)} %collective-permute-done.33.refs_1_, f32[128,384]{1,0:T(8,128)S(1)} %collective-permute-done.34.refs_2_, f32[128,384]{1,0:T(8,128)S(1)} %collective-permute-done.35.refs_3_), custom_call_target="tpu_custom_call" | custom-call | flops 12884901888 | bytes 2097152 | tf_op jit(solution)/shard_map/inverse_factor/pallas_call | solution.py:171
  240.9 13.5 %collective-permute-done.32 = f32[16,1024]{0,1:T(8,128)S(1)} collective-permute-done((f32[16,1024]{0,1:T(8,128)}, f32[16,1024]{0,1:T(8,128)S(1)}, u32[]{:S(2)}, u32[]{:S(2)}) %collective-permute-start.32) | collective-permute-done | bytes 65568 | tf_op jit(solution)/shard_map/ppermute | solution.py:194
  254.9 3.4 %fusion.8 = f32[2,256,512]{2,1,0:T(8,128)} fusion(f32[1,512,512]{2,1,0:T(8,128)S(1)} %get-tuple-element.79, f32[1,512,512]{2,1,0:T(8,128)S(1)} %get-tuple-element.78, f32[2,1024,512]{2,1,0:T(8,128)} %copy-done.2, s32[]{:T(128)S(6)} %select_n.343), kind=kOutput, calls=%fused_computation.14 | convolution fusion | flops 805830656 | bytes 4194308 | tf_op jit(solution)/shard_map/obr,osr->obs/dot_general | solution.py:372
  (181 shorter events, 85.7 us)
Async XLA Ops:
  7.2 55.7 %all-gather.3.cloned.1.call-start = ((), (), s32[]{:S(2)}) async-start(), calls=%async_computation | async-start | bytes 2621440 | tf_op jit(solution)/shard_map/all_gather | solution.py:238
  8.6 14.8 %collective-permute-start = (bf16[2,256,256]{2,1,0:T(8,128)(2,1)S(1)}, bf16[2,256,256]{2,1,0:T(8,128)(2,1)S(1)}, u32[]{:S(2)}, u32[]{:S(2)}) collective-permute-start(bf16[2,256,256]{2,1,0:T(8,128)(2,1)S(1)} %get-tuple-element.98), channel_id=1, source_target_pairs={{0,8},{8,0},{16,24},{24,16},{1,9},{9,1},{17,25},{25,17},{2,10},{10... | collective-permute-start | bytes 786440 | tf_op jit(solution)/shard_map/ppermute | solution.py:194
  11.6 14.8 %collective-permute-start.1 = (bf16[2,256,256]{2,1,0:T(8,128)(2,1)S(1)}, bf16[2,256,256]{2,1,0:T(8,128)(2,1)S(1)}, u32[]{:S(2)}, u32[]{:S(2)}) collective-permute-start(bf16[2,256,256]{2,1,0:T(8,128)(2,1)S(1)} %get-tuple-element.98), channel_id=1, source_target_pairs={{0,16},{8,24},{16,0},{24,8},{1,17},{9,25},{17,1},{25,9},{2,18},{10... | collective-permute-start | bytes 786440 | tf_op jit(solution)/shard_map/ppermute | solution.py:194
  13.1 13.3 %collective-permute-start.2 = (bf16[2,256,256]{2,1,0:T(8,128)(2,1)S(1)}, bf16[2,256,256]{2,1,0:T(8,128)(2,1)S(1)}, u32[]{:S(2)}, u32[]{:S(2)}) collective-permute-start(bf16[2,256,256]{2,1,0:T(8,128)(2,1)S(1)} %get-tuple-element.98), channel_id=1, source_target_pairs={{0,24},{8,16},{16,8},{24,0},{1,25},{9,17},{17,9},{25,1},{2,26},{10... | collective-permute-start | bytes 786440 | tf_op jit(solution)/shard_map/ppermute | solution.py:194
  13.2 21.7 %collective-permute-start.7 = (bf16[2,256,256]{2,1,0:T(8,128)(2,1)S(1)}, bf16[2,256,256]{2,1,0:T(8,128)(2,1)S(1)}, u32[]{:S(2)}, u32[]{:S(2)}) collective-permute-start(bf16[2,256,256]{2,1,0:T(8,128)(2,1)S(1)} %get-tuple-element.99), channel_id=1, source_target_pairs={{0,8},{8,0},{16,24},{24,16},{1,9},{9,1},{17,25},{25,17},{2,10},{10... | collective-permute-start | bytes 786440 | tf_op jit(solution)/shard_map/ppermute | solution.py:194
  15.1 25.8 %collective-permute-start.8 = (bf16[2,256,256]{2,1,0:T(8,128)(2,1)S(1)}, bf16[2,256,256]{2,1,0:T(8,128)(2,1)S(1)}, u32[]{:S(2)}, u32[]{:S(2)}) collective-permute-start(bf16[2,256,256]{2,1,0:T(8,128)(2,1)S(1)} %get-tuple-element.99), channel_id=1, source_target_pairs={{0,16},{8,24},{16,0},{24,8},{1,17},{9,25},{17,1},{25,9},{2,18},{10... | collective-permute-start | bytes 786440 | tf_op jit(solution)/shard_map/ppermute | solution.py:194
  16.7 120.5 %all-gather.5.cloned.1.call-start = ((), (), s32[]{:S(2)}) async-start(), calls=%async_computation.1 | async-start | bytes 4718592 | tf_op jit(solution)/shard_map/all_gather | solution.py:352
  23.4 18.3 %collective-permute-start.9 = (bf16[2,256,256]{2,1,0:T(8,128)(2,1)S(1)}, bf16[2,256,256]{2,1,0:T(8,128)(2,1)S(1)}, u32[]{:S(2)}, u32[]{:S(2)}) collective-permute-start(bf16[2,256,256]{2,1,0:T(8,128)(2,1)S(1)} %get-tuple-element.99), channel_id=1, source_target_pairs={{0,24},{8,16},{16,8},{24,0},{1,25},{9,17},{17,9},{25,1},{2,26},{10... | collective-permute-start | bytes 786440 | tf_op jit(solution)/shard_map/ppermute | solution.py:194
  27.8 20.6 %collective-permute-start.3 = (bf16[2,128,256]{2,1,0:T(8,128)(2,1)S(1)}, bf16[2,128,256]{2,1,0:T(8,128)(2,1)S(1)}, u32[]{:S(2)}, u32[]{:S(2)}) collective-permute-start(bf16[2,128,256]{2,1,0:T(8,128)(2,1)S(1)} %convolution_convert_fusion.1), channel_id=1, source_target_pairs={{0,1},{1,0},{2,3},{3,2},{4,5},{5,4},{6,7},{7,6},{8,9},{9,8},{10,11... | collective-permute-start | bytes 393224 | tf_op jit(solution)/shard_map/ppermute | solution.py:194
  29.4 19.1 %collective-permute-start.4 = (bf16[2,128,256]{2,1,0:T(8,128)(2,1)S(1)}, bf16[2,128,256]{2,1,0:T(8,128)(2,1)S(1)}, u32[]{:S(2)}, u32[]{:S(2)}) collective-permute-start(bf16[2,128,256]{2,1,0:T(8,128)(2,1)S(1)} %convolution_convert_fusion.1), channel_id=1, source_target_pairs={{0,2},{1,3},{2,0},{3,1},{4,6},{5,7},{6,4},{7,5},{8,10},{9,11},{10,... | collective-permute-start | bytes 393224 | tf_op jit(solution)/shard_map/ppermute | solution.py:194
  34.9 13.7 %collective-permute-start.5 = (bf16[2,128,256]{2,1,0:T(8,128)(2,1)S(1)}, bf16[2,128,256]{2,1,0:T(8,128)(2,1)S(1)}, u32[]{:S(2)}, u32[]{:S(2)}) collective-permute-start(bf16[2,128,256]{2,1,0:T(8,128)(2,1)S(1)} %convolution_convert_fusion.1), channel_id=1, source_target_pairs={{0,3},{1,2},{2,1},{3,0},{4,7},{5,6},{6,5},{7,4},{8,11},{9,10},{10,... | collective-permute-start | bytes 393224 | tf_op jit(solution)/shard_map/ppermute | solution.py:194
  44.7 12.0 %collective-permute-start.11 = (bf16[2,128,256]{2,1,0:T(8,128)(2,1)S(1)}, bf16[2,128,256]{2,1,0:T(8,128)(2,1)S(1)}, u32[]{:S(2)}, u32[]{:S(2)}) collective-permute-start(bf16[2,128,256]{2,1,0:T(8,128)(2,1)S(1)} %convolution_convert_fusion), channel_id=1, source_target_pairs={{0,2},{1,3},{2,0},{3,1},{4,6},{5,7},{6,4},{7,5},{8,10},{9,11},{10,... | collective-permute-start | bytes 393224 | tf_op jit(solution)/shard_map/ppermute | solution.py:194
  59.4 9.4 %collective-permute-start.14 = (bf16[2,128,512]{2,1,0:T(8,128)(2,1)}, bf16[2,128,512]{2,1,0:T(8,128)(2,1)}, u32[]{:S(2)}, u32[]{:S(2)}) collective-permute-start(bf16[2,128,512]{2,1,0:T(8,128)(2,1)} %pad_maximum_fusion.8), channel_id=1, source_target_pairs={{0,8},{8,0},{16,24},{24,16},{1,9},{9,1},{17,25},{25,17},{2,10},{10... | collective-permute-start | bytes 786440 | tf_op jit(solution)/shard_map/ppermute | solution.py:194
  60.9 14.2 %collective-permute-start.15 = (bf16[2,128,512]{2,1,0:T(8,128)(2,1)}, bf16[2,128,512]{2,1,0:T(8,128)(2,1)}, u32[]{:S(2)}, u32[]{:S(2)}) collective-permute-start(bf16[2,128,512]{2,1,0:T(8,128)(2,1)} %pad_maximum_fusion.8), channel_id=1, source_target_pairs={{0,16},{8,24},{16,0},{24,8},{1,17},{9,25},{17,1},{25,9},{2,18},{10... | collective-permute-start | bytes 786440 | tf_op jit(solution)/shard_map/ppermute | solution.py:194
  61.5 13.6 %collective-permute-start.16 = (bf16[2,128,512]{2,1,0:T(8,128)(2,1)}, bf16[2,128,512]{2,1,0:T(8,128)(2,1)}, u32[]{:S(2)}, u32[]{:S(2)}) collective-permute-start(bf16[2,128,512]{2,1,0:T(8,128)(2,1)} %pad_maximum_fusion.8), channel_id=1, source_target_pairs={{0,24},{8,16},{16,8},{24,0},{1,25},{9,17},{17,9},{25,1},{2,26},{10... | collective-permute-start | bytes 786440 | tf_op jit(solution)/shard_map/ppermute | solution.py:194
  90.1 14.2 %collective-permute-start.19 = (f32[128,384]{1,0:T(8,128)S(1)}, f32[128,384]{1,0:T(8,128)S(1)}, u32[]{:S(2)}, u32[]{:S(2)}) collective-permute-start(f32[128,384]{1,0:T(8,128)S(1)} %fusion.92), channel_id=1, source_target_pairs={{0,2},{1,3},{2,0},{3,1},{4,6},{5,7},{6,4},{7,5},{8,10},{9,11},{10,... | collective-permute-start | bytes 589832 | tf_op jit(solution)/shard_map/ppermute | solution.py:194
  142.1 9.2 %collective-permute-start.24 = (bf16[2,128,512]{2,1,0:T(8,128)(2,1)S(1)}, bf16[2,128,512]{2,1,0:T(8,128)(2,1)S(1)}, u32[]{:S(2)}, u32[]{:S(2)}) collective-permute-start(bf16[2,128,512]{2,1,0:T(8,128)(2,1)S(1)} %fusion.17), channel_id=1, source_target_pairs={{0,8},{8,0},{16,24},{24,16},{1,9},{9,1},{17,25},{25,17},{2,10},{10... | collective-permute-start | bytes 786440 | tf_op jit(solution)/shard_map/ppermute | solution.py:194
  143.0 13.8 %collective-permute-start.25 = (bf16[2,128,512]{2,1,0:T(8,128)(2,1)S(1)}, bf16[2,128,512]{2,1,0:T(8,128)(2,1)S(1)}, u32[]{:S(2)}, u32[]{:S(2)}) collective-permute-start(bf16[2,128,512]{2,1,0:T(8,128)(2,1)S(1)} %fusion.17), channel_id=1, source_target_pairs={{0,16},{8,24},{16,0},{24,8},{1,17},{9,25},{17,1},{25,9},{2,18},{10... | collective-permute-start | bytes 786440 | tf_op jit(solution)/shard_map/ppermute | solution.py:194
  144.5 12.3 %collective-permute-start.26 = (bf16[2,128,512]{2,1,0:T(8,128)(2,1)S(1)}, bf16[2,128,512]{2,1,0:T(8,128)(2,1)S(1)}, u32[]{:S(2)}, u32[]{:S(2)}) collective-permute-start(bf16[2,128,512]{2,1,0:T(8,128)(2,1)S(1)} %fusion.17), channel_id=1, source_target_pairs={{0,24},{8,16},{16,8},{24,0},{1,25},{9,17},{17,9},{25,1},{2,26},{10... | collective-permute-start | bytes 786440 | tf_op jit(solution)/shard_map/ppermute | solution.py:194
  171.8 24.7 %collective-permute-start.29 = (f32[128,384]{1,0:T(8,128)S(1)}, f32[128,384]{1,0:T(8,128)S(1)}, u32[]{:S(2)}, u32[]{:S(2)}) collective-permute-start(f32[128,384]{1,0:T(8,128)S(1)} %fusion.91), channel_id=1, source_target_pairs={{0,2},{1,3},{2,0},{3,1},{4,6},{5,7},{6,4},{7,5},{8,10},{9,11},{10,... | collective-permute-start | bytes 589832 | tf_op jit(solution)/shard_map/ppermute | solution.py:194
  175.8 31.7 %collective-permute-start.31 = (f32[32,1024]{0,1:T(8,128)S(1)}, f32[32,1024]{0,1:T(8,128)S(1)}, u32[]{:S(2)}, u32[]{:S(2)}) collective-permute-start(f32[32,1024]{0,1:T(8,128)S(1)} %constant_dynamic-slice_fusion.1), channel_id=1, source_target_pairs={{0,2},{1,3},{2,0},{3,1},{4,6},{5,7},{6,4},{7,5},{8,10},{9,11},{10,... | collective-permute-start | bytes 393224 | tf_op jit(solution)/shard_map/ppermute | solution.py:194
  209.4 9.5 %collective-permute-start.35 = (f32[128,384]{1,0:T(8,128)S(1)}, f32[128,384]{1,0:T(8,128)S(1)}, u32[]{:S(2)}, u32[]{:S(2)}) collective-permute-start(f32[128,384]{1,0:T(8,128)S(1)} %add.410.refs_0_), channel_id=1, source_target_pairs={{0,24},{8,16},{16,8},{24,0},{1,25},{9,17},{17,9},{25,1},{2,26},{10... | collective-permute-start | bytes 589832 | tf_op jit(solution)/shard_map/ppermute | solution.py:194
  238.8 15.8 %collective-permute-start.36 = (f32[512,512]{1,0:T(8,128)S(1)}, f32[512,512]{1,0:T(8,128)S(1)}, u32[]{:S(2)}, u32[]{:S(2)}) collective-permute-start(f32[512,512]{1,0:T(8,128)S(1)} %inverse_factor.3), channel_id=1, source_target_pairs={{0,4},{4,0},{1,5},{5,1},{2,6},{6,2},{3,7},{7,3},{8,12},{12,8},{9,1... | collective-permute-start | bytes 3145736 | tf_op jit(solution)/shard_map/ppermute | solution.py:194
  239.9 14.5 %collective-permute-start.32 = (f32[16,1024]{0,1:T(8,128)}, f32[16,1024]{0,1:T(8,128)S(1)}, u32[]{:S(2)}, u32[]{:S(2)}) collective-permute-start(f32[16,1024]{0,1:T(8,128)} %constant_dynamic-slice_fusion), channel_id=1, source_target_pairs={{0,1},{1,0},{2,3},{3,2},{4,5},{5,4},{6,7},{7,6},{8,9},{9,8},{10,11... | collective-permute-start | bytes 196616 | tf_op jit(solution)/shard_map/ppermute | solution.py:194
  (39 other events, 284.5 us)
Sparse Core Ops, SparseCore 0:
  16.8 44.5 all-gather.2
  90.2 46.9 all-gather.4

commit v9 on v7

--- a/solution.py
+++ b/solution.py
@@ -278,6 +278,7 @@
         ],
         axis=2,
     )
+    full_x, basis_bf = lax.optimization_barrier((full_x, basis_bf))
 
     def image_of(mixed, basis_bf):
         full = jnp.concatenate(collect(mixed, "tok"), axis=1)
@@ -289,6 +290,12 @@
             jnp.einsum("tob,obr->otr", own_x, part, preferred_element_type=jnp.float32)
             for part in split(image)
         )
+
+    def half_over_gr(value):
+        half = value.shape[0] // 2
+        own = lax.dynamic_slice_in_dim(value, gr_pos * half, half, 0)
+        other = lax.dynamic_slice_in_dim(value, (gr_pos ^ 1) * half, half, 0)
+        return own + swap(other, "gr", 1)
 
     def factor(image, last, beside):
         precision = HIGHEST if last else HIGH
@@ -315,15 +322,19 @@
         while step < gc_count:
             if 2 * step == gc_count:
                 total, beside = lax.optimization_barrier((total, beside))
-                if not last:
-                    beside = mix_seen(beside)
+                beside = half_over_gr(beside) if last else mix_seen(beside)
             total += swap(total, "gc", step)
             step *= 2
+        if last:
+            total, beside = lax.optimization_barrier((total, beside))
+            beside = lax.psum_scatter(beside, "gc", scatter_dimension=0, tiled=True)
         if packed:
             pieces = collect(total, "tok")
         else:
             pieces = [lax.all_gather(total, "tok", axis=0, tiled=True)]
         own = inverse_factor(pieces, last, 1.0 / group_cols)
+        if last:
+            own, beside = lax.optimization_barrier((own, beside))
         other = swap(own, "gr", 1)
         if not last:
             other, beside = lax.optimization_barrier((other, beside))
@@ -356,7 +367,6 @@
     of_block, of_group, placed = factor(image, True, placed)
     rows = lax.dynamic_slice_in_dim(image, tok_pos * slice_rows, slice_rows, 1)
     basis = jnp.einsum("obr,osr->obs", rows, of_block, precision=HIGH)
-    placed = lax.psum_scatter(placed, ("gr", "gc"), scatter_dimension=0, tiled=True)
     latent = jnp.concatenate(
         [
             jnp.einsum(

time: 233 us -> 232 us (level)
  waiting for transfers between devices: 83.8 us -> 75.9 us
  local copies, waits for them, and re-layouts: 14.6 us -> 21.2 us
    unnamed x4, waiting for transfers between devices: 6.49 us -> 0.07 us
    optimization_barrier x0 -> x2, local copies, waits for them, and re-layouts: none -> 5.75 us  [the longest x1 4.72 us: per_device(): full_x, basis_bf = lax.optimization_barrier((full_x, basis_bf))]
    reshape x0 -> x1, local copies, waits for them, and re-layouts: none -> 2.79 us  [per_device(): full_x = jnp.concatenate([lax.dynamic_slice_in_dim(gathered_x, (tok_pos ^...]
    concatenate x1 -> x0, local copies, waits for them, and re-layouts: 2.56 us -> none  [per_device(): jnp.concatenate([lax.dynamic_slice_in_dim(gathered_x, (tok_pos ^ k) * tok...]
    ppermute x34 -> x35, waiting for transfers between devices: 75.3 us -> 72.9 us  [swap(): lax.ppermute(value, axis, [(i, i ^ k) for i in range(lax.axis_size(axis))])]
    ppermute x34 -> x35, starting transfers between devices: 47.3 us -> 47.1 us  [swap(): lax.ppermute(value, axis, [(i, i ^ k) for i in range(lax.axis_size(axis))])]
  transfers between devices with their start and end apart: 37 -> 38, of which waited for: 24 -> 22; matrix products, arithmetic and copies ran while one was open for 12% -> 15% of each run, Pallas kernels for 17% -> 17%
where the time goes in v9:
time: 232 us; the launch traced here: 231 us
  waiting for transfers between devices  75.9 us (33%)
  starting transfers between devices  47.3 us (20%)
  Pallas kernels  38.8 us (17%)
  matrix products  24.6 us (11%)
  local copies, waits for them, and re-layouts  21.2 us (9%)
  between operations  16 us (7%)
  other arithmetic  7.61 us (3%)
    ppermute x35, waiting for transfers between devices, swap(): lax.ppermute(value, axis, [(i, i ^ k) for i in range(lax.axis_size(axis))])  72.9 us
    ppermute x35, starting transfers between devices, swap(): lax.ppermute(value, axis, [(i, i ^ k) for i in range(lax.axis_size(axis))])  47.1 us
    pallas_call x2, Pallas kernels, inverse_factor(): pl.pallas_call(functools.partial(factor_kernel, scale, exact), out_shape=...  38.8 us
    optimization_barrier x1, local copies, waits for them, and re-layouts, per_device(): full_x, basis_bf = lax.optimization_barrier((full_x, basis_bf))  4.72 us
  transfers between devices with their start and end apart: 38, of which 22 were waited for; matrix products, arithmetic and copies ran while one was open for 15% of the time, Pallas kernels for 17%

profile of v9, /device:TPU:0, one launch (start us, length us, event | category | flops | bytes accessed | tf_op | source)
XLA Modules:
  0.0 231.4 jit_solution(16598576601185314154)
XLA Ops:
  8.6 3.0 %collective-permute-start = (bf16[2,256,256]{2,1,0:T(8,128)(2,1)S(1)}, bf16[2,256,256]{2,1,0:T(8,128)(2,1)S(1)}, u32[]{:S(2)}, u32[]{:S(2)}) collective-permute-start(bf16[2,256,256]{2,1,0:T(8,128)(2,1)S(1)} %get-tuple-element.102), channel_id=1, source_target_pairs={{0,8},{8,0},{16,24},{24,16},{1,9},{9,1},{17,25},{25,17},{2,10},{10... | collective-permute-start | bytes 786440 | tf_op jit(solution)/shard_map/ppermute | solution.py:194
  22.8 3.7 %collective-permute-done.1 = bf16[2,256,256]{2,1,0:T(8,128)(2,1)S(1)} collective-permute-done((bf16[2,256,256]{2,1,0:T(8,128)(2,1)S(1)}, bf16[2,256,256]{2,1,0:T(8,128)(2,1)S(1)}, u32[]{:S(2)}, u32[]{:S(2)}) %collective-permute-start.1) | collective-permute-done | bytes 262176 | tf_op jit(solution)/shard_map/ppermute | solution.py:194
  32.0 2.9 %collective-permute-done.3 = bf16[2,256,256]{2,1,0:T(8,128)(2,1)S(1)} collective-permute-done((bf16[2,256,256]{2,1,0:T(8,128)(2,1)S(1)}, bf16[2,256,256]{2,1,0:T(8,128)(2,1)S(1)}, u32[]{:S(2)}, u32[]{:S(2)}) %collective-permute-start.3) | collective-permute-done | bytes 262176 | tf_op jit(solution)/shard_map/ppermute | solution.py:194
  34.9 3.7 %collective-permute-start.8 = (bf16[2,128,256]{2,1,0:T(8,128)(2,1)S(1)}, bf16[2,128,256]{2,1,0:T(8,128)(2,1)S(1)}, u32[]{:S(2)}, u32[]{:S(2)}) collective-permute-start(bf16[2,128,256]{2,1,0:T(8,128)(2,1)S(1)} %convolution_convert_fusion.1), channel_id=1, source_target_pairs={{0,3},{1,2},{2,1},{3,0},{4,7},{5,6},{6,5},{7,4},{8,11},{9,10},{10,... | collective-permute-start | bytes 393224 | tf_op jit(solution)/shard_map/ppermute | solution.py:194
  49.5 7.1 %collective-permute-done.11 = bf16[2,128,256]{2,1,0:T(8,128)(2,1)S(1)} collective-permute-done((bf16[2,128,256]{2,1,0:T(8,128)(2,1)S(1)}, bf16[2,128,256]{2,1,0:T(8,128)(2,1)S(1)}, u32[]{:S(2)}, u32[]{:S(2)}) %collective-permute-start.11) | collective-permute-done | bytes 131104 | tf_op jit(solution)/shard_map/ppermute | solution.py:194
  67.2 4.7 %copy.75 = bf16[512,2,1024]{0,2,1:T(8,128)(2,1)S(1)} copy(bf16[512,2,1024]{2,1,0:T(2,128)(2,1)} %reshape.52) | data formatting | bytes 4194304 | tf_op jit(solution)/shard_map/optimization_barrier | solution.py:281
  74.6 3.0 %multiply_add_fusion.1 = f32[2,1024,512]{2,1,0:T(8,128)S(1)} fusion(bf16[2,1024,512]{2,1,0:T(8,128)(2,1)} %maximum_maximum_fusion, bf16[512,2,1024]{0,2,1:T(8,128)(2,1)S(1)} %copy.75, bf16[2,128,512]{2,1,0:T(8,128)(2,1)} %collective-permute-done.16, bf16[2,128,512]{2,1,0:T(8,128)(2,1)} %collective-permute-done.15, ...), kind=kOutput, calls=%fused_computation.7 | convolution fusion | flops 1083179008 | bytes 9437184 | tf_op jit(solution)/shard_map/tob,otr->obr/dot_general | solution.py:285
  83.9 4.3 %collective-permute-done.18 = f32[128,384]{1,0:T(8,128)S(1)} collective-permute-done((f32[128,384]{1,0:T(8,128)S(1)}, f32[128,384]{1,0:T(8,128)S(1)}, u32[]{:S(2)}, u32[]{:S(2)}) %collective-permute-start.18) | collective-permute-done | bytes 196640 | tf_op jit(solution)/shard_map/ppermute | solution.py:194
  92.1 11.3 %collective-permute-done.19 = f32[128,384]{1,0:T(8,128)S(1)} collective-permute-done((f32[128,384]{1,0:T(8,128)S(1)}, f32[128,384]{1,0:T(8,128)S(1)}, u32[]{:S(2)}, u32[]{:S(2)}) %collective-permute-start.19) | collective-permute-done | bytes 196640 | tf_op jit(solution)/shard_map/ppermute | solution.py:194
  103.6 3.4 %collective-permute-start.22 = (f32[128,384]{1,0:T(8,128)S(1)}, f32[128,384]{1,0:T(8,128)S(1)}, u32[]{:S(2)}, u32[]{:S(2)}) collective-permute-start(f32[128,384]{1,0:T(8,128)S(1)} %add.362.refs_0_), channel_id=1, source_target_pairs={{0,24},{8,16},{16,8},{24,0},{1,25},{9,17},{17,9},{25,1},{2,26},{10... | collective-permute-start | bytes 589832 | tf_op jit(solution)/shard_map/ppermute | solution.py:194
  109.2 3.0 %collective-permute-done.21.refs_2_ = f32[128,384]{1,0:T(8,128)S(1)} collective-permute-done((f32[128,384]{1,0:T(8,128)S(1)}, f32[128,384]{1,0:T(8,128)S(1)}, u32[]{:S(2)}, u32[]{:S(2)}) %collective-permute-start.21) | collective-permute-done | bytes 196640 | tf_op jit(solution)/shard_map/ppermute | solution.py:194
  112.2 18.8 %inverse_factor.2 = f32[512,512]{1,0:T(8,128)S(1)} custom-call(s32[1]{0:T(128)} %bitcast.pos_ref, f32[128,384]{1,0:T(8,128)S(1)} %add.362.refs_0_, f32[128,384]{1,0:T(8,128)S(1)} %collective-permute-done.20.refs_1_, f32[128,384]{1,0:T(8,128)S(1)} %collective-permute-done.21.refs_2_, f32[128,384]{1,0:T(8,128)S(1)} %collective-permute-done.22.refs_3_), custom_call_target="tpu_custom_call" | custom-call | flops 12884901888 | bytes 2097152 | tf_op jit(solution)/shard_map/inverse_factor/pallas_call | solution.py:171
  133.5 2.9 %all-gather.5.cloned.1.call-done = f32[16,128,512]{2,1,0:T(8,128)} async-done(((f32[2,128,512]{2,1,0:T(8,128)}), f32[16,128,512]{2,1,0:T(8,128)}) %all-gather.5.cloned.1.call-update) | async-done | bytes 4194320 | tf_op jit(solution)/shard_map/all_gather | solution.py:349
  136.4 2.8 %slice_bitcast_fusion.15 = (f32[128,512]{1,0:T(8,128)S(1)}, f32[128,512]{1,0:T(8,128)S(1)}, f32[128,512]{1,0:T(8,128)S(1)}, f32[128,512]{1,0:T(8,128)S(1)}, f32[...) fusion(f32[16,128,512]{2,1,0:T(8,128)} %all-gather.5.cloned.1.c, ...), kind=kLoop, calls=%fused_computation.97 | loop fusion | bytes 8388608 | tf_op jit(solution)/shard_map/mul | solution.py:352
  144.9 4.0 %fusion.12 = bf16[2,1024,512]{2,1,0:T(8,128)(2,1)S(1)} fusion(f32[2,1024,512]{2,1,0:T(8,128)S(1)} %copy-done.1, f32[1,512,512]{2,1,0:T(8,128)S(1)} %get-tuple-element.85, f32[1,512,512]{2,1,0:T(8,128)S(1)} %get-tuple-element.84), kind=kOutput, calls=%fused_computation.19 | convolution fusion | flops 3221749760 | bytes 8388608 | tf_op jit(solution)/shard_map/obr,osr->obs/dot_general | solution.py:357
  150.6 5.5 %collective-permute-done.25 = bf16[2,128,512]{2,1,0:T(8,128)(2,1)S(1)} collective-permute-done((bf16[2,128,512]{2,1,0:T(8,128)(2,1)S(1)}, bf16[2,128,512]{2,1,0:T(8,128)(2,1)S(1)}, u32[]{:S(2)}, u32[]{:S(2)}) %collective-permute-start.25) | collective-permute-done | bytes 262176 | tf_op jit(solution)/shard_map/ppermute | solution.py:194
  161.8 3.6 %collective-permute-start.28 = (f32[128,384]{1,0:T(8,128)S(1)}, f32[128,384]{1,0:T(8,128)S(1)}, u32[]{:S(2)}, u32[]{:S(2)}) collective-permute-start(f32[128,384]{1,0:T(8,128)S(1)} %pad_maximum_fusion.10), channel_id=1, source_target_pairs={{0,1},{1,0},{2,3},{3,2},{4,5},{5,4},{6,7},{7,6},{8,9},{9,8},{10,11... | collective-permute-start | bytes 589832 | tf_op jit(solution)/shard_map/ppermute | solution.py:194
  166.4 4.2 %collective-permute-done.28 = f32[128,384]{1,0:T(8,128)S(1)} collective-permute-done((f32[128,384]{1,0:T(8,128)S(1)}, f32[128,384]{1,0:T(8,128)S(1)}, u32[]{:S(2)}, u32[]{:S(2)}) %collective-permute-start.28) | collective-permute-done | bytes 196640 | tf_op jit(solution)/shard_map/ppermute | solution.py:194
  170.9 3.6 %collective-permute-start.29 = (f32[128,384]{1,0:T(8,128)S(1)}, f32[128,384]{1,0:T(8,128)S(1)}, u32[]{:S(2)}, u32[]{:S(2)}) collective-permute-start(f32[128,384]{1,0:T(8,128)S(1)} %fusion.88), channel_id=1, source_target_pairs={{0,2},{1,3},{2,0},{3,1},{4,6},{5,7},{6,4},{7,5},{8,10},{9,11},{10,... | collective-permute-start | bytes 589832 | tf_op jit(solution)/shard_map/ppermute | solution.py:194
  174.5 9.7 %collective-permute-done.29 = f32[128,384]{1,0:T(8,128)S(1)} collective-permute-done((f32[128,384]{1,0:T(8,128)S(1)}, f32[128,384]{1,0:T(8,128)S(1)}, u32[]{:S(2)}, u32[]{:S(2)}) %collective-permute-start.29) | collective-permute-done | bytes 196640 | tf_op jit(solution)/shard_map/ppermute | solution.py:194
  188.9 3.4 %collective-permute-done.31.refs_1_ = f32[128,384]{1,0:T(8,128)S(1)} collective-permute-done((f32[128,384]{1,0:T(8,128)S(1)}, f32[128,384]{1,0:T(8,128)S(1)}, u32[]{:S(2)}, u32[]{:S(2)}) %collective-permute-start.31) | collective-permute-done | bytes 196640 | tf_op jit(solution)/shard_map/ppermute | solution.py:194
  192.6 3.1 %collective-permute-done.33.refs_3_ = f32[128,384]{1,0:T(8,128)S(1)} collective-permute-done((f32[128,384]{1,0:T(8,128)S(1)}, f32[128,384]{1,0:T(8,128)S(1)}, u32[]{:S(2)}, u32[]{:S(2)}) %collective-permute-start.33) | collective-permute-done | bytes 196640 | tf_op jit(solution)/shard_map/ppermute | solution.py:194
  195.7 20.0 %inverse_factor.3 = f32[512,512]{1,0:T(8,128)S(1)} custom-call(s32[1]{0:T(128)} %bitcast.pos_ref, f32[128,384]{1,0:T(8,128)S(1)} %add.382.refs_0_, f32[128,384]{1,0:T(8,128)S(1)} %collective-permute-done.31.refs_1_, f32[128,384]{1,0:T(8,128)S(1)} %collective-permute-done.32.refs_2_, f32[128,384]{1,0:T(8,128)S(1)} %collective-permute-done.33.refs_3_), custom_call_target="tpu_custom_call" | custom-call | flops 12884901888 | bytes 2097152 | tf_op jit(solution)/shard_map/inverse_factor/pallas_call | solution.py:171
  221.5 3.4 %fusion.8 = f32[2,256,512]{2,1,0:T(8,128)} fusion(f32[1,512,512]{2,1,0:T(8,128)S(1)} %get-tuple-element.83, f32[1,512,512]{2,1,0:T(8,128)S(1)} %get-tuple-element.82, f32[2,1024,512]{2,1,0:T(8,128)} %copy-done.2, s32[]{:T(128)S(6)} %select_n.361), kind=kOutput, calls=%fused_computation.15 | convolution fusion | flops 805830656 | bytes 4194308 | tf_op jit(solution)/shard_map/obr,osr->obs/dot_general | solution.py:369
  (190 shorter events, 80.3 us)
Async XLA Ops:
  7.2 55.3 %all-gather.3.cloned.1.call-start = ((), (), s32[]{:S(2)}) async-start(), calls=%async_computation.1 | async-start | bytes 2621440 | tf_op jit(solution)/shard_map/all_gather | solution.py:238
  8.6 14.2 %collective-permute-start = (bf16[2,256,256]{2,1,0:T(8,128)(2,1)S(1)}, bf16[2,256,256]{2,1,0:T(8,128)(2,1)S(1)}, u32[]{:S(2)}, u32[]{:S(2)}) collective-permute-start(bf16[2,256,256]{2,1,0:T(8,128)(2,1)S(1)} %get-tuple-element.102), channel_id=1, source_target_pairs={{0,8},{8,0},{16,24},{24,16},{1,9},{9,1},{17,25},{25,17},{2,10},{10... | collective-permute-start | bytes 786440 | tf_op jit(solution)/shard_map/ppermute | solution.py:194
  11.6 14.8 %collective-permute-start.1 = (bf16[2,256,256]{2,1,0:T(8,128)(2,1)S(1)}, bf16[2,256,256]{2,1,0:T(8,128)(2,1)S(1)}, u32[]{:S(2)}, u32[]{:S(2)}) collective-permute-start(bf16[2,256,256]{2,1,0:T(8,128)(2,1)S(1)} %get-tuple-element.102), channel_id=1, source_target_pairs={{0,16},{8,24},{16,0},{24,8},{1,17},{9,25},{17,1},{25,9},{2,18},{10... | collective-permute-start | bytes 786440 | tf_op jit(solution)/shard_map/ppermute | solution.py:194
  13.1 13.3 %collective-permute-start.2 = (bf16[2,256,256]{2,1,0:T(8,128)(2,1)S(1)}, bf16[2,256,256]{2,1,0:T(8,128)(2,1)S(1)}, u32[]{:S(2)}, u32[]{:S(2)}) collective-permute-start(bf16[2,256,256]{2,1,0:T(8,128)(2,1)S(1)} %get-tuple-element.102), channel_id=1, source_target_pairs={{0,24},{8,16},{16,8},{24,0},{1,25},{9,17},{17,9},{25,1},{2,26},{10... | collective-permute-start | bytes 786440 | tf_op jit(solution)/shard_map/ppermute | solution.py:194
  13.2 21.7 %collective-permute-start.3 = (bf16[2,256,256]{2,1,0:T(8,128)(2,1)S(1)}, bf16[2,256,256]{2,1,0:T(8,128)(2,1)S(1)}, u32[]{:S(2)}, u32[]{:S(2)}) collective-permute-start(bf16[2,256,256]{2,1,0:T(8,128)(2,1)S(1)} %get-tuple-element.103), channel_id=1, source_target_pairs={{0,8},{8,0},{16,24},{24,16},{1,9},{9,1},{17,25},{25,17},{2,10},{10... | collective-permute-start | bytes 786440 | tf_op jit(solution)/shard_map/ppermute | solution.py:194
  15.1 25.8 %collective-permute-start.4 = (bf16[2,256,256]{2,1,0:T(8,128)(2,1)S(1)}, bf16[2,256,256]{2,1,0:T(8,128)(2,1)S(1)}, u32[]{:S(2)}, u32[]{:S(2)}) collective-permute-start(bf16[2,256,256]{2,1,0:T(8,128)(2,1)S(1)} %get-tuple-element.103), channel_id=1, source_target_pairs={{0,16},{8,24},{16,0},{24,8},{1,17},{9,25},{17,1},{25,9},{2,18},{10... | collective-permute-start | bytes 786440 | tf_op jit(solution)/shard_map/ppermute | solution.py:194
  16.7 119.7 %all-gather.5.cloned.1.call-start = ((), (), s32[]{:S(2)}) async-start(), calls=%async_computation.2 | async-start | bytes 4718592 | tf_op jit(solution)/shard_map/all_gather | solution.py:349
  22.8 18.9 %collective-permute-start.5 = (bf16[2,256,256]{2,1,0:T(8,128)(2,1)S(1)}, bf16[2,256,256]{2,1,0:T(8,128)(2,1)S(1)}, u32[]{:S(2)}, u32[]{:S(2)}) collective-permute-start(bf16[2,256,256]{2,1,0:T(8,128)(2,1)S(1)} %get-tuple-element.103), channel_id=1, source_target_pairs={{0,24},{8,16},{16,8},{24,0},{1,25},{9,17},{17,9},{25,1},{2,26},{10... | collective-permute-start | bytes 786440 | tf_op jit(solution)/shard_map/ppermute | solution.py:194
  27.7 19.9 %collective-permute-start.6 = (bf16[2,128,256]{2,1,0:T(8,128)(2,1)S(1)}, bf16[2,128,256]{2,1,0:T(8,128)(2,1)S(1)}, u32[]{:S(2)}, u32[]{:S(2)}) collective-permute-start(bf16[2,128,256]{2,1,0:T(8,128)(2,1)S(1)} %convolution_convert_fusion.1), channel_id=1, source_target_pairs={{0,1},{1,0},{2,3},{3,2},{4,5},{5,4},{6,7},{7,6},{8,9},{9,8},{10,11... | collective-permute-start | bytes 393224 | tf_op jit(solution)/shard_map/ppermute | solution.py:194
  29.3 18.5 %collective-permute-start.7 = (bf16[2,128,256]{2,1,0:T(8,128)(2,1)S(1)}, bf16[2,128,256]{2,1,0:T(8,128)(2,1)S(1)}, u32[]{:S(2)}, u32[]{:S(2)}) collective-permute-start(bf16[2,128,256]{2,1,0:T(8,128)(2,1)S(1)} %convolution_convert_fusion.1), channel_id=1, source_target_pairs={{0,2},{1,3},{2,0},{3,1},{4,6},{5,7},{6,4},{7,5},{8,10},{9,11},{10,... | collective-permute-start | bytes 393224 | tf_op jit(solution)/shard_map/ppermute | solution.py:194
  34.9 13.0 %collective-permute-start.8 = (bf16[2,128,256]{2,1,0:T(8,128)(2,1)S(1)}, bf16[2,128,256]{2,1,0:T(8,128)(2,1)S(1)}, u32[]{:S(2)}, u32[]{:S(2)}) collective-permute-start(bf16[2,128,256]{2,1,0:T(8,128)(2,1)S(1)} %convolution_convert_fusion.1), channel_id=1, source_target_pairs={{0,3},{1,2},{2,1},{3,0},{4,7},{5,6},{6,5},{7,4},{8,11},{9,10},{10,... | collective-permute-start | bytes 393224 | tf_op jit(solution)/shard_map/ppermute | solution.py:194
  44.6 12.0 %collective-permute-start.11 = (bf16[2,128,256]{2,1,0:T(8,128)(2,1)S(1)}, bf16[2,128,256]{2,1,0:T(8,128)(2,1)S(1)}, u32[]{:S(2)}, u32[]{:S(2)}) collective-permute-start(bf16[2,128,256]{2,1,0:T(8,128)(2,1)S(1)} %convolution_convert_fusion), channel_id=1, source_target_pairs={{0,2},{1,3},{2,0},{3,1},{4,6},{5,7},{6,4},{7,5},{8,10},{9,11},{10,... | collective-permute-start | bytes 393224 | tf_op jit(solution)/shard_map/ppermute | solution.py:194
  48.3 10.1 %collective-permute-start.9 = (f32[2,128,256]{2,1,0:T(8,128)S(1)}, f32[2,128,256]{2,1,0:T(8,128)S(1)}, u32[]{:S(2)}, u32[]{:S(2)}) collective-permute-start(f32[2,128,256]{2,1,0:T(8,128)S(1)} %multiply_add_fusion.4), channel_id=1, source_target_pairs={{0,4},{4,0},{1,5},{5,1},{2,6},{6,2},{3,7},{7,3},{8,12},{12,8},{9,1... | collective-permute-start | bytes 786440 | tf_op jit(solution)/shard_map/ppermute | solution.py:194
  59.0 13.0 %collective-permute-start.14 = (bf16[2,128,512]{2,1,0:T(8,128)(2,1)S(1)}, bf16[2,128,512]{2,1,0:T(8,128)(2,1)S(1)}, u32[]{:S(2)}, u32[]{:S(2)}) collective-permute-start(bf16[2,128,512]{2,1,0:T(8,128)(2,1)S(1)} %pad_maximum_fusion.8), channel_id=1, source_target_pairs={{0,8},{8,0},{16,24},{24,16},{1,9},{9,1},{17,25},{25,17},{2,10},{10... | collective-permute-start | bytes 786440 | tf_op jit(solution)/shard_map/ppermute | solution.py:194
  60.5 14.1 %collective-permute-start.15 = (bf16[2,128,512]{2,1,0:T(8,128)(2,1)S(1)}, bf16[2,128,512]{2,1,0:T(8,128)(2,1)}, u32[]{:S(2)}, u32[]{:S(2)}) collective-permute-start(bf16[2,128,512]{2,1,0:T(8,128)(2,1)S(1)} %pad_maximum_fusion.8), channel_id=1, source_target_pairs={{0,16},{8,24},{16,0},{24,8},{1,17},{9,25},{17,1},{25,9},{2,18},{10... | collective-permute-start | bytes 786440 | tf_op jit(solution)/shard_map/ppermute | solution.py:194
  61.0 13.6 %collective-permute-start.16 = (bf16[2,128,512]{2,1,0:T(8,128)(2,1)S(1)}, bf16[2,128,512]{2,1,0:T(8,128)(2,1)}, u32[]{:S(2)}, u32[]{:S(2)}) collective-permute-start(bf16[2,128,512]{2,1,0:T(8,128)(2,1)S(1)} %pad_maximum_fusion.8), channel_id=1, source_target_pairs={{0,24},{8,16},{16,8},{24,0},{1,25},{9,17},{17,9},{25,1},{2,26},{10... | collective-permute-start | bytes 786440 | tf_op jit(solution)/shard_map/ppermute | solution.py:194
  89.3 126.4 %reduce-scatter.4.cloned.1.call-start = ((), (), s32[]{:S(2)}) async-start(), calls=%async_computation.3 | async-start | bytes 327680
  89.3 14.1 %collective-permute-start.19 = (f32[128,384]{1,0:T(8,128)S(1)}, f32[128,384]{1,0:T(8,128)S(1)}, u32[]{:S(2)}, u32[]{:S(2)}) collective-permute-start(f32[128,384]{1,0:T(8,128)S(1)} %fusion.89), channel_id=1, source_target_pairs={{0,2},{1,3},{2,0},{3,1},{4,6},{5,7},{6,4},{7,5},{8,10},{9,11},{10,... | collective-permute-start | bytes 589832 | tf_op jit(solution)/shard_map/ppermute | solution.py:194
  141.4 9.2 %collective-permute-start.24 = (bf16[2,128,512]{2,1,0:T(8,128)(2,1)S(1)}, bf16[2,128,512]{2,1,0:T(8,128)(2,1)S(1)}, u32[]{:S(2)}, u32[]{:S(2)}) collective-permute-start(bf16[2,128,512]{2,1,0:T(8,128)(2,1)S(1)} %fusion.17), channel_id=1, source_target_pairs={{0,8},{8,0},{16,24},{24,16},{1,9},{9,1},{17,25},{25,17},{2,10},{10... | collective-permute-start | bytes 786440 | tf_op jit(solution)/shard_map/ppermute | solution.py:194
  142.2 13.8 %collective-permute-start.25 = (bf16[2,128,512]{2,1,0:T(8,128)(2,1)S(1)}, bf16[2,128,512]{2,1,0:T(8,128)(2,1)S(1)}, u32[]{:S(2)}, u32[]{:S(2)}) collective-permute-start(bf16[2,128,512]{2,1,0:T(8,128)(2,1)S(1)} %fusion.17), channel_id=1, source_target_pairs={{0,16},{8,24},{16,0},{24,8},{1,17},{9,25},{17,1},{25,9},{2,18},{10... | collective-permute-start | bytes 786440 | tf_op jit(solution)/shard_map/ppermute | solution.py:194
  143.7 12.3 %collective-permute-start.26 = (bf16[2,128,512]{2,1,0:T(8,128)(2,1)S(1)}, bf16[2,128,512]{2,1,0:T(8,128)(2,1)S(1)}, u32[]{:S(2)}, u32[]{:S(2)}) collective-permute-start(bf16[2,128,512]{2,1,0:T(8,128)(2,1)S(1)} %fusion.17), channel_id=1, source_target_pairs={{0,24},{8,16},{16,8},{24,0},{1,25},{9,17},{17,9},{25,1},{2,26},{10... | collective-permute-start | bytes 786440 | tf_op jit(solution)/shard_map/ppermute | solution.py:194
  170.9 13.4 %collective-permute-start.30 = (f32[64,1024]{0,1:T(8,128)S(1)}, f32[64,1024]{0,1:T(8,128)S(1)}, u32[]{:S(2)}, u32[]{:S(2)}) collective-permute-start(f32[64,1024]{0,1:T(8,128)S(1)} %constant_dynamic-slice_fusion), channel_id=1, source_target_pairs={{0,4},{4,0},{1,5},{5,1},{2,6},{6,2},{3,7},{7,3},{8,12},{12,8},{9,1... | collective-permute-start | bytes 786440 | tf_op jit(solution)/shard_map/ppermute | solution.py:194
  170.9 13.3 %collective-permute-start.29 = (f32[128,384]{1,0:T(8,128)S(1)}, f32[128,384]{1,0:T(8,128)S(1)}, u32[]{:S(2)}, u32[]{:S(2)}) collective-permute-start(f32[128,384]{1,0:T(8,128)S(1)} %fusion.88), channel_id=1, source_target_pairs={{0,2},{1,3},{2,0},{3,1},{4,6},{5,7},{6,4},{7,5},{8,10},{9,11},{10,... | collective-permute-start | bytes 589832 | tf_op jit(solution)/shard_map/ppermute | solution.py:194
  186.1 9.5 %collective-permute-start.33 = (f32[128,384]{1,0:T(8,128)S(1)}, f32[128,384]{1,0:T(8,128)S(1)}, u32[]{:S(2)}, u32[]{:S(2)}) collective-permute-start(f32[128,384]{1,0:T(8,128)S(1)} %add.382.refs_0_), channel_id=1, source_target_pairs={{0,24},{8,16},{16,8},{24,0},{1,25},{9,17},{17,9},{25,1},{2,26},{10... | collective-permute-start | bytes 589832 | tf_op jit(solution)/shard_map/ppermute | solution.py:194
  (43 other events, 217.4 us)
Sparse Core Ops, SparseCore 0:
  16.8 44.5 all-gather.2
  89.4 46.9 all-gather.4
  189.0 19.3 reduce-scatter.3

commit v10 on v9

--- a/solution.py
+++ b/solution.py
@@ -236,14 +236,6 @@
         collect(init_bf[:, :, c * width : (c + 1) * width], "tok") for c in range(CHUNKS)
     ]
     gathered_x = lax.all_gather(acts, "tok", axis=0, tiled=True)
-    full_x = jnp.concatenate(
-        [
-            lax.dynamic_slice_in_dim(gathered_x, (tok_pos ^ k) * tok_rows, tok_rows, 0)
-            for k in range(tok_count)
-        ],
-        axis=0,
-    ).reshape(total_tokens, owned, block_cols)
-
     def combine(rows_of_links, pieces, sources):
         total = 0.0
         for piece, source in zip(pieces, sources):
@@ -278,7 +270,14 @@
         ],
         axis=2,
     )
-    full_x, basis_bf = lax.optimization_barrier((full_x, basis_bf))
+    gathered_x, basis_bf = lax.optimization_barrier((gathered_x, basis_bf))
+    full_x = jnp.concatenate(
+        [
+            lax.dynamic_slice_in_dim(gathered_x, (tok_pos ^ k) * tok_rows, tok_rows, 0)
+            for k in range(tok_count)
+        ],
+        axis=0,
+    ).reshape(total_tokens, owned, block_cols)
 
     def image_of(mixed, basis_bf):
         full = jnp.concatenate(collect(mixed, "tok"), axis=1)
@@ -347,10 +346,7 @@
     image = image_of(mixed, basis_bf)
     def mix_seen(seen):
         seen = lax.all_gather(seen, ("gr", "gc"), axis=0, tiled=True)
-        total = 0.0
-        for j in range(seen.shape[0]):
-            total += own_links[:, j][:, None, None] * seen[j][None]
-        return total
+        return jnp.sum(own_links[:, :, None, None] * seen[None], axis=1)
 
     of_block, _, second = factor(image, False, seen_by(image))
     mixed = jnp.einsum("otr,osr->ots", second, of_block, precision=HIGH).astype(jnp.bfloat16)

time: 232 us -> 231 us (level)
  local copies, waits for them, and re-layouts: 21.2 us -> 13 us
  waiting for transfers between devices: 75.9 us -> 82.5 us
    ppermute x35, waiting for transfers between devices: 72.9 us -> 79.5 us  [swap(): lax.ppermute(value, axis, [(i, i ^ k) for i in range(lax.axis_size(axis))])]
    optimization_barrier x1 -> x0, local copies, waits for them, and re-layouts: 4.72 us -> none  [per_device(): full_x, basis_bf = lax.optimization_barrier((full_x, basis_bf))]
    reduce_sum x0 -> x1, other arithmetic: none -> 2.88 us  [mix_seen(): return jnp.sum(own_links[:, :, None, None] * seen[None], axis=1)]
    mul x1 -> x0, local copies, waits for them, and re-layouts: 2.84 us -> none  [mix_seen(): total += own_links[:, j][:, None, None] * seen[j][None]]
    reshape x1 -> x0, local copies, waits for them, and re-layouts: 2.79 us -> none  [per_device(): full_x = jnp.concatenate([lax.dynamic_slice_in_dim(gathered_x, (tok_pos ^...]
    concatenate x0 -> x1, local copies, waits for them, and re-layouts: none -> 2.62 us  [per_device(): jnp.concatenate([lax.dynamic_slice_in_dim(gathered_x, (tok_pos ^ k) * tok...]
  transfers between devices with their start and end apart: 38 -> 38, of which waited for: 22 -> 24; matrix products, arithmetic and copies ran while one was open for 15% -> 12% of each run, Pallas kernels for 17% -> 17%
where the time goes in v10:
time: 231 us
  waiting for transfers between devices  82.5 us (36%)
  starting transfers between devices  46 us (20%)
  Pallas kernels  38.8 us (17%)
  matrix products  25.2 us (11%)
  between operations  15.8 us (7%)
  local copies, waits for them, and re-layouts  13 us (6%)
  other arithmetic  9.78 us (4%)
    ppermute x35, waiting for transfers between devices, swap(): lax.ppermute(value, axis, [(i, i ^ k) for i in range(lax.axis_size(axis))])  79.5 us
    ppermute x35, starting transfers between devices, swap(): lax.ppermute(value, axis, [(i, i ^ k) for i in range(lax.axis_size(axis))])  45.8 us
    pallas_call x2, Pallas kernels, inverse_factor(): pl.pallas_call(functools.partial(factor_kernel, scale, exact), out_shape=...  38.8 us
    dot_general x2, matrix products, image_of(): jnp.einsum('tob,otr->obr', full_x, full, preferred_element_type=jnp.float32)  4.88 us
  transfers between devices with their start and end apart: 38, of which 24 were waited for; matrix products, arithmetic and copies ran while one was open for 12% of the time, Pallas kernels for 17%

profile of v10, /device:TPU:0, one launch (start us, length us, event | category | flops | bytes accessed | tf_op | source)
XLA Modules:
  0.0 231.0 jit_solution(4319176622107486912)
XLA Ops:
  8.6 4.0 %collective-permute-start.2 = (bf16[2,256,256]{2,1,0:T(8,128)(2,1)S(1)}, bf16[2,256,256]{2,1,0:T(8,128)(2,1)S(1)}, u32[]{:S(2)}, u32[]{:S(2)}) collective-permute-start(bf16[2,256,256]{2,1,0:T(8,128)(2,1)S(1)} %get-tuple-element.70), channel_id=1, source_target_pairs={{0,24},{8,16},{16,8},{24,0},{1,25},{9,17},{17,9},{25,1},{2,26},{10... | collective-permute-start | bytes 786440 | tf_op jit(solution)/shard_map/ppermute | solution.py:194
  13.2 2.8 %collective-permute-start.5 = (bf16[2,256,256]{2,1,0:T(8,128)(2,1)S(1)}, bf16[2,256,256]{2,1,0:T(8,128)(2,1)S(1)}, u32[]{:S(2)}, u32[]{:S(2)}) collective-permute-start(bf16[2,256,256]{2,1,0:T(8,128)(2,1)S(1)} %get-tuple-element.71), channel_id=1, source_target_pairs={{0,24},{8,16},{16,8},{24,0},{1,25},{9,17},{17,9},{25,1},{2,26},{10... | collective-permute-start | bytes 786440 | tf_op jit(solution)/shard_map/ppermute | solution.py:194
  31.4 4.4 %collective-permute-done.5 = bf16[2,256,256]{2,1,0:T(8,128)(2,1)S(1)} collective-permute-done((bf16[2,256,256]{2,1,0:T(8,128)(2,1)S(1)}, bf16[2,256,256]{2,1,0:T(8,128)(2,1)S(1)}, u32[]{:S(2)}, u32[]{:S(2)}) %collective-permute-start.5) | collective-permute-done | bytes 262176 | tf_op jit(solution)/shard_map/ppermute | solution.py:194
  35.8 3.6 %collective-permute-start.8 = (bf16[2,128,256]{2,1,0:T(8,128)(2,1)S(1)}, bf16[2,128,256]{2,1,0:T(8,128)(2,1)S(1)}, u32[]{:S(2)}, u32[]{:S(2)}) collective-permute-start(bf16[2,128,256]{2,1,0:T(8,128)(2,1)S(1)} %convolution_convert_fusion.1), channel_id=1, source_target_pairs={{0,3},{1,2},{2,1},{3,0},{4,7},{5,6},{6,5},{7,4},{8,11},{9,10},{10,... | collective-permute-start | bytes 393224 | tf_op jit(solution)/shard_map/ppermute | solution.py:194
  48.3 7.4 %collective-permute-done.11 = bf16[2,128,256]{2,1,0:T(8,128)(2,1)S(1)} collective-permute-done((bf16[2,128,256]{2,1,0:T(8,128)(2,1)S(1)}, bf16[2,128,256]{2,1,0:T(8,128)(2,1)S(1)}, u32[]{:S(2)}, u32[]{:S(2)}) %collective-permute-start.11) | collective-permute-done | bytes 131104 | tf_op jit(solution)/shard_map/ppermute | solution.py:194
  68.2 5.3 %collective-permute-done.15 = bf16[2,128,512]{2,1,0:T(8,128)(2,1)} collective-permute-done((bf16[2,128,512]{2,1,0:T(8,128)(2,1)S(1)}, bf16[2,128,512]{2,1,0:T(8,128)(2,1)}, u32[]{:S(2)}, u32[]{:S(2)}) %collective-permute-start.15) | collective-permute-done | bytes 262176 | tf_op jit(solution)/shard_map/ppermute | solution.py:194
  73.5 3.6 %multiply_add_fusion.1 = f32[2,1024,512]{2,1,0:T(8,128)S(1)} fusion(bf16[2,1024,512]{2,1,0:T(8,128)(2,1)} %maximum_maximum_fusion, bf16[512,2,1024]{0,2,1:T(8,128)(2,1)} %bitcast.113, bf16[2,128,512]{2,1,0:T(8,128)(2,1)S(1)} %collective-permute-done.16, bf16[2,128,512]{2,1,0:T(8,128)(2,1)} %collective-permute-done.15, ...), kind=kOutput, calls=%fused_computation.8 | convolution fusion | flops 1083179008 | bytes 9437184 | tf_op jit(solution)/shard_map/tob,otr->obr/dot_general | solution.py:284
  83.8 4.3 %collective-permute-done.18 = f32[128,384]{1,0:T(8,128)S(1)} collective-permute-done((f32[128,384]{1,0:T(8,128)S(1)}, f32[128,384]{1,0:T(8,128)S(1)}, u32[]{:S(2)}, u32[]{:S(2)}) %collective-permute-start.18) | collective-permute-done | bytes 196640 | tf_op jit(solution)/shard_map/ppermute | solution.py:194
  89.2 3.7 %collective-permute-start.19 = (f32[128,384]{1,0:T(8,128)S(1)}, f32[128,384]{1,0:T(8,128)S(1)}, u32[]{:S(2)}, u32[]{:S(2)}) collective-permute-start(f32[128,384]{1,0:T(8,128)S(1)} %fusion.89), channel_id=1, source_target_pairs={{0,2},{1,3},{2,0},{3,1},{4,6},{5,7},{6,4},{7,5},{8,10},{9,11},{10,... | collective-permute-start | bytes 589832 | tf_op jit(solution)/shard_map/ppermute | solution.py:194
  92.9 8.8 %collective-permute-done.19 = f32[128,384]{1,0:T(8,128)S(1)} collective-permute-done((f32[128,384]{1,0:T(8,128)S(1)}, f32[128,384]{1,0:T(8,128)S(1)}, u32[]{:S(2)}, u32[]{:S(2)}) %collective-permute-start.19) | collective-permute-done | bytes 196640 | tf_op jit(solution)/shard_map/ppermute | solution.py:194
  105.3 5.3 %collective-permute-done.22.refs_3_ = f32[128,384]{1,0:T(8,128)S(1)} collective-permute-done((f32[128,384]{1,0:T(8,128)S(1)}, f32[128,384]{1,0:T(8,128)S(1)}, u32[]{:S(2)}, u32[]{:S(2)}) %collective-permute-start.22) | collective-permute-done | bytes 196640 | tf_op jit(solution)/shard_map/ppermute | solution.py:194
  110.5 2.8 %collective-permute-done.21.refs_2_ = f32[128,384]{1,0:T(8,128)S(1)} collective-permute-done((f32[128,384]{1,0:T(8,128)S(1)}, f32[128,384]{1,0:T(8,128)S(1)}, u32[]{:S(2)}, u32[]{:S(2)}) %collective-permute-start.21) | collective-permute-done | bytes 196640 | tf_op jit(solution)/shard_map/ppermute | solution.py:194
  113.5 18.8 %inverse_factor.2 = f32[512,512]{1,0:T(8,128)S(1)} custom-call(s32[1]{0:T(128)} %bitcast.1.pos_ref, f32[128,384]{1,0:T(8,128)S(1)} %add.317.refs_0_, f32[128,384]{1,0:T(8,128)S(1)} %collective-permute-done.20.refs_1_, f32[128,384]{1,0:T(8,128)S(1)} %collective-permute-done.21.refs_2_, f32[128,384]{1,0:T(8,128)S(1)} %collective-permute-done.22.refs_3_), custom_call_target="tpu_custom_call" | custom-call | flops 12884901888 | bytes 2097152 | tf_op jit(solution)/shard_map/inverse_factor/pallas_call | solution.py:171
  134.0 3.0 %all-gather.5.cloned.1.call-done = f32[16,128,512]{2,1,0:T(8,128)} async-done(((f32[2,128,512]{2,1,0:T(8,128)}), f32[16,128,512]{2,1,0:T(8,128)}) %all-gather.5.cloned.1.call-update) | async-done | bytes 4194320 | tf_op jit(solution)/shard_map/all_gather | solution.py:348
  137.1 2.9 %multiply_reduce_fusion = f32[2,128,512]{2,1,0:T(8,128)S(1)} fusion(f32[16,128,512]{2,1,0:T(8,128)} %all-gather.5.cloned.1.call-done, f32[2,16]{1,0:T(2,128)S(1)} %constant_dynamic-slice_fusion.4), kind=kLoop, calls=%fused_computation | loop fusion | flops 4063232 | bytes 4718720 | tf_op jit(solution)/shard_map/reduce_sum | solution.py:349
  145.0 4.0 %fusion.12 = bf16[2,1024,512]{2,1,0:T(8,128)(2,1)S(1)} fusion(f32[2,1024,512]{2,1,0:T(8,128)S(1)} %copy-done.1, f32[1,512,512]{2,1,0:T(8,128)S(1)} %get-tuple-element.53, f32[1,512,512]{2,1,0:T(8,128)S(1)} %get-tuple-element.52), kind=kOutput, calls=%fused_computation.20 | convolution fusion | flops 3221749760 | bytes 8388608 | tf_op jit(solution)/shard_map/obr,osr->obs/dot_general | solution.py:353
  151.6 4.9 %collective-permute-done.25 = bf16[2,128,512]{2,1,0:T(8,128)(2,1)S(1)} collective-permute-done((bf16[2,128,512]{2,1,0:T(8,128)(2,1)S(1)}, bf16[2,128,512]{2,1,0:T(8,128)(2,1)S(1)}, u32[]{:S(2)}, u32[]{:S(2)}) %collective-permute-start.25) | collective-permute-done | bytes 262176 | tf_op jit(solution)/shard_map/ppermute | solution.py:194
  164.0 5.4 %collective-permute-done.28 = f32[128,384]{1,0:T(8,128)S(1)} collective-permute-done((f32[128,384]{1,0:T(8,128)S(1)}, f32[128,384]{1,0:T(8,128)S(1)}, u32[]{:S(2)}, u32[]{:S(2)}) %collective-permute-start.28) | collective-permute-done | bytes 196640 | tf_op jit(solution)/shard_map/ppermute | solution.py:194
  169.7 3.9 %collective-permute-start.29 = (f32[128,384]{1,0:T(8,128)S(1)}, f32[128,384]{1,0:T(8,128)S(1)}, u32[]{:S(2)}, u32[]{:S(2)}) collective-permute-start(f32[128,384]{1,0:T(8,128)S(1)} %fusion.88), channel_id=1, source_target_pairs={{0,2},{1,3},{2,0},{3,1},{4,6},{5,7},{6,4},{7,5},{8,10},{9,11},{10,... | collective-permute-start | bytes 589832 | tf_op jit(solution)/shard_map/ppermute | solution.py:194
  173.6 9.7 %collective-permute-done.29 = f32[128,384]{1,0:T(8,128)S(1)} collective-permute-done((f32[128,384]{1,0:T(8,128)S(1)}, f32[128,384]{1,0:T(8,128)S(1)}, u32[]{:S(2)}, u32[]{:S(2)}) %collective-permute-start.29) | collective-permute-done | bytes 196640 | tf_op jit(solution)/shard_map/ppermute | solution.py:194
  188.0 4.3 %collective-permute-done.33.refs_3_ = f32[128,384]{1,0:T(8,128)S(1)} collective-permute-done((f32[128,384]{1,0:T(8,128)S(1)}, f32[128,384]{1,0:T(8,128)S(1)}, u32[]{:S(2)}, u32[]{:S(2)}) %collective-permute-start.33) | collective-permute-done | bytes 196640 | tf_op jit(solution)/shard_map/ppermute | solution.py:194
  192.3 3.0 %collective-permute-done.32.refs_2_ = f32[128,384]{1,0:T(8,128)S(1)} collective-permute-done((f32[128,384]{1,0:T(8,128)S(1)}, f32[128,384]{1,0:T(8,128)S(1)}, u32[]{:S(2)}, u32[]{:S(2)}) %collective-permute-start.32) | collective-permute-done | bytes 196640 | tf_op jit(solution)/shard_map/ppermute | solution.py:194
  195.4 20.0 %inverse_factor.3 = f32[512,512]{1,0:T(8,128)S(1)} custom-call(s32[1]{0:T(128)} %bitcast.1.pos_ref, f32[128,384]{1,0:T(8,128)S(1)} %add.322.refs_0_, f32[128,384]{1,0:T(8,128)S(1)} %collective-permute-done.31.refs_1_, f32[128,384]{1,0:T(8,128)S(1)} %collective-permute-done.32.refs_2_, f32[128,384]{1,0:T(8,128)S(1)} %collective-permute-done.33.refs_3_), custom_call_target="tpu_custom_call" | custom-call | flops 12884901888 | bytes 2097152 | tf_op jit(solution)/shard_map/inverse_factor/pallas_call | solution.py:171
  221.1 3.4 %fusion.8 = f32[2,256,512]{2,1,0:T(8,128)} fusion(f32[1,512,512]{2,1,0:T(8,128)S(1)} %get-tuple-element.51, f32[1,512,512]{2,1,0:T(8,128)S(1)} %get-tuple-element.50, f32[2,1024,512]{2,1,0:T(8,128)} %copy-done.2, s32[]{:T(128)S(6)} %select_n.361), kind=kOutput, calls=%fused_computation.16 | convolution fusion | flops 805830656 | bytes 4194308 | tf_op jit(solution)/shard_map/obr,osr->obs/dot_general | solution.py:365
  (185 shorter events, 76.1 us)
Async XLA Ops:
  7.2 54.5 %all-gather.3.cloned.1.call-start = ((), (), s32[]{:S(2)}) async-start(), calls=%async_computation.1 | async-start | bytes 2621440 | tf_op jit(solution)/shard_map/all_gather | solution.py:238
  8.6 14.1 %collective-permute-start.2 = (bf16[2,256,256]{2,1,0:T(8,128)(2,1)S(1)}, bf16[2,256,256]{2,1,0:T(8,128)(2,1)S(1)}, u32[]{:S(2)}, u32[]{:S(2)}) collective-permute-start(bf16[2,256,256]{2,1,0:T(8,128)(2,1)S(1)} %get-tuple-element.70), channel_id=1, source_target_pairs={{0,24},{8,16},{16,8},{24,0},{1,25},{9,17},{17,9},{25,1},{2,26},{10... | collective-permute-start | bytes 786440 | tf_op jit(solution)/shard_map/ppermute | solution.py:194
  12.6 12.9 %collective-permute-start.1 = (bf16[2,256,256]{2,1,0:T(8,128)(2,1)S(1)}, bf16[2,256,256]{2,1,0:T(8,128)(2,1)S(1)}, u32[]{:S(2)}, u32[]{:S(2)}) collective-permute-start(bf16[2,256,256]{2,1,0:T(8,128)(2,1)S(1)} %get-tuple-element.70), channel_id=1, source_target_pairs={{0,16},{8,24},{16,0},{24,8},{1,17},{9,25},{17,1},{25,9},{2,18},{10... | collective-permute-start | bytes 786440 | tf_op jit(solution)/shard_map/ppermute | solution.py:194
  13.1 12.9 %collective-permute-start = (bf16[2,256,256]{2,1,0:T(8,128)(2,1)S(1)}, bf16[2,256,256]{2,1,0:T(8,128)(2,1)S(1)}, u32[]{:S(2)}, u32[]{:S(2)}) collective-permute-start(bf16[2,256,256]{2,1,0:T(8,128)(2,1)S(1)} %get-tuple-element.70), channel_id=1, source_target_pairs={{0,8},{8,0},{16,24},{24,16},{1,9},{9,1},{17,25},{25,17},{2,10},{10... | collective-permute-start | bytes 786440 | tf_op jit(solution)/shard_map/ppermute | solution.py:194
  13.2 22.6 %collective-permute-start.5 = (bf16[2,256,256]{2,1,0:T(8,128)(2,1)S(1)}, bf16[2,256,256]{2,1,0:T(8,128)(2,1)S(1)}, u32[]{:S(2)}, u32[]{:S(2)}) collective-permute-start(bf16[2,256,256]{2,1,0:T(8,128)(2,1)S(1)} %get-tuple-element.71), channel_id=1, source_target_pairs={{0,24},{8,16},{16,8},{24,0},{1,25},{9,17},{17,9},{25,1},{2,26},{10... | collective-permute-start | bytes 786440 | tf_op jit(solution)/shard_map/ppermute | solution.py:194
  16.1 25.1 %collective-permute-start.4 = (bf16[2,256,256]{2,1,0:T(8,128)(2,1)S(1)}, bf16[2,256,256]{2,1,0:T(8,128)(2,1)S(1)}, u32[]{:S(2)}, u32[]{:S(2)}) collective-permute-start(bf16[2,256,256]{2,1,0:T(8,128)(2,1)S(1)} %get-tuple-element.71), channel_id=1, source_target_pairs={{0,16},{8,24},{16,0},{24,8},{1,17},{9,25},{17,1},{25,9},{2,18},{10... | collective-permute-start | bytes 786440 | tf_op jit(solution)/shard_map/ppermute | solution.py:194
  16.6 120.4 %all-gather.5.cloned.1.call-start = ((), (), s32[]{:S(2)}) async-start(), calls=%async_computation.2 | async-start | bytes 4718592 | tf_op jit(solution)/shard_map/all_gather | solution.py:348
  22.7 19.0 %collective-permute-start.3 = (bf16[2,256,256]{2,1,0:T(8,128)(2,1)S(1)}, bf16[2,256,256]{2,1,0:T(8,128)(2,1)S(1)}, u32[]{:S(2)}, u32[]{:S(2)}) collective-permute-start(bf16[2,256,256]{2,1,0:T(8,128)(2,1)S(1)} %get-tuple-element.71), channel_id=1, source_target_pairs={{0,8},{8,0},{16,24},{24,16},{1,9},{9,1},{17,25},{25,17},{2,10},{10... | collective-permute-start | bytes 786440 | tf_op jit(solution)/shard_map/ppermute | solution.py:194
  27.2 20.4 %collective-permute-start.7 = (bf16[2,128,256]{2,1,0:T(8,128)(2,1)S(1)}, bf16[2,128,256]{2,1,0:T(8,128)(2,1)S(1)}, u32[]{:S(2)}, u32[]{:S(2)}) collective-permute-start(bf16[2,128,256]{2,1,0:T(8,128)(2,1)S(1)} %convolution_convert_fusion.1), channel_id=1, source_target_pairs={{0,2},{1,3},{2,0},{3,1},{4,6},{5,7},{6,4},{7,5},{8,10},{9,11},{10,... | collective-permute-start | bytes 393224 | tf_op jit(solution)/shard_map/ppermute | solution.py:194
  29.8 18.0 %collective-permute-start.6 = (bf16[2,128,256]{2,1,0:T(8,128)(2,1)S(1)}, bf16[2,128,256]{2,1,0:T(8,128)(2,1)S(1)}, u32[]{:S(2)}, u32[]{:S(2)}) collective-permute-start(bf16[2,128,256]{2,1,0:T(8,128)(2,1)S(1)} %convolution_convert_fusion.1), channel_id=1, source_target_pairs={{0,1},{1,0},{2,3},{3,2},{4,5},{5,4},{6,7},{7,6},{8,9},{9,8},{10,11... | collective-permute-start | bytes 393224 | tf_op jit(solution)/shard_map/ppermute | solution.py:194
  35.8 12.1 %collective-permute-start.8 = (bf16[2,128,256]{2,1,0:T(8,128)(2,1)S(1)}, bf16[2,128,256]{2,1,0:T(8,128)(2,1)S(1)}, u32[]{:S(2)}, u32[]{:S(2)}) collective-permute-start(bf16[2,128,256]{2,1,0:T(8,128)(2,1)S(1)} %convolution_convert_fusion.1), channel_id=1, source_target_pairs={{0,3},{1,2},{2,1},{3,0},{4,7},{5,6},{6,5},{7,4},{8,11},{9,10},{10,... | collective-permute-start | bytes 393224 | tf_op jit(solution)/shard_map/ppermute | solution.py:194
  42.9 12.8 %collective-permute-start.11 = (bf16[2,128,256]{2,1,0:T(8,128)(2,1)S(1)}, bf16[2,128,256]{2,1,0:T(8,128)(2,1)S(1)}, u32[]{:S(2)}, u32[]{:S(2)}) collective-permute-start(bf16[2,128,256]{2,1,0:T(8,128)(2,1)S(1)} %convolution_convert_fusion), channel_id=1, source_target_pairs={{0,2},{1,3},{2,0},{3,1},{4,6},{5,7},{6,4},{7,5},{8,10},{9,11},{10,... | collective-permute-start | bytes 393224 | tf_op jit(solution)/shard_map/ppermute | solution.py:194
  45.6 10.1 %collective-permute-start.10 = (bf16[2,128,256]{2,1,0:T(8,128)(2,1)S(1)}, bf16[2,128,256]{2,1,0:T(8,128)(2,1)S(1)}, u32[]{:S(2)}, u32[]{:S(2)}) collective-permute-start(bf16[2,128,256]{2,1,0:T(8,128)(2,1)S(1)} %convolution_convert_fusion), channel_id=1, source_target_pairs={{0,1},{1,0},{2,3},{3,2},{4,5},{5,4},{6,7},{7,6},{8,9},{9,8},{10,11... | collective-permute-start | bytes 393224 | tf_op jit(solution)/shard_map/ppermute | solution.py:194
  59.1 14.4 %collective-permute-start.15 = (bf16[2,128,512]{2,1,0:T(8,128)(2,1)S(1)}, bf16[2,128,512]{2,1,0:T(8,128)(2,1)}, u32[]{:S(2)}, u32[]{:S(2)}) collective-permute-start(bf16[2,128,512]{2,1,0:T(8,128)(2,1)S(1)} %pad_maximum_fusion.8), channel_id=1, source_target_pairs={{0,16},{8,24},{16,0},{24,8},{1,17},{9,25},{17,1},{25,9},{2,18},{10... | collective-permute-start | bytes 786440 | tf_op jit(solution)/shard_map/ppermute | solution.py:194
  61.1 12.4 %collective-permute-start.14 = (bf16[2,128,512]{2,1,0:T(8,128)(2,1)S(1)}, bf16[2,128,512]{2,1,0:T(8,128)(2,1)}, u32[]{:S(2)}, u32[]{:S(2)}) collective-permute-start(bf16[2,128,512]{2,1,0:T(8,128)(2,1)S(1)} %pad_maximum_fusion.8), channel_id=1, source_target_pairs={{0,8},{8,0},{16,24},{24,16},{1,9},{9,1},{17,25},{25,17},{2,10},{10... | collective-permute-start | bytes 786440 | tf_op jit(solution)/shard_map/ppermute | solution.py:194
  89.1 126.2 %reduce-scatter.4.cloned.1.call-start = ((), (), s32[]{:S(2)}) async-start(), calls=%async_computation.3 | async-start | bytes 327680
  89.2 12.5 %collective-permute-start.19 = (f32[128,384]{1,0:T(8,128)S(1)}, f32[128,384]{1,0:T(8,128)S(1)}, u32[]{:S(2)}, u32[]{:S(2)}) collective-permute-start(f32[128,384]{1,0:T(8,128)S(1)} %fusion.89), channel_id=1, source_target_pairs={{0,2},{1,3},{2,0},{3,1},{4,6},{5,7},{6,4},{7,5},{8,10},{9,11},{10,... | collective-permute-start | bytes 589832 | tf_op jit(solution)/shard_map/ppermute | solution.py:194
  103.1 10.3 %collective-permute-start.21 = (f32[128,384]{1,0:T(8,128)S(1)}, f32[128,384]{1,0:T(8,128)S(1)}, u32[]{:S(2)}, u32[]{:S(2)}) collective-permute-start(f32[128,384]{1,0:T(8,128)S(1)} %add.317.refs_0_), channel_id=1, source_target_pairs={{0,16},{8,24},{16,0},{24,8},{1,17},{9,25},{17,1},{25,9},{2,18},{10... | collective-permute-start | bytes 589832 | tf_op jit(solution)/shard_map/ppermute | solution.py:194
  141.4 10.2 %collective-permute-start.26 = (bf16[2,128,512]{2,1,0:T(8,128)(2,1)S(1)}, bf16[2,128,512]{2,1,0:T(8,128)(2,1)S(1)}, u32[]{:S(2)}, u32[]{:S(2)}) collective-permute-start(bf16[2,128,512]{2,1,0:T(8,128)(2,1)S(1)} %fusion.17), channel_id=1, source_target_pairs={{0,24},{8,16},{16,8},{24,0},{1,25},{9,17},{17,9},{25,1},{2,26},{10... | collective-permute-start | bytes 786440 | tf_op jit(solution)/shard_map/ppermute | solution.py:194
  143.7 12.8 %collective-permute-start.25 = (bf16[2,128,512]{2,1,0:T(8,128)(2,1)S(1)}, bf16[2,128,512]{2,1,0:T(8,128)(2,1)S(1)}, u32[]{:S(2)}, u32[]{:S(2)}) collective-permute-start(bf16[2,128,512]{2,1,0:T(8,128)(2,1)S(1)} %fusion.17), channel_id=1, source_target_pairs={{0,16},{8,24},{16,0},{24,8},{1,17},{9,25},{17,1},{25,9},{2,18},{10... | collective-permute-start | bytes 786440 | tf_op jit(solution)/shard_map/ppermute | solution.py:194
  144.4 12.2 %collective-permute-start.24 = (bf16[2,128,512]{2,1,0:T(8,128)(2,1)S(1)}, bf16[2,128,512]{2,1,0:T(8,128)(2,1)S(1)}, u32[]{:S(2)}, u32[]{:S(2)}) collective-permute-start(bf16[2,128,512]{2,1,0:T(8,128)(2,1)S(1)} %fusion.17), channel_id=1, source_target_pairs={{0,8},{8,0},{16,24},{24,16},{1,9},{9,1},{17,25},{25,17},{2,10},{10... | collective-permute-start | bytes 786440 | tf_op jit(solution)/shard_map/ppermute | solution.py:194
  169.6 13.7 %collective-permute-start.30 = (f32[64,1024]{0,1:T(8,128)S(1)}, f32[64,1024]{0,1:T(8,128)S(1)}, u32[]{:S(2)}, u32[]{:S(2)}) collective-permute-start(f32[64,1024]{0,1:T(8,128)S(1)} %constant_dynamic-slice_fusion), channel_id=1, source_target_pairs={{0,4},{4,0},{1,5},{5,1},{2,6},{6,2},{3,7},{7,3},{8,12},{12,8},{9,1... | collective-permute-start | bytes 786440 | tf_op jit(solution)/shard_map/ppermute | solution.py:194
  169.7 13.6 %collective-permute-start.29 = (f32[128,384]{1,0:T(8,128)S(1)}, f32[128,384]{1,0:T(8,128)S(1)}, u32[]{:S(2)}, u32[]{:S(2)}) collective-permute-start(f32[128,384]{1,0:T(8,128)S(1)} %fusion.88), channel_id=1, source_target_pairs={{0,2},{1,3},{2,0},{3,1},{4,6},{5,7},{6,4},{7,5},{8,10},{9,11},{10,... | collective-permute-start | bytes 589832 | tf_op jit(solution)/shard_map/ppermute | solution.py:194
  184.8 10.6 %collective-permute-start.32 = (f32[128,384]{1,0:T(8,128)S(1)}, f32[128,384]{1,0:T(8,128)S(1)}, u32[]{:S(2)}, u32[]{:S(2)}) collective-permute-start(f32[128,384]{1,0:T(8,128)S(1)} %add.322.refs_0_), channel_id=1, source_target_pairs={{0,16},{8,24},{16,0},{24,8},{1,17},{9,25},{17,1},{25,9},{2,18},{10... | collective-permute-start | bytes 589832 | tf_op jit(solution)/shard_map/ppermute | solution.py:194
  (42 other events, 206.0 us)
Sparse Core Ops, SparseCore 0:
  16.7 44.5 all-gather.2
  89.2 47.7 all-gather.4
  188.1 19.8 reduce-scatter.3

commit v11 on v10

--- a/solution.py
+++ b/solution.py
@@ -337,10 +337,12 @@
         other = swap(own, "gr", 1)
         if not last:
             other, beside = lax.optimization_barrier((other, beside))
+        of_group = [jnp.where(gr_pos == g, own, other) for g in range(groups)]
+        if last:
+            return (own, other), of_group, beside
         of_block = jnp.stack(
             [jnp.where(own_groups[o] == gr_pos, own, other) for o in range(owned)]
         )
-        of_group = [jnp.where(gr_pos == g, own, other) for g in range(groups)]
         return of_block, of_group, beside
 
     image = image_of(mixed, basis_bf)
@@ -362,7 +364,10 @@
     )
     of_block, of_group, placed = factor(image, True, placed)
     rows = lax.dynamic_slice_in_dim(image, tok_pos * slice_rows, slice_rows, 1)
-    basis = jnp.einsum("obr,osr->obs", rows, of_block, precision=HIGH)
+    by_own, by_other = [
+        jnp.einsum("obr,sr->obs", rows, inverse, precision=HIGH) for inverse in of_block
+    ]
+    basis = jnp.where((own_groups == gr_pos)[:, None, None], by_own, by_other)
     latent = jnp.concatenate(
         [
             jnp.einsum(

time: 231 us -> 231 us (level)
  waiting for transfers between devices: 82.5 us -> 80 us
    ppermute x35, waiting for transfers between devices: 79.5 us -> 77 us  [swap(): lax.ppermute(value, axis, [(i, i ^ k) for i in range(lax.axis_size(axis))])]
    dot_general x1 -> x2, matrix products: 3.36 us -> 5.5 us  [per_device(): jnp.einsum('obr,sr->obs', rows, inverse, precision=HIGH)]
  transfers between devices with their start and end apart: 38 -> 38, of which waited for: 24 -> 24; matrix products, arithmetic and copies ran while one was open for 12% -> 13% of each run, Pallas kernels for 17% -> 17%
where the time goes in v11:
time: 231 us
  waiting for transfers between devices  80 us (35%)
  starting transfers between devices  46.2 us (20%)
  Pallas kernels  38.8 us (17%)
  matrix products  27.4 us (12%)
  between operations  15.9 us (7%)
  local copies, waits for them, and re-layouts  13 us (6%)
  other arithmetic  9.56 us (4%)
    ppermute x35, waiting for transfers between devices, swap(): lax.ppermute(value, axis, [(i, i ^ k) for i in range(lax.axis_size(axis))])  77 us
    ppermute x35, starting transfers between devices, swap(): lax.ppermute(value, axis, [(i, i ^ k) for i in range(lax.axis_size(axis))])  46.1 us
    pallas_call x2, Pallas kernels, inverse_factor(): pl.pallas_call(functools.partial(factor_kernel, scale, exact), out_shape=...  38.8 us
    dot_general x2, matrix products, per_device(): jnp.einsum('obr,sr->obs', rows, inverse, precision=HIGH)  5.5 us
    dot_general x2, matrix products, image_of(): jnp.einsum('tob,otr->obr', full_x, full, preferred_element_type=jnp.float32)  4.88 us
  transfers between devices with their start and end apart: 38, of which 24 were waited for; matrix products, arithmetic and copies ran while one was open for 13% of the time, Pallas kernels for 17%

profile of v11, /device:TPU:0, one launch (start us, length us, event | category | flops | bytes accessed | tf_op | source)
XLA Modules:
  0.0 230.8 jit_solution(12763699130629765910)
XLA Ops:
  8.6 4.0 %collective-permute-start.2 = (bf16[2,256,256]{2,1,0:T(8,128)(2,1)S(1)}, bf16[2,256,256]{2,1,0:T(8,128)(2,1)S(1)}, u32[]{:S(2)}, u32[]{:S(2)}) collective-permute-start(bf16[2,256,256]{2,1,0:T(8,128)(2,1)S(1)} %get-tuple-element.70), channel_id=1, source_target_pairs={{0,24},{8,16},{16,8},{24,0},{1,25},{9,17},{17,9},{25,1},{2,26},{10... | collective-permute-start | bytes 786440 | tf_op jit(solution)/shard_map/ppermute | solution.py:194
  13.2 2.8 %collective-permute-start.5 = (bf16[2,256,256]{2,1,0:T(8,128)(2,1)S(1)}, bf16[2,256,256]{2,1,0:T(8,128)(2,1)S(1)}, u32[]{:S(2)}, u32[]{:S(2)}) collective-permute-start(bf16[2,256,256]{2,1,0:T(8,128)(2,1)S(1)} %get-tuple-element.71), channel_id=1, source_target_pairs={{0,24},{8,16},{16,8},{24,0},{1,25},{9,17},{17,9},{25,1},{2,26},{10... | collective-permute-start | bytes 786440 | tf_op jit(solution)/shard_map/ppermute | solution.py:194
  31.4 4.4 %collective-permute-done.5 = bf16[2,256,256]{2,1,0:T(8,128)(2,1)S(1)} collective-permute-done((bf16[2,256,256]{2,1,0:T(8,128)(2,1)S(1)}, bf16[2,256,256]{2,1,0:T(8,128)(2,1)S(1)}, u32[]{:S(2)}, u32[]{:S(2)}) %collective-permute-start.5) | collective-permute-done | bytes 262176 | tf_op jit(solution)/shard_map/ppermute | solution.py:194
  35.8 3.6 %collective-permute-start.8 = (bf16[2,128,256]{2,1,0:T(8,128)(2,1)S(1)}, bf16[2,128,256]{2,1,0:T(8,128)(2,1)S(1)}, u32[]{:S(2)}, u32[]{:S(2)}) collective-permute-start(bf16[2,128,256]{2,1,0:T(8,128)(2,1)S(1)} %convolution_convert_fusion.1), channel_id=1, source_target_pairs={{0,3},{1,2},{2,1},{3,0},{4,7},{5,6},{6,5},{7,4},{8,11},{9,10},{10,... | collective-permute-start | bytes 393224 | tf_op jit(solution)/shard_map/ppermute | solution.py:194
  48.3 7.4 %collective-permute-done.11 = bf16[2,128,256]{2,1,0:T(8,128)(2,1)S(1)} collective-permute-done((bf16[2,128,256]{2,1,0:T(8,128)(2,1)S(1)}, bf16[2,128,256]{2,1,0:T(8,128)(2,1)S(1)}, u32[]{:S(2)}, u32[]{:S(2)}) %collective-permute-start.11) | collective-permute-done | bytes 131104 | tf_op jit(solution)/shard_map/ppermute | solution.py:194
  68.2 5.3 %collective-permute-done.15 = bf16[2,128,512]{2,1,0:T(8,128)(2,1)} collective-permute-done((bf16[2,128,512]{2,1,0:T(8,128)(2,1)S(1)}, bf16[2,128,512]{2,1,0:T(8,128)(2,1)}, u32[]{:S(2)}, u32[]{:S(2)}) %collective-permute-start.15) | collective-permute-done | bytes 262176 | tf_op jit(solution)/shard_map/ppermute | solution.py:194
  73.5 3.6 %multiply_add_fusion.1 = f32[2,1024,512]{2,1,0:T(8,128)S(1)} fusion(bf16[2,1024,512]{2,1,0:T(8,128)(2,1)} %maximum_maximum_fusion, bf16[512,2,1024]{0,2,1:T(8,128)(2,1)} %bitcast.115, bf16[2,128,512]{2,1,0:T(8,128)(2,1)S(1)} %collective-permute-done.16, bf16[2,128,512]{2,1,0:T(8,128)(2,1)} %collective-permute-done.15, ...), kind=kOutput, calls=%fused_computation.8 | convolution fusion | flops 1083179008 | bytes 9437184 | tf_op jit(solution)/shard_map/tob,otr->obr/dot_general | solution.py:284
  83.8 4.3 %collective-permute-done.18 = f32[128,384]{1,0:T(8,128)S(1)} collective-permute-done((f32[128,384]{1,0:T(8,128)S(1)}, f32[128,384]{1,0:T(8,128)S(1)}, u32[]{:S(2)}, u32[]{:S(2)}) %collective-permute-start.18) | collective-permute-done | bytes 196640 | tf_op jit(solution)/shard_map/ppermute | solution.py:194
  89.2 3.7 %collective-permute-start.19 = (f32[128,384]{1,0:T(8,128)S(1)}, f32[128,384]{1,0:T(8,128)S(1)}, u32[]{:S(2)}, u32[]{:S(2)}) collective-permute-start(f32[128,384]{1,0:T(8,128)S(1)} %fusion.89), channel_id=1, source_target_pairs={{0,2},{1,3},{2,0},{3,1},{4,6},{5,7},{6,4},{7,5},{8,10},{9,11},{10,... | collective-permute-start | bytes 589832 | tf_op jit(solution)/shard_map/ppermute | solution.py:194
  92.9 8.8 %collective-permute-done.19 = f32[128,384]{1,0:T(8,128)S(1)} collective-permute-done((f32[128,384]{1,0:T(8,128)S(1)}, f32[128,384]{1,0:T(8,128)S(1)}, u32[]{:S(2)}, u32[]{:S(2)}) %collective-permute-start.19) | collective-permute-done | bytes 196640 | tf_op jit(solution)/shard_map/ppermute | solution.py:194
  105.3 5.3 %collective-permute-done.22.refs_3_ = f32[128,384]{1,0:T(8,128)S(1)} collective-permute-done((f32[128,384]{1,0:T(8,128)S(1)}, f32[128,384]{1,0:T(8,128)S(1)}, u32[]{:S(2)}, u32[]{:S(2)}) %collective-permute-start.22) | collective-permute-done | bytes 196640 | tf_op jit(solution)/shard_map/ppermute | solution.py:194
  110.5 2.8 %collective-permute-done.21.refs_2_ = f32[128,384]{1,0:T(8,128)S(1)} collective-permute-done((f32[128,384]{1,0:T(8,128)S(1)}, f32[128,384]{1,0:T(8,128)S(1)}, u32[]{:S(2)}, u32[]{:S(2)}) %collective-permute-start.21) | collective-permute-done | bytes 196640 | tf_op jit(solution)/shard_map/ppermute | solution.py:194
  113.5 18.8 %inverse_factor.2 = f32[512,512]{1,0:T(8,128)S(1)} custom-call(s32[1]{0:T(128)} %bitcast.1.pos_ref, f32[128,384]{1,0:T(8,128)S(1)} %add.317.refs_0_, f32[128,384]{1,0:T(8,128)S(1)} %collective-permute-done.20.refs_1_, f32[128,384]{1,0:T(8,128)S(1)} %collective-permute-done.21.refs_2_, f32[128,384]{1,0:T(8,128)S(1)} %collective-permute-done.22.refs_3_), custom_call_target="tpu_custom_call" | custom-call | flops 12884901888 | bytes 2097152 | tf_op jit(solution)/shard_map/inverse_factor/pallas_call | solution.py:171
  134.2 2.9 %all-gather.5.cloned.1.call-done = f32[16,128,512]{2,1,0:T(8,128)} async-done(((f32[2,128,512]{2,1,0:T(8,128)}), f32[16,128,512]{2,1,0:T(8,128)}) %all-gather.5.cloned.1.call-update) | async-done | bytes 4194320 | tf_op jit(solution)/shard_map/all_gather | solution.py:350
  137.1 2.9 %multiply_reduce_fusion = f32[2,128,512]{2,1,0:T(8,128)S(1)} fusion(f32[16,128,512]{2,1,0:T(8,128)} %all-gather.5.cloned.1.call-done, f32[2,16]{1,0:T(2,128)S(1)} %constant_dynamic-slice_fusion.4), kind=kLoop, calls=%fused_computation | loop fusion | flops 4063232 | bytes 4718720 | tf_op jit(solution)/shard_map/reduce_sum | solution.py:351
  145.0 4.0 %fusion.8 = bf16[2,1024,512]{2,1,0:T(8,128)(2,1)S(1)} fusion(f32[2,1024,512]{2,1,0:T(8,128)S(1)} %copy-done.1, f32[1,512,512]{2,1,0:T(8,128)S(1)} %get-tuple-element.53, f32[1,512,512]{2,1,0:T(8,128)S(1)} %get-tuple-element.52), kind=kOutput, calls=%fused_computation.16 | convolution fusion | flops 3221749760 | bytes 8388608 | tf_op jit(solution)/shard_map/obr,osr->obs/dot_general | solution.py:355
  151.6 4.9 %collective-permute-done.25 = bf16[2,128,512]{2,1,0:T(8,128)(2,1)S(1)} collective-permute-done((bf16[2,128,512]{2,1,0:T(8,128)(2,1)S(1)}, bf16[2,128,512]{2,1,0:T(8,128)(2,1)S(1)}, u32[]{:S(2)}, u32[]{:S(2)}) %collective-permute-start.25) | collective-permute-done | bytes 262176 | tf_op jit(solution)/shard_map/ppermute | solution.py:194
  164.1 5.3 %collective-permute-done.28 = f32[128,384]{1,0:T(8,128)S(1)} collective-permute-done((f32[128,384]{1,0:T(8,128)S(1)}, f32[128,384]{1,0:T(8,128)S(1)}, u32[]{:S(2)}, u32[]{:S(2)}) %collective-permute-start.28) | collective-permute-done | bytes 196640 | tf_op jit(solution)/shard_map/ppermute | solution.py:194
  169.7 4.0 %collective-permute-start.29 = (f32[128,384]{1,0:T(8,128)S(1)}, f32[128,384]{1,0:T(8,128)S(1)}, u32[]{:S(2)}, u32[]{:S(2)}) collective-permute-start(f32[128,384]{1,0:T(8,128)S(1)} %fusion.88), channel_id=1, source_target_pairs={{0,2},{1,3},{2,0},{3,1},{4,6},{5,7},{6,4},{7,5},{8,10},{9,11},{10,... | collective-permute-start | bytes 589832 | tf_op jit(solution)/shard_map/ppermute | solution.py:194
  173.6 9.7 %collective-permute-done.29 = f32[128,384]{1,0:T(8,128)S(1)} collective-permute-done((f32[128,384]{1,0:T(8,128)S(1)}, f32[128,384]{1,0:T(8,128)S(1)}, u32[]{:S(2)}, u32[]{:S(2)}) %collective-permute-start.29) | collective-permute-done | bytes 196640 | tf_op jit(solution)/shard_map/ppermute | solution.py:194
  188.1 4.3 %collective-permute-done.33.refs_3_ = f32[128,384]{1,0:T(8,128)S(1)} collective-permute-done((f32[128,384]{1,0:T(8,128)S(1)}, f32[128,384]{1,0:T(8,128)S(1)}, u32[]{:S(2)}, u32[]{:S(2)}) %collective-permute-start.33) | collective-permute-done | bytes 196640 | tf_op jit(solution)/shard_map/ppermute | solution.py:194
  192.4 3.0 %collective-permute-done.32.refs_2_ = f32[128,384]{1,0:T(8,128)S(1)} collective-permute-done((f32[128,384]{1,0:T(8,128)S(1)}, f32[128,384]{1,0:T(8,128)S(1)}, u32[]{:S(2)}, u32[]{:S(2)}) %collective-permute-start.32) | collective-permute-done | bytes 196640 | tf_op jit(solution)/shard_map/ppermute | solution.py:194
  195.5 20.0 %inverse_factor.3 = f32[512,512]{1,0:T(8,128)S(1)} custom-call(s32[1]{0:T(128)} %bitcast.1.pos_ref, f32[128,384]{1,0:T(8,128)S(1)} %add.322.refs_0_, f32[128,384]{1,0:T(8,128)S(1)} %collective-permute-done.31.refs_1_, f32[128,384]{1,0:T(8,128)S(1)} %collective-permute-done.32.refs_2_, f32[128,384]{1,0:T(8,128)S(1)} %collective-permute-done.33.refs_3_), custom_call_target="tpu_custom_call" | custom-call | flops 12884901888 | bytes 2097152 | tf_op jit(solution)/shard_map/inverse_factor/pallas_call | solution.py:171
  221.0 3.2 %convolution_select_fusion = f32[2,256,512]{2,1,0:T(8,128)} fusion(f32[2,256,512]{2,1,0:T(8,128)S(1)} %fusion.45, f32[512,512]{1,0:T(8,128)S(1)} %collective-permute-done.34, f32[2,1024,512]{2,1,0:T(8,128)} %copy-done.2, s32[]{:T(128)S(6)} %select_n.357, pred[2]{0:T(512)(128)(4,1)S(1)} %copy-done.26), kind=kOutput, calls=%fused_computation.18 | convolution fusion | flops 805568512 | bytes 4194310 | tf_op jit(solution)/shard_map/obr,sr->obs/dot_general | solution.py:368
  (187 shorter events, 76.0 us)
Async XLA Ops:
  7.2 54.5 %all-gather.3.cloned.1.call-start = ((), (), s32[]{:S(2)}) async-start(), calls=%async_computation.1 | async-start | bytes 2621440 | tf_op jit(solution)/shard_map/all_gather | solution.py:238
  8.6 14.1 %collective-permute-start.2 = (bf16[2,256,256]{2,1,0:T(8,128)(2,1)S(1)}, bf16[2,256,256]{2,1,0:T(8,128)(2,1)S(1)}, u32[]{:S(2)}, u32[]{:S(2)}) collective-permute-start(bf16[2,256,256]{2,1,0:T(8,128)(2,1)S(1)} %get-tuple-element.70), channel_id=1, source_target_pairs={{0,24},{8,16},{16,8},{24,0},{1,25},{9,17},{17,9},{25,1},{2,26},{10... | collective-permute-start | bytes 786440 | tf_op jit(solution)/shard_map/ppermute | solution.py:194
  12.6 12.9 %collective-permute-start.1 = (bf16[2,256,256]{2,1,0:T(8,128)(2,1)S(1)}, bf16[2,256,256]{2,1,0:T(8,128)(2,1)S(1)}, u32[]{:S(2)}, u32[]{:S(2)}) collective-permute-start(bf16[2,256,256]{2,1,0:T(8,128)(2,1)S(1)} %get-tuple-element.70), channel_id=1, source_target_pairs={{0,16},{8,24},{16,0},{24,8},{1,17},{9,25},{17,1},{25,9},{2,18},{10... | collective-permute-start | bytes 786440 | tf_op jit(solution)/shard_map/ppermute | solution.py:194
  13.1 12.9 %collective-permute-start = (bf16[2,256,256]{2,1,0:T(8,128)(2,1)S(1)}, bf16[2,256,256]{2,1,0:T(8,128)(2,1)S(1)}, u32[]{:S(2)}, u32[]{:S(2)}) collective-permute-start(bf16[2,256,256]{2,1,0:T(8,128)(2,1)S(1)} %get-tuple-element.70), channel_id=1, source_target_pairs={{0,8},{8,0},{16,24},{24,16},{1,9},{9,1},{17,25},{25,17},{2,10},{10... | collective-permute-start | bytes 786440 | tf_op jit(solution)/shard_map/ppermute | solution.py:194
  13.2 22.6 %collective-permute-start.5 = (bf16[2,256,256]{2,1,0:T(8,128)(2,1)S(1)}, bf16[2,256,256]{2,1,0:T(8,128)(2,1)S(1)}, u32[]{:S(2)}, u32[]{:S(2)}) collective-permute-start(bf16[2,256,256]{2,1,0:T(8,128)(2,1)S(1)} %get-tuple-element.71), channel_id=1, source_target_pairs={{0,24},{8,16},{16,8},{24,0},{1,25},{9,17},{17,9},{25,1},{2,26},{10... | collective-permute-start | bytes 786440 | tf_op jit(solution)/shard_map/ppermute | solution.py:194
  16.1 25.1 %collective-permute-start.4 = (bf16[2,256,256]{2,1,0:T(8,128)(2,1)S(1)}, bf16[2,256,256]{2,1,0:T(8,128)(2,1)S(1)}, u32[]{:S(2)}, u32[]{:S(2)}) collective-permute-start(bf16[2,256,256]{2,1,0:T(8,128)(2,1)S(1)} %get-tuple-element.71), channel_id=1, source_target_pairs={{0,16},{8,24},{16,0},{24,8},{1,17},{9,25},{17,1},{25,9},{2,18},{10... | collective-permute-start | bytes 786440 | tf_op jit(solution)/shard_map/ppermute | solution.py:194
  16.6 120.4 %all-gather.5.cloned.1.call-start = ((), (), s32[]{:S(2)}) async-start(), calls=%async_computation.2 | async-start | bytes 4718592 | tf_op jit(solution)/shard_map/all_gather | solution.py:350
  22.7 19.0 %collective-permute-start.3 = (bf16[2,256,256]{2,1,0:T(8,128)(2,1)S(1)}, bf16[2,256,256]{2,1,0:T(8,128)(2,1)S(1)}, u32[]{:S(2)}, u32[]{:S(2)}) collective-permute-start(bf16[2,256,256]{2,1,0:T(8,128)(2,1)S(1)} %get-tuple-element.71), channel_id=1, source_target_pairs={{0,8},{8,0},{16,24},{24,16},{1,9},{9,1},{17,25},{25,17},{2,10},{10... | collective-permute-start | bytes 786440 | tf_op jit(solution)/shard_map/ppermute | solution.py:194
  27.2 20.4 %collective-permute-start.7 = (bf16[2,128,256]{2,1,0:T(8,128)(2,1)S(1)}, bf16[2,128,256]{2,1,0:T(8,128)(2,1)S(1)}, u32[]{:S(2)}, u32[]{:S(2)}) collective-permute-start(bf16[2,128,256]{2,1,0:T(8,128)(2,1)S(1)} %convolution_convert_fusion.1), channel_id=1, source_target_pairs={{0,2},{1,3},{2,0},{3,1},{4,6},{5,7},{6,4},{7,5},{8,10},{9,11},{10,... | collective-permute-start | bytes 393224 | tf_op jit(solution)/shard_map/ppermute | solution.py:194
  29.8 18.0 %collective-permute-start.6 = (bf16[2,128,256]{2,1,0:T(8,128)(2,1)S(1)}, bf16[2,128,256]{2,1,0:T(8,128)(2,1)S(1)}, u32[]{:S(2)}, u32[]{:S(2)}) collective-permute-start(bf16[2,128,256]{2,1,0:T(8,128)(2,1)S(1)} %convolution_convert_fusion.1), channel_id=1, source_target_pairs={{0,1},{1,0},{2,3},{3,2},{4,5},{5,4},{6,7},{7,6},{8,9},{9,8},{10,11... | collective-permute-start | bytes 393224 | tf_op jit(solution)/shard_map/ppermute | solution.py:194
  35.8 12.1 %collective-permute-start.8 = (bf16[2,128,256]{2,1,0:T(8,128)(2,1)S(1)}, bf16[2,128,256]{2,1,0:T(8,128)(2,1)S(1)}, u32[]{:S(2)}, u32[]{:S(2)}) collective-permute-start(bf16[2,128,256]{2,1,0:T(8,128)(2,1)S(1)} %convolution_convert_fusion.1), channel_id=1, source_target_pairs={{0,3},{1,2},{2,1},{3,0},{4,7},{5,6},{6,5},{7,4},{8,11},{9,10},{10,... | collective-permute-start | bytes 393224 | tf_op jit(solution)/shard_map/ppermute | solution.py:194
  42.9 12.8 %collective-permute-start.11 = (bf16[2,128,256]{2,1,0:T(8,128)(2,1)S(1)}, bf16[2,128,256]{2,1,0:T(8,128)(2,1)S(1)}, u32[]{:S(2)}, u32[]{:S(2)}) collective-permute-start(bf16[2,128,256]{2,1,0:T(8,128)(2,1)S(1)} %convolution_convert_fusion), channel_id=1, source_target_pairs={{0,2},{1,3},{2,0},{3,1},{4,6},{5,7},{6,4},{7,5},{8,10},{9,11},{10,... | collective-permute-start | bytes 393224 | tf_op jit(solution)/shard_map/ppermute | solution.py:194
  45.6 10.1 %collective-permute-start.10 = (bf16[2,128,256]{2,1,0:T(8,128)(2,1)S(1)}, bf16[2,128,256]{2,1,0:T(8,128)(2,1)S(1)}, u32[]{:S(2)}, u32[]{:S(2)}) collective-permute-start(bf16[2,128,256]{2,1,0:T(8,128)(2,1)S(1)} %convolution_convert_fusion), channel_id=1, source_target_pairs={{0,1},{1,0},{2,3},{3,2},{4,5},{5,4},{6,7},{7,6},{8,9},{9,8},{10,11... | collective-permute-start | bytes 393224 | tf_op jit(solution)/shard_map/ppermute | solution.py:194
  59.1 14.4 %collective-permute-start.15 = (bf16[2,128,512]{2,1,0:T(8,128)(2,1)S(1)}, bf16[2,128,512]{2,1,0:T(8,128)(2,1)}, u32[]{:S(2)}, u32[]{:S(2)}) collective-permute-start(bf16[2,128,512]{2,1,0:T(8,128)(2,1)S(1)} %pad_maximum_fusion.8), channel_id=1, source_target_pairs={{0,16},{8,24},{16,0},{24,8},{1,17},{9,25},{17,1},{25,9},{2,18},{10... | collective-permute-start | bytes 786440 | tf_op jit(solution)/shard_map/ppermute | solution.py:194
  61.1 12.4 %collective-permute-start.14 = (bf16[2,128,512]{2,1,0:T(8,128)(2,1)S(1)}, bf16[2,128,512]{2,1,0:T(8,128)(2,1)}, u32[]{:S(2)}, u32[]{:S(2)}) collective-permute-start(bf16[2,128,512]{2,1,0:T(8,128)(2,1)S(1)} %pad_maximum_fusion.8), channel_id=1, source_target_pairs={{0,8},{8,0},{16,24},{24,16},{1,9},{9,1},{17,25},{25,17},{2,10},{10... | collective-permute-start | bytes 786440 | tf_op jit(solution)/shard_map/ppermute | solution.py:194
  89.1 126.4 %reduce-scatter.4.cloned.1.call-start = ((), (), s32[]{:S(2)}) async-start(), calls=%async_computation.3 | async-start | bytes 327680
  89.2 12.5 %collective-permute-start.19 = (f32[128,384]{1,0:T(8,128)S(1)}, f32[128,384]{1,0:T(8,128)S(1)}, u32[]{:S(2)}, u32[]{:S(2)}) collective-permute-start(f32[128,384]{1,0:T(8,128)S(1)} %fusion.89), channel_id=1, source_target_pairs={{0,2},{1,3},{2,0},{3,1},{4,6},{5,7},{6,4},{7,5},{8,10},{9,11},{10,... | collective-permute-start | bytes 589832 | tf_op jit(solution)/shard_map/ppermute | solution.py:194
  103.1 10.3 %collective-permute-start.21 = (f32[128,384]{1,0:T(8,128)S(1)}, f32[128,384]{1,0:T(8,128)S(1)}, u32[]{:S(2)}, u32[]{:S(2)}) collective-permute-start(f32[128,384]{1,0:T(8,128)S(1)} %add.317.refs_0_), channel_id=1, source_target_pairs={{0,16},{8,24},{16,0},{24,8},{1,17},{9,25},{17,1},{25,9},{2,18},{10... | collective-permute-start | bytes 589832 | tf_op jit(solution)/shard_map/ppermute | solution.py:194
  141.4 10.2 %collective-permute-start.26 = (bf16[2,128,512]{2,1,0:T(8,128)(2,1)S(1)}, bf16[2,128,512]{2,1,0:T(8,128)(2,1)S(1)}, u32[]{:S(2)}, u32[]{:S(2)}) collective-permute-start(bf16[2,128,512]{2,1,0:T(8,128)(2,1)S(1)} %fusion.13), channel_id=1, source_target_pairs={{0,24},{8,16},{16,8},{24,0},{1,25},{9,17},{17,9},{25,1},{2,26},{10... | collective-permute-start | bytes 786440 | tf_op jit(solution)/shard_map/ppermute | solution.py:194
  143.7 12.8 %collective-permute-start.25 = (bf16[2,128,512]{2,1,0:T(8,128)(2,1)S(1)}, bf16[2,128,512]{2,1,0:T(8,128)(2,1)S(1)}, u32[]{:S(2)}, u32[]{:S(2)}) collective-permute-start(bf16[2,128,512]{2,1,0:T(8,128)(2,1)S(1)} %fusion.13), channel_id=1, source_target_pairs={{0,16},{8,24},{16,0},{24,8},{1,17},{9,25},{17,1},{25,9},{2,18},{10... | collective-permute-start | bytes 786440 | tf_op jit(solution)/shard_map/ppermute | solution.py:194
  144.4 12.2 %collective-permute-start.24 = (bf16[2,128,512]{2,1,0:T(8,128)(2,1)S(1)}, bf16[2,128,512]{2,1,0:T(8,128)(2,1)S(1)}, u32[]{:S(2)}, u32[]{:S(2)}) collective-permute-start(bf16[2,128,512]{2,1,0:T(8,128)(2,1)S(1)} %fusion.13), channel_id=1, source_target_pairs={{0,8},{8,0},{16,24},{24,16},{1,9},{9,1},{17,25},{25,17},{2,10},{10... | collective-permute-start | bytes 786440 | tf_op jit(solution)/shard_map/ppermute | solution.py:194
  169.6 13.8 %collective-permute-start.30 = (f32[64,1024]{0,1:T(8,128)S(1)}, f32[64,1024]{0,1:T(8,128)S(1)}, u32[]{:S(2)}, u32[]{:S(2)}) collective-permute-start(f32[64,1024]{0,1:T(8,128)S(1)} %constant_dynamic-slice_fusion), channel_id=1, source_target_pairs={{0,4},{4,0},{1,5},{5,1},{2,6},{6,2},{3,7},{7,3},{8,12},{12,8},{9,1... | collective-permute-start | bytes 786440 | tf_op jit(solution)/shard_map/ppermute | solution.py:194
  169.7 13.7 %collective-permute-start.29 = (f32[128,384]{1,0:T(8,128)S(1)}, f32[128,384]{1,0:T(8,128)S(1)}, u32[]{:S(2)}, u32[]{:S(2)}) collective-permute-start(f32[128,384]{1,0:T(8,128)S(1)} %fusion.88), channel_id=1, source_target_pairs={{0,2},{1,3},{2,0},{3,1},{4,6},{5,7},{6,4},{7,5},{8,10},{9,11},{10,... | collective-permute-start | bytes 589832 | tf_op jit(solution)/shard_map/ppermute | solution.py:194
  184.9 10.6 %collective-permute-start.32 = (f32[128,384]{1,0:T(8,128)S(1)}, f32[128,384]{1,0:T(8,128)S(1)}, u32[]{:S(2)}, u32[]{:S(2)}) collective-permute-start(f32[128,384]{1,0:T(8,128)S(1)} %add.322.refs_0_), channel_id=1, source_target_pairs={{0,16},{8,24},{16,0},{24,8},{1,17},{9,25},{17,1},{25,9},{2,18},{10... | collective-permute-start | bytes 589832 | tf_op jit(solution)/shard_map/ppermute | solution.py:194
  (43 other events, 208.4 us)
Sparse Core Ops, SparseCore 0:
  16.7 44.5 all-gather.2
  89.2 47.7 all-gather.4
  188.2 19.7 reduce-scatter.3

commit v12 on v11

--- a/solution.py
+++ b/solution.py
@@ -362,10 +362,18 @@
         ],
         axis=1,
     )
+    rows = split(lax.dynamic_slice_in_dim(image, tok_pos * slice_rows, slice_rows, 1))
+    rows = jnp.concatenate([rows[0], rows[0], rows[1]], axis=2)
+    placed, rows = lax.optimization_barrier((placed, rows))
     of_block, of_group, placed = factor(image, True, placed)
-    rows = lax.dynamic_slice_in_dim(image, tok_pos * slice_rows, slice_rows, 1)
     by_own, by_other = [
-        jnp.einsum("obr,sr->obs", rows, inverse, precision=HIGH) for inverse in of_block
+        jnp.einsum(
+            "obk,sk->obs",
+            rows,
+            jnp.concatenate([split(inverse)[i] for i in (0, 1, 0)], axis=1),
+            preferred_element_type=jnp.float32,
+        )
+        for inverse in of_block
     ]
     basis = jnp.where((own_groups == gr_pos)[:, None, None], by_own, by_other)
     latent = jnp.concatenate(

time: 231 us -> 231 us (level)
  matrix products: 27.4 us -> 24.8 us
    dot_general x2, matrix products: 5.5 us -> 2.99 us  [per_device(): jnp.einsum('obk,sk->obs', rows, jnp.concatenate([split(inverse)[i] for i...]
where the time goes in v12:
time: 231 us
  waiting for transfers between devices  79 us (34%)
  starting transfers between devices  46.4 us (20%)
  Pallas kernels  38.8 us (17%)
  matrix products  24.8 us (11%)
  between operations  15.9 us (7%)
  local copies, waits for them, and re-layouts  14.7 us (6%)
  other arithmetic  11.4 us (5%)
    ppermute x35, waiting for transfers between devices, swap(): lax.ppermute(value, axis, [(i, i ^ k) for i in range(lax.axis_size(axis))])  76.1 us
    ppermute x35, starting transfers between devices, swap(): lax.ppermute(value, axis, [(i, i ^ k) for i in range(lax.axis_size(axis))])  46.3 us
    pallas_call x2, Pallas kernels, inverse_factor(): pl.pallas_call(functools.partial(factor_kernel, scale, exact), out_shape=...  38.8 us
    dot_general x2, matrix products, image_of(): jnp.einsum('tob,otr->obr', full_x, full, preferred_element_type=jnp.float32)  4.88 us
  transfers between devices with their start and end apart: 38, of which 24 were waited for; matrix products, arithmetic and copies ran while one was open for 13% of the time, Pallas kernels for 17%

profile of v12, /device:TPU:0, one launch (start us, length us, event | category | flops | bytes accessed | tf_op | source)
XLA Modules:
  0.0 230.9 jit_solution(9270398037187574866)
XLA Ops:
  8.6 4.0 %collective-permute-start.2 = (bf16[2,256,256]{2,1,0:T(8,128)(2,1)S(1)}, bf16[2,256,256]{2,1,0:T(8,128)(2,1)S(1)}, u32[]{:S(2)}, u32[]{:S(2)}) collective-permute-start(bf16[2,256,256]{2,1,0:T(8,128)(2,1)S(1)} %get-tuple-element.80), channel_id=1, source_target_pairs={{0,24},{8,16},{16,8},{24,0},{1,25},{9,17},{17,9},{25,1},{2,26},{10... | collective-permute-start | bytes 786440 | tf_op jit(solution)/shard_map/ppermute | solution.py:194
  13.2 2.8 %collective-permute-start.5 = (bf16[2,256,256]{2,1,0:T(8,128)(2,1)S(1)}, bf16[2,256,256]{2,1,0:T(8,128)(2,1)S(1)}, u32[]{:S(2)}, u32[]{:S(2)}) collective-permute-start(bf16[2,256,256]{2,1,0:T(8,128)(2,1)S(1)} %get-tuple-element.81), channel_id=1, source_target_pairs={{0,24},{8,16},{16,8},{24,0},{1,25},{9,17},{17,9},{25,1},{2,26},{10... | collective-permute-start | bytes 786440 | tf_op jit(solution)/shard_map/ppermute | solution.py:194
  31.4 4.4 %collective-permute-done.5 = bf16[2,256,256]{2,1,0:T(8,128)(2,1)S(1)} collective-permute-done((bf16[2,256,256]{2,1,0:T(8,128)(2,1)S(1)}, bf16[2,256,256]{2,1,0:T(8,128)(2,1)S(1)}, u32[]{:S(2)}, u32[]{:S(2)}) %collective-permute-start.5) | collective-permute-done | bytes 262176 | tf_op jit(solution)/shard_map/ppermute | solution.py:194
  35.8 3.6 %collective-permute-start.8 = (bf16[2,128,256]{2,1,0:T(8,128)(2,1)S(1)}, bf16[2,128,256]{2,1,0:T(8,128)(2,1)S(1)}, u32[]{:S(2)}, u32[]{:S(2)}) collective-permute-start(bf16[2,128,256]{2,1,0:T(8,128)(2,1)S(1)} %convolution_convert_fusion.1), channel_id=1, source_target_pairs={{0,3},{1,2},{2,1},{3,0},{4,7},{5,6},{6,5},{7,4},{8,11},{9,10},{10,... | collective-permute-start | bytes 393224 | tf_op jit(solution)/shard_map/ppermute | solution.py:194
  48.3 7.4 %collective-permute-done.11 = bf16[2,128,256]{2,1,0:T(8,128)(2,1)S(1)} collective-permute-done((bf16[2,128,256]{2,1,0:T(8,128)(2,1)S(1)}, bf16[2,128,256]{2,1,0:T(8,128)(2,1)S(1)}, u32[]{:S(2)}, u32[]{:S(2)}) %collective-permute-start.11) | collective-permute-done | bytes 131104 | tf_op jit(solution)/shard_map/ppermute | solution.py:194
  68.2 5.3 %collective-permute-done.15 = bf16[2,128,512]{2,1,0:T(8,128)(2,1)} collective-permute-done((bf16[2,128,512]{2,1,0:T(8,128)(2,1)S(1)}, bf16[2,128,512]{2,1,0:T(8,128)(2,1)}, u32[]{:S(2)}, u32[]{:S(2)}) %collective-permute-start.15) | collective-permute-done | bytes 262176 | tf_op jit(solution)/shard_map/ppermute | solution.py:194
  73.5 3.6 %multiply_add_fusion.1 = f32[2,1024,512]{2,1,0:T(8,128)S(1)} fusion(bf16[2,1024,512]{2,1,0:T(8,128)(2,1)} %maximum_maximum_fusion, bf16[512,2,1024]{0,2,1:T(8,128)(2,1)} %bitcast.119, bf16[2,128,512]{2,1,0:T(8,128)(2,1)S(1)} %collective-permute-done.16, bf16[2,128,512]{2,1,0:T(8,128)(2,1)} %collective-permute-done.15, ...), kind=kOutput, calls=%fused_computation.8 | convolution fusion | flops 1083179008 | bytes 9437184 | tf_op jit(solution)/shard_map/tob,otr->obr/dot_general | solution.py:284
  83.8 4.3 %collective-permute-done.18 = f32[128,384]{1,0:T(8,128)S(1)} collective-permute-done((f32[128,384]{1,0:T(8,128)S(1)}, f32[128,384]{1,0:T(8,128)S(1)}, u32[]{:S(2)}, u32[]{:S(2)}) %collective-permute-start.18) | collective-permute-done | bytes 196640 | tf_op jit(solution)/shard_map/ppermute | solution.py:194
  89.2 3.7 %collective-permute-start.19 = (f32[128,384]{1,0:T(8,128)S(1)}, f32[128,384]{1,0:T(8,128)S(1)}, u32[]{:S(2)}, u32[]{:S(2)}) collective-permute-start(f32[128,384]{1,0:T(8,128)S(1)} %fusion.98), channel_id=1, source_target_pairs={{0,2},{1,3},{2,0},{3,1},{4,6},{5,7},{6,4},{7,5},{8,10},{9,11},{10,... | collective-permute-start | bytes 589832 | tf_op jit(solution)/shard_map/ppermute | solution.py:194
  92.9 8.8 %collective-permute-done.19 = f32[128,384]{1,0:T(8,128)S(1)} collective-permute-done((f32[128,384]{1,0:T(8,128)S(1)}, f32[128,384]{1,0:T(8,128)S(1)}, u32[]{:S(2)}, u32[]{:S(2)}) %collective-permute-start.19) | collective-permute-done | bytes 196640 | tf_op jit(solution)/shard_map/ppermute | solution.py:194
  105.3 5.3 %collective-permute-done.22.refs_3_ = f32[128,384]{1,0:T(8,128)S(1)} collective-permute-done((f32[128,384]{1,0:T(8,128)S(1)}, f32[128,384]{1,0:T(8,128)S(1)}, u32[]{:S(2)}, u32[]{:S(2)}) %collective-permute-start.22) | collective-permute-done | bytes 196640 | tf_op jit(solution)/shard_map/ppermute | solution.py:194
  110.5 2.8 %collective-permute-done.21.refs_2_ = f32[128,384]{1,0:T(8,128)S(1)} collective-permute-done((f32[128,384]{1,0:T(8,128)S(1)}, f32[128,384]{1,0:T(8,128)S(1)}, u32[]{:S(2)}, u32[]{:S(2)}) %collective-permute-start.21) | collective-permute-done | bytes 196640 | tf_op jit(solution)/shard_map/ppermute | solution.py:194
  113.5 18.8 %inverse_factor.2 = f32[512,512]{1,0:T(8,128)S(1)} custom-call(s32[1]{0:T(128)} %bitcast.1.pos_ref, f32[128,384]{1,0:T(8,128)S(1)} %add.317.refs_0_, f32[128,384]{1,0:T(8,128)S(1)} %collective-permute-done.20.refs_1_, f32[128,384]{1,0:T(8,128)S(1)} %collective-permute-done.21.refs_2_, f32[128,384]{1,0:T(8,128)S(1)} %collective-permute-done.22.refs_3_), custom_call_target="tpu_custom_call" | custom-call | flops 12884901888 | bytes 2097152 | tf_op jit(solution)/shard_map/inverse_factor/pallas_call | solution.py:171
  134.2 2.8 %all-gather.5.cloned.1.call-done = f32[16,128,512]{2,1,0:T(8,128)} async-done(((f32[2,128,512]{2,1,0:T(8,128)}), f32[16,128,512]{2,1,0:T(8,128)}) %all-gather.5.cloned.1.call-update) | async-done | bytes 4194320 | tf_op jit(solution)/shard_map/all_gather | solution.py:350
  137.1 2.9 %multiply_reduce_fusion = f32[2,128,512]{2,1,0:T(8,128)S(1)} fusion(f32[16,128,512]{2,1,0:T(8,128)} %all-gather.5.cloned.1.call-done, f32[2,16]{1,0:T(2,128)S(1)} %constant_dynamic-slice_fusion.4), kind=kLoop, calls=%fused_computation | loop fusion | flops 4063232 | bytes 4718720 | tf_op jit(solution)/shard_map/reduce_sum | solution.py:351
  145.0 4.0 %fusion.8 = bf16[2,1024,512]{2,1,0:T(8,128)(2,1)S(1)} fusion(f32[2,1024,512]{2,1,0:T(8,128)S(1)} %copy-done.1, f32[1,512,512]{2,1,0:T(8,128)S(1)} %get-tuple-element.59, f32[1,512,512]{2,1,0:T(8,128)S(1)} %get-tuple-element.58), kind=kOutput, calls=%fused_computation.16 | convolution fusion | flops 3221749760 | bytes 8388608 | tf_op jit(solution)/shard_map/obr,osr->obs/dot_general | solution.py:355
  151.6 4.9 %collective-permute-done.25 = bf16[2,128,512]{2,1,0:T(8,128)(2,1)S(1)} collective-permute-done((bf16[2,128,512]{2,1,0:T(8,128)(2,1)S(1)}, bf16[2,128,512]{2,1,0:T(8,128)(2,1)S(1)}, u32[]{:S(2)}, u32[]{:S(2)}) %collective-permute-start.25) | collective-permute-done | bytes 262176 | tf_op jit(solution)/shard_map/ppermute | solution.py:194
  157.8 2.8 %multiply_reduce_fusion.1 = (f32[128,512]{1,0:T(8,128)S(1)}, f32[128,512]{1,0:T(8,128)S(1)}) fusion(f32[2]{0:T(128)S(1)} %copy-done.24, f32[2]{0:T(128)S(1)} %copy-done.25, f32[2,1024,512]{2,1,0:T(8,128)S(1)} %multiply_add_fusion, s32[]{:T(128)S(6)} %select_n.352), kind=kOutput, calls=%fused_computation.90 | convolution fusion | flops 1611005952 | bytes 5768196 | tf_op jit(solution)/shard_map/obr,obs->ors/dot_general | solution.py:302
  165.7 4.8 %collective-permute-done.28 = f32[128,384]{1,0:T(8,128)S(1)} collective-permute-done((f32[128,384]{1,0:T(8,128)S(1)}, f32[128,384]{1,0:T(8,128)S(1)}, u32[]{:S(2)}, u32[]{:S(2)}) %collective-permute-start.28) | collective-permute-done | bytes 196640 | tf_op jit(solution)/shard_map/ppermute | solution.py:194
  170.9 4.0 %collective-permute-start.29 = (f32[128,384]{1,0:T(8,128)S(1)}, f32[128,384]{1,0:T(8,128)S(1)}, u32[]{:S(2)}, u32[]{:S(2)}) collective-permute-start(f32[128,384]{1,0:T(8,128)S(1)} %fusion.97), channel_id=1, source_target_pairs={{0,2},{1,3},{2,0},{3,1},{4,6},{5,7},{6,4},{7,5},{8,10},{9,11},{10,... | collective-permute-start | bytes 589832 | tf_op jit(solution)/shard_map/ppermute | solution.py:194
  174.9 9.7 %collective-permute-done.29 = f32[128,384]{1,0:T(8,128)S(1)} collective-permute-done((f32[128,384]{1,0:T(8,128)S(1)}, f32[128,384]{1,0:T(8,128)S(1)}, u32[]{:S(2)}, u32[]{:S(2)}) %collective-permute-start.29) | collective-permute-done | bytes 196640 | tf_op jit(solution)/shard_map/ppermute | solution.py:194
  189.3 4.3 %collective-permute-done.33.refs_3_ = f32[128,384]{1,0:T(8,128)S(1)} collective-permute-done((f32[128,384]{1,0:T(8,128)S(1)}, f32[128,384]{1,0:T(8,128)S(1)}, u32[]{:S(2)}, u32[]{:S(2)}) %collective-permute-start.33) | collective-permute-done | bytes 196640 | tf_op jit(solution)/shard_map/ppermute | solution.py:194
  193.7 3.0 %collective-permute-done.32.refs_2_ = f32[128,384]{1,0:T(8,128)S(1)} collective-permute-done((f32[128,384]{1,0:T(8,128)S(1)}, f32[128,384]{1,0:T(8,128)S(1)}, u32[]{:S(2)}, u32[]{:S(2)}) %collective-permute-start.32) | collective-permute-done | bytes 196640 | tf_op jit(solution)/shard_map/ppermute | solution.py:194
  196.7 20.0 %inverse_factor.3 = f32[512,512]{1,0:T(8,128)S(1)} custom-call(s32[1]{0:T(128)} %bitcast.1.pos_ref, f32[128,384]{1,0:T(8,128)S(1)} %add.322.refs_0_, f32[128,384]{1,0:T(8,128)S(1)} %collective-permute-done.31.refs_1_, f32[128,384]{1,0:T(8,128)S(1)} %collective-permute-done.32.refs_2_, f32[128,384]{1,0:T(8,128)S(1)} %collective-permute-done.33.refs_3_), custom_call_target="tpu_custom_call" | custom-call | flops 12884901888 | bytes 2097152 | tf_op jit(solution)/shard_map/inverse_factor/pallas_call | solution.py:171
  (191 shorter events, 77.0 us)
Async XLA Ops:
  7.2 54.5 %all-gather.3.cloned.1.call-start = ((), (), s32[]{:S(2)}) async-start(), calls=%async_computation.1 | async-start | bytes 2621440 | tf_op jit(solution)/shard_map/all_gather | solution.py:238
  8.6 14.1 %collective-permute-start.2 = (bf16[2,256,256]{2,1,0:T(8,128)(2,1)S(1)}, bf16[2,256,256]{2,1,0:T(8,128)(2,1)S(1)}, u32[]{:S(2)}, u32[]{:S(2)}) collective-permute-start(bf16[2,256,256]{2,1,0:T(8,128)(2,1)S(1)} %get-tuple-element.80), channel_id=1, source_target_pairs={{0,24},{8,16},{16,8},{24,0},{1,25},{9,17},{17,9},{25,1},{2,26},{10... | collective-permute-start | bytes 786440 | tf_op jit(solution)/shard_map/ppermute | solution.py:194
  12.6 12.9 %collective-permute-start.1 = (bf16[2,256,256]{2,1,0:T(8,128)(2,1)S(1)}, bf16[2,256,256]{2,1,0:T(8,128)(2,1)S(1)}, u32[]{:S(2)}, u32[]{:S(2)}) collective-permute-start(bf16[2,256,256]{2,1,0:T(8,128)(2,1)S(1)} %get-tuple-element.80), channel_id=1, source_target_pairs={{0,16},{8,24},{16,0},{24,8},{1,17},{9,25},{17,1},{25,9},{2,18},{10... | collective-permute-start | bytes 786440 | tf_op jit(solution)/shard_map/ppermute | solution.py:194
  13.1 12.9 %collective-permute-start = (bf16[2,256,256]{2,1,0:T(8,128)(2,1)S(1)}, bf16[2,256,256]{2,1,0:T(8,128)(2,1)S(1)}, u32[]{:S(2)}, u32[]{:S(2)}) collective-permute-start(bf16[2,256,256]{2,1,0:T(8,128)(2,1)S(1)} %get-tuple-element.80), channel_id=1, source_target_pairs={{0,8},{8,0},{16,24},{24,16},{1,9},{9,1},{17,25},{25,17},{2,10},{10... | collective-permute-start | bytes 786440 | tf_op jit(solution)/shard_map/ppermute | solution.py:194
  13.2 22.6 %collective-permute-start.5 = (bf16[2,256,256]{2,1,0:T(8,128)(2,1)S(1)}, bf16[2,256,256]{2,1,0:T(8,128)(2,1)S(1)}, u32[]{:S(2)}, u32[]{:S(2)}) collective-permute-start(bf16[2,256,256]{2,1,0:T(8,128)(2,1)S(1)} %get-tuple-element.81), channel_id=1, source_target_pairs={{0,24},{8,16},{16,8},{24,0},{1,25},{9,17},{17,9},{25,1},{2,26},{10... | collective-permute-start | bytes 786440 | tf_op jit(solution)/shard_map/ppermute | solution.py:194
  16.1 25.1 %collective-permute-start.4 = (bf16[2,256,256]{2,1,0:T(8,128)(2,1)S(1)}, bf16[2,256,256]{2,1,0:T(8,128)(2,1)S(1)}, u32[]{:S(2)}, u32[]{:S(2)}) collective-permute-start(bf16[2,256,256]{2,1,0:T(8,128)(2,1)S(1)} %get-tuple-element.81), channel_id=1, source_target_pairs={{0,16},{8,24},{16,0},{24,8},{1,17},{9,25},{17,1},{25,9},{2,18},{10... | collective-permute-start | bytes 786440 | tf_op jit(solution)/shard_map/ppermute | solution.py:194
  16.6 120.5 %all-gather.5.cloned.1.call-start = ((), (), s32[]{:S(2)}) async-start(), calls=%async_computation.2 | async-start | bytes 4718592 | tf_op jit(solution)/shard_map/all_gather | solution.py:350
  22.7 19.0 %collective-permute-start.3 = (bf16[2,256,256]{2,1,0:T(8,128)(2,1)S(1)}, bf16[2,256,256]{2,1,0:T(8,128)(2,1)S(1)}, u32[]{:S(2)}, u32[]{:S(2)}) collective-permute-start(bf16[2,256,256]{2,1,0:T(8,128)(2,1)S(1)} %get-tuple-element.81), channel_id=1, source_target_pairs={{0,8},{8,0},{16,24},{24,16},{1,9},{9,1},{17,25},{25,17},{2,10},{10... | collective-permute-start | bytes 786440 | tf_op jit(solution)/shard_map/ppermute | solution.py:194
  27.2 20.4 %collective-permute-start.7 = (bf16[2,128,256]{2,1,0:T(8,128)(2,1)S(1)}, bf16[2,128,256]{2,1,0:T(8,128)(2,1)S(1)}, u32[]{:S(2)}, u32[]{:S(2)}) collective-permute-start(bf16[2,128,256]{2,1,0:T(8,128)(2,1)S(1)} %convolution_convert_fusion.1), channel_id=1, source_target_pairs={{0,2},{1,3},{2,0},{3,1},{4,6},{5,7},{6,4},{7,5},{8,10},{9,11},{10,... | collective-permute-start | bytes 393224 | tf_op jit(solution)/shard_map/ppermute | solution.py:194
  29.8 18.0 %collective-permute-start.6 = (bf16[2,128,256]{2,1,0:T(8,128)(2,1)S(1)}, bf16[2,128,256]{2,1,0:T(8,128)(2,1)S(1)}, u32[]{:S(2)}, u32[]{:S(2)}) collective-permute-start(bf16[2,128,256]{2,1,0:T(8,128)(2,1)S(1)} %convolution_convert_fusion.1), channel_id=1, source_target_pairs={{0,1},{1,0},{2,3},{3,2},{4,5},{5,4},{6,7},{7,6},{8,9},{9,8},{10,11... | collective-permute-start | bytes 393224 | tf_op jit(solution)/shard_map/ppermute | solution.py:194
  35.8 12.1 %collective-permute-start.8 = (bf16[2,128,256]{2,1,0:T(8,128)(2,1)S(1)}, bf16[2,128,256]{2,1,0:T(8,128)(2,1)S(1)}, u32[]{:S(2)}, u32[]{:S(2)}) collective-permute-start(bf16[2,128,256]{2,1,0:T(8,128)(2,1)S(1)} %convolution_convert_fusion.1), channel_id=1, source_target_pairs={{0,3},{1,2},{2,1},{3,0},{4,7},{5,6},{6,5},{7,4},{8,11},{9,10},{10,... | collective-permute-start | bytes 393224 | tf_op jit(solution)/shard_map/ppermute | solution.py:194
  42.9 12.8 %collective-permute-start.11 = (bf16[2,128,256]{2,1,0:T(8,128)(2,1)S(1)}, bf16[2,128,256]{2,1,0:T(8,128)(2,1)S(1)}, u32[]{:S(2)}, u32[]{:S(2)}) collective-permute-start(bf16[2,128,256]{2,1,0:T(8,128)(2,1)S(1)} %convolution_convert_fusion), channel_id=1, source_target_pairs={{0,2},{1,3},{2,0},{3,1},{4,6},{5,7},{6,4},{7,5},{8,10},{9,11},{10,... | collective-permute-start | bytes 393224 | tf_op jit(solution)/shard_map/ppermute | solution.py:194
  45.6 10.1 %collective-permute-start.10 = (bf16[2,128,256]{2,1,0:T(8,128)(2,1)S(1)}, bf16[2,128,256]{2,1,0:T(8,128)(2,1)S(1)}, u32[]{:S(2)}, u32[]{:S(2)}) collective-permute-start(bf16[2,128,256]{2,1,0:T(8,128)(2,1)S(1)} %convolution_convert_fusion), channel_id=1, source_target_pairs={{0,1},{1,0},{2,3},{3,2},{4,5},{5,4},{6,7},{7,6},{8,9},{9,8},{10,11... | collective-permute-start | bytes 393224 | tf_op jit(solution)/shard_map/ppermute | solution.py:194
  59.1 14.4 %collective-permute-start.15 = (bf16[2,128,512]{2,1,0:T(8,128)(2,1)S(1)}, bf16[2,128,512]{2,1,0:T(8,128)(2,1)}, u32[]{:S(2)}, u32[]{:S(2)}) collective-permute-start(bf16[2,128,512]{2,1,0:T(8,128)(2,1)S(1)} %pad_maximum_fusion.9), channel_id=1, source_target_pairs={{0,16},{8,24},{16,0},{24,8},{1,17},{9,25},{17,1},{25,9},{2,18},{10... | collective-permute-start | bytes 786440 | tf_op jit(solution)/shard_map/ppermute | solution.py:194
  61.1 12.4 %collective-permute-start.14 = (bf16[2,128,512]{2,1,0:T(8,128)(2,1)S(1)}, bf16[2,128,512]{2,1,0:T(8,128)(2,1)}, u32[]{:S(2)}, u32[]{:S(2)}) collective-permute-start(bf16[2,128,512]{2,1,0:T(8,128)(2,1)S(1)} %pad_maximum_fusion.9), channel_id=1, source_target_pairs={{0,8},{8,0},{16,24},{24,16},{1,9},{9,1},{17,25},{25,17},{2,10},{10... | collective-permute-start | bytes 786440 | tf_op jit(solution)/shard_map/ppermute | solution.py:194
  89.1 127.6 %reduce-scatter.4.cloned.1.call-start = ((), (), s32[]{:S(2)}) async-start(), calls=%async_computation.3 | async-start | bytes 327680
  89.2 12.5 %collective-permute-start.19 = (f32[128,384]{1,0:T(8,128)S(1)}, f32[128,384]{1,0:T(8,128)S(1)}, u32[]{:S(2)}, u32[]{:S(2)}) collective-permute-start(f32[128,384]{1,0:T(8,128)S(1)} %fusion.98), channel_id=1, source_target_pairs={{0,2},{1,3},{2,0},{3,1},{4,6},{5,7},{6,4},{7,5},{8,10},{9,11},{10,... | collective-permute-start | bytes 589832 | tf_op jit(solution)/shard_map/ppermute | solution.py:194
  103.1 10.3 %collective-permute-start.21 = (f32[128,384]{1,0:T(8,128)S(1)}, f32[128,384]{1,0:T(8,128)S(1)}, u32[]{:S(2)}, u32[]{:S(2)}) collective-permute-start(f32[128,384]{1,0:T(8,128)S(1)} %add.317.refs_0_), channel_id=1, source_target_pairs={{0,16},{8,24},{16,0},{24,8},{1,17},{9,25},{17,1},{25,9},{2,18},{10... | collective-permute-start | bytes 589832 | tf_op jit(solution)/shard_map/ppermute | solution.py:194
  141.4 10.2 %collective-permute-start.26 = (bf16[2,128,512]{2,1,0:T(8,128)(2,1)S(1)}, bf16[2,128,512]{2,1,0:T(8,128)(2,1)S(1)}, u32[]{:S(2)}, u32[]{:S(2)}) collective-permute-start(bf16[2,128,512]{2,1,0:T(8,128)(2,1)S(1)} %fusion.24), channel_id=1, source_target_pairs={{0,24},{8,16},{16,8},{24,0},{1,25},{9,17},{17,9},{25,1},{2,26},{10... | collective-permute-start | bytes 786440 | tf_op jit(solution)/shard_map/ppermute | solution.py:194
  143.7 12.8 %collective-permute-start.25 = (bf16[2,128,512]{2,1,0:T(8,128)(2,1)S(1)}, bf16[2,128,512]{2,1,0:T(8,128)(2,1)S(1)}, u32[]{:S(2)}, u32[]{:S(2)}) collective-permute-start(bf16[2,128,512]{2,1,0:T(8,128)(2,1)S(1)} %fusion.24), channel_id=1, source_target_pairs={{0,16},{8,24},{16,0},{24,8},{1,17},{9,25},{17,1},{25,9},{2,18},{10... | collective-permute-start | bytes 786440 | tf_op jit(solution)/shard_map/ppermute | solution.py:194
  144.4 12.2 %collective-permute-start.24 = (bf16[2,128,512]{2,1,0:T(8,128)(2,1)S(1)}, bf16[2,128,512]{2,1,0:T(8,128)(2,1)S(1)}, u32[]{:S(2)}, u32[]{:S(2)}) collective-permute-start(bf16[2,128,512]{2,1,0:T(8,128)(2,1)S(1)} %fusion.24), channel_id=1, source_target_pairs={{0,8},{8,0},{16,24},{24,16},{1,9},{9,1},{17,25},{25,17},{2,10},{10... | collective-permute-start | bytes 786440 | tf_op jit(solution)/shard_map/ppermute | solution.py:194
  170.8 13.9 %collective-permute-start.30 = (f32[64,1024]{0,1:T(8,128)S(1)}, f32[64,1024]{0,1:T(8,128)S(1)}, u32[]{:S(2)}, u32[]{:S(2)}) collective-permute-start(f32[64,1024]{0,1:T(8,128)S(1)} %constant_dynamic-slice_fusion), channel_id=1, source_target_pairs={{0,4},{4,0},{1,5},{5,1},{2,6},{6,2},{3,7},{7,3},{8,12},{12,8},{9,1... | collective-permute-start | bytes 786440 | tf_op jit(solution)/shard_map/ppermute | solution.py:194
  170.9 13.7 %collective-permute-start.29 = (f32[128,384]{1,0:T(8,128)S(1)}, f32[128,384]{1,0:T(8,128)S(1)}, u32[]{:S(2)}, u32[]{:S(2)}) collective-permute-start(f32[128,384]{1,0:T(8,128)S(1)} %fusion.97), channel_id=1, source_target_pairs={{0,2},{1,3},{2,0},{3,1},{4,6},{5,7},{6,4},{7,5},{8,10},{9,11},{10,... | collective-permute-start | bytes 589832 | tf_op jit(solution)/shard_map/ppermute | solution.py:194
  186.1 10.6 %collective-permute-start.32 = (f32[128,384]{1,0:T(8,128)S(1)}, f32[128,384]{1,0:T(8,128)S(1)}, u32[]{:S(2)}, u32[]{:S(2)}) collective-permute-start(f32[128,384]{1,0:T(8,128)S(1)} %add.322.refs_0_), channel_id=1, source_target_pairs={{0,16},{8,24},{16,0},{24,8},{1,17},{9,25},{17,1},{25,9},{2,18},{10... | collective-permute-start | bytes 589832 | tf_op jit(solution)/shard_map/ppermute | solution.py:194
  (43 other events, 200.2 us)
Sparse Core Ops, SparseCore 0:
  16.7 44.5 all-gather.2
  89.2 47.7 all-gather.4
  189.4 19.7 reduce-scatter.3
